TPU v7x, 768 devices: a whole 4x8x12 slice. The times are simulated.
768 devices in a mesh: grp: 8 (over x, z_hi), fsdp: 16 (over y, core), seq: 6 (over z_lo).
Axes of the slice: x: 4, y: 8, z: 12 (z_hi: 2, z_lo: 6; z = z_hi * 6 + z_lo), core: 2. Of those that a mesh axis runs over, the one named last changes fastest.
Arguments:
- latents: bfloat16 [128, 768, 1536], P(('grp', 'fsdp'), 'seq'), may hold values from -6 to 6
- norm_gain: float32 [1536], replicated, may hold values from 0.1 to 1.9
- w_qkv: bfloat16 [3, 1536, 1536], P(None, ('grp', 'fsdp'), 'seq'), may hold values from -0.15625 to 0.15625
- w_out: bfloat16 [1536, 1536], P('seq', ('grp', 'fsdp')), may hold values from -0.15625 to 0.15625
- head_temp: float32 [24], P('seq'), may hold values from 0.5 to 40
- lengths: int32 [128], P(('grp', 'fsdp')), may hold values from 384 to 768, as said below
Outputs:
- attended: bfloat16 [128, 768, 1536], P(('grp', 'fsdp'), 'seq')
Inputs may be any that keep to these rules, and one draw needn't show every extreme that they name: `lengths`: at least one clip has all 768 frames live.
All inputs are finite; a program needn't handle non-finite values.
Results may differ from a plain program's by a relative error of at most 0.02.
The roundings to bfloat16 on the way count: a program that leaves them out, or rounds other values in their place, can miss the bound.
Values may be sent and summed in bfloat16 or wider, within the bound.
No kernel may reach another device: no remote copies, remote signals or barrier semaphores. Data moves between devices by JAX's collectives and lax.ppermute only.
A program may use at most 64 MiB of HBM per device.

v0:
```python
import jax
import jax.numpy as jnp
from jax import lax
from jax.sharding import PartitionSpec as P

HD = 64


def on_device(latents, norm_gain, w_qkv, w_out, head_temp, lengths):
    frames = latents[0]
    values = frames.astype(jnp.float32)
    rms = jnp.sqrt(jnp.mean(values * values, axis=-1, keepdims=True) + 1e-06)
    normed = (values / rms * norm_gain).astype(jnp.bfloat16)
    whole = lax.all_gather(normed, "seq", axis=0, tiled=True)
    total_rows = whole.shape[0]
    local_width = w_qkv.shape[2]
    local_heads = local_width // HD
    projected = jnp.einsum(
        "ld,kde->kle",
        whole,
        lax.all_gather(w_qkv, ("grp", "fsdp"), axis=1, tiled=True),
        preferred_element_type=jnp.float32,
    ).astype(jnp.bfloat16)
    query = projected[0].reshape(total_rows, local_heads, HD)
    key_part = projected[1].reshape(total_rows, local_heads, HD)
    value = projected[2].reshape(total_rows, local_heads, HD)
    scores = jnp.einsum("qhd,khd->hqk", query, key_part, preferred_element_type=jnp.float32)
    scores = scores * (head_temp / 8.0)[:, None, None]
    live = jnp.arange(total_rows, dtype=jnp.int32) < lengths[0]
    scores = jnp.where(live[None, None, :], scores, -1e30)
    probs = jax.nn.softmax(scores, axis=-1).astype(jnp.bfloat16)
    heads_out = jnp.einsum("hqk,khd->qhd", probs, value, preferred_element_type=jnp.float32).astype(
        jnp.bfloat16
    )
    heads_out = heads_out.reshape(total_rows, local_width)
    out_piece = lax.all_gather(w_out, ("grp", "fsdp"), axis=1, tiled=True)
    summed = lax.psum_scatter(
        jnp.dot(heads_out, out_piece, preferred_element_type=jnp.float32).astype(jnp.bfloat16),
        "seq",
        scatter_dimension=0,
        tiled=True,
    )
    return summed[None]


def solution(mesh):
    in_specs = (
        P(("grp", "fsdp"), "seq", None),
        P(),
        P(None, ("grp", "fsdp"), "seq"),
        P("seq", ("grp", "fsdp")),
        P("seq"),
        P(("grp", "fsdp")),
    )
    out_specs = P(("grp", "fsdp"), "seq", None)
    return jax.shard_map(
        on_device, mesh=mesh, in_specs=in_specs, out_specs=out_specs, check_vma=False
    )
```

profile of v0, /device:TPU:1, one launch (start us, length us, event | category | flops | bytes accessed | tf_op | source)
XLA Modules:
  0.0 377.5 jit_solution(11575700481517875371)
XLA Ops:
  6.5 0.0 all-gather.4.cloned.1.call-start
  6.5 1.2 fusion.22
  7.7 1.9 fusion.24
  9.6 0.0 all-gather.4.cloned.1.call-update
  9.6 0.0 all-gather.6.cloned.1.call-start
  9.7 1.3 copy.9
  11.0 0.0 all-gather.6.cloned.1.call-update
  11.1 0.0 reduce-scatter.2.cloned.1.call-start
  11.8 275.7 %all-gather = bf16[128,12,256]{2,1,0:T(8,128)(2,1)S(1)} all-gather(bf16[1,12,256]{2,1,0:T(8,128)(2,1)} %bitcast.36), channel_id=1, replica_groups=mesh['grp'=8,'fsdp'=16,'seq'=6] {'grp','fsdp'}, dimensions={0}, use_global_device_ids=true | all-gather | bytes 792576 | tf_op jit(solution)/shard_map/all_gather | solution.py:36
  287.4 0.2 reshape.24
  287.6 0.7 broadcast_multiply_fusion
  288.3 0.0 all-gather.4.cloned.1.call-done
  288.3 0.0 all-gather.6.cloned.1.call-done
  288.3 4.7 %fusion.16 = bf16[3,768,256]{1,2,0:T(8,128)(2,1)S(1)} fusion(bf16[3,1536,256]{2,0,1:T(4,128)(2,1)} %all-gather.6.cloned.1.call-done, bf16[768,1536]{1,0:T(8,128)(2,1)} %all-gather.4.cloned.1.call-done), kind=kOutput, calls=%fused_computation.15 | convolution fusion | flops 1812529152 | bytes 5898240 | tf_op jit(solution)/shard_map/ld,kde->kle/dot_general | solution.py:18
  293.0 0.1 fusion.26
  293.1 5.5 %fusion.27 = (f32[4,768]{1,0:T(4,128)S(1)}, f32[4,768,768]{1,2,0:T(8,128)}) fusion(f32[4]{0:T(128)S(1)} %broadcast_multiply_fusion, pred[768]{0:T(1024)(128)(4,1)S(1)} %iota_compare_fusion, bf16[768,4,64]{0,2,1:T(8,128)(2,1)S(1)} %bitcast.34, bf16[768,4,64]{0,2,1:T(8,128)(2,1)S(1)} %bitcast.33), kind=kOutput, calls=%fused_computation.27 | convolution fusion | flops 311427840 | bytes 10236688 | tf_op jit(solution)/shard_map/sub | solution.py:31
  298.6 4.6 %fusion.21 = bf16[4,64,768]{2,1,0:T(8,128)(2,1)S(1)} fusion(bf16[768,4,64]{0,2,1:T(8,128)(2,1)S(1)} %bitcast.32, f32[4,768,768]{1,2,0:T(8,128)} %get-tuple-element.9, f32[4,768]{1,0:T(4,128)S(1)} %get-tuple-element.8), kind=kOutput, calls=%fused_computation.16 | convolution fusion | flops 306905088 | bytes 10235904 | tf_op jit(solution)/shard_map/hqk,khd->qhd/dot_general | solution.py:32
  303.2 2.2 convolution_convert_fusion
  305.4 0.0 reduce-scatter.2.cloned.1.call-update
  305.5 65.5 %reduce-scatter.2.cloned.1.call-done = bf16[128,1536]{1,0:T(8,128)(2,1)} async-done(((bf16[768,1536]{1,0:T(8,128)(2,1)}), bf16[128,1536]{1,0:T(8,128)(2,1)}) %reduce-scatter.2.cloned.1.call-update) | async-done | bytes 393232 | tf_op jit(solution)/shard_map/reduce_scatter | solution.py:37
  (2 shorter events, 0.0 us)
Async XLA Ops:
  6.5 281.8 %all-gather.4.cloned.1.call-start = ((), (), s32[]{:S(2)}) async-start(), calls=%async_computation.1 | async-start | bytes 2752512 | tf_op jit(solution)/shard_map/all_gather | solution.py:14
  9.6 278.7 %all-gather.6.cloned.1.call-start = ((), (), s32[]{:S(2)}) async-start(), calls=%async_computation.2 | async-start | bytes 3170304 | tf_op jit(solution)/shard_map/all_gather | solution.py:21
  11.1 359.9 %reduce-scatter.2.cloned.1.call-start = ((), (), s32[]{:S(2)}) async-start(), calls=%async_computation.3 | async-start | bytes 2752512 | tf_op jit(solution)/shard_map/reduce_scatter | solution.py:37
Sparse Core Ops, SparseCore 0:
  9.8 78.0 all-gather.3
  93.3 146.8 all-gather.5
  305.6 65.3 reduce-scatter.1
where the time goes:
time: 378 us
  blocking collectives  276 us (73%)
  waiting for transfers between devices  65.6 us (17%)
  matrix products  17 us (4%)
  between operations  13.8 us (4%)
    all_gather x1, blocking collectives, on_device(): out_piece = lax.all_gather(w_out, ('grp', 'fsdp'), axis=1, tiled=True)  276 us
    reduce_scatter x1, waiting for transfers between devices, on_device(): lax.psum_scatter(jnp.dot(heads_out, out_piece, preferred_element_type=jnp...  65.5 us
  transfers between devices with their start and end apart: 3, of which 1 were waited for; matrix products, arithmetic and copies ran while one was open for 1% of the time, Pallas kernels for 0%

commit v1 on v0

v1 whole, which is shorter than its diff:
```python
import jax
import jax.numpy as jnp
import numpy as np
from jax import lax
from jax.sharding import Mesh, PartitionSpec as P

HD = 64
AXES = ("x", "zh", "y", "c", "zl")
SIZES = (4, 2, 8, 2, 6)


def index_of(x, zh, y, c, zl):
    return (((x * 2 + zh) * 8 + y) * 2 + c) * 6 + zl


def permute(value, move):
    nx, nh, ny, nc, nl = SIZES
    pairs = [
        (index_of(x, zh, y, c, zl), index_of(*move(x, zh, y, c, zl)))
        for x in range(nx)
        for zh in range(nh)
        for y in range(ny)
        for c in range(nc)
        for zl in range(nl)
    ]
    return lax.ppermute(value, AXES, pairs)


def other_half(value):
    return permute(value, lambda x, zh, y, c, zl: (x, 1 - zh, y, c, zl))


def other_core(value):
    return permute(value, lambda x, zh, y, c, zl: (x, zh, y, 1 - c, zl))


def y_shift(value, step):
    return permute(value, lambda x, zh, y, c, zl: (x, zh, (y + step) % 8, c, zl))


def gather_by_exchange(value, axes, count):
    copies = jnp.broadcast_to(value[None], (count,) + value.shape)
    return lax.all_to_all(copies, axes, 0, 0, tiled=True)


def pair(own, other, axis):
    first = lax.axis_index(axis) == 0
    return jnp.stack([jnp.where(first, own, other), jnp.where(first, other, own)])


def gather_y_ring(value):
    y = lax.axis_index("y")
    whole = jnp.zeros((8,) + value.shape, value.dtype)

    def put(buffer, block, distance):
        return lax.dynamic_update_slice_in_dim(buffer, block[None], lax.rem(y + distance, 8), 0)

    up = down = value
    whole = put(whole, value, 0)
    for step in range(1, 5):
        up = y_shift(up, 1)
        whole = put(whole, up, 8 - step)
        if step < 4:
            down = y_shift(down, -1)
            whole = put(whole, down, step)
    return whole


def feature_at():
    c, y, x, zh, r = np.meshgrid(
        np.arange(2), np.arange(8), np.arange(4), np.arange(2), np.arange(12), indexing="ij"
    )
    return ((((x * 2 + zh) * 8 + y) * 2 + c) * 12 + r).reshape(-1).astype(np.int32)


def whole_w_qkv(w_qkv):
    rows = w_qkv.transpose(1, 0, 2).reshape(12, 768)
    halves = pair(rows, other_half(rows), "zh").reshape(24, 768)
    by_x = gather_by_exchange(halves, "x", 4)
    by_y = gather_y_ring(by_x.reshape(96, 768))
    by_core = pair(by_y, other_core(by_y), "c").reshape(1536, 768)
    place = jnp.asarray(feature_at())
    chosen = (jnp.arange(1536, dtype=jnp.int32)[:, None] == place[None, :]).astype(jnp.bfloat16)
    return jnp.dot(chosen, by_core, preferred_element_type=jnp.float32).astype(jnp.bfloat16)


def half_w_out(w_out):
    turned = w_out.T
    by_z = gather_by_exchange(turned, ("zh", "zl"), 12)
    rows = by_z.reshape(2, 6, 12, 256).transpose(0, 2, 1, 3).reshape(24, 1536)
    by_x = gather_by_exchange(rows, "x", 4)
    return lax.all_gather(by_x.reshape(96, 1536), "y", axis=0, tiled=True)


def project_out(heads_out, own_rows, other_rows):
    place = jnp.asarray(feature_at()[:768])
    core = lax.axis_index("c")
    total = 0.0
    for rows, at in ((own_rows, core), (other_rows, 1 - core)):
        part = lax.dot_general(
            heads_out, rows, (((1,), (1,)), ((), ())), preferred_element_type=jnp.float32
        ).astype(jnp.bfloat16)
        chosen = (place[:, None] + at * 12 == jnp.arange(1536, dtype=jnp.int32)[None, :]).astype(
            jnp.bfloat16
        )
        total = total + jnp.dot(part, chosen, preferred_element_type=jnp.float32)
    return total.astype(jnp.bfloat16)


def on_device(latents, norm_gain, w_qkv, w_out, head_temp, lengths):
    frames = latents[0]
    values = frames.astype(jnp.float32)
    rms = jnp.sqrt(jnp.mean(values * values, axis=-1, keepdims=True) + 1e-06)
    normed = (values / rms * norm_gain).astype(jnp.bfloat16)
    whole = lax.all_gather(normed, "zl", axis=0, tiled=True)
    total_rows = whole.shape[0]
    local_width = w_qkv.shape[2]
    local_heads = local_width // HD
    weights = lax.optimization_barrier(whole_w_qkv(w_qkv))
    own_rows = half_w_out(w_out)
    projected = jnp.dot(whole, weights, preferred_element_type=jnp.float32).astype(jnp.bfloat16)
    query, key_part, value = (
        projected[:, k * local_width : (k + 1) * local_width].reshape(total_rows, local_heads, HD)
        for k in range(3)
    )
    scores = jnp.einsum("qhd,khd->hqk", query, key_part, preferred_element_type=jnp.float32)
    scores = scores * (head_temp / 8.0)[:, None, None]
    live = jnp.arange(total_rows, dtype=jnp.int32) < lengths[0]
    scores = jnp.where(live[None, None, :], scores, -1e30)
    probs = jax.nn.softmax(scores, axis=-1).astype(jnp.bfloat16)
    heads_out = jnp.einsum("hqk,khd->qhd", probs, value, preferred_element_type=jnp.float32).astype(
        jnp.bfloat16
    )
    heads_out, own_rows = lax.optimization_barrier((heads_out, own_rows))
    other_rows = other_core(own_rows)
    blocks = heads_out.reshape(6, total_rows // 6, local_width)
    own = lax.all_to_all(blocks, "zl", 0, 0, tiled=True)
    own = own.transpose(1, 0, 2).reshape(total_rows // 6, 6 * local_width)
    attended = project_out(own, own_rows, other_rows)
    return attended[None]


def solution(mesh):
    split = Mesh(mesh.devices.reshape(SIZES), AXES)
    clip = ("x", "zh", "y", "c")
    in_specs = (
        P(clip, "zl", None),
        P(),
        P(None, clip, "zl"),
        P("zl", clip),
        P("zl"),
        P(clip),
    )
    out_specs = P(clip, "zl", None)
    return jax.shard_map(
        on_device, mesh=split, in_specs=in_specs, out_specs=out_specs, check_vma=False
    )
```

time: 378 us -> 192 us (0.51)
  blocking collectives: 276 us -> 26.3 us
  starting transfers between devices: 0.09 us -> 64.6 us
  waiting for transfers between devices: 65.6 us -> 51.8 us
  matrix products: 17 us -> 25.8 us
    all_gather x1 -> x0, blocking collectives: 276 us -> none  [on_device(): out_piece = lax.all_gather(w_out, ('grp', 'fsdp'), axis=1, tiled=True)]
    reduce_scatter x1 -> x0, waiting for transfers between devices: 65.5 us -> none  [on_device(): lax.psum_scatter(jnp.dot(heads_out, out_piece, preferred_element_type=jnp...]
    ppermute x0 -> x10, starting transfers between devices: none -> 52.9 us  [permute(): return lax.ppermute(value, AXES, pairs)]
    all_to_all x0 -> x2, blocking collectives: none -> 26.3 us  [gather_by_exchange(): return lax.all_to_all(copies, axes, 0, 0, tiled=True)]
    all_to_all x0 -> x2, waiting for transfers between devices: none -> 22.6 us  [the longest x1 17 us: on_device(): own = lax.all_to_all(blocks, 'zl', 0, 0, tiled=True)]
    all_gather x2, waiting for transfers between devices: 0.01 us -> 18.9 us  [the longest x1 18.9 us: half_w_out(): return lax.all_gather(by_x.reshape(96, 1536), 'y', axis=0, tiled=True)]
    all_to_all x0 -> x2, starting transfers between devices: none -> 11.6 us  [the longest x1 8.18 us: on_device(): own = lax.all_to_all(blocks, 'zl', 0, 0, tiled=True)]
    ppermute x0 -> x10, waiting for transfers between devices: none -> 10.3 us  [permute(): return lax.ppermute(value, AXES, pairs)]
  transfers between devices with their start and end apart: 3 -> 14, of which waited for: 1 -> 8; matrix products, arithmetic and copies ran while one was open for 1% -> 14% of each run, Pallas kernels for 0% -> 0%
where the time goes in v1:
time: 192 us
  starting transfers between devices  64.6 us (34%)
  waiting for transfers between devices  51.8 us (27%)
  blocking collectives  26.3 us (14%)
  matrix products  25.8 us (13%)
  between operations  14.5 us (8%)
  local copies, waits for them, and re-layouts  4.78 us (2%)
  other arithmetic  3.63 us (2%)
    ppermute x10, starting transfers between devices, permute(): return lax.ppermute(value, AXES, pairs)  52.9 us
    all_to_all x2, blocking collectives, gather_by_exchange(): return lax.all_to_all(copies, axes, 0, 0, tiled=True)  26.3 us
    all_gather x1, waiting for transfers between devices, half_w_out(): return lax.all_gather(by_x.reshape(96, 1536), 'y', axis=0, tiled=True)  18.9 us
    all_to_all x1, waiting for transfers between devices, on_device(): own = lax.all_to_all(blocks, 'zl', 0, 0, tiled=True)  17 us
    ppermute x10, waiting for transfers between devices, permute(): return lax.ppermute(value, AXES, pairs)  10.3 us
    all_to_all x1, starting transfers between devices, on_device(): own = lax.all_to_all(blocks, 'zl', 0, 0, tiled=True)  8.18 us
    dot_general x2, matrix products, project_out(): total = total + jnp.dot(part, chosen, preferred_element_type=jnp.float32)  7.42 us
    all_to_all x1, waiting for transfers between devices, gather_by_exchange(): return lax.all_to_all(copies, axes, 0, 0, tiled=True)  5.61 us
  transfers between devices with their start and end apart: 14, of which 8 were waited for; matrix products, arithmetic and copies ran while one was open for 14% of the time, Pallas kernels for 0%

profile of v1, /device:TPU:1, one launch (start us, length us, event | category | flops | bytes accessed | tf_op | source)
XLA Modules:
  0.0 191.5 jit_solution(1086050749561407160)
XLA Ops:
  7.7 1.9 fusion.22
  10.5 15.7 %collective-permute-start = (bf16[12,768]{1,0:T(8,128)(2,1)S(1)}, bf16[12,768]{1,0:T(8,128)(2,1)S(1)}, u32[]{:S(2)}, u32[]{:S(2)}) collective-permute-start(bf16[12,768]{1,0:T(8,128)(2,1)S(1)} %bitcast.83), channel_id=1, source_target_pairs={{0,96},{1,97},{2,98},{3,99},{4,100},{5,101},{6,102},{7,103},{8,104... | collective-permute-start | bytes 55304 | tf_op jit(solution)/shard_map/ppermute | solution.py:26
  27.5 8.7 %all_to_all.20 = bf16[4,24,768]{2,1,0:T(8,128)(2,1)S(1)} all-to-all(bf16[4,24,768]{2,1,0:T(8,128)(2,1)S(1)} %broadcast_in_dim.73), channel_id=1, replica_groups=mesh['x'=4,'zh'=2,'y'=8,'c'=2,'zl'=6] {'x'}, dimensions={0} | all-to-all | bytes 294912 | tf_op jit(solution)/shard_map/all_to_all | solution.py:43
  36.2 3.2 %collective-permute-start.1 = (bf16[96,768]{1,0:T(8,128)(2,1)S(1)}, bf16[96,768]{1,0:T(8,128)(2,1)S(1)}, u32[]{:S(2)}, u32[]{:S(2)}) collective-permute-start(bf16[96,768]{1,0:T(8,128)(2,1)S(1)} %bitcast.71), channel_id=1, source_target_pairs={{0,12},{1,13},{2,14},{3,15},{4,16},{5,17},{6,18},{7,19},{8,20},{9,... | collective-permute-start | bytes 442376 | tf_op jit(solution)/shard_map/ppermute | solution.py:26
  39.4 3.8 %collective-permute-start.2 = (bf16[96,768]{1,0:T(8,128)(2,1)S(1)}, bf16[96,768]{1,0:T(8,128)(2,1)S(1)}, u32[]{:S(2)}, u32[]{:S(2)}) collective-permute-start(bf16[96,768]{1,0:T(8,128)(2,1)S(1)} %bitcast.72), channel_id=1, source_target_pairs={{0,84},{1,85},{2,86},{3,87},{4,88},{5,89},{6,90},{7,91},{8,92},{9,... | collective-permute-start | bytes 442376 | tf_op jit(solution)/shard_map/ppermute | solution.py:26
  44.2 1.9 collective-permute-start.3
  46.2 4.6 %collective-permute-start.4 = (bf16[96,768]{1,0:T(8,128)(2,1)S(1)}, bf16[96,768]{1,0:T(8,128)(2,1)S(1)}, u32[]{:S(2)}, u32[]{:S(2)}) collective-permute-start(bf16[96,768]{1,0:T(8,128)(2,1)S(1)} %collective-permute-done.2), channel_id=1, source_target_pairs={{0,84},{1,85},{2,86},{3,87},{4,88},{5,89},{6,90},{7,91},{8,92},{9,... | collective-permute-start | bytes 442376 | tf_op jit(solution)/shard_map/ppermute | solution.py:26
  53.6 4.6 %collective-permute-start.6 = (bf16[96,768]{1,0:T(8,128)(2,1)S(1)}, bf16[96,768]{1,0:T(8,128)(2,1)S(1)}, u32[]{:S(2)}, u32[]{:S(2)}) collective-permute-start(bf16[96,768]{1,0:T(8,128)(2,1)S(1)} %collective-permute-done.4), channel_id=1, source_target_pairs={{0,84},{1,85},{2,86},{3,87},{4,88},{5,89},{6,90},{7,91},{8,92},{9,... | collective-permute-start | bytes 442376 | tf_op jit(solution)/shard_map/ppermute | solution.py:26
  59.2 1.9 collective-permute-start.7
  61.2 6.3 %collective-permute-done.7 = bf16[96,768]{1,0:T(8,128)(2,1)S(1)} collective-permute-done((bf16[96,768]{1,0:T(8,128)(2,1)S(1)}, bf16[96,768]{1,0:T(8,128)(2,1)S(1)}, u32[]{:S(2)}, u32[]{:S(2)}) %collective-permute-start.7) | collective-permute-done | bytes 147488 | tf_op jit(solution)/shard_map/ppermute | solution.py:26
  67.5 9.6 %collective-permute-start.8 = (bf16[8,96,768]{2,1,0:T(8,128)(2,1)S(1)}, bf16[8,96,768]{2,1,0:T(8,128)(2,1)S(1)}, u32[]{:S(2)}, u32[]{:S(2)}) collective-permute-start(bf16[8,96,768]{2,1,0:T(8,128)(2,1)S(1)} %bitcast_dynamic-update-slice_fusion), channel_id=1, source_target_pairs={{0,6},{1,7},{2,8},{3,9},{4,10},{5,11},{6,0},{7,1},{8,2},{9,3},{10,... | collective-permute-start | bytes 3538952 | tf_op jit(solution)/shard_map/ppermute | solution.py:26
  77.2 17.6 %all_to_all.21 = bf16[12,12,256]{2,1,0:T(8,128)(2,1)S(1)} all-to-all(bf16[12,12,256]{2,1,0:T(8,128)(2,1)S(1)} %broadcast_in_dim.83), channel_id=1, replica_groups=mesh['x'=4,'zh'=2,'y'=8,'c'=2,'zl'=6] {'zh','zl'}, dimensions={0} | all-to-all | bytes 147456 | tf_op jit(solution)/shard_map/all_to_all | solution.py:43
  95.6 3.5 %all-to-all-start.2 = ((bf16[4,24,1536]{2,1,0:T(8,128)(2,1)}), bf16[4,24,1536]{2,1,0:T(8,128)(2,1)S(1)}, u32[]{:S(2)}, u32[]{:S(2)}) async-start(bf16[4,24,1536]{2,1,0:T(8,128)(2,1)} %broadcast_in_dim.85), calls=%async_computation.2 | async-start | bytes 589824 | tf_op jit(solution)/shard_map/all_to_all | solution.py:43
  99.1 5.6 %all-to-all-done.2 = bf16[4,24,1536]{2,1,0:T(8,128)(2,1)S(1)} async-done(((bf16[4,24,1536]{2,1,0:T(8,128)(2,1)}), bf16[4,24,1536]{2,1,0:T(8,128)(2,1)S(1)}, u32[]{:S(2)}, u32[]{:S(2)}) %all-to-all-start.2) | async-done | bytes 294944 | tf_op jit(solution)/shard_map/all_to_all | solution.py:43
  107.1 4.4 %fusion.12 = bf16[1536,768]{1,0:T(8,128)(2,1)S(1)} fusion(bf16[1536,768]{1,0:T(8,128)(2,1)S(1)} %bitcast.69, s32[1536]{0:T(1024)S(1)} %copy-done.4), kind=kOutput, calls=%fused_computation.17 | convolution fusion | flops 3627417600 | bytes 4724736 | tf_op jit(solution)/shard_map/dot_general | solution.py:84
  111.5 3.8 %convolution_convert_fusion = bf16[768,768]{0,1:T(8,128)(2,1)S(1)} fusion(bf16[768,1536]{1,0:T(8,128)(2,1)} %all-gather.3.cloned.1.call-done, bf16[1536,768]{1,0:T(8,128)(2,1)S(1)} %fusion.12), kind=kOutput, calls=%fused_computation.24 | convolution fusion | flops 1812529152 | bytes 5898240 | tf_op jit(solution)/shard_map/dot_general | solution.py:121
  115.4 5.5 %fusion.25 = (f32[4,768]{1,0:T(4,128)S(1)}, f32[4,768,768]{1,2,0:T(8,128)}) fusion(f32[4]{0:T(128)S(1)} %broadcast_multiply_fusion, pred[768]{0:T(1024)(128)(4,1)S(1)} %iota_compare_fusion.14, bf16[768,4,64]{0,2,1:T(8,128)(2,1)S(1)} %bitcast.76, bf16[768,4,64]{0,2,1:T(8,128)(2,1)S(1)} %bitcast.75), kind=kOutput, calls=%fused_computation.54 | convolution fusion | flops 311427840 | bytes 10236688 | tf_op jit(solution)/shard_map/sub | solution.py:130
  120.9 4.8 %fusion.19 = bf16[768,4,64]{0,2,1:T(8,128)(2,1)S(1)} fusion(bf16[768,4,64]{0,2,1:T(8,128)(2,1)S(1)} %bitcast.74, f32[4,768,768]{1,2,0:T(8,128)} %get-tuple-element.19, f32[4,768]{1,0:T(4,128)S(1)} %get-tuple-element.18), kind=kOutput, calls=%fused_computation.26 | convolution fusion | flops 306905088 | bytes 10235904 | tf_op jit(solution)/shard_map/hqk,khd->qhd/dot_general | solution.py:131
  125.7 18.9 %all-gather.5.cloned.1.call-done = bf16[768,1536]{1,0:T(8,128)(2,1)} async-done(((bf16[96,1536]{1,0:T(8,128)(2,1)}), bf16[768,1536]{1,0:T(8,128)(2,1)}) %all-gather.5.cloned.1.call-update) | async-done | bytes 2359312 | tf_op jit(solution)/shard_map/all_gather | solution.py:92
  144.5 5.7 %collective-permute-start.9 = (bf16[768,1536]{1,0:T(8,128)(2,1)}, bf16[768,1536]{1,0:T(8,128)(2,1)}, u32[]{:S(2)}, u32[]{:S(2)}) collective-permute-start(bf16[768,1536]{1,0:T(8,128)(2,1)} %all-gather.5.cloned.1.call-done), channel_id=1, source_target_pairs={{0,6},{1,7},{2,8},{3,9},{4,10},{5,11},{6,0},{7,1},{8,2},{9,3},{10,... | collective-permute-start | bytes 7077896 | tf_op jit(solution)/shard_map/ppermute | solution.py:26
  151.8 8.2 %all-to-all-start.3 = ((bf16[6,128,256]{2,1,0:T(8,128)(2,1)}), bf16[6,128,256]{2,1,0:T(8,128)(2,1)S(1)}, u32[]{:S(2)}, u32[]{:S(2)}) async-start(bf16[6,128,256]{2,1,0:T(8,128)(2,1)} %copy.20), calls=%async_computation.3 | async-start | bytes 786432 | tf_op jit(solution)/shard_map/all_to_all | solution.py:137
  160.0 17.0 %all-to-all-done.3 = bf16[6,128,256]{2,1,0:T(8,128)(2,1)S(1)} async-done(((bf16[6,128,256]{2,1,0:T(8,128)(2,1)}), bf16[6,128,256]{2,1,0:T(8,128)(2,1)S(1)}, u32[]{:S(2)}, u32[]{:S(2)}) %all-to-all-start.3) | async-done | bytes 393248 | tf_op jit(solution)/shard_map/all_to_all | solution.py:137
  177.3 3.3 %fusion.7 = f32[128,1536]{1,0:T(8,128)S(1)} fusion(s32[768]{0:T(1024)S(1)} %get-tuple-element.17, bf16[128,1536]{0,1:T(8,128)(2,1)S(1)} %bitcast.77, bf16[768,1536]{1,0:T(8,128)(2,1)} %all-gather.5.cloned.1.call-done), kind=kOutput, calls=%fused_computation.13 | convolution fusion | flops 605257728 | bytes 3542016 | tf_op jit(solution)/shard_map/dot_general | solution.py:106
  180.6 4.1 %fusion.17 = bf16[1,128,1536]{2,1,0:T(8,128)(2,1)} fusion(f32[128,1536]{1,0:T(8,128)S(1)} %fusion.7, s32[768]{0:T(1024)S(1)} %get-tuple-element.16, bf16[128,1536]{0,1:T(8,128)(2,1)S(1)} %bitcast.78, bf16[768,1536]{1,0:T(8,128)(2,1)} %collective-permute-done.9), kind=kOutput, calls=%fused_computation.23 | convolution fusion | flops 605650944 | bytes 3935232 | tf_op jit(solution)/shard_map/dot_general | solution.py:106
  (56 shorter events, 12.5 us)
Async XLA Ops:
  6.5 105.0 %all-gather.3.cloned.1.call-start = ((), (), s32[]{:S(2)}) async-start(), calls=%async_computation.4 | async-start | bytes 2752512 | tf_op jit(solution)/shard_map/all_gather | solution.py:115
  9.6 67.5 %copy-start.1 = (bf16[256,12]{0,1:T(8,128)(2,1)S(1)}, bf16[256,12]{0,1:T(8,128)(2,1)}, u32[]{:S(2)}) copy-start(bf16[256,12]{0,1:T(8,128)(2,1)} %param.11) | copy-start | bytes 18436
  10.5 17.0 %collective-permute-start = (bf16[12,768]{1,0:T(8,128)(2,1)S(1)}, bf16[12,768]{1,0:T(8,128)(2,1)S(1)}, u32[]{:S(2)}, u32[]{:S(2)}) collective-permute-start(bf16[12,768]{1,0:T(8,128)(2,1)S(1)} %bitcast.83), channel_id=1, source_target_pairs={{0,96},{1,97},{2,98},{3,99},{4,100},{5,101},{6,102},{7,103},{8,104... | collective-permute-start | bytes 55304 | tf_op jit(solution)/shard_map/ppermute | solution.py:26
  36.2 8.0 %collective-permute-start.1 = (bf16[96,768]{1,0:T(8,128)(2,1)S(1)}, bf16[96,768]{1,0:T(8,128)(2,1)S(1)}, u32[]{:S(2)}, u32[]{:S(2)}) collective-permute-start(bf16[96,768]{1,0:T(8,128)(2,1)S(1)} %bitcast.71), channel_id=1, source_target_pairs={{0,12},{1,13},{2,14},{3,15},{4,16},{5,17},{6,18},{7,19},{8,20},{9,... | collective-permute-start | bytes 442376 | tf_op jit(solution)/shard_map/ppermute | solution.py:26
  39.4 6.7 %collective-permute-start.2 = (bf16[96,768]{1,0:T(8,128)(2,1)S(1)}, bf16[96,768]{1,0:T(8,128)(2,1)S(1)}, u32[]{:S(2)}, u32[]{:S(2)}) collective-permute-start(bf16[96,768]{1,0:T(8,128)(2,1)S(1)} %bitcast.72), channel_id=1, source_target_pairs={{0,84},{1,85},{2,86},{3,87},{4,88},{5,89},{6,90},{7,91},{8,92},{9,... | collective-permute-start | bytes 442376 | tf_op jit(solution)/shard_map/ppermute | solution.py:26
  43.4 62.7 %copy-start.3 = (f32[4]{0:T(128)S(1)}, f32[4]{0:T(128)}, u32[]{:S(2)}) copy-start(f32[4]{0:T(128)} %param.12) | copy-start | bytes 52
  44.2 7.5 %collective-permute-start.3 = (bf16[96,768]{1,0:T(8,128)(2,1)S(1)}, bf16[96,768]{1,0:T(8,128)(2,1)S(1)}, u32[]{:S(2)}, u32[]{:S(2)}) collective-permute-start(bf16[96,768]{1,0:T(8,128)(2,1)S(1)} %collective-permute-done.1), channel_id=1, source_target_pairs={{0,12},{1,13},{2,14},{3,15},{4,16},{5,17},{6,18},{7,19},{8,20},{9,... | collective-permute-start | bytes 442376 | tf_op jit(solution)/shard_map/ppermute | solution.py:26
  46.2 7.5 %collective-permute-start.4 = (bf16[96,768]{1,0:T(8,128)(2,1)S(1)}, bf16[96,768]{1,0:T(8,128)(2,1)S(1)}, u32[]{:S(2)}, u32[]{:S(2)}) collective-permute-start(bf16[96,768]{1,0:T(8,128)(2,1)S(1)} %collective-permute-done.2), channel_id=1, source_target_pairs={{0,84},{1,85},{2,86},{3,87},{4,88},{5,89},{6,90},{7,91},{8,92},{9,... | collective-permute-start | bytes 442376 | tf_op jit(solution)/shard_map/ppermute | solution.py:26
  51.7 7.5 %collective-permute-start.5 = (bf16[96,768]{1,0:T(8,128)(2,1)S(1)}, bf16[96,768]{1,0:T(8,128)(2,1)S(1)}, u32[]{:S(2)}, u32[]{:S(2)}) collective-permute-start(bf16[96,768]{1,0:T(8,128)(2,1)S(1)} %collective-permute-done.3), channel_id=1, source_target_pairs={{0,12},{1,13},{2,14},{3,15},{4,16},{5,17},{6,18},{7,19},{8,20},{9,... | collective-permute-start | bytes 442376 | tf_op jit(solution)/shard_map/ppermute | solution.py:26
  53.6 7.6 %collective-permute-start.6 = (bf16[96,768]{1,0:T(8,128)(2,1)S(1)}, bf16[96,768]{1,0:T(8,128)(2,1)S(1)}, u32[]{:S(2)}, u32[]{:S(2)}) collective-permute-start(bf16[96,768]{1,0:T(8,128)(2,1)S(1)} %collective-permute-done.4), channel_id=1, source_target_pairs={{0,84},{1,85},{2,86},{3,87},{4,88},{5,89},{6,90},{7,91},{8,92},{9,... | collective-permute-start | bytes 442376 | tf_op jit(solution)/shard_map/ppermute | solution.py:26
  59.2 8.2 %collective-permute-start.7 = (bf16[96,768]{1,0:T(8,128)(2,1)S(1)}, bf16[96,768]{1,0:T(8,128)(2,1)S(1)}, u32[]{:S(2)}, u32[]{:S(2)}) collective-permute-start(bf16[96,768]{1,0:T(8,128)(2,1)S(1)} %collective-permute-done.5), channel_id=1, source_target_pairs={{0,12},{1,13},{2,14},{3,15},{4,16},{5,17},{6,18},{7,19},{8,20},{9,... | collective-permute-start | bytes 442376 | tf_op jit(solution)/shard_map/ppermute | solution.py:26
  67.5 38.6 %collective-permute-start.8 = (bf16[8,96,768]{2,1,0:T(8,128)(2,1)S(1)}, bf16[8,96,768]{2,1,0:T(8,128)(2,1)S(1)}, u32[]{:S(2)}, u32[]{:S(2)}) collective-permute-start(bf16[8,96,768]{2,1,0:T(8,128)(2,1)S(1)} %bitcast_dynamic-update-slice_fusion), channel_id=1, source_target_pairs={{0,6},{1,7},{2,8},{3,9},{4,10},{5,11},{6,0},{7,1},{8,2},{9,3},{10,... | collective-permute-start | bytes 3538952 | tf_op jit(solution)/shard_map/ppermute | solution.py:26
  95.6 9.1 %all-to-all-start.2 = ((bf16[4,24,1536]{2,1,0:T(8,128)(2,1)}), bf16[4,24,1536]{2,1,0:T(8,128)(2,1)S(1)}, u32[]{:S(2)}, u32[]{:S(2)}) async-start(bf16[4,24,1536]{2,1,0:T(8,128)(2,1)} %broadcast_in_dim.85), calls=%async_computation.2 | async-start | bytes 589824 | tf_op jit(solution)/shard_map/all_to_all | solution.py:43
  99.0 45.5 %all-gather.5.cloned.1.call-start = ((), (), s32[]{:S(2)}) async-start(), calls=%async_computation.5 | async-start | bytes 2654208 | tf_op jit(solution)/shard_map/all_gather | solution.py:92
  104.7 0.7 copy-start
  106.4 0.7 copy-start.4
  125.7 34.3 %copy-start.2 = (s32[768]{0:T(1024)S(1)}, s32[768]{0:T(1024)}, u32[]{:S(2)}) copy-start(s32[768]{0:T(1024)} %constant.71.clone) | copy-start | bytes 9220
  144.5 36.0 %collective-permute-start.9 = (bf16[768,1536]{1,0:T(8,128)(2,1)}, bf16[768,1536]{1,0:T(8,128)(2,1)}, u32[]{:S(2)}, u32[]{:S(2)}) collective-permute-start(bf16[768,1536]{1,0:T(8,128)(2,1)} %all-gather.5.cloned.1.call-done), channel_id=1, source_target_pairs={{0,6},{1,7},{2,8},{3,9},{4,10},{5,11},{6,0},{7,1},{8,2},{9,3},{10,... | collective-permute-start | bytes 7077896 | tf_op jit(solution)/shard_map/ppermute | solution.py:26
  151.8 25.2 %all-to-all-start.3 = ((bf16[6,128,256]{2,1,0:T(8,128)(2,1)}), bf16[6,128,256]{2,1,0:T(8,128)(2,1)S(1)}, u32[]{:S(2)}, u32[]{:S(2)}) async-start(bf16[6,128,256]{2,1,0:T(8,128)(2,1)} %copy.20), calls=%async_computation.3 | async-start | bytes 786432 | tf_op jit(solution)/shard_map/all_to_all | solution.py:137
Sparse Core Ops, SparseCore 0:
  9.8 75.1 all-gather.2
  105.5 38.9 all-gather.4

commit v2 on v0

v2 whole, which is shorter than its diff:
```python
import jax
import jax.numpy as jnp
import numpy as np
from jax import lax
from jax.sharding import Mesh, PartitionSpec as P

HD = 64
AXES = ("x", "zh", "y", "c", "zl")
SIZES = (4, 2, 8, 2, 6)


def permute(value, move):
    pairs = []
    for place in np.ndindex(*SIZES):
        goal = move(*place)
        if goal is not None:
            pairs.append(
                (int(np.ravel_multi_index(place, SIZES)), int(np.ravel_multi_index(goal, SIZES)))
            )
    return lax.ppermute(value, AXES, pairs)


def other_core(value):
    return permute(value, lambda x, zh, y, c, zl: (x, zh, y, 1 - c, zl))


def z_shift(value, step):
    return permute(
        value,
        lambda x, zh, y, c, zl: (x, zh, y, c, zl + step) if 0 <= zl + step < 6 else None,
    )


def gather_by_exchange(value, axes, count):
    copies = jnp.broadcast_to(value[None], (count,) + value.shape)
    return lax.all_to_all(copies, axes, 0, 0, tiled=True)


def after(value, *others):
    return lax.optimization_barrier((value,) + others)[0]


def relay_frames(shard):
    ups, downs = [shard], [shard]
    for _ in range(5):
        ups.append(z_shift(ups[-1], 1))
        downs.append(z_shift(downs[-1], -1))
    return ups, downs


def in_order(ups, downs):
    place = lax.axis_index("zl")
    whole = jnp.zeros((6,) + ups[0].shape, ups[0].dtype)
    whole = lax.dynamic_update_slice_in_dim(whole, ups[0][None], place, 0)
    for ahead in range(1, 6):
        block = jnp.where(place + ahead <= 5, downs[ahead], ups[6 - ahead])
        whole = lax.dynamic_update_slice_in_dim(whole, block[None], lax.rem(place + ahead, 6), 0)
    return whole.reshape(-1, whole.shape[-1])


def by_place(own, other, axis):
    first = lax.axis_index(axis) == 0
    return jnp.where(first, own, other), jnp.where(first, other, own)


def apart_shift(value):
    return permute(
        value, lambda x, zh, y, c, zl: (x, zh, (y + 1 - 2 * c) % 8, c, zl)
    )


def stack_by_y(own, other):
    y = lax.axis_index("y")
    turn = 1 - 2 * lax.axis_index("c")
    whole = jnp.zeros((8,) + own[0].shape, own[0].dtype)
    for step, block in enumerate(own):
        at = lax.rem(y - turn * step + 8, 8)
        whole = lax.dynamic_update_slice_in_dim(whole, block[None], at, 0)
    for step in range(1, 4):
        at = lax.rem(y + turn * step + 8, 8)
        whole = lax.dynamic_update_slice_in_dim(whole, other[step - 1][None], at, 0)
    return whole


def stack_by_x(own, below, above, across):
    x = lax.axis_index("x")
    whole = jnp.zeros((4,) + own.shape, own.dtype)
    for step, block in ((0, own), (3, below), (1, above), (2, across)):
        whole = lax.dynamic_update_slice_in_dim(whole, block[None], lax.rem(x + step, 4), 0)
    return whole


def x_shift(value, step):
    return permute(value, lambda x, zh, y, c, zl: ((x + step) % 4, zh, y, c, zl))


def on_device(latents, norm_gain, w_qkv, w_out, head_temp, lengths):
    frames = latents[0]
    values = frames.astype(jnp.float32)
    rms = jnp.sqrt(jnp.mean(values * values, axis=-1, keepdims=True) + 1e-06)
    normed = (values / rms * norm_gain).astype(jnp.bfloat16)
    ups, downs = relay_frames(normed)

    rows = w_qkv.transpose(1, 0, 2).reshape(12, 768)
    rows = jnp.concatenate(by_place(rows, other_core(rows), "c"))
    by_x = gather_by_exchange(after(rows, normed), ("x", "zh"), 8)
    block = by_x.reshape(192, 768)
    steps = [block]
    for step in range(1, 5):
        ready = steps[-1]
        if step == 2:
            ready = after(ready, ups[2], downs[2])
        if step == 4:
            ready = after(ready, ups[3], downs[3])
        steps.append(apart_shift(ready))
    others = other_core(after(jnp.stack(steps[1:4]), ups[4], downs[4]))
    by_y = stack_by_y(steps, others).reshape(8, 8, 24, 768)
    weights = lax.optimization_barrier(by_y.transpose(1, 0, 2, 3).reshape(1536, 768))

    by_z = gather_by_exchange(after(w_out.T, steps[1]), ("zh", "zl"), 12)
    by_z = by_z.reshape(2, 2, 3, 12, 256)
    mine, given = by_place(by_z[:, 0], by_z[:, 1], "c")
    first, second = by_place(mine, other_core(given), "c")
    columns = jnp.stack([first, second], axis=1)
    columns = columns.transpose(0, 1, 3, 2, 4).reshape(48, 768)
    out_by_y = gather_by_exchange(after(columns, steps[2]), "y", 8).reshape(384, 768)
    out_by_y = after(out_by_y, ups[5], downs[5], others)
    out_by_x = stack_by_x(
        out_by_y, x_shift(out_by_y, 1), x_shift(out_by_y, 3), x_shift(out_by_y, 2)
    )

    whole = in_order(ups, downs)
    total_rows = whole.shape[0]
    local_width = w_qkv.shape[2]
    local_heads = local_width // HD
    projected = jnp.dot(whole, weights, preferred_element_type=jnp.float32).astype(jnp.bfloat16)
    query, key_part, value = (
        projected[:, k * local_width : (k + 1) * local_width].reshape(total_rows, local_heads, HD)
        for k in range(3)
    )
    scores = jnp.einsum("qhd,khd->hqk", query, key_part, preferred_element_type=jnp.float32)
    scores = scores * (head_temp / 8.0)[:, None, None]
    live = jnp.arange(total_rows, dtype=jnp.int32) < lengths[0]
    scores = jnp.where(live[None, None, :], scores, -1e30)
    probs = jax.nn.softmax(scores, axis=-1).astype(jnp.bfloat16)
    heads_out = jnp.einsum("hqk,khd->qhd", probs, value, preferred_element_type=jnp.float32).astype(
        jnp.bfloat16
    )
    blocks = heads_out.reshape(6, total_rows // 6, local_width)
    own = lax.all_to_all(blocks, "zl", 0, 0, tiled=True)
    out_own = out_by_x.reshape(4, 8, 2, 24, 768).transpose(0, 2, 1, 3, 4).reshape(1536, 768)
    out_other = other_core(after(out_own, blocks))
    own, out_own, out_other = lax.optimization_barrier((own, out_own, out_other))
    own = own.transpose(1, 0, 2).reshape(total_rows // 6, 6 * local_width)
    half = 3 * local_width
    mine, given = by_place(own[:, :half], own[:, half:], "c")
    attended = sum(
        lax.dot_general(part, rows, (((1,), (1,)), ((), ())), preferred_element_type=jnp.float32)
        for part, rows in ((mine, out_own), (given, out_other))
    ).astype(jnp.bfloat16)
    return attended[None]


def solution(mesh):
    split = Mesh(mesh.devices.reshape(SIZES), AXES)
    clip = ("x", "zh", "y", "c")
    in_specs = (
        P(clip, "zl", None),
        P(),
        P(None, clip, "zl"),
        P("zl", clip),
        P("zl"),
        P(clip),
    )
    out_specs = P(clip, "zl", None)
    return jax.shard_map(
        on_device, mesh=split, in_specs=in_specs, out_specs=out_specs, check_vma=False
    )
```

time: 378 us -> 196 us (0.52)
  the two profiles are of different devices: /device:TPU:1 before, /device:TPU:30 now
where the time goes in v2:
time: 196 us; the launch traced here: 194 us
  starting transfers between devices  96.6 us (49%)
  blocking collectives  28.3 us (14%)
  matrix products  18.8 us (10%)
  waiting for transfers between devices  18.6 us (9%)
  local copies, waits for them, and re-layouts  18 us (9%)
  other arithmetic  12.5 us (6%)
    ppermute x21, starting transfers between devices, permute(): return lax.ppermute(value, AXES, pairs)  64.4 us
    all_to_all x3, starting transfers between devices, gather_by_exchange(): return lax.all_to_all(copies, axes, 0, 0, tiled=True)  32.2 us
    all_to_all x1, blocking collectives, on_device(): own = lax.all_to_all(blocks, 'zl', 0, 0, tiled=True)  28.3 us
    ppermute x21, waiting for transfers between devices, permute(): return lax.ppermute(value, AXES, pairs)  17.5 us
    dynamic_update_slice x5, other arithmetic, in_order(): lax.dynamic_update_slice_in_dim(whole, block[None], lax.rem(place + ahead...  7.24 us
    sub x1, matrix products, on_device(): probs = jax.nn.softmax(scores, axis=-1).astype(jnp.bfloat16)  5.51 us
    dot_general x1, matrix products, on_device(): jnp.einsum('hqk,khd->qhd', probs, value, preferred_element_type=jnp.float32)  5.37 us
    dot_general x2, matrix products, on_device(): lax.dot_general(part, rows, (((1,), (1,)), ((), ())), preferred_element_t...  4.26 us
  transfers between devices with their start and end apart: 24, of which 3 were waited for; matrix products, arithmetic and copies ran while one was open for 20% of the time, Pallas kernels for 0%

profile of v2, /device:TPU:30, one launch (start us, length us, event | category | flops | bytes accessed | tf_op | source)
XLA Modules:
  0.0 194.2 jit_solution(10172938670062793613)
XLA Ops:
  0.8 2.1 %collective-permute-start.10 = (bf16[12,768]{1,0:T(8,128)(2,1)S(1)}, bf16[12,768]{1,0:T(8,128)(2,1)S(1)}, u32[]{:S(2)}, u32[]{:S(2)}) collective-permute-start(bf16[12,768]{1,0:T(8,128)(2,1)S(1)} %bitcast.141), channel_id=1, source_target_pairs={{0,6},{1,7},{2,8},{3,9},{4,10},{5,11},{6,0},{7,1},{8,2},{9,3},{10,... | collective-permute-start | bytes 55304 | tf_op jit(solution)/shard_map/ppermute | solution.py:20
  6.0 17.4 %all-to-all-start = ((bf16[8,24,768]{2,1,0:T(8,128)(2,1)}), bf16[8,24,768]{2,1,0:T(8,128)(2,1)S(1)}, u32[]{:S(2)}, u32[]{:S(2)}) async-start(bf16[8,24,768]{2,1,0:T(8,128)(2,1)} %broadcast_in_dim.95), calls=%async_computation | async-start | bytes 589824 | tf_op jit(solution)/shard_map/all_to_all | solution.py:36
  23.5 3.4 %collective-permute-start.1 = (bf16[128,1536]{1,0:T(8,128)(2,1)S(1)}, bf16[128,1536]{1,0:T(8,128)(2,1)S(1)}, u32[]{:S(2)}, u32[]{:S(2)}) collective-permute-start(bf16[128,1536]{1,0:T(8,128)(2,1)S(1)} %fusion.16), channel_id=1, source_target_pairs={{0,1},{1,2},{2,3},{3,4},{4,5},{6,7},{7,8},{8,9},{9,10},{10,11},{12... | collective-permute-start | bytes 1179656 | tf_op jit(solution)/shard_map/ppermute | solution.py:20
  28.2 13.7 %collective-permute-done.1 = bf16[128,1536]{1,0:T(8,128)(2,1)S(1)} collective-permute-done((bf16[128,1536]{1,0:T(8,128)(2,1)S(1)}, bf16[128,1536]{1,0:T(8,128)(2,1)S(1)}, u32[]{:S(2)}, u32[]{:S(2)}) %collective-permute-start.1) | collective-permute-done | bytes 393248 | tf_op jit(solution)/shard_map/ppermute | solution.py:20
  41.9 5.1 %collective-permute-start.2 = (bf16[128,1536]{1,0:T(8,128)(2,1)S(1)}, bf16[128,1536]{1,0:T(8,128)(2,1)}, u32[]{:S(2)}, u32[]{:S(2)}) collective-permute-start(bf16[128,1536]{1,0:T(8,128)(2,1)S(1)} %collective-permute-done.1), channel_id=1, source_target_pairs={{0,1},{1,2},{2,3},{3,4},{4,5},{6,7},{7,8},{8,9},{9,10},{10,11},{12... | collective-permute-start | bytes 1179656 | tf_op jit(solution)/shard_map/ppermute | solution.py:20
  48.4 4.7 %collective-permute-start.11 = (bf16[192,768]{1,0:T(8,128)(2,1)S(1)}, bf16[192,768]{1,0:T(8,128)(2,1)S(1)}, u32[]{:S(2)}, u32[]{:S(2)}) collective-permute-start(bf16[192,768]{1,0:T(8,128)(2,1)S(1)} %bitcast.131), channel_id=1, source_target_pairs={{0,12},{1,13},{2,14},{3,15},{4,16},{5,17},{6,90},{7,91},{8,92},{9,... | collective-permute-start | bytes 884744 | tf_op jit(solution)/shard_map/ppermute | solution.py:20
  56.3 5.3 %collective-permute-start.3 = (bf16[128,1536]{1,0:T(8,128)(2,1)}, bf16[128,1536]{1,0:T(8,128)(2,1)}, u32[]{:S(2)}, u32[]{:S(2)}) collective-permute-start(bf16[128,1536]{1,0:T(8,128)(2,1)} %collective-permute-done.2), channel_id=1, source_target_pairs={{0,1},{1,2},{2,3},{3,4},{4,5},{6,7},{7,8},{8,9},{9,10},{10,11},{12... | collective-permute-start | bytes 1179656 | tf_op jit(solution)/shard_map/ppermute | solution.py:20
  62.3 9.5 %all-to-all-start.2 = ((bf16[12,12,256]{2,1,0:T(8,128)(2,1)}), bf16[12,12,256]{2,1,0:T(8,128)(2,1)S(1)}, u32[]{:S(2)}, u32[]{:S(2)}) async-start(bf16[12,12,256]{2,1,0:T(8,128)(2,1)} %broadcast_in_dim.103), calls=%async_computation.2 | async-start | bytes 196608 | tf_op jit(solution)/shard_map/all_to_all | solution.py:36
  73.4 3.9 %collective-permute-start.12 = (bf16[192,768]{1,0:T(8,128)(2,1)S(1)}, bf16[192,768]{1,0:T(8,128)(2,1)}, u32[]{:S(2)}, u32[]{:S(2)}) collective-permute-start(bf16[192,768]{1,0:T(8,128)(2,1)S(1)} %collective-permute-done.11), channel_id=1, source_target_pairs={{0,12},{1,13},{2,14},{3,15},{4,16},{5,17},{6,90},{7,91},{8,92},{9,... | collective-permute-start | bytes 884744 | tf_op jit(solution)/shard_map/ppermute | solution.py:20
  77.2 5.3 %collective-permute-start.4 = (bf16[128,1536]{1,0:T(8,128)(2,1)}, bf16[128,1536]{1,0:T(8,128)(2,1)}, u32[]{:S(2)}, u32[]{:S(2)}) collective-permute-start(bf16[128,1536]{1,0:T(8,128)(2,1)} %collective-permute-done.3), channel_id=1, source_target_pairs={{0,1},{1,2},{2,3},{3,4},{4,5},{6,7},{7,8},{8,9},{9,10},{10,11},{12... | collective-permute-start | bytes 1179656 | tf_op jit(solution)/shard_map/ppermute | solution.py:20
  87.0 4.0 %collective-permute-start.13 = (bf16[192,768]{1,0:T(8,128)(2,1)}, bf16[192,768]{1,0:T(8,128)(2,1)S(1)}, u32[]{:S(2)}, u32[]{:S(2)}) collective-permute-start(bf16[192,768]{1,0:T(8,128)(2,1)} %collective-permute-done.12), channel_id=1, source_target_pairs={{0,12},{1,13},{2,14},{3,15},{4,16},{5,17},{6,90},{7,91},{8,92},{9,... | collective-permute-start | bytes 884744 | tf_op jit(solution)/shard_map/ppermute | solution.py:20
  92.0 5.2 %all-to-all-start.3 = ((bf16[8,48,768]{2,1,0:T(8,128)(2,1)}), bf16[8,48,768]{2,1,0:T(8,128)(2,1)S(1)}, u32[]{:S(2)}, u32[]{:S(2)}) async-start(bf16[8,48,768]{2,1,0:T(8,128)(2,1)} %broadcast_in_dim.104), calls=%async_computation.3 | async-start | bytes 1179648 | tf_op jit(solution)/shard_map/all_to_all | solution.py:36
  97.2 4.7 %collective-permute-start.5 = (bf16[128,1536]{1,0:T(8,128)(2,1)}, bf16[128,1536]{1,0:T(8,128)(2,1)S(1)}, u32[]{:S(2)}, u32[]{:S(2)}) collective-permute-start(bf16[128,1536]{1,0:T(8,128)(2,1)} %collective-permute-done.4), channel_id=1, source_target_pairs={{0,1},{1,2},{2,3},{3,4},{4,5},{6,7},{7,8},{8,9},{9,10},{10,11},{12... | collective-permute-start | bytes 1179656 | tf_op jit(solution)/shard_map/ppermute | solution.py:20
  104.2 4.6 %collective-permute-start.14 = (bf16[192,768]{1,0:T(8,128)(2,1)S(1)}, bf16[192,768]{1,0:T(8,128)(2,1)S(1)}, u32[]{:S(2)}, u32[]{:S(2)}) collective-permute-start(bf16[192,768]{1,0:T(8,128)(2,1)S(1)} %collective-permute-done.13), channel_id=1, source_target_pairs={{0,12},{1,13},{2,14},{3,15},{4,16},{5,17},{6,90},{7,91},{8,92},{9,... | collective-permute-start | bytes 884744 | tf_op jit(solution)/shard_map/ppermute | solution.py:20
  108.8 2.0 %pad_maximum_fusion = bf16[3,192,768]{2,1,0:T(8,128)(2,1)} fusion(bf16[1,192,768]{2,1,0:T(8,128)(2,1)S(1)} %bitcast.130, bf16[1,192,768]{2,1,0:T(8,128)(2,1)} %bitcast.11, bf16[1,192,768]{2,1,0:T(8,128)(2,1)S(1)} %bitcast.129), kind=kLoop, calls=%fused_computation.20 | loop fusion | flops 884736 | bytes 1769472 | tf_op jit(solution)/shard_map/stack | solution.py:116
  120.1 2.3 %collective-permute-start.17 = (bf16[384,768]{1,0:T(8,128)(2,1)S(1)}, bf16[384,768]{1,0:T(8,128)(2,1)}, u32[]{:S(2)}, u32[]{:S(2)}) collective-permute-start(bf16[384,768]{1,0:T(8,128)(2,1)S(1)} %bitcast.123), channel_id=1, source_target_pairs={{0,192},{1,193},{2,194},{3,195},{4,196},{5,197},{6,198},{7,199},{8... | collective-permute-start | bytes 1769480 | tf_op jit(solution)/shard_map/ppermute | solution.py:20
  122.3 3.6 %collective-permute-start.18 = (bf16[384,768]{1,0:T(8,128)(2,1)S(1)}, bf16[384,768]{1,0:T(8,128)(2,1)}, u32[]{:S(2)}, u32[]{:S(2)}) collective-permute-start(bf16[384,768]{1,0:T(8,128)(2,1)S(1)} %bitcast.124), channel_id=1, source_target_pairs={{0,576},{1,577},{2,578},{3,579},{4,580},{5,581},{6,582},{7,583},{8... | collective-permute-start | bytes 1769480 | tf_op jit(solution)/shard_map/ppermute | solution.py:20
  125.9 3.4 %collective-permute-start.19 = (bf16[384,768]{1,0:T(8,128)(2,1)S(1)}, bf16[384,768]{1,0:T(8,128)(2,1)}, u32[]{:S(2)}, u32[]{:S(2)}) collective-permute-start(bf16[384,768]{1,0:T(8,128)(2,1)S(1)} %bitcast.125), channel_id=1, source_target_pairs={{0,384},{1,385},{2,386},{3,387},{4,388},{5,389},{6,390},{7,391},{8... | collective-permute-start | bytes 1769480 | tf_op jit(solution)/shard_map/ppermute | solution.py:20
  132.4 3.7 %convolution_convert_fusion = bf16[768,768]{0,1:T(8,128)(2,1)S(1)} fusion(bf16[768,1536]{1,0:T(8,128)(2,1)} %bitcast.6, bf16[1536,768]{1,0:T(8,128)(2,1)S(1)} %bitcast.122), kind=kOutput, calls=%fused_computation.13 | convolution fusion | flops 1812529152 | bytes 5898240 | tf_op jit(solution)/shard_map/dot_general | solution.py:136
  136.2 5.5 %fusion.33 = (f32[4,768]{1,0:T(4,128)S(1)}, f32[4,768,768]{1,2,0:T(8,128)}) fusion(f32[4]{0:T(128)S(1)} %broadcast_multiply_fusion, pred[768]{0:T(1024)(128)(4,1)S(1)} %iota_compare_fusion, bf16[768,4,64]{0,2,1:T(8,128)(2,1)S(1)} %bitcast.137, bf16[768,4,64]{0,2,1:T(8,128)(2,1)S(1)} %bitcast.136), kind=kOutput, calls=%fused_computation.68 | convolution fusion | flops 311427840 | bytes 10236688 | tf_op jit(solution)/shard_map/sub | solution.py:145
  141.8 5.4 %fusion.11 = bf16[768,4,64]{0,2,1:T(8,128)(2,1)} fusion(bf16[768,4,64]{0,2,1:T(8,128)(2,1)S(1)} %bitcast.135, f32[4,768,768]{1,2,0:T(8,128)} %get-tuple-element.35, f32[4,768]{1,0:T(4,128)S(1)} %get-tuple-element.34), kind=kOutput, calls=%fused_computation.15 | convolution fusion | flops 306905088 | bytes 10235904 | tf_op jit(solution)/shard_map/hqk,khd->qhd/dot_general | solution.py:146
  149.9 3.7 %collective-permute-done.18 = bf16[384,768]{1,0:T(8,128)(2,1)} collective-permute-done((bf16[384,768]{1,0:T(8,128)(2,1)S(1)}, bf16[384,768]{1,0:T(8,128)(2,1)}, u32[]{:S(2)}, u32[]{:S(2)}) %collective-permute-start.18) | collective-permute-done | bytes 589856 | tf_op jit(solution)/shard_map/ppermute | solution.py:20
  161.4 28.3 %all_to_all.20 = bf16[6,128,256]{2,1,0:T(8,128)(2,1)S(1)} all-to-all(bf16[6,128,256]{2,1,0:T(8,128)(2,1)S(1)} %copy.30), channel_id=1, replica_groups=mesh['x'=4,'zh'=2,'y'=8,'c'=2,'zl'=6] {'zl'}, dimensions={0} | all-to-all | bytes 786432 | tf_op jit(solution)/shard_map/all_to_all | solution.py:150
  189.9 2.6 %fusion.20 = f32[128,1536]{1,0:T(8,128)S(1)} fusion(bf16[1536,768]{1,0:T(8,128)(2,1)} %collective-permute-done.20, pred[]{:T(512)S(6)} %eq.2, bf16[128,1536]{0,1:T(8,128)(2,1)S(1)} %bitcast.127), kind=kOutput, calls=%fused_computation.41 | convolution fusion | flops 302088192 | bytes 3538945 | tf_op jit(solution)/shard_map/dot_general | solution.py:158
  (94 shorter events, 43.6 us)
Async XLA Ops:
  0.8 4.4 %collective-permute-start.10 = (bf16[12,768]{1,0:T(8,128)(2,1)S(1)}, bf16[12,768]{1,0:T(8,128)(2,1)S(1)}, u32[]{:S(2)}, u32[]{:S(2)}) collective-permute-start(bf16[12,768]{1,0:T(8,128)(2,1)S(1)} %bitcast.141), channel_id=1, source_target_pairs={{0,6},{1,7},{2,8},{3,9},{4,10},{5,11},{6,0},{7,1},{8,2},{9,3},{10,... | collective-permute-start | bytes 55304 | tf_op jit(solution)/shard_map/ppermute | solution.py:20
  6.0 42.3 %all-to-all-start = ((bf16[8,24,768]{2,1,0:T(8,128)(2,1)}), bf16[8,24,768]{2,1,0:T(8,128)(2,1)S(1)}, u32[]{:S(2)}, u32[]{:S(2)}) async-start(bf16[8,24,768]{2,1,0:T(8,128)(2,1)} %broadcast_in_dim.95), calls=%async_computation | async-start | bytes 589824 | tf_op jit(solution)/shard_map/all_to_all | solution.py:36
  23.5 18.4 %collective-permute-start.1 = (bf16[128,1536]{1,0:T(8,128)(2,1)S(1)}, bf16[128,1536]{1,0:T(8,128)(2,1)S(1)}, u32[]{:S(2)}, u32[]{:S(2)}) collective-permute-start(bf16[128,1536]{1,0:T(8,128)(2,1)S(1)} %fusion.16), channel_id=1, source_target_pairs={{0,1},{1,2},{2,3},{3,4},{4,5},{6,7},{7,8},{8,9},{9,10},{10,11},{12... | collective-permute-start | bytes 1179656 | tf_op jit(solution)/shard_map/ppermute | solution.py:20
  26.9 20.2 %collective-permute-start = (bf16[128,1536]{1,0:T(8,128)(2,1)S(1)}, bf16[128,1536]{1,0:T(8,128)(2,1)S(1)}, u32[]{:S(2)}, u32[]{:S(2)}) collective-permute-start(bf16[128,1536]{1,0:T(8,128)(2,1)S(1)} %fusion.16), channel_id=1, source_target_pairs={{1,0},{2,1},{3,2},{4,3},{5,4},{7,6},{8,7},{9,8},{10,9},{11,10},{13... | collective-permute-start | bytes 1179656 | tf_op jit(solution)/shard_map/ppermute | solution.py:20
  41.9 14.4 %collective-permute-start.2 = (bf16[128,1536]{1,0:T(8,128)(2,1)S(1)}, bf16[128,1536]{1,0:T(8,128)(2,1)}, u32[]{:S(2)}, u32[]{:S(2)}) collective-permute-start(bf16[128,1536]{1,0:T(8,128)(2,1)S(1)} %collective-permute-done.1), channel_id=1, source_target_pairs={{0,1},{1,2},{2,3},{3,4},{4,5},{6,7},{7,8},{8,9},{9,10},{10,11},{12... | collective-permute-start | bytes 1179656 | tf_op jit(solution)/shard_map/ppermute | solution.py:20
  47.1 24.8 %collective-permute-start.6 = (bf16[128,1536]{1,0:T(8,128)(2,1)S(1)}, bf16[128,1536]{1,0:T(8,128)(2,1)}, u32[]{:S(2)}, u32[]{:S(2)}) collective-permute-start(bf16[128,1536]{1,0:T(8,128)(2,1)S(1)} %collective-permute-done), channel_id=1, source_target_pairs={{1,0},{2,1},{3,2},{4,3},{5,4},{7,6},{8,7},{9,8},{10,9},{11,10},{13... | collective-permute-start | bytes 1179656 | tf_op jit(solution)/shard_map/ppermute | solution.py:20
  48.4 13.3 %collective-permute-start.11 = (bf16[192,768]{1,0:T(8,128)(2,1)S(1)}, bf16[192,768]{1,0:T(8,128)(2,1)S(1)}, u32[]{:S(2)}, u32[]{:S(2)}) collective-permute-start(bf16[192,768]{1,0:T(8,128)(2,1)S(1)} %bitcast.131), channel_id=1, source_target_pairs={{0,12},{1,13},{2,14},{3,15},{4,16},{5,17},{6,90},{7,91},{8,92},{9,... | collective-permute-start | bytes 884744 | tf_op jit(solution)/shard_map/ppermute | solution.py:20
  56.3 20.9 %collective-permute-start.3 = (bf16[128,1536]{1,0:T(8,128)(2,1)}, bf16[128,1536]{1,0:T(8,128)(2,1)}, u32[]{:S(2)}, u32[]{:S(2)}) collective-permute-start(bf16[128,1536]{1,0:T(8,128)(2,1)} %collective-permute-done.2), channel_id=1, source_target_pairs={{0,1},{1,2},{2,3},{3,4},{4,5},{6,7},{7,8},{8,9},{9,10},{10,11},{12... | collective-permute-start | bytes 1179656 | tf_op jit(solution)/shard_map/ppermute | solution.py:20
  62.3 21.4 %all-to-all-start.2 = ((bf16[12,12,256]{2,1,0:T(8,128)(2,1)}), bf16[12,12,256]{2,1,0:T(8,128)(2,1)S(1)}, u32[]{:S(2)}, u32[]{:S(2)}) async-start(bf16[12,12,256]{2,1,0:T(8,128)(2,1)} %broadcast_in_dim.103), calls=%async_computation.2 | async-start | bytes 196608 | tf_op jit(solution)/shard_map/all_to_all | solution.py:36
  71.8 13.8 %collective-permute-start.7 = (bf16[128,1536]{1,0:T(8,128)(2,1)}, bf16[128,1536]{1,0:T(8,128)(2,1)}, u32[]{:S(2)}, u32[]{:S(2)}) collective-permute-start(bf16[128,1536]{1,0:T(8,128)(2,1)} %collective-permute-done.6), channel_id=1, source_target_pairs={{1,0},{2,1},{3,2},{4,3},{5,4},{7,6},{8,7},{9,8},{10,9},{11,10},{13... | collective-permute-start | bytes 1179656 | tf_op jit(solution)/shard_map/ppermute | solution.py:20
  73.4 13.6 %collective-permute-start.12 = (bf16[192,768]{1,0:T(8,128)(2,1)S(1)}, bf16[192,768]{1,0:T(8,128)(2,1)}, u32[]{:S(2)}, u32[]{:S(2)}) collective-permute-start(bf16[192,768]{1,0:T(8,128)(2,1)S(1)} %collective-permute-done.11), channel_id=1, source_target_pairs={{0,12},{1,13},{2,14},{3,15},{4,16},{5,17},{6,90},{7,91},{8,92},{9,... | collective-permute-start | bytes 884744 | tf_op jit(solution)/shard_map/ppermute | solution.py:20
  77.2 20.0 %collective-permute-start.4 = (bf16[128,1536]{1,0:T(8,128)(2,1)}, bf16[128,1536]{1,0:T(8,128)(2,1)}, u32[]{:S(2)}, u32[]{:S(2)}) collective-permute-start(bf16[128,1536]{1,0:T(8,128)(2,1)} %collective-permute-done.3), channel_id=1, source_target_pairs={{0,1},{1,2},{2,3},{3,4},{4,5},{6,7},{7,8},{8,9},{9,10},{10,11},{12... | collective-permute-start | bytes 1179656 | tf_op jit(solution)/shard_map/ppermute | solution.py:20
  83.7 3.3 %collective-permute-start.16 = (bf16[2,3,12,256]{3,2,1,0:T(8,128)(2,1)S(1)}, bf16[2,3,12,256]{3,2,1,0:T(8,128)(2,1)S(1)}, u32[]{:S(2)}, u32[]{:S(2)}) collective-permute-start(bf16[2,3,12,256]{3,2,1,0:T(8,128)(2,1)S(1)} %fusion.29), channel_id=1, source_target_pairs={{0,6},{1,7},{2,8},{3,9},{4,10},{5,11},{6,0},{7,1},{8,2},{9,3},{10,... | collective-permute-start | bytes 110600 | tf_op jit(solution)/shard_map/ppermute | solution.py:20
  85.6 17.3 %collective-permute-start.8 = (bf16[128,1536]{1,0:T(8,128)(2,1)}, bf16[128,1536]{1,0:T(8,128)(2,1)}, u32[]{:S(2)}, u32[]{:S(2)}) collective-permute-start(bf16[128,1536]{1,0:T(8,128)(2,1)} %collective-permute-done.7), channel_id=1, source_target_pairs={{1,0},{2,1},{3,2},{4,3},{5,4},{7,6},{8,7},{9,8},{10,9},{11,10},{13... | collective-permute-start | bytes 1179656 | tf_op jit(solution)/shard_map/ppermute | solution.py:20
  87.0 17.2 %collective-permute-start.13 = (bf16[192,768]{1,0:T(8,128)(2,1)}, bf16[192,768]{1,0:T(8,128)(2,1)S(1)}, u32[]{:S(2)}, u32[]{:S(2)}) collective-permute-start(bf16[192,768]{1,0:T(8,128)(2,1)} %collective-permute-done.12), channel_id=1, source_target_pairs={{0,12},{1,13},{2,14},{3,15},{4,16},{5,17},{6,90},{7,91},{8,92},{9,... | collective-permute-start | bytes 884744 | tf_op jit(solution)/shard_map/ppermute | solution.py:20
  92.0 28.1 %all-to-all-start.3 = ((bf16[8,48,768]{2,1,0:T(8,128)(2,1)}), bf16[8,48,768]{2,1,0:T(8,128)(2,1)S(1)}, u32[]{:S(2)}, u32[]{:S(2)}) async-start(bf16[8,48,768]{2,1,0:T(8,128)(2,1)} %broadcast_in_dim.104), calls=%async_computation.3 | async-start | bytes 1179648 | tf_op jit(solution)/shard_map/all_to_all | solution.py:36
  97.2 15.5 %collective-permute-start.5 = (bf16[128,1536]{1,0:T(8,128)(2,1)}, bf16[128,1536]{1,0:T(8,128)(2,1)S(1)}, u32[]{:S(2)}, u32[]{:S(2)}) collective-permute-start(bf16[128,1536]{1,0:T(8,128)(2,1)} %collective-permute-done.4), channel_id=1, source_target_pairs={{0,1},{1,2},{2,3},{3,4},{4,5},{6,7},{7,8},{8,9},{9,10},{10,11},{12... | collective-permute-start | bytes 1179656 | tf_op jit(solution)/shard_map/ppermute | solution.py:20
  102.9 16.2 %collective-permute-start.9 = (bf16[128,1536]{1,0:T(8,128)(2,1)}, bf16[128,1536]{1,0:T(8,128)(2,1)S(1)}, u32[]{:S(2)}, u32[]{:S(2)}) collective-permute-start(bf16[128,1536]{1,0:T(8,128)(2,1)} %collective-permute-done.8), channel_id=1, source_target_pairs={{1,0},{2,1},{3,2},{4,3},{5,4},{7,6},{8,7},{9,8},{10,9},{11,10},{13... | collective-permute-start | bytes 1179656 | tf_op jit(solution)/shard_map/ppermute | solution.py:20
  104.2 15.8 %collective-permute-start.14 = (bf16[192,768]{1,0:T(8,128)(2,1)S(1)}, bf16[192,768]{1,0:T(8,128)(2,1)S(1)}, u32[]{:S(2)}, u32[]{:S(2)}) collective-permute-start(bf16[192,768]{1,0:T(8,128)(2,1)S(1)} %collective-permute-done.13), channel_id=1, source_target_pairs={{0,12},{1,13},{2,14},{3,15},{4,16},{5,17},{6,90},{7,91},{8,92},{9,... | collective-permute-start | bytes 884744 | tf_op jit(solution)/shard_map/ppermute | solution.py:20
  110.8 9.3 %collective-permute-start.15 = (bf16[3,192,768]{2,1,0:T(8,128)(2,1)}, bf16[3,192,768]{2,1,0:T(8,128)(2,1)}, u32[]{:S(2)}, u32[]{:S(2)}) collective-permute-start(bf16[3,192,768]{2,1,0:T(8,128)(2,1)} %pad_maximum_fusion), channel_id=1, source_target_pairs={{0,6},{1,7},{2,8},{3,9},{4,10},{5,11},{6,0},{7,1},{8,2},{9,3},{10,... | collective-permute-start | bytes 2654216 | tf_op jit(solution)/shard_map/ppermute | solution.py:20
  120.1 28.7 %collective-permute-start.17 = (bf16[384,768]{1,0:T(8,128)(2,1)S(1)}, bf16[384,768]{1,0:T(8,128)(2,1)}, u32[]{:S(2)}, u32[]{:S(2)}) collective-permute-start(bf16[384,768]{1,0:T(8,128)(2,1)S(1)} %bitcast.123), channel_id=1, source_target_pairs={{0,192},{1,193},{2,194},{3,195},{4,196},{5,197},{6,198},{7,199},{8... | collective-permute-start | bytes 1769480 | tf_op jit(solution)/shard_map/ppermute | solution.py:20
  122.3 31.3 %collective-permute-start.18 = (bf16[384,768]{1,0:T(8,128)(2,1)S(1)}, bf16[384,768]{1,0:T(8,128)(2,1)}, u32[]{:S(2)}, u32[]{:S(2)}) collective-permute-start(bf16[384,768]{1,0:T(8,128)(2,1)S(1)} %bitcast.124), channel_id=1, source_target_pairs={{0,576},{1,577},{2,578},{3,579},{4,580},{5,581},{6,582},{7,583},{8... | collective-permute-start | bytes 1769480 | tf_op jit(solution)/shard_map/ppermute | solution.py:20
  125.9 28.8 %collective-permute-start.19 = (bf16[384,768]{1,0:T(8,128)(2,1)S(1)}, bf16[384,768]{1,0:T(8,128)(2,1)}, u32[]{:S(2)}, u32[]{:S(2)}) collective-permute-start(bf16[384,768]{1,0:T(8,128)(2,1)S(1)} %bitcast.125), channel_id=1, source_target_pairs={{0,384},{1,385},{2,386},{3,387},{4,388},{5,389},{6,390},{7,391},{8... | collective-permute-start | bytes 1769480 | tf_op jit(solution)/shard_map/ppermute | solution.py:20
  159.2 30.5 %collective-permute-start.20 = (bf16[1536,768]{1,0:T(8,128)(2,1)S(1)}, bf16[1536,768]{1,0:T(8,128)(2,1)}, u32[]{:S(2)}, u32[]{:S(2)}) collective-permute-start(bf16[1536,768]{1,0:T(8,128)(2,1)S(1)} %bitcast.118), channel_id=1, source_target_pairs={{0,6},{1,7},{2,8},{3,9},{4,10},{5,11},{6,0},{7,1},{8,2},{9,3},{10,... | collective-permute-start | bytes 7077896 | tf_op jit(solution)/shard_map/ppermute | solution.py:20
  (9 other events, 301.4 us)

commit v3 on v0

v3 whole, which is shorter than its diff:
```python
import functools

import jax
import jax.numpy as jnp
import numpy as np
from jax import lax
from jax.experimental import pallas as pl
from jax.experimental.pallas import tpu as pltpu
from jax.sharding import Mesh, PartitionSpec as P

HD = 64
AXES = ("x", "zh", "y", "c", "zl")
SIZES = (4, 2, 8, 2, 6)


def permute(value, move):
    pairs = []
    for place in np.ndindex(*SIZES):
        goal = move(*place)
        if goal is not None:
            pairs.append(
                (int(np.ravel_multi_index(place, SIZES)), int(np.ravel_multi_index(goal, SIZES)))
            )
    return lax.ppermute(value, AXES, pairs)


def other_core(value):
    return permute(value, lambda x, zh, y, c, zl: (x, zh, y, 1 - c, zl))


def even_links(value):
    return permute(value, lambda x, zh, y, c, zl: (x, zh, y, c, zl ^ 1))


def odd_links(value):
    return permute(
        value, lambda x, zh, y, c, zl: (x, zh, y, c, ((zl - 1) ^ 1) + 1) if 0 < zl < 5 else None
    )


def x_swap(value, which):
    goal = {"even": (1, 0, 3, 2), "odd": (3, 2, 1, 0), "across": (2, 3, 0, 1)}[which]
    return permute(value, lambda x, zh, y, c, zl: (goal[x], zh, y, c, zl))


def gather_y(value):
    copies = jnp.broadcast_to(value[None], (8,) + value.shape)
    return lax.all_to_all(copies, "y", 0, 0, tiled=True).reshape(-1, value.shape[1])


def after(value, *others):
    return lax.optimization_barrier((value,) + others)[0]


def gather_x(block):
    return jnp.stack([block] + [x_swap(block, which) for which in ("even", "odd", "across")])


def x_places(x):
    return x, x + 1 - 2 * lax.rem(x, 2), 3 - x, lax.rem(x + 2, 4)


def reorder():
    y, zh, r = np.meshgrid(np.arange(8), np.arange(2), np.arange(24), indexing="ij")
    matrix = np.zeros((384, 384), np.float32)
    matrix[np.arange(384), ((zh * 8 + y) * 24 + r).reshape(-1)] = 1
    return jnp.asarray(matrix, jnp.bfloat16)


def attend_kernel(place_ref, length_ref, temp_ref, *refs):
    frames, weights_hbm, move_ref, out_ref = refs[:11], refs[11:13], refs[13], refs[14]
    x_buf, w_in, w_buf, qkv, sems = refs[15:]
    place, x, core = place_ref[0], place_ref[1], place_ref[2]
    turn = 1 - 2 * lax.rem(place, 2)

    pieces = [(frames[0], place, None)]
    for step in range(1, 6):
        for ref, at in (
            (frames[step], place + turn * step),
            (frames[5 + step], place - turn * step),
        ):
            pieces.append((ref, at, (at >= 0) & (at <= 5)))

    copies = [
        pltpu.make_async_copy(ref, x_buf.at[at], sems.at[number])
        for number, (ref, at, _) in enumerate(pieces)
    ]
    w_copies = [
        pltpu.make_async_copy(weights_hbm[which], w_in.at[which], sems.at[11 + which])
        for which in range(2)
    ]
    for copy in w_copies:
        copy.start()
    for copy, (_, _, valid) in zip(copies, pieces):
        if valid is None:
            copy.start()
        else:
            pl.when(valid)(copy.start)

    for copy in w_copies:
        copy.wait()
    for which, half in ((0, core), (1, 1 - core)):
        for number, at in enumerate(x_places(x)):
            rows = pl.ds(pl.multiple_of(at * 384, 384), 384)
            w_buf[half, rows, :] = lax.dot_general(
                move_ref[...],
                w_in[which, number],
                (((0,), (0,)), ((), ())),
                preferred_element_type=jnp.float32,
            ).astype(jnp.bfloat16)
    for copy, (_, _, valid) in zip(copies, pieces):
        if valid is None:
            copy.wait()
        else:
            pl.when(valid)(copy.wait)

    total = x_buf.shape[0] * x_buf.shape[1]
    for two in range(2):
        qkv[two] = jnp.dot(
            x_buf[...].reshape(total, x_buf.shape[2]),
            w_buf[two],
            preferred_element_type=jnp.float32,
        ).astype(jnp.bfloat16)

    live = lax.broadcasted_iota(jnp.int32, (1, total), 1) < length_ref[0]
    lane = lax.broadcasted_iota(jnp.int32, (128, 128), 1)
    row = lax.broadcasted_iota(jnp.int32, (256, 1), 0)

    def query_block(block, carry):
        rows = pl.ds(pl.multiple_of(block * 128, 128), 128)
        for two in range(2):
            query = qkv[two, rows, :128]
            none = jnp.zeros_like(query)
            query = jnp.concatenate(
                [jnp.where(lane < HD, query, none), jnp.where(lane < HD, none, query)]
            )
            scores = lax.dot_general(
                query,
                qkv[two, :, 128:256],
                (((1,), (1,)), ((), ())),
                preferred_element_type=jnp.float32,
            )
            scale = jnp.where(row < 128, temp_ref[2 * two] / 8.0, temp_ref[2 * two + 1] / 8.0)
            scores = jnp.where(live, scores * scale, -1e30)
            scores = jnp.exp(scores - jnp.max(scores, axis=-1, keepdims=True))
            probs = scores * (1.0 / jnp.sum(scores, axis=-1, keepdims=True))
            mixed = jnp.dot(
                probs.astype(jnp.bfloat16), qkv[two, :, 256:], preferred_element_type=jnp.float32
            )
            mixed = jnp.where(lane < HD, mixed[:128], mixed[128:])
            out_ref[block, :, two * 128 : two * 128 + 128] = mixed.astype(jnp.bfloat16)
        return carry

    lax.fori_loop(0, 6, query_block, 0)


SMEM = pl.BlockSpec(memory_space=pltpu.SMEM)
VMEM = pl.BlockSpec(memory_space=pltpu.VMEM)
ANYWHERE = pl.BlockSpec(memory_space=pl.ANY)


def attend(place, length, temp, frames, weights):
    shard = frames[0].shape
    return pl.pallas_call(
        attend_kernel,
        out_shape=jax.ShapeDtypeStruct((6, shard[0], 256), jnp.bfloat16),
        in_specs=[SMEM] * 3 + [ANYWHERE] * 13 + [VMEM],
        out_specs=VMEM,
        scratch_shapes=[
            pltpu.VMEM((6,) + shard, jnp.bfloat16),
            pltpu.VMEM((2, 4, 384, 384), jnp.bfloat16),
            pltpu.VMEM((2, 1536, 384), jnp.bfloat16),
            pltpu.VMEM((2, 6 * shard[0], 384), jnp.bfloat16),
            pltpu.SemaphoreType.DMA((13,)),
        ],
        compiler_params=pltpu.CompilerParams(vmem_limit_bytes=28 * 2**20),
        cost_estimate=pl.CostEstimate(
            flops=3 * 10**9, bytes_accessed=5 * 10**6, transcendentals=2 * 10**6
        ),
    )(place, length, temp, *frames, *weights, reorder())


def project_kernel(place_ref, heads_ref, own_ref, other_ref, move_ref, out_ref):
    x, core = place_ref[1], place_ref[2]
    first = jnp.concatenate([heads_ref[at, :, :128] for at in range(6)], axis=1)
    second = jnp.concatenate([heads_ref[at, :, 128:] for at in range(6)], axis=1)
    mine = jnp.where(core == 0, first, second)
    given = jnp.where(core == 0, second, first)
    sides = (((1,), (1,)), ((), ()))
    for number, at in enumerate(x_places(x)):
        columns = pl.ds(pl.multiple_of(at * 384, 384), 384)
        total = lax.dot_general(
            mine, own_ref[number], sides, preferred_element_type=jnp.float32
        ) + lax.dot_general(given, other_ref[number], sides, preferred_element_type=jnp.float32)
        out_ref[:, columns] = jnp.dot(
            total.astype(jnp.bfloat16), move_ref[...], preferred_element_type=jnp.float32
        ).astype(jnp.bfloat16)


def project(place, heads, own, other):
    return pl.pallas_call(
        project_kernel,
        out_shape=jax.ShapeDtypeStruct((heads.shape[1], 1536), jnp.bfloat16),
        in_specs=[SMEM] + [VMEM] * 4,
        out_specs=VMEM,
        compiler_params=pltpu.CompilerParams(vmem_limit_bytes=20 * 2**20),
        cost_estimate=pl.CostEstimate(
            flops=8 * 10**8, bytes_accessed=6 * 10**6, transcendentals=0
        ),
    )(place, heads, own, other, reorder())


def on_device(latents, norm_gain, w_qkv, w_out, head_temp, lengths):
    rows = w_qkv.reshape(3, 12, 2, 128).transpose(2, 1, 0, 3).reshape(1, 2, 12, 384)
    rows = jnp.broadcast_to(rows, (2, 2, 12, 384)).reshape(4, 12, 384)
    rows = lax.all_to_all(rows, ("zh", "c"), 0, 0, tiled=True).reshape(48, 384)

    frames = latents[0]
    values = frames.astype(jnp.float32)
    rms = jnp.sqrt(jnp.mean(values * values, axis=-1, keepdims=True) + 1e-06)
    normed = (values / rms * norm_gain).astype(jnp.bfloat16)
    evens, odds = [normed], [normed]
    for _ in range(5):
        even, odd = even_links(odds[-1]), odd_links(evens[-1])
        evens.append(even)
        odds.append(odd)

    by_y = gather_y(after(rows, normed))
    by_x = gather_x(after(by_y, evens[1], odds[1]))

    turned = w_out.T.reshape(1, 12, 2, 128).transpose(0, 2, 1, 3)
    turned = jnp.broadcast_to(turned, (12, 2, 12, 128)).reshape(2, 6, 2, 12, 128)
    turned = turned.reshape(24, 12, 128)
    columns = lax.all_to_all(after(turned, by_y), ("zh", "zl", "c"), 0, 0, tiled=True)
    columns = columns.reshape(2, 6, 2, 12, 128).transpose(0, 2, 3, 1, 4).reshape(48, 768)
    out_by_y = gather_y(after(columns, evens[2], odds[2]))

    weights = (by_x, other_core(after(by_x, evens[3], odds[3])))
    out_own = gather_x(after(out_by_y, evens[4], odds[4]))

    place = jnp.stack([lax.axis_index(axis) for axis in ("zl", "x", "c")]).astype(jnp.int32)
    blocks = attend(place, lengths, head_temp, evens + odds[1:], weights)
    own = lax.all_to_all(blocks, "zl", 0, 0, tiled=True)
    out_other = other_core(after(out_own, blocks))
    return project(place, own, out_own, out_other)[None]


def solution(mesh):
    split = Mesh(mesh.devices.reshape(SIZES), AXES)
    clip = ("x", "zh", "y", "c")
    in_specs = (
        P(clip, "zl", None),
        P(),
        P(None, clip, "zl"),
        P("zl", clip),
        P("zl"),
        P(clip),
    )
    out_specs = P(clip, "zl", None)
    return jax.shard_map(
        on_device, mesh=split, in_specs=in_specs, out_specs=out_specs, check_vma=False
    )
```

time: 378 us -> 179 us (0.47)
  blocking collectives: 276 us -> 69.1 us
  starting transfers between devices: 0.09 us -> 68.2 us
  waiting for transfers between devices: 65.6 us -> 9.43 us
  Pallas kernels: 0 us -> 17.6 us
  matrix products: 17 us -> 0 us
  between operations: 13.8 us -> 1.04 us
  local copies, waits for them, and re-layouts: 1.6 us -> 6.22 us
    all_gather x1 -> x0, blocking collectives: 276 us -> none  [on_device(): out_piece = lax.all_gather(w_out, ('grp', 'fsdp'), axis=1, tiled=True)]
    all_to_all x0 -> x3, blocking collectives: none -> 69.1 us  [the longest x1 25.4 us: on_device(): rows = lax.all_to_all(rows, ('zh', 'c'), 0, 0, tiled=True).reshape(48, 384)]
    reduce_scatter x1 -> x0, waiting for transfers between devices: 65.5 us -> none  [on_device(): lax.psum_scatter(jnp.dot(heads_out, out_piece, preferred_element_type=jnp...]
    ppermute x0 -> x18, starting transfers between devices: none -> 57.2 us  [permute(): return lax.ppermute(value, AXES, pairs)]
    pallas_call x0 -> x2, Pallas kernels: none -> 17.6 us  [the longest x1 13.6 us: attend(): pl.pallas_call(attend_kernel, out_shape=jax.ShapeDtypeStruct((6, shard[0]...]
    dot_general x3 -> x0, matrix products: 11.5 us -> none  [the longest x1 4.66 us: on_device(): jnp.einsum('ld,kde->kle', whole, lax.all_gather(w_qkv, ('grp', 'fsdp'), a...]
    all_to_all x0 -> x2, starting transfers between devices: none -> 11 us  [gather_y(): lax.all_to_all(copies, 'y', 0, 0, tiled=True).reshape(-1, value.shape[1])]
    sub x1 -> x0, matrix products: 5.51 us -> none  [on_device(): probs = jax.nn.softmax(scores, axis=-1).astype(jnp.bfloat16)]
  transfers between devices with their start and end apart: 3 -> 20, of which waited for: 1 -> 3; matrix products, arithmetic and copies ran while one was open for 1% -> 2% of each run, Pallas kernels for 0% -> 8%
where the time goes in v3:
time: 179 us; the launch traced here: 177 us
  blocking collectives  69.1 us (39%)
  starting transfers between devices  68.2 us (38%)
  Pallas kernels  17.6 us (10%)
  waiting for transfers between devices  9.43 us (5%)
  local copies, waits for them, and re-layouts  6.22 us (3%)
  other arithmetic  5.72 us (3%)
    ppermute x18, starting transfers between devices, permute(): return lax.ppermute(value, AXES, pairs)  57.2 us
    all_to_all x1, blocking collectives, on_device(): rows = lax.all_to_all(rows, ('zh', 'c'), 0, 0, tiled=True).reshape(48, 384)  25.4 us
    all_to_all x1, blocking collectives, on_device(): own = lax.all_to_all(blocks, 'zl', 0, 0, tiled=True)  23.1 us
    all_to_all x1, blocking collectives, on_device(): lax.all_to_all(after(turned, by_y), ('zh', 'zl', 'c'), 0, 0, tiled=True)  20.7 us
    pallas_call x1, Pallas kernels, attend(): pl.pallas_call(attend_kernel, out_shape=jax.ShapeDtypeStruct((6, shard[0]...  13.6 us
    all_to_all x2, starting transfers between devices, gather_y(): lax.all_to_all(copies, 'y', 0, 0, tiled=True).reshape(-1, value.shape[1])  11 us
    ppermute x18, waiting for transfers between devices, permute(): return lax.ppermute(value, AXES, pairs)  4.75 us
    all_to_all x2, waiting for transfers between devices, gather_y(): lax.all_to_all(copies, 'y', 0, 0, tiled=True).reshape(-1, value.shape[1])  4.68 us
  transfers between devices with their start and end apart: 20, of which 3 were waited for; matrix products, arithmetic and copies ran while one was open for 2% of the time, Pallas kernels for 8%

profile of v3, /device:TPU:1, one launch (start us, length us, event | category | flops | bytes accessed | tf_op | source)
XLA Modules:
  0.0 177.4 jit_solution(10114392303981479454)
XLA Ops:
  2.4 4.8 %collective-permute-start = (bf16[128,1536]{1,0:T(8,128)(2,1)S(1)}, bf16[128,1536]{1,0:T(8,128)(2,1)S(1)}, u32[]{:S(2)}, u32[]{:S(2)}) collective-permute-start(bf16[128,1536]{1,0:T(8,128)(2,1)S(1)} %fusion.2.refs_0_), channel_id=1, source_target_pairs={{0,1},{1,0},{2,3},{3,2},{4,5},{5,4},{6,7},{7,6},{8,9},{9,8},{10,11... | collective-permute-start | bytes 1179656 | tf_op jit(solution)/shard_map/ppermute | solution.py:24
  8.7 25.4 %all_to_all.25 = bf16[4,12,384]{2,1,0:T(8,128)(2,1)S(1)} all-to-all(bf16[4,12,384]{2,1,0:T(8,128)(2,1)S(1)} %bitcast.46), channel_id=1, replica_groups=mesh['x'=4,'zh'=2,'y'=8,'c'=2,'zl'=6] {'zh','c'}, dimensions={0} | all-to-all | bytes 73728 | tf_op jit(solution)/shard_map/all_to_all | solution.py:216
  34.9 6.8 %all-to-all-start.1 = ((bf16[8,48,384]{2,1,0:T(8,128)(2,1)}), bf16[8,48,384]{2,1,0:T(8,128)(2,1)S(1)}, u32[]{:S(2)}, u32[]{:S(2)}) async-start(bf16[8,48,384]{2,1,0:T(8,128)(2,1)} %broadcast_in_dim.16), calls=%async_computation.1 | async-start | bytes 589824 | tf_op jit(solution)/shard_map/all_to_all | solution.py:48
  42.4 5.5 %collective-permute-start.2 = (bf16[128,1536]{1,0:T(8,128)(2,1)S(1)}, bf16[128,1536]{1,0:T(8,128)(2,1)S(1)}, u32[]{:S(2)}, u32[]{:S(2)}) collective-permute-start(bf16[128,1536]{1,0:T(8,128)(2,1)S(1)} %collective-permute-done.1.refs_6_), channel_id=1, source_target_pairs={{0,1},{1,0},{2,3},{3,2},{4,5},{5,4},{6,7},{7,6},{8,9},{9,8},{10,11... | collective-permute-start | bytes 1179656 | tf_op jit(solution)/shard_map/ppermute | solution.py:24
  48.0 4.7 %all-to-all-done.1 = bf16[8,48,384]{2,1,0:T(8,128)(2,1)S(1)} async-done(((bf16[8,48,384]{2,1,0:T(8,128)(2,1)}), bf16[8,48,384]{2,1,0:T(8,128)(2,1)S(1)}, u32[]{:S(2)}, u32[]{:S(2)}) %all-to-all-start.1) | async-done | bytes 294944 | tf_op jit(solution)/shard_map/all_to_all | solution.py:48
  52.6 4.6 %collective-permute-start.12 = (bf16[384,384]{1,0:T(8,128)(2,1)S(1)}, bf16[384,384]{1,0:T(8,128)(2,1)}, u32[]{:S(2)}, u32[]{:S(2)}) collective-permute-start(bf16[384,384]{1,0:T(8,128)(2,1)S(1)} %bitcast.37), channel_id=1, source_target_pairs={{0,384},{1,385},{2,386},{3,387},{4,388},{5,389},{6,390},{7,391},{8... | collective-permute-start | bytes 884744 | tf_op jit(solution)/shard_map/ppermute | solution.py:24
  57.3 2.8 %collective-permute-start.11 = (bf16[384,384]{1,0:T(8,128)(2,1)S(1)}, bf16[384,384]{1,0:T(8,128)(2,1)}, u32[]{:S(2)}, u32[]{:S(2)}) collective-permute-start(bf16[384,384]{1,0:T(8,128)(2,1)S(1)} %bitcast.38), channel_id=1, source_target_pairs={{0,576},{1,577},{2,578},{3,579},{4,580},{5,581},{6,582},{7,583},{8... | collective-permute-start | bytes 884744 | tf_op jit(solution)/shard_map/ppermute | solution.py:24
  60.1 1.9 %collective-permute-start.10 = (bf16[384,384]{1,0:T(8,128)(2,1)S(1)}, bf16[384,384]{1,0:T(8,128)(2,1)S(1)}, u32[]{:S(2)}, u32[]{:S(2)}) collective-permute-start(bf16[384,384]{1,0:T(8,128)(2,1)S(1)} %bitcast.39), channel_id=1, source_target_pairs={{0,192},{1,193},{2,194},{3,195},{4,196},{5,197},{6,198},{7,199},{8... | collective-permute-start | bytes 884744 | tf_op jit(solution)/shard_map/ppermute | solution.py:24
  62.0 4.3 %collective-permute-start.4 = (bf16[128,1536]{1,0:T(8,128)(2,1)S(1)}, bf16[128,1536]{1,0:T(8,128)(2,1)}, u32[]{:S(2)}, u32[]{:S(2)}) collective-permute-start(bf16[128,1536]{1,0:T(8,128)(2,1)S(1)} %collective-permute-done.3.refs_7_), channel_id=1, source_target_pairs={{0,1},{1,0},{2,3},{3,2},{4,5},{5,4},{6,7},{7,6},{8,9},{9,8},{10,11... | collective-permute-start | bytes 1179656 | tf_op jit(solution)/shard_map/ppermute | solution.py:24
  67.8 20.7 %all_to_all.26 = bf16[24,12,128]{2,1,0:T(8,128)(2,1)S(1)} all-to-all(bf16[24,12,128]{2,1,0:T(8,128)(2,1)S(1)} %bitcast.41), channel_id=1, replica_groups=mesh['x'=4,'zh'=2,'y'=8,'c'=2,'zl'=6] {'zh','zl','c'}, dimensions={0} | all-to-all | bytes 147456 | tf_op jit(solution)/shard_map/all_to_all | solution.py:234
  89.4 4.2 %all-to-all-start.4 = ((bf16[8,48,768]{2,1,0:T(8,128)(2,1)}), bf16[8,48,768]{2,1,0:T(8,128)(2,1)}, u32[]{:S(2)}, u32[]{:S(2)}) async-start(bf16[8,48,768]{2,1,0:T(8,128)(2,1)} %broadcast_in_dim.36), calls=%async_computation.4 | async-start | bytes 1179648 | tf_op jit(solution)/shard_map/all_to_all | solution.py:48
  95.8 2.5 %collective-permute-start.13 = (bf16[4,384,384]{2,1,0:T(8,128)(2,1)S(1)}, bf16[4,384,384]{2,1,0:T(8,128)(2,1)S(1)}, u32[]{:S(2)}, u32[]{:S(2)}) collective-permute-start(bf16[4,384,384]{2,1,0:T(8,128)(2,1)S(1)} %pad_maximum_fusion.1.refs_11_), channel_id=1, source_target_pairs={{0,6},{1,7},{2,8},{3,9},{4,10},{5,11},{6,0},{7,1},{8,2},{9,3},{10,... | collective-permute-start | bytes 3538952 | tf_op jit(solution)/shard_map/ppermute | solution.py:24
  98.3 1.5 collective-permute-start.7
  99.8 3.2 %collective-permute-start.6 = (bf16[128,1536]{1,0:T(8,128)(2,1)}, bf16[128,1536]{1,0:T(8,128)(2,1)}, u32[]{:S(2)}, u32[]{:S(2)}) collective-permute-start(bf16[128,1536]{1,0:T(8,128)(2,1)} %collective-permute-done.5.refs_8_), channel_id=1, source_target_pairs={{0,1},{1,0},{2,3},{3,2},{4,5},{5,4},{6,7},{7,6},{8,9},{9,8},{10,11... | collective-permute-start | bytes 1179656 | tf_op jit(solution)/shard_map/ppermute | solution.py:24
  103.0 9.2 %collective-permute-start.8 = (bf16[128,1536]{1,0:T(8,128)(2,1)}, bf16[128,1536]{1,0:T(8,128)(2,1)}, u32[]{:S(2)}, u32[]{:S(2)}) collective-permute-start(bf16[128,1536]{1,0:T(8,128)(2,1)} %collective-permute-done.7.refs_9_), channel_id=1, source_target_pairs={{0,1},{1,0},{2,3},{3,2},{4,5},{5,4},{6,7},{7,6},{8,9},{9,8},{10,11... | collective-permute-start | bytes 1179656 | tf_op jit(solution)/shard_map/ppermute | solution.py:24
  114.1 5.2 %collective-permute-start.16 = (bf16[384,768]{1,0:T(8,128)(2,1)}, bf16[384,768]{1,0:T(8,128)(2,1)}, u32[]{:S(2)}, u32[]{:S(2)}) collective-permute-start(bf16[384,768]{1,0:T(8,128)(2,1)} %bitcast.18), channel_id=1, source_target_pairs={{0,384},{1,385},{2,386},{3,387},{4,388},{5,389},{6,390},{7,391},{8... | collective-permute-start | bytes 1769480 | tf_op jit(solution)/shard_map/ppermute | solution.py:24
  119.3 2.8 %collective-permute-start.15 = (bf16[384,768]{1,0:T(8,128)(2,1)}, bf16[384,768]{1,0:T(8,128)(2,1)}, u32[]{:S(2)}, u32[]{:S(2)}) collective-permute-start(bf16[384,768]{1,0:T(8,128)(2,1)} %bitcast.18), channel_id=1, source_target_pairs={{0,576},{1,577},{2,578},{3,579},{4,580},{5,581},{6,582},{7,583},{8... | collective-permute-start | bytes 1769480 | tf_op jit(solution)/shard_map/ppermute | solution.py:24
  122.0 2.2 %collective-permute-start.14 = (bf16[384,768]{1,0:T(8,128)(2,1)}, bf16[384,768]{1,0:T(8,128)(2,1)}, u32[]{:S(2)}, u32[]{:S(2)}) collective-permute-start(bf16[384,768]{1,0:T(8,128)(2,1)} %bitcast.18), channel_id=1, source_target_pairs={{0,192},{1,193},{2,194},{3,195},{4,196},{5,197},{6,198},{7,199},{8... | collective-permute-start | bytes 1769480 | tf_op jit(solution)/shard_map/ppermute | solution.py:24
  128.0 13.6 %shard_map.82 = bf16[6,128,256]{2,1,0:T(8,128)(2,1)S(1)} custom-call(s32[3]{0:T(128)S(1)} %pad_add_fusion.place_ref, s32[1]{0:T(128)S(6)} %copy.23.length_ref, f32[4]{0:T(128)S(1)} %copy-done.7, bf16[128,1536]{1,0:T(8,128)(2,1)S(1)} %fusion.2.refs_0_, bf16[128,1536]{1,0:T(8,128)(2,1)S(1)} %collective-permute-done.refs_1_, bf16[128,1536]{1,0:T(8,128)(2,1)S(1)} %copy-done.6, ...), custom_call_target="tpu_custom_call" | custom-call | flops 3000000000 | bytes 5000000 | tf_op jit(solution)/shard_map/pallas_call | solution.py:164
  141.6 4.3 %collective-permute-done.15 = bf16[384,768]{1,0:T(8,128)(2,1)} collective-permute-done((bf16[384,768]{1,0:T(8,128)(2,1)}, bf16[384,768]{1,0:T(8,128)(2,1)}, u32[]{:S(2)}, u32[]{:S(2)}) %collective-permute-start.15) | collective-permute-done | bytes 589856 | tf_op jit(solution)/shard_map/ppermute | solution.py:24
  146.0 1.9 %pad_maximum_fusion.own_ref = bf16[4,384,768]{2,1,0:T(8,128)(2,1)S(1)} fusion(bf16[1,384,768]{2,1,0:T(8,128)(2,1)} %bitcast.22, bf16[1,384,768]{2,1,0:T(8,128)(2,1)} %bitcast.21, bf16[1,384,768]{2,1,0:T(8,128)(2,1)} %bitcast.20, bf16[1,384,768]{2,1,0:T(8,128)(2,1)} %bitcast.19), kind=kLoop, calls=%fused_computation | loop fusion | flops 3538944 | bytes 4718592 | tf_op jit(solution)/shard_map/stack | solution.py:56
  147.9 2.4 %collective-permute-start.17 = (bf16[4,384,768]{2,1,0:T(8,128)(2,1)S(1)}, bf16[4,384,768]{2,1,0:T(8,128)(2,1)S(1)}, u32[]{:S(2)}, u32[]{:S(2)}) collective-permute-start(bf16[4,384,768]{2,1,0:T(8,128)(2,1)S(1)} %pad_maximum_fusion.own_ref), channel_id=1, source_target_pairs={{0,6},{1,7},{2,8},{3,9},{4,10},{5,11},{6,0},{7,1},{8,2},{9,3},{10,... | collective-permute-start | bytes 7077896 | tf_op jit(solution)/shard_map/ppermute | solution.py:24
  150.3 23.1 %all_to_all.27.heads_ref = bf16[6,128,256]{2,1,0:T(8,128)(2,1)S(1)} all-to-all(bf16[6,128,256]{2,1,0:T(8,128)(2,1)S(1)} %shard_map.82), channel_id=1, replica_groups=mesh['x'=4,'zh'=2,'y'=8,'c'=2,'zl'=6] {'zl'}, dimensions={0} | all-to-all | bytes 786432 | tf_op jit(solution)/shard_map/all_to_all | solution.py:243
  173.4 4.0 %shard_map.83 = bf16[128,1536]{1,0:T(8,128)(2,1)} custom-call(s32[3]{0:T(128)S(1)} %pad_add_fusion.place_ref, bf16[6,128,256]{2,1,0:T(8,128)(2,1)S(1)} %all_to_all.27.heads_ref, bf16[4,384,768]{2,1,0:T(8,128)(2,1)S(1)} %pad_maximum_fusion.own_ref, bf16[4,384,768]{2,1,0:T(8,128)(2,1)S(1)} %collective-permute-done.17.other_ref, bf16[384,384]{1,0:T(8,128)(2,1)S(1)} %copy-done), custom_call_target="tpu_custom_call" | custom-call | flops 800000000 | bytes 6000000 | tf_op jit(solution)/shard_map/pallas_call | solution.py:201
  (63 shorter events, 14.7 us)
Async XLA Ops:
  0.0 67.7 %copy-start.10 = (bf16[256,12]{0,1:T(8,128)(2,1)S(1)}, bf16[256,12]{0,1:T(8,128)(2,1)}, u32[]{:S(2)}) copy-start(bf16[256,12]{0,1:T(8,128)(2,1)} %param.11) | copy-start | bytes 18436
  2.4 39.4 %collective-permute-start = (bf16[128,1536]{1,0:T(8,128)(2,1)S(1)}, bf16[128,1536]{1,0:T(8,128)(2,1)S(1)}, u32[]{:S(2)}, u32[]{:S(2)}) collective-permute-start(bf16[128,1536]{1,0:T(8,128)(2,1)S(1)} %fusion.2.refs_0_), channel_id=1, source_target_pairs={{0,1},{1,0},{2,3},{3,2},{4,5},{5,4},{6,7},{7,6},{8,9},{9,8},{10,11... | collective-permute-start | bytes 1179656 | tf_op jit(solution)/shard_map/ppermute | solution.py:24
  7.2 35.2 %collective-permute-start.1 = (bf16[128,1536]{1,0:T(8,128)(2,1)S(1)}, bf16[128,1536]{1,0:T(8,128)(2,1)S(1)}, u32[]{:S(2)}, u32[]{:S(2)}) collective-permute-start(bf16[128,1536]{1,0:T(8,128)(2,1)S(1)} %fusion.2.refs_0_), channel_id=1, source_target_pairs={{1,2},{2,1},{3,4},{4,3},{7,8},{8,7},{9,10},{10,9},{13,14},{14,13},... | collective-permute-start | bytes 1179656 | tf_op jit(solution)/shard_map/ppermute | solution.py:24
  34.9 17.7 %all-to-all-start.1 = ((bf16[8,48,384]{2,1,0:T(8,128)(2,1)}), bf16[8,48,384]{2,1,0:T(8,128)(2,1)S(1)}, u32[]{:S(2)}, u32[]{:S(2)}) async-start(bf16[8,48,384]{2,1,0:T(8,128)(2,1)} %broadcast_in_dim.16), calls=%async_computation.1 | async-start | bytes 589824 | tf_op jit(solution)/shard_map/all_to_all | solution.py:48
  41.7 20.3 %collective-permute-start.3 = (bf16[128,1536]{1,0:T(8,128)(2,1)S(1)}, bf16[128,1536]{1,0:T(8,128)(2,1)S(1)}, u32[]{:S(2)}, u32[]{:S(2)}) collective-permute-start(bf16[128,1536]{1,0:T(8,128)(2,1)S(1)} %collective-permute-done.refs_1_), channel_id=1, source_target_pairs={{1,2},{2,1},{3,4},{4,3},{7,8},{8,7},{9,10},{10,9},{13,14},{14,13},... | collective-permute-start | bytes 1179656 | tf_op jit(solution)/shard_map/ppermute | solution.py:24
  42.4 51.2 %copy-start.1 = (bf16[128,1536]{1,0:T(8,128)(2,1)}, bf16[128,1536]{1,0:T(8,128)(2,1)S(1)}, u32[]{:S(2)}) copy-start(bf16[128,1536]{1,0:T(8,128)(2,1)S(1)} %collective-permute-done.1.refs_6_) | copy-start | bytes 1179652
  42.4 23.9 %collective-permute-start.2 = (bf16[128,1536]{1,0:T(8,128)(2,1)S(1)}, bf16[128,1536]{1,0:T(8,128)(2,1)S(1)}, u32[]{:S(2)}, u32[]{:S(2)}) collective-permute-start(bf16[128,1536]{1,0:T(8,128)(2,1)S(1)} %collective-permute-done.1.refs_6_), channel_id=1, source_target_pairs={{0,1},{1,0},{2,3},{3,2},{4,5},{5,4},{6,7},{7,6},{8,9},{9,8},{10,11... | collective-permute-start | bytes 1179656 | tf_op jit(solution)/shard_map/ppermute | solution.py:24
  52.6 41.0 %copy-start.8 = (bf16[8,48,384]{2,1,0:T(8,128)(2,1)}, bf16[8,48,384]{2,1,0:T(8,128)(2,1)S(1)}, u32[]{:S(2)}) copy-start(bf16[8,48,384]{2,1,0:T(8,128)(2,1)S(1)} %all-to-all-done.1) | copy-start | bytes 884740
  52.6 41.0 %collective-permute-start.12 = (bf16[384,384]{1,0:T(8,128)(2,1)S(1)}, bf16[384,384]{1,0:T(8,128)(2,1)}, u32[]{:S(2)}, u32[]{:S(2)}) collective-permute-start(bf16[384,384]{1,0:T(8,128)(2,1)S(1)} %bitcast.37), channel_id=1, source_target_pairs={{0,384},{1,385},{2,386},{3,387},{4,388},{5,389},{6,390},{7,391},{8... | collective-permute-start | bytes 884744 | tf_op jit(solution)/shard_map/ppermute | solution.py:24
  57.3 36.3 %collective-permute-start.11 = (bf16[384,384]{1,0:T(8,128)(2,1)S(1)}, bf16[384,384]{1,0:T(8,128)(2,1)}, u32[]{:S(2)}, u32[]{:S(2)}) collective-permute-start(bf16[384,384]{1,0:T(8,128)(2,1)S(1)} %bitcast.38), channel_id=1, source_target_pairs={{0,576},{1,577},{2,578},{3,579},{4,580},{5,581},{6,582},{7,583},{8... | collective-permute-start | bytes 884744 | tf_op jit(solution)/shard_map/ppermute | solution.py:24
  60.1 33.5 %collective-permute-start.10 = (bf16[384,384]{1,0:T(8,128)(2,1)S(1)}, bf16[384,384]{1,0:T(8,128)(2,1)S(1)}, u32[]{:S(2)}, u32[]{:S(2)}) collective-permute-start(bf16[384,384]{1,0:T(8,128)(2,1)S(1)} %bitcast.39), channel_id=1, source_target_pairs={{0,192},{1,193},{2,194},{3,195},{4,196},{5,197},{6,198},{7,199},{8... | collective-permute-start | bytes 884744 | tf_op jit(solution)/shard_map/ppermute | solution.py:24
  62.0 33.8 %collective-permute-start.4 = (bf16[128,1536]{1,0:T(8,128)(2,1)S(1)}, bf16[128,1536]{1,0:T(8,128)(2,1)}, u32[]{:S(2)}, u32[]{:S(2)}) collective-permute-start(bf16[128,1536]{1,0:T(8,128)(2,1)S(1)} %collective-permute-done.3.refs_7_), channel_id=1, source_target_pairs={{0,1},{1,0},{2,3},{3,2},{4,5},{5,4},{6,7},{7,6},{8,9},{9,8},{10,11... | collective-permute-start | bytes 1179656 | tf_op jit(solution)/shard_map/ppermute | solution.py:24
  66.3 29.5 %collective-permute-start.5 = (bf16[128,1536]{1,0:T(8,128)(2,1)S(1)}, bf16[128,1536]{1,0:T(8,128)(2,1)}, u32[]{:S(2)}, u32[]{:S(2)}) collective-permute-start(bf16[128,1536]{1,0:T(8,128)(2,1)S(1)} %collective-permute-done.2.refs_2_), channel_id=1, source_target_pairs={{1,2},{2,1},{3,4},{4,3},{7,8},{8,7},{9,10},{10,9},{13,14},{14,13},... | collective-permute-start | bytes 1179656 | tf_op jit(solution)/shard_map/ppermute | solution.py:24
  88.5 36.6 %copy-start.7 = (f32[4]{0:T(128)S(1)}, f32[4]{0:T(128)}, u32[]{:S(2)}) copy-start(f32[4]{0:T(128)} %temp_ref.1) | copy-start | bytes 52
  89.4 24.7 %all-to-all-start.4 = ((bf16[8,48,768]{2,1,0:T(8,128)(2,1)}), bf16[8,48,768]{2,1,0:T(8,128)(2,1)}, u32[]{:S(2)}, u32[]{:S(2)}) async-start(bf16[8,48,768]{2,1,0:T(8,128)(2,1)} %broadcast_in_dim.36), calls=%async_computation.4 | async-start | bytes 1179648 | tf_op jit(solution)/shard_map/all_to_all | solution.py:48
  95.8 29.2 %collective-permute-start.13 = (bf16[4,384,384]{2,1,0:T(8,128)(2,1)S(1)}, bf16[4,384,384]{2,1,0:T(8,128)(2,1)S(1)}, u32[]{:S(2)}, u32[]{:S(2)}) collective-permute-start(bf16[4,384,384]{2,1,0:T(8,128)(2,1)S(1)} %pad_maximum_fusion.1.refs_11_), channel_id=1, source_target_pairs={{0,6},{1,7},{2,8},{3,9},{4,10},{5,11},{6,0},{7,1},{8,2},{9,3},{10,... | collective-permute-start | bytes 3538952 | tf_op jit(solution)/shard_map/ppermute | solution.py:24
  98.3 4.7 %collective-permute-start.7 = (bf16[128,1536]{1,0:T(8,128)(2,1)}, bf16[128,1536]{1,0:T(8,128)(2,1)}, u32[]{:S(2)}, u32[]{:S(2)}) collective-permute-start(bf16[128,1536]{1,0:T(8,128)(2,1)} %collective-permute-done.4.refs_3_), channel_id=1, source_target_pairs={{1,2},{2,1},{3,4},{4,3},{7,8},{8,7},{9,10},{10,9},{13,14},{14,13},... | collective-permute-start | bytes 1179656 | tf_op jit(solution)/shard_map/ppermute | solution.py:24
  99.8 12.8 %collective-permute-start.6 = (bf16[128,1536]{1,0:T(8,128)(2,1)}, bf16[128,1536]{1,0:T(8,128)(2,1)}, u32[]{:S(2)}, u32[]{:S(2)}) collective-permute-start(bf16[128,1536]{1,0:T(8,128)(2,1)} %collective-permute-done.5.refs_8_), channel_id=1, source_target_pairs={{0,1},{1,0},{2,3},{3,2},{4,5},{5,4},{6,7},{7,6},{8,9},{9,8},{10,11... | collective-permute-start | bytes 1179656 | tf_op jit(solution)/shard_map/ppermute | solution.py:24
  103.0 19.0 %collective-permute-start.8 = (bf16[128,1536]{1,0:T(8,128)(2,1)}, bf16[128,1536]{1,0:T(8,128)(2,1)}, u32[]{:S(2)}, u32[]{:S(2)}) collective-permute-start(bf16[128,1536]{1,0:T(8,128)(2,1)} %collective-permute-done.7.refs_9_), channel_id=1, source_target_pairs={{0,1},{1,0},{2,3},{3,2},{4,5},{5,4},{6,7},{7,6},{8,9},{9,8},{10,11... | collective-permute-start | bytes 1179656 | tf_op jit(solution)/shard_map/ppermute | solution.py:24
  112.6 12.4 %collective-permute-start.9 = (bf16[128,1536]{1,0:T(8,128)(2,1)}, bf16[128,1536]{1,0:T(8,128)(2,1)}, u32[]{:S(2)}, u32[]{:S(2)}) collective-permute-start(bf16[128,1536]{1,0:T(8,128)(2,1)} %collective-permute-done.6.refs_4_), channel_id=1, source_target_pairs={{1,2},{2,1},{3,4},{4,3},{7,8},{8,7},{9,10},{10,9},{13,14},{14,13},... | collective-permute-start | bytes 1179656 | tf_op jit(solution)/shard_map/ppermute | solution.py:24
  114.1 27.6 %collective-permute-start.16 = (bf16[384,768]{1,0:T(8,128)(2,1)}, bf16[384,768]{1,0:T(8,128)(2,1)}, u32[]{:S(2)}, u32[]{:S(2)}) collective-permute-start(bf16[384,768]{1,0:T(8,128)(2,1)} %bitcast.18), channel_id=1, source_target_pairs={{0,384},{1,385},{2,386},{3,387},{4,388},{5,389},{6,390},{7,391},{8... | collective-permute-start | bytes 1769480 | tf_op jit(solution)/shard_map/ppermute | solution.py:24
  119.3 26.7 %collective-permute-start.15 = (bf16[384,768]{1,0:T(8,128)(2,1)}, bf16[384,768]{1,0:T(8,128)(2,1)}, u32[]{:S(2)}, u32[]{:S(2)}) collective-permute-start(bf16[384,768]{1,0:T(8,128)(2,1)} %bitcast.18), channel_id=1, source_target_pairs={{0,576},{1,577},{2,578},{3,579},{4,580},{5,581},{6,582},{7,583},{8... | collective-permute-start | bytes 1769480 | tf_op jit(solution)/shard_map/ppermute | solution.py:24
  122.0 23.9 %collective-permute-start.14 = (bf16[384,768]{1,0:T(8,128)(2,1)}, bf16[384,768]{1,0:T(8,128)(2,1)}, u32[]{:S(2)}, u32[]{:S(2)}) collective-permute-start(bf16[384,768]{1,0:T(8,128)(2,1)} %bitcast.18), channel_id=1, source_target_pairs={{0,192},{1,193},{2,194},{3,195},{4,196},{5,197},{6,198},{7,199},{8... | collective-permute-start | bytes 1769480 | tf_op jit(solution)/shard_map/ppermute | solution.py:24
  147.9 25.5 %collective-permute-start.17 = (bf16[4,384,768]{2,1,0:T(8,128)(2,1)S(1)}, bf16[4,384,768]{2,1,0:T(8,128)(2,1)S(1)}, u32[]{:S(2)}, u32[]{:S(2)}) collective-permute-start(bf16[4,384,768]{2,1,0:T(8,128)(2,1)S(1)} %pad_maximum_fusion.own_ref), channel_id=1, source_target_pairs={{0,6},{1,7},{2,8},{3,9},{4,10},{5,11},{6,0},{7,1},{8,2},{9,3},{10,... | collective-permute-start | bytes 7077896 | tf_op jit(solution)/shard_map/ppermute | solution.py:24
  (7 other events, 103.5 us)

commit v4 on v3

--- a/solution.py
+++ b/solution.py
@@ -28,13 +28,13 @@
     return permute(value, lambda x, zh, y, c, zl: (x, zh, y, 1 - c, zl))
 
 
-def even_links(value):
-    return permute(value, lambda x, zh, y, c, zl: (x, zh, y, c, zl ^ 1))
-
-
-def odd_links(value):
+def other_triple(value):
+    return permute(value, lambda x, zh, y, c, zl: (x, zh, y, c, (zl + 3) % 6))
+
+
+def triple_shift(value, step):
     return permute(
-        value, lambda x, zh, y, c, zl: (x, zh, y, c, ((zl - 1) ^ 1) + 1) if 0 < zl < 5 else None
+        value, lambda x, zh, y, c, zl: (x, zh, y, c, zl // 3 * 3 + (zl + step) % 3)
     )
 
 
@@ -53,7 +53,7 @@
 
 
 def gather_x(block):
-    return jnp.stack([block] + [x_swap(block, which) for which in ("even", "odd", "across")])
+    return [block] + [x_swap(block, which) for which in ("even", "odd", "across")]
 
 
 def x_places(x):
@@ -68,51 +68,41 @@
 
 
 def attend_kernel(place_ref, length_ref, temp_ref, *refs):
-    frames, weights_hbm, move_ref, out_ref = refs[:11], refs[11:13], refs[13], refs[14]
-    x_buf, w_in, w_buf, qkv, sems = refs[15:]
+    frames, weights, move_ref, out_ref = refs[:6], refs[6:14], refs[14], refs[15]
+    x_buf, w_in, w_buf, qkv, sems = refs[16:]
     place, x, core = place_ref[0], place_ref[1], place_ref[2]
-    turn = 1 - 2 * lax.rem(place, 2)
-
-    pieces = [(frames[0], place, None)]
-    for step in range(1, 6):
-        for ref, at in (
-            (frames[step], place + turn * step),
-            (frames[5 + step], place - turn * step),
-        ):
-            pieces.append((ref, at, (at >= 0) & (at <= 5)))
-
+    base, within = place // 3 * 3, lax.rem(place, 3)
+    below, above = lax.rem(within + 2, 3), lax.rem(within + 1, 3)
+    slots = (
+        place,
+        base + below,
+        base + above,
+        3 - base + within,
+        3 - base + below,
+        3 - base + above,
+    )
+    w_copies = [
+        pltpu.make_async_copy(ref, w_in.at[number], sems.at[6 + number])
+        for number, ref in enumerate(weights)
+    ]
     copies = [
         pltpu.make_async_copy(ref, x_buf.at[at], sems.at[number])
-        for number, (ref, at, _) in enumerate(pieces)
+        for number, (ref, at) in enumerate(zip(frames, slots))
     ]
-    w_copies = [
-        pltpu.make_async_copy(weights_hbm[which], w_in.at[which], sems.at[11 + which])
-        for which in range(2)
-    ]
-    for copy in w_copies:
+    for copy in w_copies + copies:
         copy.start()
-    for copy, (_, _, valid) in zip(copies, pieces):
-        if valid is None:
-            copy.start()
-        else:
-            pl.when(valid)(copy.start)
-
-    for copy in w_copies:
-        copy.wait()
     for which, half in ((0, core), (1, 1 - core)):
         for number, at in enumerate(x_places(x)):
+            w_copies[4 * which + number].wait()
             rows = pl.ds(pl.multiple_of(at * 384, 384), 384)
             w_buf[half, rows, :] = lax.dot_general(
                 move_ref[...],
-                w_in[which, number],
+                w_in[4 * which + number],
                 (((0,), (0,)), ((), ())),
                 preferred_element_type=jnp.float32,
             ).astype(jnp.bfloat16)
-    for copy, (_, _, valid) in zip(copies, pieces):
-        if valid is None:
-            copy.wait()
-        else:
-            pl.when(valid)(copy.wait)
+    for copy in copies:
+        copy.wait()
 
     total = x_buf.shape[0] * x_buf.shape[1]
     for two in range(2):
@@ -164,14 +154,14 @@
     return pl.pallas_call(
         attend_kernel,
         out_shape=jax.ShapeDtypeStruct((6, shard[0], 256), jnp.bfloat16),
-        in_specs=[SMEM] * 3 + [ANYWHERE] * 13 + [VMEM],
+        in_specs=[SMEM] * 3 + [ANYWHERE] * 14 + [VMEM],
         out_specs=VMEM,
         scratch_shapes=[
             pltpu.VMEM((6,) + shard, jnp.bfloat16),
-            pltpu.VMEM((2, 4, 384, 384), jnp.bfloat16),
+            pltpu.VMEM((8, 384, 384), jnp.bfloat16),
             pltpu.VMEM((2, 1536, 384), jnp.bfloat16),
             pltpu.VMEM((2, 6 * shard[0], 384), jnp.bfloat16),
-            pltpu.SemaphoreType.DMA((13,)),
+            pltpu.SemaphoreType.DMA((14,)),
         ],
         compiler_params=pltpu.CompilerParams(vmem_limit_bytes=28 * 2**20),
         cost_estimate=pl.CostEstimate(
@@ -180,7 +170,8 @@
     )(place, length, temp, *frames, *weights, reorder())
 
 
-def project_kernel(place_ref, heads_ref, own_ref, other_ref, move_ref, out_ref):
+def project_kernel(place_ref, heads_ref, *refs):
+    own, other, move_ref, out_ref = refs[:4], refs[4:8], refs[8], refs[9]
     x, core = place_ref[1], place_ref[2]
     first = jnp.concatenate([heads_ref[at, :, :128] for at in range(6)], axis=1)
     second = jnp.concatenate([heads_ref[at, :, 128:] for at in range(6)], axis=1)
@@ -190,8 +181,8 @@
     for number, at in enumerate(x_places(x)):
         columns = pl.ds(pl.multiple_of(at * 384, 384), 384)
         total = lax.dot_general(
-            mine, own_ref[number], sides, preferred_element_type=jnp.float32
-        ) + lax.dot_general(given, other_ref[number], sides, preferred_element_type=jnp.float32)
+            mine, own[number][...], sides, preferred_element_type=jnp.float32
+        ) + lax.dot_general(given, other[number][...], sides, preferred_element_type=jnp.float32)
         out_ref[:, columns] = jnp.dot(
             total.astype(jnp.bfloat16), move_ref[...], preferred_element_type=jnp.float32
         ).astype(jnp.bfloat16)
@@ -201,47 +192,50 @@
     return pl.pallas_call(
         project_kernel,
         out_shape=jax.ShapeDtypeStruct((heads.shape[1], 1536), jnp.bfloat16),
-        in_specs=[SMEM] + [VMEM] * 4,
+        in_specs=[SMEM] + [VMEM] * 10,
         out_specs=VMEM,
         compiler_params=pltpu.CompilerParams(vmem_limit_bytes=20 * 2**20),
         cost_estimate=pl.CostEstimate(
             flops=8 * 10**8, bytes_accessed=6 * 10**6, transcendentals=0
         ),
-    )(place, heads, own, other, reorder())
+    )(place, heads, *own, *other, reorder())
 
 
 def on_device(latents, norm_gain, w_qkv, w_out, head_temp, lengths):
-    rows = w_qkv.reshape(3, 12, 2, 128).transpose(2, 1, 0, 3).reshape(1, 2, 12, 384)
-    rows = jnp.broadcast_to(rows, (2, 2, 12, 384)).reshape(4, 12, 384)
-    rows = lax.all_to_all(rows, ("zh", "c"), 0, 0, tiled=True).reshape(48, 384)
-
     frames = latents[0]
     values = frames.astype(jnp.float32)
     rms = jnp.sqrt(jnp.mean(values * values, axis=-1, keepdims=True) + 1e-06)
     normed = (values / rms * norm_gain).astype(jnp.bfloat16)
-    evens, odds = [normed], [normed]
-    for _ in range(5):
-        even, odd = even_links(odds[-1]), odd_links(evens[-1])
-        evens.append(even)
-        odds.append(odd)
-
-    by_y = gather_y(after(rows, normed))
-    by_x = gather_x(after(by_y, evens[1], odds[1]))
-
-    turned = w_out.T.reshape(1, 12, 2, 128).transpose(0, 2, 1, 3)
-    turned = jnp.broadcast_to(turned, (12, 2, 12, 128)).reshape(2, 6, 2, 12, 128)
-    turned = turned.reshape(24, 12, 128)
-    columns = lax.all_to_all(after(turned, by_y), ("zh", "zl", "c"), 0, 0, tiled=True)
-    columns = columns.reshape(2, 6, 2, 12, 128).transpose(0, 2, 3, 1, 4).reshape(48, 768)
-    out_by_y = gather_y(after(columns, evens[2], odds[2]))
-
-    weights = (by_x, other_core(after(by_x, evens[3], odds[3])))
-    out_own = gather_x(after(out_by_y, evens[4], odds[4]))
+    across = other_triple(normed)
+
+    rows = w_qkv.reshape(3, 12, 2, 128).transpose(2, 1, 0, 3).reshape(2, 12, 384)
+    columns = w_out.T.reshape(12, 2, 128).transpose(1, 0, 2)
+    both = jnp.concatenate([rows, columns], axis=2).reshape(1, 2, 48, 128)
+    both = jnp.broadcast_to(both, (12, 2, 48, 128)).reshape(24, 48, 128)
+    both = lax.all_to_all(after(both, normed), ("zh", "zl", "c"), 0, 0, tiled=True)
+    both = both.reshape(2, 6, 2, 12, 512)
+    rows = lax.dynamic_index_in_dim(both[..., :384], lax.axis_index("zl"), 1, keepdims=False)
+    rows = rows.reshape(48, 384)
+    columns = after(both, across)[..., 384:].transpose(0, 2, 3, 1, 4).reshape(48, 768)
+
+    own_triple = [triple_shift(normed, 1), triple_shift(normed, 2)]
+    by_y = gather_y(rows)
+    out_by_y = gather_y(after(columns, by_y, *own_triple))
+    by_x = gather_x(by_y)
+    far_triple = [triple_shift(across, 1), triple_shift(across, 2)]
+    other_by_x = [other_core(block) for block in by_x]
+    out_own = gather_x(out_by_y)
 
     place = jnp.stack([lax.axis_index(axis) for axis in ("zl", "x", "c")]).astype(jnp.int32)
-    blocks = attend(place, lengths, head_temp, evens + odds[1:], weights)
+    blocks = attend(
+        place,
+        lengths,
+        head_temp,
+        [normed] + own_triple + [across] + far_triple,
+        by_x + other_by_x,
+    )
     own = lax.all_to_all(blocks, "zl", 0, 0, tiled=True)
-    out_other = other_core(after(out_own, blocks))
+    out_other = [other_core(block) for block in out_own]
     return project(place, own, out_own, out_other)[None]
 
 

time: 179 us -> 178 us (level)
  blocking collectives: 69.1 us -> 0 us
  waiting for transfers between devices: 9.43 us -> 44.6 us
  starting transfers between devices: 68.2 us -> 91.3 us
  local copies, waits for them, and re-layouts: 6.22 us -> 15.7 us
  other arithmetic: 5.72 us -> 1.5 us
  Pallas kernels: 17.6 us -> 21.1 us
    all_to_all x3 -> x0, blocking collectives: 69.1 us -> none  [the longest x1 25.4 us: on_device(): rows = lax.all_to_all(rows, ('zh', 'c'), 0, 0, tiled=True).reshape(48, 384)]
    all_to_all x0 -> x2, starting transfers between devices: none -> 22.9 us  [the longest x1 16.7 us: on_device(): lax.all_to_all(after(both, normed), ('zh', 'zl', 'c'), 0, 0, tiled=True)]
    ppermute x18 -> x19, waiting for transfers between devices: 4.75 us -> 26.3 us  [permute(): return lax.ppermute(value, AXES, pairs)]
    all_to_all x0 -> x2, waiting for transfers between devices: none -> 18.3 us  [the longest x1 11.2 us: on_device(): lax.all_to_all(after(both, normed), ('zh', 'zl', 'c'), 0, 0, tiled=True)]
    unnamed x23 -> x39, local copies, waits for them, and re-layouts: 3.71 us -> 11.4 us
    all_to_all x2, waiting for transfers between devices: 4.68 us -> 0.01 us  [gather_y(): lax.all_to_all(copies, 'y', 0, 0, tiled=True).reshape(-1, value.shape[1])]
    another operation x2 -> x0, other arithmetic: 3.3 us -> none  [gather_x(): jnp.stack([block] + [x_swap(block, which) for which in ('even', 'odd', 'a...]
    all_to_all x2, starting transfers between devices: 11 us -> 13.8 us  [gather_y(): lax.all_to_all(copies, 'y', 0, 0, tiled=True).reshape(-1, value.shape[1])]
  transfers between devices with their start and end apart: 20 -> 23, of which waited for: 3 -> 4; matrix products, arithmetic and copies ran while one was open for 2% -> 1% of each run, Pallas kernels for 8% -> 9%
where the time goes in v4:
time: 178 us; the launch traced here: 175 us
  starting transfers between devices  91.3 us (51%)
  waiting for transfers between devices  44.6 us (25%)
  Pallas kernels  21.1 us (12%)
  local copies, waits for them, and re-layouts  15.7 us (9%)
    ppermute x19, starting transfers between devices, permute(): return lax.ppermute(value, AXES, pairs)  54.7 us
    ppermute x19, waiting for transfers between devices, permute(): return lax.ppermute(value, AXES, pairs)  26.3 us
    all_to_all x1, starting transfers between devices, on_device(): lax.all_to_all(after(both, normed), ('zh', 'zl', 'c'), 0, 0, tiled=True)  16.7 us
    pallas_call x1, Pallas kernels, attend(): pl.pallas_call(attend_kernel, out_shape=jax.ShapeDtypeStruct((6, shard[0]...  16.2 us
    all_to_all x2, starting transfers between devices, gather_y(): lax.all_to_all(copies, 'y', 0, 0, tiled=True).reshape(-1, value.shape[1])  13.8 us
    unnamed x39, local copies, waits for them, and re-layouts  11.4 us
    all_to_all x1, waiting for transfers between devices, on_device(): lax.all_to_all(after(both, normed), ('zh', 'zl', 'c'), 0, 0, tiled=True)  11.2 us
    all_to_all x1, waiting for transfers between devices, on_device(): own = lax.all_to_all(blocks, 'zl', 0, 0, tiled=True)  7.14 us
  transfers between devices with their start and end apart: 23, of which 4 were waited for; matrix products, arithmetic and copies ran while one was open for 1% of the time, Pallas kernels for 9%

profile of v4, /device:TPU:1, one launch (start us, length us, event | category | flops | bytes accessed | tf_op | source)
XLA Modules:
  0.0 175.4 jit_solution(5817105849389867163)
XLA Ops:
  4.4 16.7 %all-to-all-start = ((bf16[24,48,128]{2,1,0:T(8,128)(2,1)}), bf16[24,48,128]{2,1,0:T(8,128)(2,1)S(1)}, u32[]{:S(2)}, u32[]{:S(2)}) async-start(bf16[24,48,128]{2,1,0:T(8,128)(2,1)} %bitcast.8), calls=%async_computation | async-start | bytes 589824 | tf_op jit(solution)/shard_map/all_to_all | solution.py:215
  21.1 5.1 %collective-permute-start.2 = (bf16[128,1536]{1,0:T(8,128)(2,1)S(1)}, bf16[128,1536]{1,0:T(8,128)(2,1)S(1)}, u32[]{:S(2)}, u32[]{:S(2)}) collective-permute-start(bf16[128,1536]{1,0:T(8,128)(2,1)S(1)} %fusion.2.refs_0_), channel_id=1, source_target_pairs={{0,3},{1,4},{2,5},{3,0},{4,1},{5,2},{6,9},{7,10},{8,11},{9,6},{10,... | collective-permute-start | bytes 1179656 | tf_op jit(solution)/shard_map/ppermute | solution.py:24
  26.3 11.2 %all-to-all-done = bf16[24,48,128]{2,1,0:T(8,128)(2,1)S(1)} async-done(((bf16[24,48,128]{2,1,0:T(8,128)(2,1)}), bf16[24,48,128]{2,1,0:T(8,128)(2,1)S(1)}, u32[]{:S(2)}, u32[]{:S(2)}) %all-to-all-start) | async-done | bytes 294944 | tf_op jit(solution)/shard_map/all_to_all | solution.py:215
  38.5 6.8 %all-to-all-start.1 = ((bf16[8,48,384]{2,1,0:T(8,128)(2,1)}), bf16[8,48,384]{2,1,0:T(8,128)(2,1)S(1)}, u32[]{:S(2)}, u32[]{:S(2)}) async-start(bf16[8,48,384]{2,1,0:T(8,128)(2,1)} %broadcast_in_dim.28), calls=%async_computation.1 | async-start | bytes 589824 | tf_op jit(solution)/shard_map/all_to_all | solution.py:48
  45.3 3.7 %collective-permute-start.1 = (bf16[128,1536]{1,0:T(8,128)(2,1)S(1)}, bf16[128,1536]{1,0:T(8,128)(2,1)S(1)}, u32[]{:S(2)}, u32[]{:S(2)}) collective-permute-start(bf16[128,1536]{1,0:T(8,128)(2,1)S(1)} %fusion.2.refs_0_), channel_id=1, source_target_pairs={{0,2},{1,0},{2,1},{3,5},{4,3},{5,4},{6,8},{7,6},{8,7},{9,11},{10,9... | collective-permute-start | bytes 1179656 | tf_op jit(solution)/shard_map/ppermute | solution.py:24
  51.0 9.1 %collective-permute-done.2.refs_3_ = bf16[128,1536]{1,0:T(8,128)(2,1)S(1)} collective-permute-done((bf16[128,1536]{1,0:T(8,128)(2,1)S(1)}, bf16[128,1536]{1,0:T(8,128)(2,1)S(1)}, u32[]{:S(2)}, u32[]{:S(2)}) %collective-permute-start.2) | collective-permute-done | bytes 393248 | tf_op jit(solution)/shard_map/ppermute | solution.py:24
  60.2 17.2 %collective-permute-done.refs_1_ = bf16[128,1536]{1,0:T(8,128)(2,1)S(1)} collective-permute-done((bf16[128,1536]{1,0:T(8,128)(2,1)S(1)}, bf16[128,1536]{1,0:T(8,128)(2,1)S(1)}, u32[]{:S(2)}, u32[]{:S(2)}) %collective-permute-start) | collective-permute-done | bytes 393248 | tf_op jit(solution)/shard_map/ppermute | solution.py:24
  78.3 6.9 %all-to-all-start.3 = ((bf16[8,48,768]{2,1,0:T(8,128)(2,1)}), bf16[8,48,768]{2,1,0:T(8,128)(2,1)S(1)}, u32[]{:S(2)}, u32[]{:S(2)}) async-start(bf16[8,48,768]{2,1,0:T(8,128)(2,1)} %broadcast_in_dim.29), calls=%async_computation.3 | async-start | bytes 1179648 | tf_op jit(solution)/shard_map/all_to_all | solution.py:48
  87.1 4.7 %collective-permute-start.7 = (bf16[384,384]{1,0:T(8,128)(2,1)S(1)}, bf16[384,384]{1,0:T(8,128)(2,1)S(1)}, u32[]{:S(2)}, u32[]{:S(2)}) collective-permute-start(bf16[384,384]{1,0:T(8,128)(2,1)S(1)} %bitcast.30), channel_id=1, source_target_pairs={{0,384},{1,385},{2,386},{3,387},{4,388},{5,389},{6,390},{7,391},{8... | collective-permute-start | bytes 884744 | tf_op jit(solution)/shard_map/ppermute | solution.py:24
  91.8 2.8 %collective-permute-start.6 = (bf16[384,384]{1,0:T(8,128)(2,1)S(1)}, bf16[384,384]{1,0:T(8,128)(2,1)}, u32[]{:S(2)}, u32[]{:S(2)}) collective-permute-start(bf16[384,384]{1,0:T(8,128)(2,1)S(1)} %bitcast.31), channel_id=1, source_target_pairs={{0,576},{1,577},{2,578},{3,579},{4,580},{5,581},{6,582},{7,583},{8... | collective-permute-start | bytes 884744 | tf_op jit(solution)/shard_map/ppermute | solution.py:24
  94.6 1.9 %collective-permute-start.5 = (bf16[384,384]{1,0:T(8,128)(2,1)S(1)}, bf16[384,384]{1,0:T(8,128)(2,1)}, u32[]{:S(2)}, u32[]{:S(2)}) collective-permute-start(bf16[384,384]{1,0:T(8,128)(2,1)S(1)} %bitcast.32), channel_id=1, source_target_pairs={{0,192},{1,193},{2,194},{3,195},{4,196},{5,197},{6,198},{7,199},{8... | collective-permute-start | bytes 884744 | tf_op jit(solution)/shard_map/ppermute | solution.py:24
  96.5 3.4 %collective-permute-start.3 = (bf16[128,1536]{1,0:T(8,128)(2,1)S(1)}, bf16[128,1536]{1,0:T(8,128)(2,1)S(1)}, u32[]{:S(2)}, u32[]{:S(2)}) collective-permute-start(bf16[128,1536]{1,0:T(8,128)(2,1)S(1)} %collective-permute-done.2.refs_3_), channel_id=1, source_target_pairs={{0,1},{1,2},{2,0},{3,4},{4,5},{5,3},{6,7},{7,8},{8,6},{9,10},{10,1... | collective-permute-start | bytes 1179656 | tf_op jit(solution)/shard_map/ppermute | solution.py:24
  100.7 3.7 %collective-permute-start.8 = (bf16[384,384]{1,0:T(8,128)(2,1)S(1)}, bf16[384,384]{1,0:T(8,128)(2,1)S(1)}, u32[]{:S(2)}, u32[]{:S(2)}) collective-permute-start(bf16[384,384]{1,0:T(8,128)(2,1)S(1)} %bitcast.33), channel_id=1, source_target_pairs={{0,6},{1,7},{2,8},{3,9},{4,10},{5,11},{6,0},{7,1},{8,2},{9,3},{10,... | collective-permute-start | bytes 884744 | tf_op jit(solution)/shard_map/ppermute | solution.py:24
  104.4 1.9 %collective-permute-start.11 = (bf16[384,384]{1,0:T(8,128)(2,1)S(1)}, bf16[384,384]{1,0:T(8,128)(2,1)}, u32[]{:S(2)}, u32[]{:S(2)}) collective-permute-start(bf16[384,384]{1,0:T(8,128)(2,1)S(1)} %collective-permute-done.7.refs_9_), channel_id=1, source_target_pairs={{0,6},{1,7},{2,8},{3,9},{4,10},{5,11},{6,0},{7,1},{8,2},{9,3},{10,... | collective-permute-start | bytes 884744 | tf_op jit(solution)/shard_map/ppermute | solution.py:24
  107.0 2.4 %collective-permute-start.10 = (bf16[384,384]{1,0:T(8,128)(2,1)}, bf16[384,384]{1,0:T(8,128)(2,1)}, u32[]{:S(2)}, u32[]{:S(2)}) collective-permute-start(bf16[384,384]{1,0:T(8,128)(2,1)} %collective-permute-done.6.refs_8_), channel_id=1, source_target_pairs={{0,6},{1,7},{2,8},{3,9},{4,10},{5,11},{6,0},{7,1},{8,2},{9,3},{10,... | collective-permute-start | bytes 884744 | tf_op jit(solution)/shard_map/ppermute | solution.py:24
  109.4 1.9 %collective-permute-start.9 = (bf16[384,384]{1,0:T(8,128)(2,1)}, bf16[384,384]{1,0:T(8,128)(2,1)}, u32[]{:S(2)}, u32[]{:S(2)}) collective-permute-start(bf16[384,384]{1,0:T(8,128)(2,1)} %collective-permute-done.5.refs_7_), channel_id=1, source_target_pairs={{0,6},{1,7},{2,8},{3,9},{4,10},{5,11},{6,0},{7,1},{8,2},{9,3},{10,... | collective-permute-start | bytes 884744 | tf_op jit(solution)/shard_map/ppermute | solution.py:24
  112.9 5.2 %collective-permute-start.14 = (bf16[384,768]{1,0:T(8,128)(2,1)S(1)}, bf16[384,768]{1,0:T(8,128)(2,1)S(1)}, u32[]{:S(2)}, u32[]{:S(2)}) collective-permute-start(bf16[384,768]{1,0:T(8,128)(2,1)S(1)} %bitcast.25), channel_id=1, source_target_pairs={{0,384},{1,385},{2,386},{3,387},{4,388},{5,389},{6,390},{7,391},{8... | collective-permute-start | bytes 1769480 | tf_op jit(solution)/shard_map/ppermute | solution.py:24
  118.8 2.8 %collective-permute-start.13 = (bf16[384,768]{1,0:T(8,128)(2,1)S(1)}, bf16[384,768]{1,0:T(8,128)(2,1)S(1)}, u32[]{:S(2)}, u32[]{:S(2)}) collective-permute-start(bf16[384,768]{1,0:T(8,128)(2,1)S(1)} %bitcast.26), channel_id=1, source_target_pairs={{0,576},{1,577},{2,578},{3,579},{4,580},{5,581},{6,582},{7,583},{8... | collective-permute-start | bytes 1769480 | tf_op jit(solution)/shard_map/ppermute | solution.py:24
  130.4 16.2 %shard_map.82 = bf16[6,128,256]{2,1,0:T(8,128)(2,1)} custom-call(s32[3]{0:T(128)S(1)} %pad_add_fusion.place_ref, s32[1]{0:T(128)S(6)} %copy.18.length_ref, f32[4]{0:T(128)S(1)} %copy-done.16, bf16[128,1536]{1,0:T(8,128)(2,1)S(1)} %fusion.2.refs_0_, bf16[128,1536]{1,0:T(8,128)(2,1)S(1)} %copy-done.7, bf16[128,1536]{1,0:T(8,128)(2,1)S(1)} %copy-done.5, ...), custom_call_target="tpu_custom_call" | custom-call | flops 3000000000 | bytes 5000000 | tf_op jit(solution)/shard_map/pallas_call | solution.py:154
  146.6 6.2 %all-to-all-start.2 = ((bf16[6,128,256]{2,1,0:T(8,128)(2,1)}), bf16[6,128,256]{2,1,0:T(8,128)(2,1)S(1)}, u32[]{:S(2)}, u32[]{:S(2)}) async-start(bf16[6,128,256]{2,1,0:T(8,128)(2,1)} %shard_map.82), calls=%async_computation.2 | async-start | bytes 786432 | tf_op jit(solution)/shard_map/all_to_all | solution.py:237
  152.8 3.2 %collective-permute-start.15 = (bf16[384,768]{1,0:T(8,128)(2,1)S(1)}, bf16[384,768]{1,0:T(8,128)(2,1)S(1)}, u32[]{:S(2)}, u32[]{:S(2)}) collective-permute-start(bf16[384,768]{1,0:T(8,128)(2,1)S(1)} %bitcast.28), channel_id=1, source_target_pairs={{0,6},{1,7},{2,8},{3,9},{4,10},{5,11},{6,0},{7,1},{8,2},{9,3},{10,... | collective-permute-start | bytes 1769480 | tf_op jit(solution)/shard_map/ppermute | solution.py:24
  158.0 2.4 %collective-permute-start.17 = (bf16[384,768]{1,0:T(8,128)(2,1)S(1)}, bf16[384,768]{1,0:T(8,128)(2,1)}, u32[]{:S(2)}, u32[]{:S(2)}) collective-permute-start(bf16[384,768]{1,0:T(8,128)(2,1)S(1)} %collective-permute-done.13.refs_2_), channel_id=1, source_target_pairs={{0,6},{1,7},{2,8},{3,9},{4,10},{5,11},{6,0},{7,1},{8,2},{9,3},{10,... | collective-permute-start | bytes 1769480 | tf_op jit(solution)/shard_map/ppermute | solution.py:24
  162.4 7.1 %all-to-all-done.2.heads_ref = bf16[6,128,256]{2,1,0:T(8,128)(2,1)S(1)} async-done(((bf16[6,128,256]{2,1,0:T(8,128)(2,1)}), bf16[6,128,256]{2,1,0:T(8,128)(2,1)S(1)}, u32[]{:S(2)}, u32[]{:S(2)}) %all-to-all-start.2) | async-done | bytes 393248 | tf_op jit(solution)/shard_map/all_to_all | solution.py:237
  170.5 4.9 %shard_map.83 = bf16[128,1536]{1,0:T(8,128)(2,1)} custom-call(s32[3]{0:T(128)S(1)} %pad_add_fusion.place_ref, bf16[6,128,256]{2,1,0:T(8,128)(2,1)S(1)} %all-to-all-done.2.heads_ref, bf16[384,768]{1,0:T(8,128)(2,1)S(1)} %bitcast.29, bf16[384,768]{1,0:T(8,128)(2,1)S(1)} %collective-permute-done.12.refs_1_, ...), custom_call_target="tpu_custom_call" | custom-call | flops 800000000 | bytes 6000000 | tf_op jit(solution)/shard_map/pallas_call | solution.py:192
  (83 shorter events, 26.9 us)
Async XLA Ops:
  4.4 33.0 %all-to-all-start = ((bf16[24,48,128]{2,1,0:T(8,128)(2,1)}), bf16[24,48,128]{2,1,0:T(8,128)(2,1)S(1)}, u32[]{:S(2)}, u32[]{:S(2)}) async-start(bf16[24,48,128]{2,1,0:T(8,128)(2,1)} %bitcast.8), calls=%async_computation | async-start | bytes 589824 | tf_op jit(solution)/shard_map/all_to_all | solution.py:215
  21.1 38.9 %collective-permute-start.2 = (bf16[128,1536]{1,0:T(8,128)(2,1)S(1)}, bf16[128,1536]{1,0:T(8,128)(2,1)S(1)}, u32[]{:S(2)}, u32[]{:S(2)}) collective-permute-start(bf16[128,1536]{1,0:T(8,128)(2,1)S(1)} %fusion.2.refs_0_), channel_id=1, source_target_pairs={{0,3},{1,4},{2,5},{3,0},{4,1},{5,2},{6,9},{7,10},{8,11},{9,6},{10,... | collective-permute-start | bytes 1179656 | tf_op jit(solution)/shard_map/ppermute | solution.py:24
  38.5 38.9 %all-to-all-start.1 = ((bf16[8,48,384]{2,1,0:T(8,128)(2,1)}), bf16[8,48,384]{2,1,0:T(8,128)(2,1)S(1)}, u32[]{:S(2)}, u32[]{:S(2)}) async-start(bf16[8,48,384]{2,1,0:T(8,128)(2,1)} %broadcast_in_dim.28), calls=%async_computation.1 | async-start | bytes 589824 | tf_op jit(solution)/shard_map/all_to_all | solution.py:48
  45.3 14.9 %collective-permute-start.1 = (bf16[128,1536]{1,0:T(8,128)(2,1)S(1)}, bf16[128,1536]{1,0:T(8,128)(2,1)S(1)}, u32[]{:S(2)}, u32[]{:S(2)}) collective-permute-start(bf16[128,1536]{1,0:T(8,128)(2,1)S(1)} %fusion.2.refs_0_), channel_id=1, source_target_pairs={{0,2},{1,0},{2,1},{3,5},{4,3},{5,4},{6,8},{7,6},{8,7},{9,11},{10,9... | collective-permute-start | bytes 1179656 | tf_op jit(solution)/shard_map/ppermute | solution.py:24
  49.0 28.3 %collective-permute-start = (bf16[128,1536]{1,0:T(8,128)(2,1)S(1)}, bf16[128,1536]{1,0:T(8,128)(2,1)S(1)}, u32[]{:S(2)}, u32[]{:S(2)}) collective-permute-start(bf16[128,1536]{1,0:T(8,128)(2,1)S(1)} %fusion.2.refs_0_), channel_id=1, source_target_pairs={{0,1},{1,2},{2,0},{3,4},{4,5},{5,3},{6,7},{7,8},{8,6},{9,10},{10,1... | collective-permute-start | bytes 1179656 | tf_op jit(solution)/shard_map/ppermute | solution.py:24
  78.3 45.2 %copy-start = (bf16[384,384]{1,0:T(8,128)(2,1)S(1)}, bf16[384,384]{1,0:T(8,128)(2,1)}, u32[]{:S(2)}) copy-start(bf16[384,384]{1,0:T(8,128)(2,1)} %constant.26.clone.refs_14_.refs_8_) | copy-start | bytes 884740
  78.3 34.6 %all-to-all-start.3 = ((bf16[8,48,768]{2,1,0:T(8,128)(2,1)}), bf16[8,48,768]{2,1,0:T(8,128)(2,1)S(1)}, u32[]{:S(2)}, u32[]{:S(2)}) async-start(bf16[8,48,768]{2,1,0:T(8,128)(2,1)} %broadcast_in_dim.29), calls=%async_computation.3 | async-start | bytes 1179648 | tf_op jit(solution)/shard_map/all_to_all | solution.py:48
  85.2 14.7 %collective-permute-start.4 = (bf16[128,1536]{1,0:T(8,128)(2,1)S(1)}, bf16[128,1536]{1,0:T(8,128)(2,1)S(1)}, u32[]{:S(2)}, u32[]{:S(2)}) collective-permute-start(bf16[128,1536]{1,0:T(8,128)(2,1)S(1)} %collective-permute-done.2.refs_3_), channel_id=1, source_target_pairs={{0,2},{1,0},{2,1},{3,5},{4,3},{5,4},{6,8},{7,6},{8,7},{9,11},{10,9... | collective-permute-start | bytes 1179656 | tf_op jit(solution)/shard_map/ppermute | solution.py:24
  87.1 17.2 %collective-permute-start.7 = (bf16[384,384]{1,0:T(8,128)(2,1)S(1)}, bf16[384,384]{1,0:T(8,128)(2,1)S(1)}, u32[]{:S(2)}, u32[]{:S(2)}) collective-permute-start(bf16[384,384]{1,0:T(8,128)(2,1)S(1)} %bitcast.30), channel_id=1, source_target_pairs={{0,384},{1,385},{2,386},{3,387},{4,388},{5,389},{6,390},{7,391},{8... | collective-permute-start | bytes 884744 | tf_op jit(solution)/shard_map/ppermute | solution.py:24
  91.8 15.2 %collective-permute-start.6 = (bf16[384,384]{1,0:T(8,128)(2,1)S(1)}, bf16[384,384]{1,0:T(8,128)(2,1)}, u32[]{:S(2)}, u32[]{:S(2)}) collective-permute-start(bf16[384,384]{1,0:T(8,128)(2,1)S(1)} %bitcast.31), channel_id=1, source_target_pairs={{0,576},{1,577},{2,578},{3,579},{4,580},{5,581},{6,582},{7,583},{8... | collective-permute-start | bytes 884744 | tf_op jit(solution)/shard_map/ppermute | solution.py:24
  94.6 14.9 %collective-permute-start.5 = (bf16[384,384]{1,0:T(8,128)(2,1)S(1)}, bf16[384,384]{1,0:T(8,128)(2,1)}, u32[]{:S(2)}, u32[]{:S(2)}) collective-permute-start(bf16[384,384]{1,0:T(8,128)(2,1)S(1)} %bitcast.32), channel_id=1, source_target_pairs={{0,192},{1,193},{2,194},{3,195},{4,196},{5,197},{6,198},{7,199},{8... | collective-permute-start | bytes 884744 | tf_op jit(solution)/shard_map/ppermute | solution.py:24
  96.5 15.6 %collective-permute-start.3 = (bf16[128,1536]{1,0:T(8,128)(2,1)S(1)}, bf16[128,1536]{1,0:T(8,128)(2,1)S(1)}, u32[]{:S(2)}, u32[]{:S(2)}) collective-permute-start(bf16[128,1536]{1,0:T(8,128)(2,1)S(1)} %collective-permute-done.2.refs_3_), channel_id=1, source_target_pairs={{0,1},{1,2},{2,0},{3,4},{4,5},{5,3},{6,7},{7,8},{8,6},{9,10},{10,1... | collective-permute-start | bytes 1179656 | tf_op jit(solution)/shard_map/ppermute | solution.py:24
  100.7 17.4 %collective-permute-start.8 = (bf16[384,384]{1,0:T(8,128)(2,1)S(1)}, bf16[384,384]{1,0:T(8,128)(2,1)S(1)}, u32[]{:S(2)}, u32[]{:S(2)}) collective-permute-start(bf16[384,384]{1,0:T(8,128)(2,1)S(1)} %bitcast.33), channel_id=1, source_target_pairs={{0,6},{1,7},{2,8},{3,9},{4,10},{5,11},{6,0},{7,1},{8,2},{9,3},{10,... | collective-permute-start | bytes 884744 | tf_op jit(solution)/shard_map/ppermute | solution.py:24
  104.4 17.1 %collective-permute-start.11 = (bf16[384,384]{1,0:T(8,128)(2,1)S(1)}, bf16[384,384]{1,0:T(8,128)(2,1)}, u32[]{:S(2)}, u32[]{:S(2)}) collective-permute-start(bf16[384,384]{1,0:T(8,128)(2,1)S(1)} %collective-permute-done.7.refs_9_), channel_id=1, source_target_pairs={{0,6},{1,7},{2,8},{3,9},{4,10},{5,11},{6,0},{7,1},{8,2},{9,3},{10,... | collective-permute-start | bytes 884744 | tf_op jit(solution)/shard_map/ppermute | solution.py:24
  107.0 16.4 %collective-permute-start.10 = (bf16[384,384]{1,0:T(8,128)(2,1)}, bf16[384,384]{1,0:T(8,128)(2,1)}, u32[]{:S(2)}, u32[]{:S(2)}) collective-permute-start(bf16[384,384]{1,0:T(8,128)(2,1)} %collective-permute-done.6.refs_8_), channel_id=1, source_target_pairs={{0,6},{1,7},{2,8},{3,9},{4,10},{5,11},{6,0},{7,1},{8,2},{9,3},{10,... | collective-permute-start | bytes 884744 | tf_op jit(solution)/shard_map/ppermute | solution.py:24
  109.4 14.0 %collective-permute-start.9 = (bf16[384,384]{1,0:T(8,128)(2,1)}, bf16[384,384]{1,0:T(8,128)(2,1)}, u32[]{:S(2)}, u32[]{:S(2)}) collective-permute-start(bf16[384,384]{1,0:T(8,128)(2,1)} %collective-permute-done.5.refs_7_), channel_id=1, source_target_pairs={{0,6},{1,7},{2,8},{3,9},{4,10},{5,11},{6,0},{7,1},{8,2},{9,3},{10,... | collective-permute-start | bytes 884744 | tf_op jit(solution)/shard_map/ppermute | solution.py:24
  112.9 43.2 %collective-permute-start.14 = (bf16[384,768]{1,0:T(8,128)(2,1)S(1)}, bf16[384,768]{1,0:T(8,128)(2,1)S(1)}, u32[]{:S(2)}, u32[]{:S(2)}) collective-permute-start(bf16[384,768]{1,0:T(8,128)(2,1)S(1)} %bitcast.25), channel_id=1, source_target_pairs={{0,384},{1,385},{2,386},{3,387},{4,388},{5,389},{6,390},{7,391},{8... | collective-permute-start | bytes 1769480 | tf_op jit(solution)/shard_map/ppermute | solution.py:24
  118.8 39.3 %collective-permute-start.13 = (bf16[384,768]{1,0:T(8,128)(2,1)S(1)}, bf16[384,768]{1,0:T(8,128)(2,1)S(1)}, u32[]{:S(2)}, u32[]{:S(2)}) collective-permute-start(bf16[384,768]{1,0:T(8,128)(2,1)S(1)} %bitcast.26), channel_id=1, source_target_pairs={{0,576},{1,577},{2,578},{3,579},{4,580},{5,581},{6,582},{7,583},{8... | collective-permute-start | bytes 1769480 | tf_op jit(solution)/shard_map/ppermute | solution.py:24
  121.5 38.9 %collective-permute-start.12 = (bf16[384,768]{1,0:T(8,128)(2,1)S(1)}, bf16[384,768]{1,0:T(8,128)(2,1)S(1)}, u32[]{:S(2)}, u32[]{:S(2)}) collective-permute-start(bf16[384,768]{1,0:T(8,128)(2,1)S(1)} %bitcast.27), channel_id=1, source_target_pairs={{0,192},{1,193},{2,194},{3,195},{4,196},{5,197},{6,198},{7,199},{8... | collective-permute-start | bytes 1769480 | tf_op jit(solution)/shard_map/ppermute | solution.py:24
  146.6 22.9 %all-to-all-start.2 = ((bf16[6,128,256]{2,1,0:T(8,128)(2,1)}), bf16[6,128,256]{2,1,0:T(8,128)(2,1)S(1)}, u32[]{:S(2)}, u32[]{:S(2)}) async-start(bf16[6,128,256]{2,1,0:T(8,128)(2,1)} %shard_map.82), calls=%async_computation.2 | async-start | bytes 786432 | tf_op jit(solution)/shard_map/all_to_all | solution.py:237
  152.8 16.7 %collective-permute-start.15 = (bf16[384,768]{1,0:T(8,128)(2,1)S(1)}, bf16[384,768]{1,0:T(8,128)(2,1)S(1)}, u32[]{:S(2)}, u32[]{:S(2)}) collective-permute-start(bf16[384,768]{1,0:T(8,128)(2,1)S(1)} %bitcast.28), channel_id=1, source_target_pairs={{0,6},{1,7},{2,8},{3,9},{4,10},{5,11},{6,0},{7,1},{8,2},{9,3},{10,... | collective-permute-start | bytes 1769480 | tf_op jit(solution)/shard_map/ppermute | solution.py:24
  156.1 13.4 %collective-permute-start.18 = (bf16[384,768]{1,0:T(8,128)(2,1)S(1)}, bf16[384,768]{1,0:T(8,128)(2,1)}, u32[]{:S(2)}, u32[]{:S(2)}) collective-permute-start(bf16[384,768]{1,0:T(8,128)(2,1)S(1)} %collective-permute-done.14.refs_3_), channel_id=1, source_target_pairs={{0,6},{1,7},{2,8},{3,9},{4,10},{5,11},{6,0},{7,1},{8,2},{9,3},{10,... | collective-permute-start | bytes 1769480 | tf_op jit(solution)/shard_map/ppermute | solution.py:24
  158.0 11.5 %collective-permute-start.17 = (bf16[384,768]{1,0:T(8,128)(2,1)S(1)}, bf16[384,768]{1,0:T(8,128)(2,1)}, u32[]{:S(2)}, u32[]{:S(2)}) collective-permute-start(bf16[384,768]{1,0:T(8,128)(2,1)S(1)} %collective-permute-done.13.refs_2_), channel_id=1, source_target_pairs={{0,6},{1,7},{2,8},{3,9},{4,10},{5,11},{6,0},{7,1},{8,2},{9,3},{10,... | collective-permute-start | bytes 1769480 | tf_op jit(solution)/shard_map/ppermute | solution.py:24
  160.5 9.1 %collective-permute-start.16 = (bf16[384,768]{1,0:T(8,128)(2,1)S(1)}, bf16[384,768]{1,0:T(8,128)(2,1)}, u32[]{:S(2)}, u32[]{:S(2)}) collective-permute-start(bf16[384,768]{1,0:T(8,128)(2,1)S(1)} %collective-permute-done.12.refs_1_), channel_id=1, source_target_pairs={{0,6},{1,7},{2,8},{3,9},{4,10},{5,11},{6,0},{7,1},{8,2},{9,3},{10,... | collective-permute-start | bytes 1769480 | tf_op jit(solution)/shard_map/ppermute | solution.py:24
  (18 other events, 81.3 us)

commit v5 on v4

v5 whole, which is shorter than its diff:
```python
import functools

import jax
import jax.numpy as jnp
import numpy as np
from jax import lax
from jax.experimental import pallas as pl
from jax.experimental.pallas import tpu as pltpu
from jax.sharding import Mesh, PartitionSpec as P

HD = 64
AXES = ("x", "zh", "y", "c", "zl")
SIZES = (4, 2, 8, 2, 6)


def permute(value, move):
    pairs = []
    for place in np.ndindex(*SIZES):
        goal = move(*place)
        if goal is not None:
            pairs.append(
                (int(np.ravel_multi_index(place, SIZES)), int(np.ravel_multi_index(goal, SIZES)))
            )
    return lax.ppermute(value, AXES, pairs)


def other_core(value):
    return permute(value, lambda x, zh, y, c, zl: (x, zh, y, 1 - c, zl))


def y_shift(value, step):
    return permute(value, lambda x, zh, y, c, zl: (x, zh, (y + step) % 8, c, zl))


def x_swap(value, which):
    goal = {"even": (1, 0, 3, 2), "odd": (3, 2, 1, 0), "across": (2, 3, 0, 1)}[which]
    return permute(value, lambda x, zh, y, c, zl: (goal[x], zh, y, c, zl))


def gather(value, axes, count):
    copies = jnp.broadcast_to(value[None], (count,) + value.shape)
    return lax.all_to_all(copies, axes, 0, 0, tiled=True).reshape(-1, value.shape[1])


def after(value, *others):
    return lax.optimization_barrier((value,) + others)[0]


def put(whole, block, at):
    return lax.dynamic_update_slice_in_dim(whole, block[None], at, 0)


def gather_x(block):
    x = lax.axis_index("x")
    whole = put(jnp.zeros((4,) + block.shape, block.dtype), block, x)
    for which, at in (("even", x ^ 1), ("odd", 3 - x), ("across", (x + 2) % 4)):
        whole = put(whole, x_swap(block, which), at)
    return whole.reshape(-1, block.shape[1])


def gather_y(block):
    y = lax.axis_index("y")
    whole = put(jnp.zeros((8,) + block.shape, block.dtype), block, y)
    up = down = block
    for step in range(1, 5):
        up = y_shift(up, 1)
        whole = put(whole, up, (y + 8 - step) % 8)
        if step < 4:
            down = y_shift(down, -1)
            whole = put(whole, down, (y + step) % 8)
    return whole.reshape(-1, block.shape[1])


def reorder():
    y, zh, r = np.meshgrid(np.arange(8), np.arange(2), np.arange(24), indexing="ij")
    matrix = np.zeros((384, 384), np.float32)
    matrix[np.arange(384), ((zh * 8 + y) * 24 + r).reshape(-1)] = 1
    return jnp.asarray(matrix, jnp.bfloat16)


def reorder_all():
    y, x, zh, r = np.meshgrid(
        np.arange(8), np.arange(4), np.arange(2), np.arange(24), indexing="ij"
    )
    matrix = np.zeros((1536, 1536), np.float32)
    matrix[np.arange(1536), (((x * 2 + zh) * 8 + y) * 24 + r).reshape(-1)] = 1
    return jnp.asarray(matrix, jnp.bfloat16)


def attend_kernel(core_ref, length_ref, temp_ref, frames, own_w, other_w, move_ref, *refs):
    out_ref, x_buf, w_in, w_buf, qkv, sems = refs
    core = core_ref[0]
    w_copies = [
        pltpu.make_async_copy(ref, w_in.at[number], sems.at[number])
        for number, ref in enumerate((own_w, other_w))
    ]
    x_copy = pltpu.make_async_copy(frames, x_buf, sems.at[2])
    for copy in w_copies + [x_copy]:
        copy.start()
    for which, half in ((0, core), (1, 1 - core)):
        w_copies[which].wait()
        for at in range(4):
            rows = slice(at * 384, at * 384 + 384)
            w_buf[half, rows, :] = lax.dot_general(
                move_ref[...],
                w_in[which, rows, :],
                (((0,), (0,)), ((), ())),
                preferred_element_type=jnp.float32,
            ).astype(jnp.bfloat16)
    x_copy.wait()

    total = x_buf.shape[0]
    for two in range(2):
        qkv[two] = jnp.dot(
            x_buf[...],
            w_buf[two],
            preferred_element_type=jnp.float32,
        ).astype(jnp.bfloat16)

    live = lax.broadcasted_iota(jnp.int32, (1, total), 1) < length_ref[0]
    lane = lax.broadcasted_iota(jnp.int32, (128, 128), 1)
    row = lax.broadcasted_iota(jnp.int32, (256, 1), 0)

    def query_block(block, carry):
        rows = pl.ds(pl.multiple_of(block * 128, 128), 128)
        for two in range(2):
            query = qkv[two, rows, :128]
            none = jnp.zeros_like(query)
            query = jnp.concatenate(
                [jnp.where(lane < HD, query, none), jnp.where(lane < HD, none, query)]
            )
            scores = lax.dot_general(
                query,
                qkv[two, :, 128:256],
                (((1,), (1,)), ((), ())),
                preferred_element_type=jnp.float32,
            )
            scale = jnp.where(row < 128, temp_ref[2 * two] / 8.0, temp_ref[2 * two + 1] / 8.0)
            scores = jnp.where(live, scores * scale, -1e30)
            scores = jnp.exp(scores - jnp.max(scores, axis=-1, keepdims=True))
            probs = scores * (1.0 / jnp.sum(scores, axis=-1, keepdims=True))
            mixed = jnp.dot(
                probs.astype(jnp.bfloat16), qkv[two, :, 256:], preferred_element_type=jnp.float32
            )
            mixed = jnp.where(lane < HD, mixed[:128], mixed[128:])
            out_ref[block, :, two * 128 : two * 128 + 128] = mixed.astype(jnp.bfloat16)
        return carry

    lax.fori_loop(0, 6, query_block, 0)


SMEM = pl.BlockSpec(memory_space=pltpu.SMEM)
VMEM = pl.BlockSpec(memory_space=pltpu.VMEM)
HBM = pl.BlockSpec(memory_space=pltpu.HBM)


def attend(core, length, temp, frames, own_w, other_w):
    rows, width = frames.shape
    return pl.pallas_call(
        attend_kernel,
        out_shape=jax.ShapeDtypeStruct((6, rows // 6, 256), jnp.bfloat16),
        in_specs=[SMEM] * 3 + [HBM] * 3 + [VMEM],
        out_specs=VMEM,
        scratch_shapes=[
            pltpu.VMEM((rows, width), jnp.bfloat16),
            pltpu.VMEM((2, width, 384), jnp.bfloat16),
            pltpu.VMEM((2, width, 384), jnp.bfloat16),
            pltpu.VMEM((2, rows, 384), jnp.bfloat16),
            pltpu.SemaphoreType.DMA((3,)),
        ],
        compiler_params=pltpu.CompilerParams(vmem_limit_bytes=58 * 2**20),
        cost_estimate=pl.CostEstimate(
            flops=3 * 10**9, bytes_accessed=5 * 10**6, transcendentals=2 * 10**6
        ),
    )(core, length, temp, frames, own_w, other_w, reorder())


def project_kernel(core_ref, heads_ref, own_ref, other_ref, move_hbm, out_ref, move_ref, sem):
    core = core_ref[0]
    move_copy = pltpu.make_async_copy(move_hbm, move_ref, sem)
    move_copy.start()
    first = jnp.concatenate([heads_ref[at, :, :128] for at in range(6)], axis=1)
    second = jnp.concatenate([heads_ref[at, :, 128:] for at in range(6)], axis=1)
    mine = jnp.where(core == 0, first, second)
    given = jnp.where(core == 0, second, first)
    sides = (((1,), (1,)), ((), ()))
    total = lax.dot_general(mine, own_ref[...], sides, preferred_element_type=jnp.float32)
    total += lax.dot_general(given, other_ref[...], sides, preferred_element_type=jnp.float32)
    move_copy.wait()
    out_ref[...] = jnp.dot(
        total.astype(jnp.bfloat16), move_ref[...], preferred_element_type=jnp.float32
    ).astype(jnp.bfloat16)


def project(core, heads, own, other):
    return pl.pallas_call(
        project_kernel,
        out_shape=jax.ShapeDtypeStruct((heads.shape[1], 1536), jnp.bfloat16),
        in_specs=[SMEM] + [VMEM] * 3 + [HBM],
        out_specs=VMEM,
        scratch_shapes=[pltpu.VMEM((1536, 1536), jnp.bfloat16), pltpu.SemaphoreType.DMA],
        compiler_params=pltpu.CompilerParams(vmem_limit_bytes=24 * 2**20),
        cost_estimate=pl.CostEstimate(
            flops=12 * 10**8, bytes_accessed=10 * 10**6, transcendentals=0
        ),
    )(core, heads, own, other, reorder_all())


def on_device(latents, norm_gain, w_qkv, w_out, head_temp, lengths):
    rows = w_qkv.reshape(3, 12, 2, 128).transpose(2, 1, 0, 3).reshape(2, 12, 384)
    columns = w_out.T.reshape(12, 2, 128).transpose(1, 0, 2)
    both = jnp.concatenate([rows, columns], axis=2).reshape(1, 2, 48, 128)
    both = jnp.broadcast_to(both, (12, 2, 48, 128)).reshape(24, 48, 128)
    both = lax.all_to_all(both, ("zh", "zl", "c"), 0, 0, tiled=True)
    both = both.reshape(2, 6, 2, 12, 512)
    rows = lax.dynamic_index_in_dim(both[..., :384], lax.axis_index("zl"), 1, keepdims=False)
    rows = rows.reshape(48, 384)

    frames = latents[0]
    values = frames.astype(jnp.float32)
    rms = jnp.sqrt(jnp.mean(values * values, axis=-1, keepdims=True) + 1e-06)
    normed = (values / rms * norm_gain).astype(jnp.bfloat16)
    whole = lax.all_gather(normed, "zl", axis=0, tiled=True)

    own_w = gather(rows, ("x", "y"), 32)
    other_w = other_core(own_w)
    columns = both[..., 384:].transpose(0, 2, 3, 1, 4).reshape(48, 768)
    out_own = gather_y(gather_x(columns))

    core = lax.axis_index("c").reshape(1).astype(jnp.int32)
    blocks = attend(core, lengths, head_temp, whole, own_w, other_w)
    own = lax.all_to_all(blocks, "zl", 0, 0, tiled=True)
    out_other = other_core(out_own)
    return project(core, own, out_own, out_other)[None]


def solution(mesh):
    split = Mesh(mesh.devices.reshape(SIZES), AXES)
    clip = ("x", "zh", "y", "c")
    in_specs = (
        P(clip, "zl", None),
        P(),
        P(None, clip, "zl"),
        P("zl", clip),
        P("zl"),
        P(clip),
    )
    out_specs = P(clip, "zl", None)
    return jax.shard_map(
        on_device, mesh=split, in_specs=in_specs, out_specs=out_specs, check_vma=False
    )
```

time: 178 us -> 185 us (1.039)
  starting transfers between devices: 91.3 us -> 75.4 us
  between operations: 1.13 us -> 14.5 us
  waiting for transfers between devices: 44.6 us -> 55.8 us
    ppermute x19 -> x12, starting transfers between devices: 54.7 us -> 44 us  [permute(): return lax.ppermute(value, AXES, pairs)]
    all_to_all x1, waiting for transfers between devices: 7.14 us -> 17 us  [on_device(): own = lax.all_to_all(blocks, 'zl', 0, 0, tiled=True)]
    unnamed x39 -> x5, local copies, waits for them, and re-layouts: 11.4 us -> 2.35 us
    dynamic_update_slice x0 -> x12, local copies, waits for them, and re-layouts: none -> 7.56 us  [put(): return lax.dynamic_update_slice_in_dim(whole, block[None], at, 0)]
    all_to_all x3 -> x2, starting transfers between devices: 30.5 us -> 25.9 us  [the longest x1 16.7 us: on_device(): both = lax.all_to_all(both, ('zh', 'zl', 'c'), 0, 0, tiled=True)]
    all_to_all x3 -> x2, waiting for transfers between devices: 11.2 us -> 12.7 us  [the longest x1 12.7 us: on_device(): both = lax.all_to_all(both, ('zh', 'zl', 'c'), 0, 0, tiled=True)]
    ppermute x19 -> x12, waiting for transfers between devices: 26.3 us -> 26.1 us  [permute(): return lax.ppermute(value, AXES, pairs)]
  transfers between devices with their start and end apart: 23 -> 16, of which waited for: 4 -> 5; matrix products, arithmetic and copies ran while one was open for 1% -> 7% of each run, Pallas kernels for 9% -> 8%
where the time goes in v5:
time: 185 us; the launch traced here: 184 us
  starting transfers between devices  75.4 us (41%)
  waiting for transfers between devices  55.8 us (30%)
  Pallas kernels  20.2 us (11%)
  local copies, waits for them, and re-layouts  14.7 us (8%)
  between operations  14.5 us (8%)
  other arithmetic  3.11 us (2%)
    ppermute x12, starting transfers between devices, permute(): return lax.ppermute(value, AXES, pairs)  44 us
    ppermute x12, waiting for transfers between devices, permute(): return lax.ppermute(value, AXES, pairs)  26.1 us
    all_to_all x1, waiting for transfers between devices, on_device(): own = lax.all_to_all(blocks, 'zl', 0, 0, tiled=True)  17 us
    all_to_all x1, starting transfers between devices, on_device(): both = lax.all_to_all(both, ('zh', 'zl', 'c'), 0, 0, tiled=True)  16.7 us
    pallas_call x1, Pallas kernels, attend(): pl.pallas_call(attend_kernel, out_shape=jax.ShapeDtypeStruct((6, rows //...  15 us
    all_to_all x1, waiting for transfers between devices, on_device(): both = lax.all_to_all(both, ('zh', 'zl', 'c'), 0, 0, tiled=True)  12.7 us
    all_to_all x1, starting transfers between devices, gather(): lax.all_to_all(copies, axes, 0, 0, tiled=True).reshape(-1, value.shape[1])  9.25 us
    dynamic_update_slice x12, local copies, waits for them, and re-layouts, put(): return lax.dynamic_update_slice_in_dim(whole, block[None], at, 0)  7.56 us
  transfers between devices with their start and end apart: 16, of which 5 were waited for; matrix products, arithmetic and copies ran while one was open for 7% of the time, Pallas kernels for 8%

profile of v5, /device:TPU:1, one launch (start us, length us, event | category | flops | bytes accessed | tf_op | source)
XLA Modules:
  0.0 183.7 jit_solution(6422230738437287203)
XLA Ops:
  8.9 16.7 %all-to-all-start = ((bf16[24,48,128]{2,1,0:T(8,128)(2,1)}), bf16[24,48,128]{2,1,0:T(8,128)(2,1)S(1)}, u32[]{:S(2)}, u32[]{:S(2)}) async-start(bf16[24,48,128]{2,1,0:T(8,128)(2,1)} %bitcast.6), calls=%async_computation | async-start | bytes 589824 | tf_op jit(solution)/shard_map/all_to_all | solution.py:214
  26.8 1.9 %fusion.2 = bf16[128,1536]{1,0:T(8,128)(2,1)} fusion(bf16[1,128,1536]{2,1,0:T(8,128)(2,1)} %param.8, f32[1536]{0:T(1024)} %param.9, f32[128]{0:T(128)S(1)} %add_sqrt_fusion), kind=kLoop, calls=%fused_computation.4 | loop fusion | flops 786432 | bytes 793088 | tf_op jit(solution)/shard_map/convert_element_type | solution.py:222
  28.8 12.7 %all-to-all-done = bf16[24,48,128]{2,1,0:T(8,128)(2,1)S(1)} async-done(((bf16[24,48,128]{2,1,0:T(8,128)(2,1)}), bf16[24,48,128]{2,1,0:T(8,128)(2,1)S(1)}, u32[]{:S(2)}, u32[]{:S(2)}) %all-to-all-start) | async-done | bytes 294944 | tf_op jit(solution)/shard_map/all_to_all | solution.py:214
  41.9 3.1 %collective-permute-start.1 = (bf16[48,768]{1,0:T(8,128)(2,1)S(1)}, bf16[48,768]{1,0:T(8,128)(2,1)S(1)}, u32[]{:S(2)}, u32[]{:S(2)}) collective-permute-start(bf16[48,768]{1,0:T(8,128)(2,1)S(1)} %bitcast.53), channel_id=1, source_target_pairs={{0,192},{1,193},{2,194},{3,195},{4,196},{5,197},{6,198},{7,199},{8... | collective-permute-start | bytes 221192 | tf_op jit(solution)/shard_map/ppermute | solution.py:24
  45.0 3.7 %collective-permute-start.2 = (bf16[48,768]{1,0:T(8,128)(2,1)S(1)}, bf16[48,768]{1,0:T(8,128)(2,1)S(1)}, u32[]{:S(2)}, u32[]{:S(2)}) collective-permute-start(bf16[48,768]{1,0:T(8,128)(2,1)S(1)} %bitcast.54), channel_id=1, source_target_pairs={{0,576},{1,577},{2,578},{3,579},{4,580},{5,581},{6,582},{7,583},{8... | collective-permute-start | bytes 221192 | tf_op jit(solution)/shard_map/ppermute | solution.py:24
  48.7 2.6 %collective-permute-start.3 = (bf16[48,768]{1,0:T(8,128)(2,1)S(1)}, bf16[48,768]{1,0:T(8,128)(2,1)S(1)}, u32[]{:S(2)}, u32[]{:S(2)}) collective-permute-start(bf16[48,768]{1,0:T(8,128)(2,1)S(1)} %bitcast.55), channel_id=1, source_target_pairs={{0,384},{1,385},{2,386},{3,387},{4,388},{5,389},{6,390},{7,391},{8... | collective-permute-start | bytes 221192 | tf_op jit(solution)/shard_map/ppermute | solution.py:24
  52.5 9.3 %all-to-all-start.1 = ((bf16[32,48,384]{2,1,0:T(8,128)(2,1)}), bf16[32,48,384]{2,1,0:T(8,128)(2,1)S(1)}, u32[]{:S(2)}, u32[]{:S(2)}) async-start(bf16[32,48,384]{2,1,0:T(8,128)(2,1)} %broadcast_in_dim.58), calls=%async_computation.1 | async-start | bytes 2359296 | tf_op jit(solution)/shard_map/all_to_all | solution.py:42
  65.0 3.1 %collective-permute-start.4 = (bf16[192,768]{1,0:T(8,128)(2,1)}, bf16[192,768]{1,0:T(8,128)(2,1)}, u32[]{:S(2)}, u32[]{:S(2)}) collective-permute-start(bf16[192,768]{1,0:T(8,128)(2,1)} %bitcast.13), channel_id=1, source_target_pairs={{0,12},{1,13},{2,14},{3,15},{4,16},{5,17},{6,18},{7,19},{8,20},{9,... | collective-permute-start | bytes 884744 | tf_op jit(solution)/shard_map/ppermute | solution.py:24
  68.2 3.4 %collective-permute-start.5 = (bf16[192,768]{1,0:T(8,128)(2,1)}, bf16[192,768]{1,0:T(8,128)(2,1)}, u32[]{:S(2)}, u32[]{:S(2)}) collective-permute-start(bf16[192,768]{1,0:T(8,128)(2,1)} %bitcast.13), channel_id=1, source_target_pairs={{0,84},{1,85},{2,86},{3,87},{4,88},{5,89},{6,90},{7,91},{8,92},{9,... | collective-permute-start | bytes 884744 | tf_op jit(solution)/shard_map/ppermute | solution.py:24
  72.8 22.7 %collective-permute-done.4 = bf16[192,768]{1,0:T(8,128)(2,1)} collective-permute-done((bf16[192,768]{1,0:T(8,128)(2,1)}, bf16[192,768]{1,0:T(8,128)(2,1)}, u32[]{:S(2)}, u32[]{:S(2)}) %collective-permute-start.4) | collective-permute-done | bytes 294944 | tf_op jit(solution)/shard_map/ppermute | solution.py:24
  95.5 1.9 %collective-permute-start.6 = (bf16[192,768]{1,0:T(8,128)(2,1)}, bf16[192,768]{1,0:T(8,128)(2,1)S(1)}, u32[]{:S(2)}, u32[]{:S(2)}) collective-permute-start(bf16[192,768]{1,0:T(8,128)(2,1)} %collective-permute-done.4), channel_id=1, source_target_pairs={{0,12},{1,13},{2,14},{3,15},{4,16},{5,17},{6,18},{7,19},{8,20},{9,... | collective-permute-start | bytes 884744 | tf_op jit(solution)/shard_map/ppermute | solution.py:24
  97.4 4.6 %collective-permute-start.7 = (bf16[192,768]{1,0:T(8,128)(2,1)}, bf16[192,768]{1,0:T(8,128)(2,1)S(1)}, u32[]{:S(2)}, u32[]{:S(2)}) collective-permute-start(bf16[192,768]{1,0:T(8,128)(2,1)} %collective-permute-done.5), channel_id=1, source_target_pairs={{0,84},{1,85},{2,86},{3,87},{4,88},{5,89},{6,90},{7,91},{8,92},{9,... | collective-permute-start | bytes 884744 | tf_op jit(solution)/shard_map/ppermute | solution.py:24
  104.0 1.2 collective-permute-done.6
  105.1 1.9 %collective-permute-start.8 = (bf16[192,768]{1,0:T(8,128)(2,1)S(1)}, bf16[192,768]{1,0:T(8,128)(2,1)}, u32[]{:S(2)}, u32[]{:S(2)}) collective-permute-start(bf16[192,768]{1,0:T(8,128)(2,1)S(1)} %collective-permute-done.6), channel_id=1, source_target_pairs={{0,12},{1,13},{2,14},{3,15},{4,16},{5,17},{6,18},{7,19},{8,20},{9,... | collective-permute-start | bytes 884744 | tf_op jit(solution)/shard_map/ppermute | solution.py:24
  107.1 4.6 %collective-permute-start.9 = (bf16[192,768]{1,0:T(8,128)(2,1)S(1)}, bf16[192,768]{1,0:T(8,128)(2,1)S(1)}, u32[]{:S(2)}, u32[]{:S(2)}) collective-permute-start(bf16[192,768]{1,0:T(8,128)(2,1)S(1)} %collective-permute-done.7), channel_id=1, source_target_pairs={{0,84},{1,85},{2,86},{3,87},{4,88},{5,89},{6,90},{7,91},{8,92},{9,... | collective-permute-start | bytes 884744 | tf_op jit(solution)/shard_map/ppermute | solution.py:24
  111.7 2.2 %collective-permute-done.8 = bf16[192,768]{1,0:T(8,128)(2,1)} collective-permute-done((bf16[192,768]{1,0:T(8,128)(2,1)S(1)}, bf16[192,768]{1,0:T(8,128)(2,1)}, u32[]{:S(2)}, u32[]{:S(2)}) %collective-permute-start.8) | collective-permute-done | bytes 294944 | tf_op jit(solution)/shard_map/ppermute | solution.py:24
  113.9 1.9 %collective-permute-start.10 = (bf16[192,768]{1,0:T(8,128)(2,1)}, bf16[192,768]{1,0:T(8,128)(2,1)}, u32[]{:S(2)}, u32[]{:S(2)}) collective-permute-start(bf16[192,768]{1,0:T(8,128)(2,1)} %collective-permute-done.8), channel_id=1, source_target_pairs={{0,12},{1,13},{2,14},{3,15},{4,16},{5,17},{6,18},{7,19},{8,20},{9,... | collective-permute-start | bytes 884744 | tf_op jit(solution)/shard_map/ppermute | solution.py:24
  116.9 6.1 %collective-permute-start = (bf16[1536,384]{1,0:T(8,128)(2,1)S(1)}, bf16[1536,384]{1,0:T(8,128)(2,1)}, u32[]{:S(2)}, u32[]{:S(2)}) collective-permute-start(bf16[1536,384]{1,0:T(8,128)(2,1)S(1)} %bitcast.49), channel_id=1, source_target_pairs={{0,6},{1,7},{2,8},{3,9},{4,10},{5,11},{6,0},{7,1},{8,2},{9,3},{10,... | collective-permute-start | bytes 3538952 | tf_op jit(solution)/shard_map/ppermute | solution.py:24
  124.0 7.1 %collective-permute-start.11 = (bf16[1536,768]{1,0:T(8,128)(2,1)S(1)}, bf16[1536,768]{1,0:T(8,128)(2,1)}, u32[]{:S(2)}, u32[]{:S(2)}) collective-permute-start(bf16[1536,768]{1,0:T(8,128)(2,1)S(1)} %bitcast.47), channel_id=1, source_target_pairs={{0,6},{1,7},{2,8},{3,9},{4,10},{5,11},{6,0},{7,1},{8,2},{9,3},{10,... | collective-permute-start | bytes 7077896 | tf_op jit(solution)/shard_map/ppermute | solution.py:24
  131.9 15.0 %shard_map.82 = bf16[6,128,256]{2,1,0:T(8,128)(2,1)} custom-call(s32[1]{0:T(128)} %bitcast.core_ref, s32[1]{0:T(128)S(6)} %copy.31.length_ref, f32[4]{0:T(128)} %temp_ref.1, bf16[768,1536]{1,0:T(8,128)(2,1)} %all-gather.2.cloned.1.call-done.frames, bf16[1536,384]{1,0:T(8,128)(2,1)} %bitcast.50, bf16[1536,384]{1,0:T(8,128)(2,1)} %collective-permute-done.other_w, ...), custom_call_target="tpu_custom_call" | custom-call | flops 3000000000 | bytes 5000000 | tf_op jit(solution)/shard_map/pallas_call | solution.py:159
  146.9 5.4 %all-to-all-start.2 = ((bf16[6,128,256]{2,1,0:T(8,128)(2,1)}), bf16[6,128,256]{2,1,0:T(8,128)(2,1)S(1)}, u32[]{:S(2)}, u32[]{:S(2)}) async-start(bf16[6,128,256]{2,1,0:T(8,128)(2,1)} %shard_map.82), calls=%async_computation.2 | async-start | bytes 786432 | tf_op jit(solution)/shard_map/all_to_all | solution.py:232
  152.3 17.0 %all-to-all-done.2.heads_ref = bf16[6,128,256]{2,1,0:T(8,128)(2,1)S(1)} async-done(((bf16[6,128,256]{2,1,0:T(8,128)(2,1)}), bf16[6,128,256]{2,1,0:T(8,128)(2,1)S(1)}, u32[]{:S(2)}, u32[]{:S(2)}) %all-to-all-start.2) | async-done | bytes 393248 | tf_op jit(solution)/shard_map/all_to_all | solution.py:232
  169.4 2.3 %copy-done = bf16[1536,1536]{1,0:T(8,128)(2,1)S(1)} copy-done((bf16[1536,1536]{1,0:T(8,128)(2,1)S(1)}, bf16[1536,1536]{1,0:T(8,128)(2,1)}, u32[]{:S(2)}) %copy-start) | copy-done | bytes 4718616
  171.7 5.2 %shard_map.83 = bf16[128,1536]{1,0:T(8,128)(2,1)} custom-call(s32[1]{0:T(128)} %bitcast.core_ref, bf16[6,128,256]{2,1,0:T(8,128)(2,1)S(1)} %all-to-all-done.2.heads_ref, bf16[1536,768]{1,0:T(8,128)(2,1)S(1)} %bitcast.48, bf16[1536,768]{1,0:T(8,128)(2,1)} %collective-permute-done.11.other_ref, bf16[1536,1536]{1,0:T(8,128)(2,1)S(1)} %copy-done), custom_call_target="tpu_custom_call" | custom-call | flops 1200000000 | bytes 10000000 | tf_op jit(solution)/shard_map/pallas_call | solution.py:196
  (49 shorter events, 13.6 us)
Async XLA Ops:
  8.9 32.6 %all-to-all-start = ((bf16[24,48,128]{2,1,0:T(8,128)(2,1)}), bf16[24,48,128]{2,1,0:T(8,128)(2,1)S(1)}, u32[]{:S(2)}, u32[]{:S(2)}) async-start(bf16[24,48,128]{2,1,0:T(8,128)(2,1)} %bitcast.6), calls=%async_computation | async-start | bytes 589824 | tf_op jit(solution)/shard_map/all_to_all | solution.py:214
  25.6 106.3 %all-gather.2.cloned.1.call-start = ((), (), s32[]{:S(2)}) async-start(), calls=%async_computation.3 | async-start | bytes 2752512 | tf_op jit(solution)/shard_map/all_gather | solution.py:223
  41.9 21.2 %collective-permute-start.1 = (bf16[48,768]{1,0:T(8,128)(2,1)S(1)}, bf16[48,768]{1,0:T(8,128)(2,1)S(1)}, u32[]{:S(2)}, u32[]{:S(2)}) collective-permute-start(bf16[48,768]{1,0:T(8,128)(2,1)S(1)} %bitcast.53), channel_id=1, source_target_pairs={{0,192},{1,193},{2,194},{3,195},{4,196},{5,197},{6,198},{7,199},{8... | collective-permute-start | bytes 221192 | tf_op jit(solution)/shard_map/ppermute | solution.py:24
  45.0 18.7 %collective-permute-start.2 = (bf16[48,768]{1,0:T(8,128)(2,1)S(1)}, bf16[48,768]{1,0:T(8,128)(2,1)S(1)}, u32[]{:S(2)}, u32[]{:S(2)}) collective-permute-start(bf16[48,768]{1,0:T(8,128)(2,1)S(1)} %bitcast.54), channel_id=1, source_target_pairs={{0,576},{1,577},{2,578},{3,579},{4,580},{5,581},{6,582},{7,583},{8... | collective-permute-start | bytes 221192 | tf_op jit(solution)/shard_map/ppermute | solution.py:24
  48.7 15.7 %collective-permute-start.3 = (bf16[48,768]{1,0:T(8,128)(2,1)S(1)}, bf16[48,768]{1,0:T(8,128)(2,1)S(1)}, u32[]{:S(2)}, u32[]{:S(2)}) collective-permute-start(bf16[48,768]{1,0:T(8,128)(2,1)S(1)} %bitcast.55), channel_id=1, source_target_pairs={{0,384},{1,385},{2,386},{3,387},{4,388},{5,389},{6,390},{7,391},{8... | collective-permute-start | bytes 221192 | tf_op jit(solution)/shard_map/ppermute | solution.py:24
  52.5 64.4 %all-to-all-start.1 = ((bf16[32,48,384]{2,1,0:T(8,128)(2,1)}), bf16[32,48,384]{2,1,0:T(8,128)(2,1)S(1)}, u32[]{:S(2)}, u32[]{:S(2)}) async-start(bf16[32,48,384]{2,1,0:T(8,128)(2,1)} %broadcast_in_dim.58), calls=%async_computation.1 | async-start | bytes 2359296 | tf_op jit(solution)/shard_map/all_to_all | solution.py:42
  65.0 30.5 %collective-permute-start.4 = (bf16[192,768]{1,0:T(8,128)(2,1)}, bf16[192,768]{1,0:T(8,128)(2,1)}, u32[]{:S(2)}, u32[]{:S(2)}) collective-permute-start(bf16[192,768]{1,0:T(8,128)(2,1)} %bitcast.13), channel_id=1, source_target_pairs={{0,12},{1,13},{2,14},{3,15},{4,16},{5,17},{6,18},{7,19},{8,20},{9,... | collective-permute-start | bytes 884744 | tf_op jit(solution)/shard_map/ppermute | solution.py:24
  68.2 29.2 %collective-permute-start.5 = (bf16[192,768]{1,0:T(8,128)(2,1)}, bf16[192,768]{1,0:T(8,128)(2,1)}, u32[]{:S(2)}, u32[]{:S(2)}) collective-permute-start(bf16[192,768]{1,0:T(8,128)(2,1)} %bitcast.13), channel_id=1, source_target_pairs={{0,84},{1,85},{2,86},{3,87},{4,88},{5,89},{6,90},{7,91},{8,92},{9,... | collective-permute-start | bytes 884744 | tf_op jit(solution)/shard_map/ppermute | solution.py:24
  95.5 9.7 %collective-permute-start.6 = (bf16[192,768]{1,0:T(8,128)(2,1)}, bf16[192,768]{1,0:T(8,128)(2,1)S(1)}, u32[]{:S(2)}, u32[]{:S(2)}) collective-permute-start(bf16[192,768]{1,0:T(8,128)(2,1)} %collective-permute-done.4), channel_id=1, source_target_pairs={{0,12},{1,13},{2,14},{3,15},{4,16},{5,17},{6,18},{7,19},{8,20},{9,... | collective-permute-start | bytes 884744 | tf_op jit(solution)/shard_map/ppermute | solution.py:24
  97.4 9.6 %collective-permute-start.7 = (bf16[192,768]{1,0:T(8,128)(2,1)}, bf16[192,768]{1,0:T(8,128)(2,1)S(1)}, u32[]{:S(2)}, u32[]{:S(2)}) collective-permute-start(bf16[192,768]{1,0:T(8,128)(2,1)} %collective-permute-done.5), channel_id=1, source_target_pairs={{0,84},{1,85},{2,86},{3,87},{4,88},{5,89},{6,90},{7,91},{8,92},{9,... | collective-permute-start | bytes 884744 | tf_op jit(solution)/shard_map/ppermute | solution.py:24
  105.1 8.8 %collective-permute-start.8 = (bf16[192,768]{1,0:T(8,128)(2,1)S(1)}, bf16[192,768]{1,0:T(8,128)(2,1)}, u32[]{:S(2)}, u32[]{:S(2)}) collective-permute-start(bf16[192,768]{1,0:T(8,128)(2,1)S(1)} %collective-permute-done.6), channel_id=1, source_target_pairs={{0,12},{1,13},{2,14},{3,15},{4,16},{5,17},{6,18},{7,19},{8,20},{9,... | collective-permute-start | bytes 884744 | tf_op jit(solution)/shard_map/ppermute | solution.py:24
  107.1 9.8 %collective-permute-start.9 = (bf16[192,768]{1,0:T(8,128)(2,1)S(1)}, bf16[192,768]{1,0:T(8,128)(2,1)S(1)}, u32[]{:S(2)}, u32[]{:S(2)}) collective-permute-start(bf16[192,768]{1,0:T(8,128)(2,1)S(1)} %collective-permute-done.7), channel_id=1, source_target_pairs={{0,84},{1,85},{2,86},{3,87},{4,88},{5,89},{6,90},{7,91},{8,92},{9,... | collective-permute-start | bytes 884744 | tf_op jit(solution)/shard_map/ppermute | solution.py:24
  113.9 9.1 %collective-permute-start.10 = (bf16[192,768]{1,0:T(8,128)(2,1)}, bf16[192,768]{1,0:T(8,128)(2,1)}, u32[]{:S(2)}, u32[]{:S(2)}) collective-permute-start(bf16[192,768]{1,0:T(8,128)(2,1)} %collective-permute-done.8), channel_id=1, source_target_pairs={{0,12},{1,13},{2,14},{3,15},{4,16},{5,17},{6,18},{7,19},{8,20},{9,... | collective-permute-start | bytes 884744 | tf_op jit(solution)/shard_map/ppermute | solution.py:24
  116.9 15.0 %copy-start.1 = (bf16[32,48,384]{2,1,0:T(8,128)(2,1)}, bf16[32,48,384]{2,1,0:T(8,128)(2,1)S(1)}, u32[]{:S(2)}) copy-start(bf16[32,48,384]{2,1,0:T(8,128)(2,1)S(1)} %all-to-all-done.1) | copy-start | bytes 3538948
  116.9 15.0 %collective-permute-start = (bf16[1536,384]{1,0:T(8,128)(2,1)S(1)}, bf16[1536,384]{1,0:T(8,128)(2,1)}, u32[]{:S(2)}, u32[]{:S(2)}) collective-permute-start(bf16[1536,384]{1,0:T(8,128)(2,1)S(1)} %bitcast.49), channel_id=1, source_target_pairs={{0,6},{1,7},{2,8},{3,9},{4,10},{5,11},{6,0},{7,1},{8,2},{9,3},{10,... | collective-permute-start | bytes 3538952 | tf_op jit(solution)/shard_map/ppermute | solution.py:24
  124.0 28.3 %collective-permute-start.11 = (bf16[1536,768]{1,0:T(8,128)(2,1)S(1)}, bf16[1536,768]{1,0:T(8,128)(2,1)}, u32[]{:S(2)}, u32[]{:S(2)}) collective-permute-start(bf16[1536,768]{1,0:T(8,128)(2,1)S(1)} %bitcast.47), channel_id=1, source_target_pairs={{0,6},{1,7},{2,8},{3,9},{4,10},{5,11},{6,0},{7,1},{8,2},{9,3},{10,... | collective-permute-start | bytes 7077896 | tf_op jit(solution)/shard_map/ppermute | solution.py:24
  146.9 22.5 %all-to-all-start.2 = ((bf16[6,128,256]{2,1,0:T(8,128)(2,1)}), bf16[6,128,256]{2,1,0:T(8,128)(2,1)S(1)}, u32[]{:S(2)}, u32[]{:S(2)}) async-start(bf16[6,128,256]{2,1,0:T(8,128)(2,1)} %shard_map.82), calls=%async_computation.2 | async-start | bytes 786432 | tf_op jit(solution)/shard_map/all_to_all | solution.py:232
  169.4 2.3 %copy-start = (bf16[1536,1536]{1,0:T(8,128)(2,1)S(1)}, bf16[1536,1536]{1,0:T(8,128)(2,1)}, u32[]{:S(2)}) copy-start(bf16[1536,1536]{1,0:T(8,128)(2,1)} %constant.99.clone.move_hbm) | copy-start | bytes 14155780
Sparse Core Ops, SparseCore 0:
  28.9 68.1 all-gather.1

commit v6 on v4

--- a/solution.py
+++ b/solution.py
@@ -38,26 +38,44 @@
     )
 
 
+def y_shift(value, step):
+    return permute(value, lambda x, zh, y, c, zl: (x, zh, (y + step) % 8, c, zl))
+
+
 def x_swap(value, which):
     goal = {"even": (1, 0, 3, 2), "odd": (3, 2, 1, 0), "across": (2, 3, 0, 1)}[which]
     return permute(value, lambda x, zh, y, c, zl: (goal[x], zh, y, c, zl))
 
 
-def gather_y(value):
-    copies = jnp.broadcast_to(value[None], (8,) + value.shape)
-    return lax.all_to_all(copies, "y", 0, 0, tiled=True).reshape(-1, value.shape[1])
+def gather(value, axes, count):
+    copies = jnp.broadcast_to(value[None], (count,) + value.shape)
+    return lax.all_to_all(copies, axes, 0, 0, tiled=True).reshape(-1, value.shape[1])
 
 
 def after(value, *others):
     return lax.optimization_barrier((value,) + others)[0]
 
 
-def gather_x(block):
-    return [block] + [x_swap(block, which) for which in ("even", "odd", "across")]
-
-
-def x_places(x):
-    return x, x + 1 - 2 * lax.rem(x, 2), 3 - x, lax.rem(x + 2, 4)
+def put(whole, block, at):
+    return lax.dynamic_update_slice_in_dim(whole, block[None], at, 0)
+
+
+def gather_x(block, tie):
+    x = lax.axis_index("x")
+    whole = put(jnp.zeros((4,) + block.shape, block.dtype), block, x)
+    whole = put(whole, x_swap(block, "even"), x ^ 1)
+    whole = put(whole, x_swap(block, "odd"), 3 - x)
+    whole = put(whole, x_swap(after(block, *tie), "across"), (x + 2) % 4)
+    return whole.reshape(-1, block.shape[1])
+
+
+def ring_y(block):
+    ups, downs = [block], [block]
+    for step in range(1, 5):
+        ups.append(y_shift(ups[-1], 1))
+        if step < 4:
+            downs.append(y_shift(downs[-1], -1))
+    return ups, downs
 
 
 def reorder():
@@ -67,10 +85,19 @@
     return jnp.asarray(matrix, jnp.bfloat16)
 
 
+def reorder_all():
+    y, x, zh, r = np.meshgrid(
+        np.arange(8), np.arange(4), np.arange(2), np.arange(24), indexing="ij"
+    )
+    matrix = np.zeros((1536, 1536), np.float32)
+    matrix[np.arange(1536), (((x * 2 + zh) * 8 + y) * 24 + r).reshape(-1)] = 1
+    return jnp.asarray(matrix, jnp.bfloat16)
+
+
 def attend_kernel(place_ref, length_ref, temp_ref, *refs):
-    frames, weights, move_ref, out_ref = refs[:6], refs[6:14], refs[14], refs[15]
-    x_buf, w_in, w_buf, qkv, sems = refs[16:]
-    place, x, core = place_ref[0], place_ref[1], place_ref[2]
+    frames, weights, move_ref, out_ref = refs[:6], refs[6:8], refs[8], refs[9]
+    x_buf, w_in, w_buf, qkv, sems = refs[10:]
+    place, core = place_ref[0], place_ref[1]
     base, within = place // 3 * 3, lax.rem(place, 3)
     below, above = lax.rem(within + 2, 3), lax.rem(within + 1, 3)
     slots = (
@@ -92,12 +119,12 @@
     for copy in w_copies + copies:
         copy.start()
     for which, half in ((0, core), (1, 1 - core)):
-        for number, at in enumerate(x_places(x)):
-            w_copies[4 * which + number].wait()
-            rows = pl.ds(pl.multiple_of(at * 384, 384), 384)
+        w_copies[which].wait()
+        for at in range(4):
+            rows = slice(at * 384, at * 384 + 384)
             w_buf[half, rows, :] = lax.dot_general(
                 move_ref[...],
-                w_in[4 * which + number],
+                w_in[which, rows, :],
                 (((0,), (0,)), ((), ())),
                 preferred_element_type=jnp.float32,
             ).astype(jnp.bfloat16)
@@ -146,7 +173,7 @@
 
 SMEM = pl.BlockSpec(memory_space=pltpu.SMEM)
 VMEM = pl.BlockSpec(memory_space=pltpu.VMEM)
-ANYWHERE = pl.BlockSpec(memory_space=pl.ANY)
+HBM = pl.BlockSpec(memory_space=pltpu.HBM)
 
 
 def attend(place, length, temp, frames, weights):
@@ -154,16 +181,16 @@
     return pl.pallas_call(
         attend_kernel,
         out_shape=jax.ShapeDtypeStruct((6, shard[0], 256), jnp.bfloat16),
-        in_specs=[SMEM] * 3 + [ANYWHERE] * 14 + [VMEM],
+        in_specs=[SMEM] * 3 + [HBM] * 8 + [VMEM],
         out_specs=VMEM,
         scratch_shapes=[
             pltpu.VMEM((6,) + shard, jnp.bfloat16),
-            pltpu.VMEM((8, 384, 384), jnp.bfloat16),
+            pltpu.VMEM((2, 1536, 384), jnp.bfloat16),
             pltpu.VMEM((2, 1536, 384), jnp.bfloat16),
             pltpu.VMEM((2, 6 * shard[0], 384), jnp.bfloat16),
-            pltpu.SemaphoreType.DMA((14,)),
+            pltpu.SemaphoreType.DMA((8,)),
         ],
-        compiler_params=pltpu.CompilerParams(vmem_limit_bytes=28 * 2**20),
+        compiler_params=pltpu.CompilerParams(vmem_limit_bytes=58 * 2**20),
         cost_estimate=pl.CostEstimate(
             flops=3 * 10**9, bytes_accessed=5 * 10**6, transcendentals=2 * 10**6
         ),
@@ -171,71 +198,86 @@
 
 
 def project_kernel(place_ref, heads_ref, *refs):
-    own, other, move_ref, out_ref = refs[:4], refs[4:8], refs[8], refs[9]
-    x, core = place_ref[1], place_ref[2]
+    own, other = refs[:8], (refs[8], refs[9])
+    move_hbm, out_ref, parts, move_ref, sem = refs[10:]
+    core, y = place_ref[1], place_ref[2]
+    move_copy = pltpu.make_async_copy(move_hbm, move_ref, sem)
+    move_copy.start()
     first = jnp.concatenate([heads_ref[at, :, :128] for at in range(6)], axis=1)
     second = jnp.concatenate([heads_ref[at, :, 128:] for at in range(6)], axis=1)
     mine = jnp.where(core == 0, first, second)
     given = jnp.where(core == 0, second, first)
     sides = (((1,), (1,)), ((), ()))
-    for number, at in enumerate(x_places(x)):
-        columns = pl.ds(pl.multiple_of(at * 384, 384), 384)
-        total = lax.dot_general(
-            mine, own[number][...], sides, preferred_element_type=jnp.float32
-        ) + lax.dot_general(given, other[number][...], sides, preferred_element_type=jnp.float32)
-        out_ref[:, columns] = jnp.dot(
-            total.astype(jnp.bfloat16), move_ref[...], preferred_element_type=jnp.float32
-        ).astype(jnp.bfloat16)
+    for number, distance in enumerate((0, 7, 1, 6, 2, 5, 3, 4)):
+        part = lax.dot_general(mine, own[number][...], sides, preferred_element_type=jnp.float32)
+        rows = other[0][number] if number < 5 else other[1][number - 5]
+        part += lax.dot_general(given, rows, sides, preferred_element_type=jnp.float32)
+        parts[lax.rem(y + distance, 8)] = part.astype(jnp.bfloat16)
+    move_copy.wait()
+    total = jnp.zeros(out_ref.shape, jnp.float32)
+    for at in range(8):
+        total += jnp.dot(
+            parts[at], move_ref[at * 192 : at * 192 + 192], preferred_element_type=jnp.float32
+        )
+    out_ref[...] = total.astype(jnp.bfloat16)
 
 
 def project(place, heads, own, other):
+    rows = heads.shape[1]
     return pl.pallas_call(
         project_kernel,
-        out_shape=jax.ShapeDtypeStruct((heads.shape[1], 1536), jnp.bfloat16),
-        in_specs=[SMEM] + [VMEM] * 10,
+        out_shape=jax.ShapeDtypeStruct((rows, 1536), jnp.bfloat16),
+        in_specs=[SMEM] + [VMEM] * 11 + [HBM],
         out_specs=VMEM,
-        compiler_params=pltpu.CompilerParams(vmem_limit_bytes=20 * 2**20),
+        scratch_shapes=[
+            pltpu.VMEM((8, rows, 192), jnp.bfloat16),
+            pltpu.VMEM((1536, 1536), jnp.bfloat16),
+            pltpu.SemaphoreType.DMA,
+        ],
+        compiler_params=pltpu.CompilerParams(vmem_limit_bytes=24 * 2**20),
         cost_estimate=pl.CostEstimate(
-            flops=8 * 10**8, bytes_accessed=6 * 10**6, transcendentals=0
+            flops=12 * 10**8, bytes_accessed=10 * 10**6, transcendentals=0
         ),
-    )(place, heads, *own, *other, reorder())
+    )(place, heads, *own, *other, reorder_all())
 
 
 def on_device(latents, norm_gain, w_qkv, w_out, head_temp, lengths):
+    rows = w_qkv.reshape(3, 12, 2, 128).transpose(2, 1, 0, 3).reshape(2, 12, 384)
+    columns = w_out.T.reshape(12, 2, 128).transpose(1, 0, 2)
+    both = jnp.concatenate([rows, columns], axis=2).reshape(1, 2, 48, 128)
+    both = jnp.broadcast_to(both, (12, 2, 48, 128)).reshape(24, 48, 128)
+    both = lax.all_to_all(both, ("zh", "zl", "c"), 0, 0, tiled=True)
+    both = both.reshape(2, 6, 2, 12, 512)
+    rows = lax.dynamic_index_in_dim(both[..., :384], lax.axis_index("zl"), 1, keepdims=False)
+    rows = rows.reshape(48, 384)
+
     frames = latents[0]
     values = frames.astype(jnp.float32)
     rms = jnp.sqrt(jnp.mean(values * values, axis=-1, keepdims=True) + 1e-06)
     normed = (values / rms * norm_gain).astype(jnp.bfloat16)
     across = other_triple(normed)
-
-    rows = w_qkv.reshape(3, 12, 2, 128).transpose(2, 1, 0, 3).reshape(2, 12, 384)
-    columns = w_out.T.reshape(12, 2, 128).transpose(1, 0, 2)
-    both = jnp.concatenate([rows, columns], axis=2).reshape(1, 2, 48, 128)
-    both = jnp.broadcast_to(both, (12, 2, 48, 128)).reshape(24, 48, 128)
-    both = lax.all_to_all(after(both, normed), ("zh", "zl", "c"), 0, 0, tiled=True)
-    both = both.reshape(2, 6, 2, 12, 512)
-    rows = lax.dynamic_index_in_dim(both[..., :384], lax.axis_index("zl"), 1, keepdims=False)
-    rows = rows.reshape(48, 384)
-    columns = after(both, across)[..., 384:].transpose(0, 2, 3, 1, 4).reshape(48, 768)
-
     own_triple = [triple_shift(normed, 1), triple_shift(normed, 2)]
-    by_y = gather_y(rows)
-    out_by_y = gather_y(after(columns, by_y, *own_triple))
-    by_x = gather_x(by_y)
     far_triple = [triple_shift(across, 1), triple_shift(across, 2)]
-    other_by_x = [other_core(block) for block in by_x]
-    out_own = gather_x(out_by_y)
-
-    place = jnp.stack([lax.axis_index(axis) for axis in ("zl", "x", "c")]).astype(jnp.int32)
+
+    columns = both[..., 384:].transpose(0, 2, 3, 1, 4).reshape(48, 768)
+
+    by_y = gather(after(rows, normed), "y", 8)
+    out_by_x = gather_x(columns, [across])
+    own_w = gather(by_y, "x", 4)
+    other_w = other_core(own_w)
+    ups, downs = ring_y(after(out_by_x, *own_triple))
+    out_own = [ups[0], ups[1], downs[1], ups[2], downs[2], ups[3], downs[3], ups[4]]
+    out_other = [other_core(jnp.stack(out_own[:5])), other_core(jnp.stack(out_own[5:]))]
+
+    place = jnp.stack([lax.axis_index(axis) for axis in ("zl", "c", "y")]).astype(jnp.int32)
     blocks = attend(
         place,
         lengths,
         head_temp,
         [normed] + own_triple + [across] + far_triple,
-        by_x + other_by_x,
+        [own_w, other_w],
     )
     own = lax.all_to_all(blocks, "zl", 0, 0, tiled=True)
-    out_other = [other_core(block) for block in out_own]
     return project(place, own, out_own, out_other)[None]
 
 

time: 178 us -> 178 us (level)
  the two profiles are of different devices: /device:TPU:1 before, /device:TPU:30 now
where the time goes in v6:
time: 178 us; the launch traced here: 177 us
  starting transfers between devices  96.7 us (54%)
  waiting for transfers between devices  42.8 us (24%)
  Pallas kernels  19.7 us (11%)
  local copies, waits for them, and re-layouts  15.7 us (9%)
    ppermute x18, starting transfers between devices, permute(): return lax.ppermute(value, AXES, pairs)  62.3 us
    all_to_all x1, waiting for transfers between devices, on_device(): both = lax.all_to_all(both, ('zh', 'zl', 'c'), 0, 0, tiled=True)  17.4 us
    all_to_all x1, starting transfers between devices, on_device(): both = lax.all_to_all(both, ('zh', 'zl', 'c'), 0, 0, tiled=True)  15.4 us
    pallas_call x1, Pallas kernels, attend(): pl.pallas_call(attend_kernel, out_shape=jax.ShapeDtypeStruct((6, shard[0]...  15.1 us
    ppermute x18, waiting for transfers between devices, permute(): return lax.ppermute(value, AXES, pairs)  13.4 us
    all_to_all x2, starting transfers between devices, gather(): lax.all_to_all(copies, axes, 0, 0, tiled=True).reshape(-1, value.shape[1])  12.1 us
    all_to_all x1, waiting for transfers between devices, on_device(): own = lax.all_to_all(blocks, 'zl', 0, 0, tiled=True)  12 us
    unnamed x33, local copies, waits for them, and re-layouts  9.34 us
  transfers between devices with their start and end apart: 22, of which 7 were waited for; matrix products, arithmetic and copies ran while one was open for 4% of the time, Pallas kernels for 9%

profile of v6, /device:TPU:30, one launch (start us, length us, event | category | flops | bytes accessed | tf_op | source)
XLA Modules:
  0.0 177.2 jit_solution(15874521269650201447)
XLA Ops:
  2.4 15.4 %all-to-all-start = ((bf16[24,48,128]{2,1,0:T(8,128)(2,1)}), bf16[24,48,128]{2,1,0:T(8,128)(2,1)S(1)}, u32[]{:S(2)}, u32[]{:S(2)}) async-start(bf16[24,48,128]{2,1,0:T(8,128)(2,1)} %bitcast.8), calls=%async_computation | async-start | bytes 589824 | tf_op jit(solution)/shard_map/all_to_all | solution.py:249
  18.2 17.4 %all-to-all-done = bf16[24,48,128]{2,1,0:T(8,128)(2,1)S(1)} async-done(((bf16[24,48,128]{2,1,0:T(8,128)(2,1)}), bf16[24,48,128]{2,1,0:T(8,128)(2,1)S(1)}, u32[]{:S(2)}, u32[]{:S(2)}) %all-to-all-start) | async-done | bytes 294944 | tf_op jit(solution)/shard_map/all_to_all | solution.py:249
  36.5 7.3 %all-to-all-start.1 = ((bf16[8,48,384]{2,1,0:T(8,128)(2,1)}), bf16[8,48,384]{2,1,0:T(8,128)(2,1)S(1)}, u32[]{:S(2)}, u32[]{:S(2)}) async-start(bf16[8,48,384]{2,1,0:T(8,128)(2,1)} %broadcast_in_dim.39), calls=%async_computation.1 | async-start | bytes 589824 | tf_op jit(solution)/shard_map/all_to_all | solution.py:52
  43.9 3.0 %collective-permute-start.2 = (bf16[128,1536]{1,0:T(8,128)(2,1)S(1)}, bf16[128,1536]{1,0:T(8,128)(2,1)}, u32[]{:S(2)}, u32[]{:S(2)}) collective-permute-start(bf16[128,1536]{1,0:T(8,128)(2,1)S(1)} %fusion.2.refs_0_), channel_id=1, source_target_pairs={{0,3},{1,4},{2,5},{3,0},{4,1},{5,2},{6,9},{7,10},{8,11},{9,6},{10,... | collective-permute-start | bytes 1179656 | tf_op jit(solution)/shard_map/ppermute | solution.py:24
  46.8 2.4 %collective-permute-start = (bf16[128,1536]{1,0:T(8,128)(2,1)S(1)}, bf16[128,1536]{1,0:T(8,128)(2,1)S(1)}, u32[]{:S(2)}, u32[]{:S(2)}) collective-permute-start(bf16[128,1536]{1,0:T(8,128)(2,1)S(1)} %fusion.2.refs_0_), channel_id=1, source_target_pairs={{0,1},{1,2},{2,0},{3,4},{4,5},{5,3},{6,7},{7,8},{8,6},{9,10},{10,1... | collective-permute-start | bytes 1179656 | tf_op jit(solution)/shard_map/ppermute | solution.py:24
  49.2 4.4 %collective-permute-start.1 = (bf16[128,1536]{1,0:T(8,128)(2,1)S(1)}, bf16[128,1536]{1,0:T(8,128)(2,1)S(1)}, u32[]{:S(2)}, u32[]{:S(2)}) collective-permute-start(bf16[128,1536]{1,0:T(8,128)(2,1)S(1)} %fusion.2.refs_0_), channel_id=1, source_target_pairs={{0,2},{1,0},{2,1},{3,5},{4,3},{5,4},{6,8},{7,6},{8,7},{9,11},{10,9... | collective-permute-start | bytes 1179656 | tf_op jit(solution)/shard_map/ppermute | solution.py:24
  54.8 4.8 %all-to-all-start.2 = ((bf16[4,384,384]{2,1,0:T(8,128)(2,1)}), bf16[4,384,384]{2,1,0:T(8,128)(2,1)}, u32[]{:S(2)}, u32[]{:S(2)}) async-start(bf16[4,384,384]{2,1,0:T(8,128)(2,1)} %broadcast_in_dim.41), calls=%async_computation.2 | async-start | bytes 2359296 | tf_op jit(solution)/shard_map/all_to_all | solution.py:52
  59.7 2.8 %collective-permute-start.6 = (bf16[48,768]{1,0:T(8,128)(2,1)S(1)}, bf16[48,768]{1,0:T(8,128)(2,1)S(1)}, u32[]{:S(2)}, u32[]{:S(2)}) collective-permute-start(bf16[48,768]{1,0:T(8,128)(2,1)S(1)} %bitcast.55), channel_id=1, source_target_pairs={{0,192},{1,193},{2,194},{3,195},{4,196},{5,197},{6,198},{7,199},{8... | collective-permute-start | bytes 221192 | tf_op jit(solution)/shard_map/ppermute | solution.py:24
  62.5 3.1 %collective-permute-start.7 = (bf16[48,768]{1,0:T(8,128)(2,1)S(1)}, bf16[48,768]{1,0:T(8,128)(2,1)S(1)}, u32[]{:S(2)}, u32[]{:S(2)}) collective-permute-start(bf16[48,768]{1,0:T(8,128)(2,1)S(1)} %bitcast.56), channel_id=1, source_target_pairs={{0,576},{1,577},{2,578},{3,579},{4,580},{5,581},{6,582},{7,583},{8... | collective-permute-start | bytes 221192 | tf_op jit(solution)/shard_map/ppermute | solution.py:24
  66.8 3.3 %collective-permute-start.8 = (bf16[48,768]{1,0:T(8,128)(2,1)S(1)}, bf16[48,768]{1,0:T(8,128)(2,1)S(1)}, u32[]{:S(2)}, u32[]{:S(2)}) collective-permute-start(bf16[48,768]{1,0:T(8,128)(2,1)S(1)} %bitcast.57), channel_id=1, source_target_pairs={{0,384},{1,385},{2,386},{3,387},{4,388},{5,389},{6,390},{7,391},{8... | collective-permute-start | bytes 221192 | tf_op jit(solution)/shard_map/ppermute | solution.py:24
  70.2 5.0 %collective-permute-done.6 = bf16[48,768]{1,0:T(8,128)(2,1)S(1)} collective-permute-done((bf16[48,768]{1,0:T(8,128)(2,1)S(1)}, bf16[48,768]{1,0:T(8,128)(2,1)S(1)}, u32[]{:S(2)}, u32[]{:S(2)}) %collective-permute-start.6) | collective-permute-done | bytes 73760 | tf_op jit(solution)/shard_map/ppermute | solution.py:24
  76.6 4.6 %collective-permute-start.9 = (bf16[192,768]{1,0:T(8,128)(2,1)S(1)}, bf16[192,768]{1,0:T(8,128)(2,1)S(1)}, u32[]{:S(2)}, u32[]{:S(2)}) collective-permute-start(bf16[192,768]{1,0:T(8,128)(2,1)S(1)} %bitcast.45), channel_id=1, source_target_pairs={{0,12},{1,13},{2,14},{3,15},{4,16},{5,17},{6,18},{7,19},{8,20},{9,... | collective-permute-start | bytes 884744 | tf_op jit(solution)/shard_map/ppermute | solution.py:24
  83.1 9.3 %collective-permute-start.3 = (bf16[128,1536]{1,0:T(8,128)(2,1)}, bf16[128,1536]{1,0:T(8,128)(2,1)S(1)}, u32[]{:S(2)}, u32[]{:S(2)}) collective-permute-start(bf16[128,1536]{1,0:T(8,128)(2,1)} %collective-permute-done.2.refs_3_), channel_id=1, source_target_pairs={{0,1},{1,2},{2,0},{3,4},{4,5},{5,3},{6,7},{7,8},{8,6},{9,10},{10,1... | collective-permute-start | bytes 1179656 | tf_op jit(solution)/shard_map/ppermute | solution.py:24
  92.4 1.9 %collective-permute-start.4 = (bf16[128,1536]{1,0:T(8,128)(2,1)}, bf16[128,1536]{1,0:T(8,128)(2,1)}, u32[]{:S(2)}, u32[]{:S(2)}) collective-permute-start(bf16[128,1536]{1,0:T(8,128)(2,1)} %collective-permute-done.2.refs_3_), channel_id=1, source_target_pairs={{0,2},{1,0},{2,1},{3,5},{4,3},{5,4},{6,8},{7,6},{8,7},{9,11},{10,9... | collective-permute-start | bytes 1179656 | tf_op jit(solution)/shard_map/ppermute | solution.py:24
  97.0 5.1 %collective-permute-start.11 = (bf16[192,768]{1,0:T(8,128)(2,1)S(1)}, bf16[192,768]{1,0:T(8,128)(2,1)S(1)}, u32[]{:S(2)}, u32[]{:S(2)}) collective-permute-start(bf16[192,768]{1,0:T(8,128)(2,1)S(1)} %collective-permute-done.9.refs_1_), channel_id=1, source_target_pairs={{0,12},{1,13},{2,14},{3,15},{4,16},{5,17},{6,18},{7,19},{8,20},{9,... | collective-permute-start | bytes 884744 | tf_op jit(solution)/shard_map/ppermute | solution.py:24
  105.6 3.5 %collective-permute-done.11.refs_3_ = bf16[192,768]{1,0:T(8,128)(2,1)S(1)} collective-permute-done((bf16[192,768]{1,0:T(8,128)(2,1)S(1)}, bf16[192,768]{1,0:T(8,128)(2,1)S(1)}, u32[]{:S(2)}, u32[]{:S(2)}) %collective-permute-start.11) | collective-permute-done | bytes 294944 | tf_op jit(solution)/shard_map/ppermute | solution.py:24
  109.1 5.6 %collective-permute-start.13 = (bf16[192,768]{1,0:T(8,128)(2,1)S(1)}, bf16[192,768]{1,0:T(8,128)(2,1)S(1)}, u32[]{:S(2)}, u32[]{:S(2)}) collective-permute-start(bf16[192,768]{1,0:T(8,128)(2,1)S(1)} %collective-permute-done.11.refs_3_), channel_id=1, source_target_pairs={{0,12},{1,13},{2,14},{3,15},{4,16},{5,17},{6,18},{7,19},{8,20},{9,... | collective-permute-start | bytes 884744 | tf_op jit(solution)/shard_map/ppermute | solution.py:24
  121.0 5.4 %collective-permute-start.15 = (bf16[192,768]{1,0:T(8,128)(2,1)S(1)}, bf16[192,768]{1,0:T(8,128)(2,1)S(1)}, u32[]{:S(2)}, u32[]{:S(2)}) collective-permute-start(bf16[192,768]{1,0:T(8,128)(2,1)S(1)} %collective-permute-done.13.refs_5_), channel_id=1, source_target_pairs={{0,12},{1,13},{2,14},{3,15},{4,16},{5,17},{6,18},{7,19},{8,20},{9,... | collective-permute-start | bytes 884744 | tf_op jit(solution)/shard_map/ppermute | solution.py:24
  127.7 15.1 %shard_map.82 = bf16[6,128,256]{2,1,0:T(8,128)(2,1)} custom-call(s32[3]{0:T(128)} %pad_add_fusion.place_ref, s32[1]{0:T(128)S(6)} %copy.27.length_ref, f32[4]{0:T(128)} %temp_ref.1, bf16[128,1536]{1,0:T(8,128)(2,1)} %copy-done.9, bf16[128,1536]{1,0:T(8,128)(2,1)} %copy-done.11, bf16[128,1536]{1,0:T(8,128)(2,1)} %copy-done.12, ...), custom_call_target="tpu_custom_call" | custom-call | flops 3000000000 | bytes 5000000 | tf_op jit(solution)/shard_map/pallas_call | solution.py:181
  142.8 7.0 %all-to-all-start.3 = ((bf16[6,128,256]{2,1,0:T(8,128)(2,1)}), bf16[6,128,256]{2,1,0:T(8,128)(2,1)S(1)}, u32[]{:S(2)}, u32[]{:S(2)}) async-start(bf16[6,128,256]{2,1,0:T(8,128)(2,1)} %shard_map.82), calls=%async_computation.3 | async-start | bytes 786432 | tf_op jit(solution)/shard_map/all_to_all | solution.py:280
  151.8 2.4 %collective-permute-done.17.refs_9_ = bf16[3,192,768]{2,1,0:T(8,128)(2,1)S(1)} collective-permute-done((bf16[3,192,768]{2,1,0:T(8,128)(2,1)S(1)}, bf16[3,192,768]{2,1,0:T(8,128)(2,1)S(1)}, u32[]{:S(2)}, u32[]{:S(2)}) %collective-permute-start.17) | collective-permute-done | bytes 884768 | tf_op jit(solution)/shard_map/ppermute | solution.py:24
  155.1 12.0 %all-to-all-done.3.heads_ref = bf16[6,128,256]{2,1,0:T(8,128)(2,1)S(1)} async-done(((bf16[6,128,256]{2,1,0:T(8,128)(2,1)}), bf16[6,128,256]{2,1,0:T(8,128)(2,1)S(1)}, u32[]{:S(2)}, u32[]{:S(2)}) %all-to-all-start.3) | async-done | bytes 393248 | tf_op jit(solution)/shard_map/all_to_all | solution.py:280
  167.1 2.3 %copy-done = bf16[1536,1536]{1,0:T(8,128)(2,1)S(1)} copy-done((bf16[1536,1536]{1,0:T(8,128)(2,1)S(1)}, bf16[1536,1536]{1,0:T(8,128)(2,1)}, u32[]{:S(2)}) %copy-start) | copy-done | bytes 4718616
  172.5 4.6 %shard_map.83 = bf16[128,1536]{1,0:T(8,128)(2,1)} custom-call(s32[3]{0:T(128)S(1)} %copy-done.7, bf16[6,128,256]{2,1,0:T(8,128)(2,1)S(1)} %all-to-all-done.3.heads_ref, bf16[192,768]{1,0:T(8,128)(2,1)S(1)} %bitcast.48, bf16[192,768]{1,0:T(8,128)(2,1)S(1)} %collective-permute-done.9.refs_1_, bf16[192,768]{1,0:T(8,128)(2,1)S(1)} %copy-done.2, ...), custom_call_target="tpu_custom_call" | custom-call | flops 1200000000 | bytes 10000000 | tf_op jit(solution)/shard_map/pallas_call | solution.py:227
  (83 shorter events, 28.6 us)
Async XLA Ops:
  2.4 33.1 %all-to-all-start = ((bf16[24,48,128]{2,1,0:T(8,128)(2,1)}), bf16[24,48,128]{2,1,0:T(8,128)(2,1)S(1)}, u32[]{:S(2)}, u32[]{:S(2)}) async-start(bf16[24,48,128]{2,1,0:T(8,128)(2,1)} %bitcast.8), calls=%async_computation | async-start | bytes 589824 | tf_op jit(solution)/shard_map/all_to_all | solution.py:249
  18.2 36.6 %copy-start.9 = (bf16[128,1536]{1,0:T(8,128)(2,1)}, bf16[128,1536]{1,0:T(8,128)(2,1)S(1)}, u32[]{:S(2)}) copy-start(bf16[128,1536]{1,0:T(8,128)(2,1)S(1)} %fusion.2.refs_0_) | copy-start | bytes 1179652
  36.5 17.1 %all-to-all-start.1 = ((bf16[8,48,384]{2,1,0:T(8,128)(2,1)}), bf16[8,48,384]{2,1,0:T(8,128)(2,1)S(1)}, u32[]{:S(2)}, u32[]{:S(2)}) async-start(bf16[8,48,384]{2,1,0:T(8,128)(2,1)} %broadcast_in_dim.39), calls=%async_computation.1 | async-start | bytes 589824 | tf_op jit(solution)/shard_map/all_to_all | solution.py:52
  43.9 23.0 %collective-permute-start.2 = (bf16[128,1536]{1,0:T(8,128)(2,1)S(1)}, bf16[128,1536]{1,0:T(8,128)(2,1)}, u32[]{:S(2)}, u32[]{:S(2)}) collective-permute-start(bf16[128,1536]{1,0:T(8,128)(2,1)S(1)} %fusion.2.refs_0_), channel_id=1, source_target_pairs={{0,3},{1,4},{2,5},{3,0},{4,1},{5,2},{6,9},{7,10},{8,11},{9,6},{10,... | collective-permute-start | bytes 1179656 | tf_op jit(solution)/shard_map/ppermute | solution.py:24
  46.8 29.7 %collective-permute-start = (bf16[128,1536]{1,0:T(8,128)(2,1)S(1)}, bf16[128,1536]{1,0:T(8,128)(2,1)S(1)}, u32[]{:S(2)}, u32[]{:S(2)}) collective-permute-start(bf16[128,1536]{1,0:T(8,128)(2,1)S(1)} %fusion.2.refs_0_), channel_id=1, source_target_pairs={{0,1},{1,2},{2,0},{3,4},{4,5},{5,3},{6,7},{7,8},{8,6},{9,10},{10,1... | collective-permute-start | bytes 1179656 | tf_op jit(solution)/shard_map/ppermute | solution.py:24
  49.2 27.4 %collective-permute-start.1 = (bf16[128,1536]{1,0:T(8,128)(2,1)S(1)}, bf16[128,1536]{1,0:T(8,128)(2,1)S(1)}, u32[]{:S(2)}, u32[]{:S(2)}) collective-permute-start(bf16[128,1536]{1,0:T(8,128)(2,1)S(1)} %fusion.2.refs_0_), channel_id=1, source_target_pairs={{0,2},{1,0},{2,1},{3,5},{4,3},{5,4},{6,8},{7,6},{8,7},{9,11},{10,9... | collective-permute-start | bytes 1179656 | tf_op jit(solution)/shard_map/ppermute | solution.py:24
  54.8 39.6 %all-to-all-start.2 = ((bf16[4,384,384]{2,1,0:T(8,128)(2,1)}), bf16[4,384,384]{2,1,0:T(8,128)(2,1)}, u32[]{:S(2)}, u32[]{:S(2)}) async-start(bf16[4,384,384]{2,1,0:T(8,128)(2,1)} %broadcast_in_dim.41), calls=%async_computation.2 | async-start | bytes 2359296 | tf_op jit(solution)/shard_map/all_to_all | solution.py:52
  59.7 15.4 %collective-permute-start.6 = (bf16[48,768]{1,0:T(8,128)(2,1)S(1)}, bf16[48,768]{1,0:T(8,128)(2,1)S(1)}, u32[]{:S(2)}, u32[]{:S(2)}) collective-permute-start(bf16[48,768]{1,0:T(8,128)(2,1)S(1)} %bitcast.55), channel_id=1, source_target_pairs={{0,192},{1,193},{2,194},{3,195},{4,196},{5,197},{6,198},{7,199},{8... | collective-permute-start | bytes 221192 | tf_op jit(solution)/shard_map/ppermute | solution.py:24
  62.5 12.7 %collective-permute-start.7 = (bf16[48,768]{1,0:T(8,128)(2,1)S(1)}, bf16[48,768]{1,0:T(8,128)(2,1)S(1)}, u32[]{:S(2)}, u32[]{:S(2)}) collective-permute-start(bf16[48,768]{1,0:T(8,128)(2,1)S(1)} %bitcast.56), channel_id=1, source_target_pairs={{0,576},{1,577},{2,578},{3,579},{4,580},{5,581},{6,582},{7,583},{8... | collective-permute-start | bytes 221192 | tf_op jit(solution)/shard_map/ppermute | solution.py:24
  66.8 9.7 %collective-permute-start.8 = (bf16[48,768]{1,0:T(8,128)(2,1)S(1)}, bf16[48,768]{1,0:T(8,128)(2,1)S(1)}, u32[]{:S(2)}, u32[]{:S(2)}) collective-permute-start(bf16[48,768]{1,0:T(8,128)(2,1)S(1)} %bitcast.57), channel_id=1, source_target_pairs={{0,384},{1,385},{2,386},{3,387},{4,388},{5,389},{6,390},{7,391},{8... | collective-permute-start | bytes 221192 | tf_op jit(solution)/shard_map/ppermute | solution.py:24
  76.6 38.8 %copy-start.12 = (bf16[128,1536]{1,0:T(8,128)(2,1)}, bf16[128,1536]{1,0:T(8,128)(2,1)S(1)}, u32[]{:S(2)}) copy-start(bf16[128,1536]{1,0:T(8,128)(2,1)S(1)} %collective-permute-done.1.refs_2_) | copy-start | bytes 1179652
  76.6 20.4 %collective-permute-start.9 = (bf16[192,768]{1,0:T(8,128)(2,1)S(1)}, bf16[192,768]{1,0:T(8,128)(2,1)S(1)}, u32[]{:S(2)}, u32[]{:S(2)}) collective-permute-start(bf16[192,768]{1,0:T(8,128)(2,1)S(1)} %bitcast.45), channel_id=1, source_target_pairs={{0,12},{1,13},{2,14},{3,15},{4,16},{5,17},{6,18},{7,19},{8,20},{9,... | collective-permute-start | bytes 884744 | tf_op jit(solution)/shard_map/ppermute | solution.py:24
  81.2 21.0 %collective-permute-start.10 = (bf16[192,768]{1,0:T(8,128)(2,1)S(1)}, bf16[192,768]{1,0:T(8,128)(2,1)S(1)}, u32[]{:S(2)}, u32[]{:S(2)}) collective-permute-start(bf16[192,768]{1,0:T(8,128)(2,1)S(1)} %bitcast.46), channel_id=1, source_target_pairs={{0,84},{1,85},{2,86},{3,87},{4,88},{5,89},{6,90},{7,91},{8,92},{9,... | collective-permute-start | bytes 884744 | tf_op jit(solution)/shard_map/ppermute | solution.py:24
  83.1 35.9 %collective-permute-start.3 = (bf16[128,1536]{1,0:T(8,128)(2,1)}, bf16[128,1536]{1,0:T(8,128)(2,1)S(1)}, u32[]{:S(2)}, u32[]{:S(2)}) collective-permute-start(bf16[128,1536]{1,0:T(8,128)(2,1)} %collective-permute-done.2.refs_3_), channel_id=1, source_target_pairs={{0,1},{1,2},{2,0},{3,4},{4,5},{5,3},{6,7},{7,8},{8,6},{9,10},{10,1... | collective-permute-start | bytes 1179656 | tf_op jit(solution)/shard_map/ppermute | solution.py:24
  92.4 35.2 %collective-permute-start.4 = (bf16[128,1536]{1,0:T(8,128)(2,1)}, bf16[128,1536]{1,0:T(8,128)(2,1)}, u32[]{:S(2)}, u32[]{:S(2)}) collective-permute-start(bf16[128,1536]{1,0:T(8,128)(2,1)} %collective-permute-done.2.refs_3_), channel_id=1, source_target_pairs={{0,2},{1,0},{2,1},{3,5},{4,3},{5,4},{6,8},{7,6},{8,7},{9,11},{10,9... | collective-permute-start | bytes 1179656 | tf_op jit(solution)/shard_map/ppermute | solution.py:24
  94.4 33.3 %collective-permute-start.5 = (bf16[1536,384]{1,0:T(8,128)(2,1)}, bf16[1536,384]{1,0:T(8,128)(2,1)}, u32[]{:S(2)}, u32[]{:S(2)}) collective-permute-start(bf16[1536,384]{1,0:T(8,128)(2,1)} %bitcast.10.refs_6_), channel_id=1, source_target_pairs={{0,6},{1,7},{2,8},{3,9},{4,10},{5,11},{6,0},{7,1},{8,2},{9,3},{10,... | collective-permute-start | bytes 3538952 | tf_op jit(solution)/shard_map/ppermute | solution.py:24
  97.0 12.0 %collective-permute-start.11 = (bf16[192,768]{1,0:T(8,128)(2,1)S(1)}, bf16[192,768]{1,0:T(8,128)(2,1)S(1)}, u32[]{:S(2)}, u32[]{:S(2)}) collective-permute-start(bf16[192,768]{1,0:T(8,128)(2,1)S(1)} %collective-permute-done.9.refs_1_), channel_id=1, source_target_pairs={{0,12},{1,13},{2,14},{3,15},{4,16},{5,17},{6,18},{7,19},{8,20},{9,... | collective-permute-start | bytes 884744 | tf_op jit(solution)/shard_map/ppermute | solution.py:24
  102.2 13.2 %collective-permute-start.12 = (bf16[192,768]{1,0:T(8,128)(2,1)S(1)}, bf16[192,768]{1,0:T(8,128)(2,1)}, u32[]{:S(2)}, u32[]{:S(2)}) collective-permute-start(bf16[192,768]{1,0:T(8,128)(2,1)S(1)} %collective-permute-done.10.refs_2_), channel_id=1, source_target_pairs={{0,84},{1,85},{2,86},{3,87},{4,88},{5,89},{6,90},{7,91},{8,92},{9,... | collective-permute-start | bytes 884744 | tf_op jit(solution)/shard_map/ppermute | solution.py:24
  109.1 11.9 %collective-permute-start.13 = (bf16[192,768]{1,0:T(8,128)(2,1)S(1)}, bf16[192,768]{1,0:T(8,128)(2,1)S(1)}, u32[]{:S(2)}, u32[]{:S(2)}) collective-permute-start(bf16[192,768]{1,0:T(8,128)(2,1)S(1)} %collective-permute-done.11.refs_3_), channel_id=1, source_target_pairs={{0,12},{1,13},{2,14},{3,15},{4,16},{5,17},{6,18},{7,19},{8,20},{9,... | collective-permute-start | bytes 884744 | tf_op jit(solution)/shard_map/ppermute | solution.py:24
  117.1 38.0 %collective-permute-start.16 = (bf16[5,192,768]{2,1,0:T(8,128)(2,1)}, bf16[5,192,768]{2,1,0:T(8,128)(2,1)S(1)}, u32[]{:S(2)}, u32[]{:S(2)}) collective-permute-start(bf16[5,192,768]{2,1,0:T(8,128)(2,1)} %bitcast_dynamic-update-slice_fusion), channel_id=1, source_target_pairs={{0,6},{1,7},{2,8},{3,9},{4,10},{5,11},{6,0},{7,1},{8,2},{9,3},{10,... | collective-permute-start | bytes 4423688 | tf_op jit(solution)/shard_map/ppermute | solution.py:24
  119.1 30.7 %collective-permute-start.14 = (bf16[192,768]{1,0:T(8,128)(2,1)}, bf16[192,768]{1,0:T(8,128)(2,1)S(1)}, u32[]{:S(2)}, u32[]{:S(2)}) collective-permute-start(bf16[192,768]{1,0:T(8,128)(2,1)} %collective-permute-done.12.refs_4_), channel_id=1, source_target_pairs={{0,84},{1,85},{2,86},{3,87},{4,88},{5,89},{6,90},{7,91},{8,92},{9,... | collective-permute-start | bytes 884744 | tf_op jit(solution)/shard_map/ppermute | solution.py:24
  121.0 28.7 %collective-permute-start.15 = (bf16[192,768]{1,0:T(8,128)(2,1)S(1)}, bf16[192,768]{1,0:T(8,128)(2,1)S(1)}, u32[]{:S(2)}, u32[]{:S(2)}) collective-permute-start(bf16[192,768]{1,0:T(8,128)(2,1)S(1)} %collective-permute-done.13.refs_5_), channel_id=1, source_target_pairs={{0,12},{1,13},{2,14},{3,15},{4,16},{5,17},{6,18},{7,19},{8,20},{9,... | collective-permute-start | bytes 884744 | tf_op jit(solution)/shard_map/ppermute | solution.py:24
  142.8 24.3 %all-to-all-start.3 = ((bf16[6,128,256]{2,1,0:T(8,128)(2,1)}), bf16[6,128,256]{2,1,0:T(8,128)(2,1)S(1)}, u32[]{:S(2)}, u32[]{:S(2)}) async-start(bf16[6,128,256]{2,1,0:T(8,128)(2,1)} %shard_map.82), calls=%async_computation.3 | async-start | bytes 786432 | tf_op jit(solution)/shard_map/all_to_all | solution.py:280
  149.8 4.3 %collective-permute-start.17 = (bf16[3,192,768]{2,1,0:T(8,128)(2,1)S(1)}, bf16[3,192,768]{2,1,0:T(8,128)(2,1)S(1)}, u32[]{:S(2)}, u32[]{:S(2)}) collective-permute-start(bf16[3,192,768]{2,1,0:T(8,128)(2,1)S(1)} %pad_maximum_fusion), channel_id=1, source_target_pairs={{0,6},{1,7},{2,8},{3,9},{4,10},{5,11},{6,0},{7,1},{8,2},{9,3},{10,... | collective-permute-start | bytes 2654216 | tf_op jit(solution)/shard_map/ppermute | solution.py:24
  (12 other events, 132.9 us)

commit v7 on v5

--- a/solution.py
+++ b/solution.py
@@ -28,10 +28,6 @@
     return permute(value, lambda x, zh, y, c, zl: (x, zh, y, 1 - c, zl))
 
 
-def y_shift(value, step):
-    return permute(value, lambda x, zh, y, c, zl: (x, zh, (y + step) % 8, c, zl))
-
-
 def x_swap(value, which):
     goal = {"even": (1, 0, 3, 2), "odd": (3, 2, 1, 0), "across": (2, 3, 0, 1)}[which]
     return permute(value, lambda x, zh, y, c, zl: (goal[x], zh, y, c, zl))
@@ -46,28 +42,16 @@
     return lax.optimization_barrier((value,) + others)[0]
 
 
-def put(whole, block, at):
-    return lax.dynamic_update_slice_in_dim(whole, block[None], at, 0)
-
-
 def gather_x(block):
     x = lax.axis_index("x")
-    whole = put(jnp.zeros((4,) + block.shape, block.dtype), block, x)
-    for which, at in (("even", x ^ 1), ("odd", 3 - x), ("across", (x + 2) % 4)):
-        whole = put(whole, x_swap(block, which), at)
-    return whole.reshape(-1, block.shape[1])
-
-
-def gather_y(block):
-    y = lax.axis_index("y")
-    whole = put(jnp.zeros((8,) + block.shape, block.dtype), block, y)
-    up = down = block
-    for step in range(1, 5):
-        up = y_shift(up, 1)
-        whole = put(whole, up, (y + 8 - step) % 8)
-        if step < 4:
-            down = y_shift(down, -1)
-            whole = put(whole, down, (y + step) % 8)
+    whole = jnp.zeros((4,) + block.shape, block.dtype)
+    for value, at in (
+        (block, x),
+        (x_swap(block, "even"), x ^ 1),
+        (x_swap(block, "odd"), 3 - x),
+        (x_swap(block, "across"), (x + 2) % 4),
+    ):
+        whole = lax.dynamic_update_slice_in_dim(whole, value[None], at, 0)
     return whole.reshape(-1, block.shape[1])
 
 
@@ -99,11 +83,11 @@
         copy.start()
     for which, half in ((0, core), (1, 1 - core)):
         w_copies[which].wait()
-        for at in range(4):
-            rows = slice(at * 384, at * 384 + 384)
+        for number in range(4):
+            rows = slice(number * 384, number * 384 + 384)
             w_buf[half, rows, :] = lax.dot_general(
                 move_ref[...],
-                w_in[which, rows, :],
+                w_in[which, number],
                 (((0,), (0,)), ((), ())),
                 preferred_element_type=jnp.float32,
             ).astype(jnp.bfloat16)
@@ -163,7 +147,7 @@
         out_specs=VMEM,
         scratch_shapes=[
             pltpu.VMEM((rows, width), jnp.bfloat16),
-            pltpu.VMEM((2, width, 384), jnp.bfloat16),
+            pltpu.VMEM((2, 4, 384, 384), jnp.bfloat16),
             pltpu.VMEM((2, width, 384), jnp.bfloat16),
             pltpu.VMEM((2, rows, 384), jnp.bfloat16),
             pltpu.SemaphoreType.DMA((3,)),
@@ -175,18 +159,33 @@
     )(core, length, temp, frames, own_w, other_w, reorder())
 
 
-def project_kernel(core_ref, heads_ref, own_ref, other_ref, move_hbm, out_ref, move_ref, sem):
+def project_kernel(core_ref, heads_hbm, own_hbm, other_hbm, move_hbm, out_ref, *scratch):
+    heads_ref, own_ref, other_ref, move_ref, sems = scratch
     core = core_ref[0]
-    move_copy = pltpu.make_async_copy(move_hbm, move_ref, sem)
-    move_copy.start()
+    copies = [
+        pltpu.make_async_copy(source, goal, sems.at[number])
+        for number, (source, goal) in enumerate(
+            (
+                (heads_hbm, heads_ref),
+                (own_hbm, own_ref),
+                (other_hbm, other_ref),
+                (move_hbm, move_ref),
+            )
+        )
+    ]
+    for copy in copies:
+        copy.start()
+    copies[0].wait()
     first = jnp.concatenate([heads_ref[at, :, :128] for at in range(6)], axis=1)
     second = jnp.concatenate([heads_ref[at, :, 128:] for at in range(6)], axis=1)
     mine = jnp.where(core == 0, first, second)
     given = jnp.where(core == 0, second, first)
     sides = (((1,), (1,)), ((), ()))
+    copies[1].wait()
     total = lax.dot_general(mine, own_ref[...], sides, preferred_element_type=jnp.float32)
+    copies[2].wait()
     total += lax.dot_general(given, other_ref[...], sides, preferred_element_type=jnp.float32)
-    move_copy.wait()
+    copies[3].wait()
     out_ref[...] = jnp.dot(
         total.astype(jnp.bfloat16), move_ref[...], preferred_element_type=jnp.float32
     ).astype(jnp.bfloat16)
@@ -196,10 +195,16 @@
     return pl.pallas_call(
         project_kernel,
         out_shape=jax.ShapeDtypeStruct((heads.shape[1], 1536), jnp.bfloat16),
-        in_specs=[SMEM] + [VMEM] * 3 + [HBM],
+        in_specs=[SMEM] + [HBM] * 4,
         out_specs=VMEM,
-        scratch_shapes=[pltpu.VMEM((1536, 1536), jnp.bfloat16), pltpu.SemaphoreType.DMA],
-        compiler_params=pltpu.CompilerParams(vmem_limit_bytes=24 * 2**20),
+        scratch_shapes=[
+            pltpu.VMEM(heads.shape, jnp.bfloat16),
+            pltpu.VMEM(own.shape, jnp.bfloat16),
+            pltpu.VMEM(own.shape, jnp.bfloat16),
+            pltpu.VMEM((1536, 1536), jnp.bfloat16),
+            pltpu.SemaphoreType.DMA((4,)),
+        ],
+        compiler_params=pltpu.CompilerParams(vmem_limit_bytes=58 * 2**20),
         cost_estimate=pl.CostEstimate(
             flops=12 * 10**8, bytes_accessed=10 * 10**6, transcendentals=0
         ),
@@ -207,29 +212,31 @@
 
 
 def on_device(latents, norm_gain, w_qkv, w_out, head_temp, lengths):
-    rows = w_qkv.reshape(3, 12, 2, 128).transpose(2, 1, 0, 3).reshape(2, 12, 384)
-    columns = w_out.T.reshape(12, 2, 128).transpose(1, 0, 2)
-    both = jnp.concatenate([rows, columns], axis=2).reshape(1, 2, 48, 128)
-    both = jnp.broadcast_to(both, (12, 2, 48, 128)).reshape(24, 48, 128)
-    both = lax.all_to_all(both, ("zh", "zl", "c"), 0, 0, tiled=True)
-    both = both.reshape(2, 6, 2, 12, 512)
-    rows = lax.dynamic_index_in_dim(both[..., :384], lax.axis_index("zl"), 1, keepdims=False)
-    rows = rows.reshape(48, 384)
-
     frames = latents[0]
     values = frames.astype(jnp.float32)
     rms = jnp.sqrt(jnp.mean(values * values, axis=-1, keepdims=True) + 1e-06)
     normed = (values / rms * norm_gain).astype(jnp.bfloat16)
     whole = lax.all_gather(normed, "zl", axis=0, tiled=True)
 
-    own_w = gather(rows, ("x", "y"), 32)
+    rows = w_qkv.reshape(3, 12, 2, 128).transpose(2, 1, 0, 3).reshape(2, 12, 384)
+    columns = w_out.T.reshape(12, 2, 128).transpose(1, 0, 2)
+    both = jnp.concatenate([rows, columns], axis=2).reshape(1, 2, 48, 128)
+    both = jnp.broadcast_to(both, (12, 2, 48, 128)).reshape(24, 48, 128)
+    both = lax.all_to_all(after(both, normed), ("zh", "zl", "c"), 0, 0, tiled=True)
+    both = both.reshape(2, 6, 2, 12, 512)
+    rows = lax.dynamic_index_in_dim(both[..., :384], lax.axis_index("zl"), 1, keepdims=False)
+    rows = rows.reshape(48, 384)
+    by_y = gather(rows, "y", 8)
+    columns = both[..., 384:].transpose(0, 2, 3, 1, 4).reshape(48, 768)
+    own_w = gather(by_y, "x", 4).reshape(4, 384, 384)
+    out_by_x, own_w = lax.optimization_barrier((gather_x(columns), own_w))
     other_w = other_core(own_w)
-    columns = both[..., 384:].transpose(0, 2, 3, 1, 4).reshape(48, 768)
-    out_own = gather_y(gather_x(columns))
+    out_own = lax.all_gather(out_by_x, "y", axis=0, tiled=True)
 
     core = lax.axis_index("c").reshape(1).astype(jnp.int32)
     blocks = attend(core, lengths, head_temp, whole, own_w, other_w)
     own = lax.all_to_all(blocks, "zl", 0, 0, tiled=True)
+    own, out_own = lax.optimization_barrier((own, out_own))
     out_other = other_core(out_own)
     return project(core, own, out_own, out_other)[None]
 

time: 185 us -> 158 us (0.85)
  starting transfers between devices: 75.4 us -> 47.5 us
  blocking collectives: 0 us -> 24.7 us
  waiting for transfers between devices: 55.8 us -> 39 us
  local copies, waits for them, and re-layouts: 14.7 us -> 7.84 us
    all_to_all x0 -> x1, blocking collectives: none -> 24.7 us  [on_device(): own = lax.all_to_all(blocks, 'zl', 0, 0, tiled=True)]
    ppermute x12 -> x5, starting transfers between devices: 44 us -> 19.5 us  [permute(): return lax.ppermute(value, AXES, pairs)]
    ppermute x12 -> x5, waiting for transfers between devices: 26.1 us -> 12.5 us  [permute(): return lax.ppermute(value, AXES, pairs)]
    all_to_all x2 -> x1, waiting for transfers between devices: 29.7 us -> 16.3 us  [on_device(): lax.all_to_all(after(both, normed), ('zh', 'zl', 'c'), 0, 0, tiled=True)]
    all_to_all x1 -> x2, waiting for transfers between devices: 0.01 us -> 10.2 us  [gather(): lax.all_to_all(copies, axes, 0, 0, tiled=True).reshape(-1, value.shape[1])]
    dynamic_update_slice x12 -> x4, local copies, waits for them, and re-layouts: 7.56 us -> 0.04 us  [gather_x(): whole = lax.dynamic_update_slice_in_dim(whole, value[None], at, 0)]
    all_to_all x2 -> x1, starting transfers between devices: 22.1 us -> 16.7 us  [on_device(): lax.all_to_all(after(both, normed), ('zh', 'zl', 'c'), 0, 0, tiled=True)]
    all_to_all x1 -> x2, starting transfers between devices: 9.25 us -> 11.2 us  [gather(): lax.all_to_all(copies, axes, 0, 0, tiled=True).reshape(-1, value.shape[1])]
  transfers between devices with their start and end apart: 16 -> 10, of which waited for: 5 -> 6; matrix products, arithmetic and copies ran while one was open for 7% -> 3% of each run, Pallas kernels for 8% -> 10%
where the time goes in v7:
time: 158 us; the launch traced here: 157 us
  starting transfers between devices  47.5 us (30%)
  waiting for transfers between devices  39 us (25%)
  blocking collectives  24.7 us (16%)
  Pallas kernels  20.7 us (13%)
  between operations  14.3 us (9%)
  local copies, waits for them, and re-layouts  7.84 us (5%)
  other arithmetic  3.1 us (2%)
    all_to_all x1, blocking collectives, on_device(): own = lax.all_to_all(blocks, 'zl', 0, 0, tiled=True)  24.7 us
    ppermute x5, starting transfers between devices, permute(): return lax.ppermute(value, AXES, pairs)  19.5 us
    all_to_all x1, starting transfers between devices, on_device(): lax.all_to_all(after(both, normed), ('zh', 'zl', 'c'), 0, 0, tiled=True)  16.7 us
    all_to_all x1, waiting for transfers between devices, on_device(): lax.all_to_all(after(both, normed), ('zh', 'zl', 'c'), 0, 0, tiled=True)  16.3 us
    pallas_call x1, Pallas kernels, attend(): pl.pallas_call(attend_kernel, out_shape=jax.ShapeDtypeStruct((6, rows //...  15 us
    ppermute x5, waiting for transfers between devices, permute(): return lax.ppermute(value, AXES, pairs)  12.5 us
    all_to_all x2, starting transfers between devices, gather(): lax.all_to_all(copies, axes, 0, 0, tiled=True).reshape(-1, value.shape[1])  11.2 us
    all_to_all x2, waiting for transfers between devices, gather(): lax.all_to_all(copies, axes, 0, 0, tiled=True).reshape(-1, value.shape[1])  10.2 us
  transfers between devices with their start and end apart: 10, of which 6 were waited for; matrix products, arithmetic and copies ran while one was open for 3% of the time, Pallas kernels for 10%

profile of v7, /device:TPU:1, one launch (start us, length us, event | category | flops | bytes accessed | tf_op | source)
XLA Modules:
  0.0 157.1 jit_solution(13776954677209493102)
XLA Ops:
  6.5 1.2 fusion
  7.7 1.9 %fusion.2 = bf16[128,1536]{1,0:T(8,128)(2,1)} fusion(bf16[1,128,1536]{2,1,0:T(8,128)(2,1)} %param.8, f32[1536]{0:T(1024)} %param.9, f32[128]{0:T(128)S(1)} %add_sqrt_fusion), kind=kLoop, calls=%fused_computation.4 | loop fusion | flops 786432 | bytes 793088 | tf_op jit(solution)/shard_map/convert_element_type | solution.py:218
  9.6 0.8 reshape.41
  11.2 0.7 broadcast_in_dim.40
  12.0 16.7 %all-to-all-start = ((bf16[24,48,128]{2,1,0:T(8,128)(2,1)}), bf16[24,48,128]{2,1,0:T(8,128)(2,1)S(1)}, u32[]{:S(2)}, u32[]{:S(2)}) async-start(bf16[24,48,128]{2,1,0:T(8,128)(2,1)} %bitcast.6), calls=%async_computation | async-start | bytes 589824 | tf_op jit(solution)/shard_map/all_to_all | solution.py:225
  28.7 16.3 %all-to-all-done = bf16[24,48,128]{2,1,0:T(8,128)(2,1)S(1)} async-done(((bf16[24,48,128]{2,1,0:T(8,128)(2,1)}), bf16[24,48,128]{2,1,0:T(8,128)(2,1)S(1)}, u32[]{:S(2)}, u32[]{:S(2)}) %all-to-all-start) | async-done | bytes 294944 | tf_op jit(solution)/shard_map/all_to_all | solution.py:225
  46.0 7.2 %all-to-all-start.1 = ((bf16[8,48,384]{2,1,0:T(8,128)(2,1)}), bf16[8,48,384]{2,1,0:T(8,128)(2,1)S(1)}, u32[]{:S(2)}, u32[]{:S(2)}) async-start(bf16[8,48,384]{2,1,0:T(8,128)(2,1)} %broadcast_in_dim.45), calls=%async_computation.1 | async-start | bytes 589824 | tf_op jit(solution)/shard_map/all_to_all | solution.py:38
  53.2 10.2 %all-to-all-done.1 = bf16[8,48,384]{2,1,0:T(8,128)(2,1)S(1)} async-done(((bf16[8,48,384]{2,1,0:T(8,128)(2,1)}), bf16[8,48,384]{2,1,0:T(8,128)(2,1)S(1)}, u32[]{:S(2)}, u32[]{:S(2)}) %all-to-all-start.1) | async-done | bytes 294944 | tf_op jit(solution)/shard_map/all_to_all | solution.py:38
  63.5 1.2 broadcast_in_dim.47
  64.6 4.0 %all-to-all-start.2 = ((bf16[4,384,384]{2,1,0:T(8,128)(2,1)}), bf16[4,384,384]{2,1,0:T(8,128)(2,1)S(1)}, u32[]{:S(2)}, u32[]{:S(2)}) async-start(bf16[4,384,384]{2,1,0:T(8,128)(2,1)} %broadcast_in_dim.47), calls=%async_computation.2 | async-start | bytes 2359296 | tf_op jit(solution)/shard_map/all_to_all | solution.py:38
  68.8 3.4 %collective-permute-start = (bf16[48,768]{1,0:T(8,128)(2,1)S(1)}, bf16[48,768]{1,0:T(8,128)(2,1)S(1)}, u32[]{:S(2)}, u32[]{:S(2)}) collective-permute-start(bf16[48,768]{1,0:T(8,128)(2,1)S(1)} %bitcast.33), channel_id=1, source_target_pairs={{0,192},{1,193},{2,194},{3,195},{4,196},{5,197},{6,198},{7,199},{8... | collective-permute-start | bytes 221192 | tf_op jit(solution)/shard_map/ppermute | solution.py:24
  72.2 3.7 %collective-permute-start.1 = (bf16[48,768]{1,0:T(8,128)(2,1)S(1)}, bf16[48,768]{1,0:T(8,128)(2,1)S(1)}, u32[]{:S(2)}, u32[]{:S(2)}) collective-permute-start(bf16[48,768]{1,0:T(8,128)(2,1)S(1)} %bitcast.34), channel_id=1, source_target_pairs={{0,576},{1,577},{2,578},{3,579},{4,580},{5,581},{6,582},{7,583},{8... | collective-permute-start | bytes 221192 | tf_op jit(solution)/shard_map/ppermute | solution.py:24
  75.9 2.5 %collective-permute-start.2 = (bf16[48,768]{1,0:T(8,128)(2,1)S(1)}, bf16[48,768]{1,0:T(8,128)(2,1)S(1)}, u32[]{:S(2)}, u32[]{:S(2)}) collective-permute-start(bf16[48,768]{1,0:T(8,128)(2,1)S(1)} %bitcast.35), channel_id=1, source_target_pairs={{0,384},{1,385},{2,386},{3,387},{4,388},{5,389},{6,390},{7,391},{8... | collective-permute-start | bytes 221192 | tf_op jit(solution)/shard_map/ppermute | solution.py:24
  78.5 3.3 %collective-permute-done = bf16[48,768]{1,0:T(8,128)(2,1)S(1)} collective-permute-done((bf16[48,768]{1,0:T(8,128)(2,1)S(1)}, bf16[48,768]{1,0:T(8,128)(2,1)S(1)}, u32[]{:S(2)}, u32[]{:S(2)}) %collective-permute-start) | collective-permute-done | bytes 73760 | tf_op jit(solution)/shard_map/ppermute | solution.py:24
  81.8 3.0 %collective-permute-done.2 = bf16[48,768]{1,0:T(8,128)(2,1)S(1)} collective-permute-done((bf16[48,768]{1,0:T(8,128)(2,1)S(1)}, bf16[48,768]{1,0:T(8,128)(2,1)S(1)}, u32[]{:S(2)}, u32[]{:S(2)}) %collective-permute-start.2) | collective-permute-done | bytes 73760 | tf_op jit(solution)/shard_map/ppermute | solution.py:24
  85.6 6.3 %collective-permute-start.3 = (bf16[4,384,384]{2,1,0:T(8,128)(2,1)S(1)}, bf16[4,384,384]{2,1,0:T(8,128)(2,1)S(1)}, u32[]{:S(2)}, u32[]{:S(2)}) collective-permute-start(bf16[4,384,384]{2,1,0:T(8,128)(2,1)S(1)} %all-to-all-done.2.own_w), channel_id=1, source_target_pairs={{0,6},{1,7},{2,8},{3,9},{4,10},{5,11},{6,0},{7,1},{8,2},{9,3},{10,... | collective-permute-start | bytes 3538952 | tf_op jit(solution)/shard_map/ppermute | solution.py:24
  92.6 1.8 %collective-permute-done.3.other_w = bf16[4,384,384]{2,1,0:T(8,128)(2,1)S(1)} collective-permute-done((bf16[4,384,384]{2,1,0:T(8,128)(2,1)S(1)}, bf16[4,384,384]{2,1,0:T(8,128)(2,1)S(1)}, u32[]{:S(2)}, u32[]{:S(2)}) %collective-permute-start.3) | collective-permute-done | bytes 1179680 | tf_op jit(solution)/shard_map/ppermute | solution.py:24
  94.4 1.0 copy-done.3
  95.5 15.0 %shard_map.82 = bf16[6,128,256]{2,1,0:T(8,128)(2,1)} custom-call(s32[1]{0:T(128)} %bitcast.core_ref, s32[1]{0:T(128)S(6)} %copy.23.length_ref, f32[4]{0:T(128)} %temp_ref.1, bf16[768,1536]{1,0:T(8,128)(2,1)} %all-gather.3.cloned.1.call-done.frames, bf16[4,384,384]{2,1,0:T(8,128)(2,1)} %copy-done.1, bf16[4,384,384]{2,1,0:T(8,128)(2,1)} %copy-done.3, ...), custom_call_target="tpu_custom_call" | custom-call | flops 3000000000 | bytes 5000000 | tf_op jit(solution)/shard_map/pallas_call | solution.py:143
  110.5 24.7 %all_to_all.20.heads_hbm = bf16[6,128,256]{2,1,0:T(8,128)(2,1)} all-to-all(bf16[6,128,256]{2,1,0:T(8,128)(2,1)} %shard_map.82), channel_id=1, replica_groups=mesh['x'=4,'zh'=2,'y'=8,'c'=2,'zl'=6] {'zl'}, dimensions={0} | all-to-all | bytes 786432 | tf_op jit(solution)/shard_map/all_to_all | solution.py:238
  135.2 3.6 %collective-permute-start.4 = (bf16[1536,768]{1,0:T(8,128)(2,1)}, bf16[1536,768]{1,0:T(8,128)(2,1)S(1)}, u32[]{:S(2)}, u32[]{:S(2)}) collective-permute-start(bf16[1536,768]{1,0:T(8,128)(2,1)} %all-gather.5.cloned.1.call-done.own_hbm), channel_id=1, source_target_pairs={{0,6},{1,7},{2,8},{3,9},{4,10},{5,11},{6,0},{7,1},{8,2},{9,3},{10,... | collective-permute-start | bytes 7077896 | tf_op jit(solution)/shard_map/ppermute | solution.py:24
  138.8 4.3 %collective-permute-done.4.other_hbm = bf16[1536,768]{1,0:T(8,128)(2,1)S(1)} collective-permute-done((bf16[1536,768]{1,0:T(8,128)(2,1)}, bf16[1536,768]{1,0:T(8,128)(2,1)S(1)}, u32[]{:S(2)}, u32[]{:S(2)}) %collective-permute-start.4) | collective-permute-done | bytes 2359328 | tf_op jit(solution)/shard_map/ppermute | solution.py:24
  143.1 1.4 copy-done
  144.5 5.7 %shard_map.83 = bf16[128,1536]{1,0:T(8,128)(2,1)} custom-call(s32[1]{0:T(128)} %bitcast.core_ref, bf16[6,128,256]{2,1,0:T(8,128)(2,1)} %all_to_all.20.heads_hbm, bf16[1536,768]{1,0:T(8,128)(2,1)} %all-gather.5.cloned.1.call-done.own_hbm, bf16[1536,768]{1,0:T(8,128)(2,1)} %copy-done, bf16[1536,1536]{1,0:T(8,128)(2,1)} %constant.51.clone.move_hbm), custom_call_target="tpu_custom_call" | custom-call | flops 1200000000 | bytes 10000000 | tf_op jit(solution)/shard_map/pallas_call | solution.py:195
  (35 shorter events, 2.8 us)
Async XLA Ops:
  6.5 87.9 %all-gather.3.cloned.1.call-start = ((), (), s32[]{:S(2)}) async-start(), calls=%async_computation.4 | async-start | bytes 2752512 | tf_op jit(solution)/shard_map/all_gather | solution.py:219
  12.0 33.0 %all-to-all-start = ((bf16[24,48,128]{2,1,0:T(8,128)(2,1)}), bf16[24,48,128]{2,1,0:T(8,128)(2,1)S(1)}, u32[]{:S(2)}, u32[]{:S(2)}) async-start(bf16[24,48,128]{2,1,0:T(8,128)(2,1)} %bitcast.6), calls=%async_computation | async-start | bytes 589824 | tf_op jit(solution)/shard_map/all_to_all | solution.py:225
  46.0 17.5 %all-to-all-start.1 = ((bf16[8,48,384]{2,1,0:T(8,128)(2,1)}), bf16[8,48,384]{2,1,0:T(8,128)(2,1)S(1)}, u32[]{:S(2)}, u32[]{:S(2)}) async-start(bf16[8,48,384]{2,1,0:T(8,128)(2,1)} %broadcast_in_dim.45), calls=%async_computation.1 | async-start | bytes 589824 | tf_op jit(solution)/shard_map/all_to_all | solution.py:38
  64.6 20.2 %all-to-all-start.2 = ((bf16[4,384,384]{2,1,0:T(8,128)(2,1)}), bf16[4,384,384]{2,1,0:T(8,128)(2,1)S(1)}, u32[]{:S(2)}, u32[]{:S(2)}) async-start(bf16[4,384,384]{2,1,0:T(8,128)(2,1)} %broadcast_in_dim.47), calls=%async_computation.2 | async-start | bytes 2359296 | tf_op jit(solution)/shard_map/all_to_all | solution.py:38
  68.6 66.5 %all-gather.5.cloned.1.call-start = ((), (), s32[]{:S(2)}) async-start(), calls=%async_computation.5 | async-start | bytes 2654208 | tf_op jit(solution)/shard_map/all_gather | solution.py:234
  68.8 12.9 %collective-permute-start = (bf16[48,768]{1,0:T(8,128)(2,1)S(1)}, bf16[48,768]{1,0:T(8,128)(2,1)S(1)}, u32[]{:S(2)}, u32[]{:S(2)}) collective-permute-start(bf16[48,768]{1,0:T(8,128)(2,1)S(1)} %bitcast.33), channel_id=1, source_target_pairs={{0,192},{1,193},{2,194},{3,195},{4,196},{5,197},{6,198},{7,199},{8... | collective-permute-start | bytes 221192 | tf_op jit(solution)/shard_map/ppermute | solution.py:24
  72.2 9.6 %collective-permute-start.1 = (bf16[48,768]{1,0:T(8,128)(2,1)S(1)}, bf16[48,768]{1,0:T(8,128)(2,1)S(1)}, u32[]{:S(2)}, u32[]{:S(2)}) collective-permute-start(bf16[48,768]{1,0:T(8,128)(2,1)S(1)} %bitcast.34), channel_id=1, source_target_pairs={{0,576},{1,577},{2,578},{3,579},{4,580},{5,581},{6,582},{7,583},{8... | collective-permute-start | bytes 221192 | tf_op jit(solution)/shard_map/ppermute | solution.py:24
  75.9 8.9 %collective-permute-start.2 = (bf16[48,768]{1,0:T(8,128)(2,1)S(1)}, bf16[48,768]{1,0:T(8,128)(2,1)S(1)}, u32[]{:S(2)}, u32[]{:S(2)}) collective-permute-start(bf16[48,768]{1,0:T(8,128)(2,1)S(1)} %bitcast.35), channel_id=1, source_target_pairs={{0,384},{1,385},{2,386},{3,387},{4,388},{5,389},{6,390},{7,391},{8... | collective-permute-start | bytes 221192 | tf_op jit(solution)/shard_map/ppermute | solution.py:24
  84.9 0.7 copy-start.2
  84.9 9.5 %copy-start.1 = (bf16[4,384,384]{2,1,0:T(8,128)(2,1)}, bf16[4,384,384]{2,1,0:T(8,128)(2,1)S(1)}, u32[]{:S(2)}) copy-start(bf16[4,384,384]{2,1,0:T(8,128)(2,1)S(1)} %all-to-all-done.2.own_w) | copy-start | bytes 3538948
  85.6 8.8 %collective-permute-start.3 = (bf16[4,384,384]{2,1,0:T(8,128)(2,1)S(1)}, bf16[4,384,384]{2,1,0:T(8,128)(2,1)S(1)}, u32[]{:S(2)}, u32[]{:S(2)}) collective-permute-start(bf16[4,384,384]{2,1,0:T(8,128)(2,1)S(1)} %all-to-all-done.2.own_w), channel_id=1, source_target_pairs={{0,6},{1,7},{2,8},{3,9},{4,10},{5,11},{6,0},{7,1},{8,2},{9,3},{10,... | collective-permute-start | bytes 3538952 | tf_op jit(solution)/shard_map/ppermute | solution.py:24
  94.4 1.0 copy-start.3
  135.2 8.0 %collective-permute-start.4 = (bf16[1536,768]{1,0:T(8,128)(2,1)}, bf16[1536,768]{1,0:T(8,128)(2,1)S(1)}, u32[]{:S(2)}, u32[]{:S(2)}) collective-permute-start(bf16[1536,768]{1,0:T(8,128)(2,1)} %all-gather.5.cloned.1.call-done.own_hbm), channel_id=1, source_target_pairs={{0,6},{1,7},{2,8},{3,9},{4,10},{5,11},{6,0},{7,1},{8,2},{9,3},{10,... | collective-permute-start | bytes 7077896 | tf_op jit(solution)/shard_map/ppermute | solution.py:24
  143.1 1.4 copy-start
Sparse Core Ops, SparseCore 0:
  9.8 77.4 all-gather.2
  89.6 39.7 all-gather.4

commit v8 on v7

v8 whole, which is shorter than its diff:
```python
import functools

import jax
import jax.numpy as jnp
import numpy as np
from jax import lax
from jax.experimental import pallas as pl
from jax.experimental.pallas import tpu as pltpu
from jax.sharding import Mesh, PartitionSpec as P

HD = 64
AXES = ("x", "zh", "y", "c", "zl")
SIZES = (4, 2, 8, 2, 6)


def permute(value, move):
    pairs = []
    for place in np.ndindex(*SIZES):
        goal = move(*place)
        if goal is not None:
            pairs.append(
                (int(np.ravel_multi_index(place, SIZES)), int(np.ravel_multi_index(goal, SIZES)))
            )
    return lax.ppermute(value, AXES, pairs)


def other_core(value):
    return permute(value, lambda x, zh, y, c, zl: (x, zh, y, 1 - c, zl))


def x_swap(value, which):
    goal = {"even": (1, 0, 3, 2), "odd": (3, 2, 1, 0), "across": (2, 3, 0, 1)}[which]
    return permute(value, lambda x, zh, y, c, zl: (goal[x], zh, y, c, zl))


def gather(value, axes, count):
    copies = jnp.broadcast_to(value[None], (count,) + value.shape)
    return lax.all_to_all(copies, axes, 0, 0, tiled=True).reshape(-1, value.shape[1])


def after(value, *others):
    return lax.optimization_barrier((value,) + others)[0]


def gather_x(block):
    x = lax.axis_index("x")
    whole = jnp.zeros((4,) + block.shape, block.dtype)
    for value, at in (
        (block, x),
        (x_swap(block, "even"), x ^ 1),
        (x_swap(block, "odd"), 3 - x),
        (x_swap(block, "across"), (x + 2) % 4),
    ):
        whole = lax.dynamic_update_slice_in_dim(whole, value[None], at, 0)
    return whole.reshape(-1, block.shape[1])


def attend_kernel(core_ref, length_ref, temp_ref, frames, own_w, other_w, *refs):
    out_ref, x_buf, w_buf, qkv, sems = refs
    core = core_ref[0]
    copies = []
    for number in range(4):
        rows = pl.ds(number * 384, 384)
        for source, half in ((own_w, core), (other_w, 1 - core)):
            columns = pl.ds(pl.multiple_of(half * 384, 128), 384)
            copies.append((source.at[rows], w_buf.at[rows, columns]))
    for number in range(6):
        rows = pl.ds(number * 128, 128)
        copies.append((frames.at[rows], x_buf.at[rows]))
    copies = [
        pltpu.make_async_copy(source, goal, sems.at[number])
        for number, (source, goal) in enumerate(copies)
    ]
    for copy in copies:
        copy.start()
    for copy in copies:
        copy.wait()
    qkv[...] = jnp.dot(
        x_buf[...], w_buf[...], preferred_element_type=jnp.float32
    ).astype(jnp.bfloat16)

    total = x_buf.shape[0]
    live = lax.broadcasted_iota(jnp.int32, (total, 1), 0) < length_ref[0]
    lane = lax.broadcasted_iota(jnp.int32, (total, 128), 1)
    place = lax.broadcasted_iota(jnp.int32, (1, 2 * total), 1)
    for two in range(2):
        query, key_part, value = (
            qkv[:, two * 384 + k * 128 : two * 384 + k * 128 + 128] for k in range(3)
        )
        none = jnp.zeros_like(query)
        query = jnp.concatenate(
            [jnp.where(lane < HD, query, none), jnp.where(lane < HD, none, query)]
        )
        scores = lax.dot_general(
            key_part, query, (((1,), (1,)), ((), ())), preferred_element_type=jnp.float32
        )
        scale = jnp.where(place < total, temp_ref[2 * two] / 8.0, temp_ref[2 * two + 1] / 8.0)
        scores = jnp.where(live, scores * scale, -1e30)
        scores = jnp.exp(scores - jnp.max(scores, axis=0, keepdims=True))
        mixed = lax.dot_general(
            value,
            scores.astype(jnp.bfloat16),
            (((0,), (0,)), ((), ())),
            preferred_element_type=jnp.float32,
        )
        mixed = mixed / jnp.sum(scores, axis=0, keepdims=True)
        mixed = jnp.concatenate([mixed[:HD, :total], mixed[HD:, total:]]).T
        out_ref[:, :, two * 128 : two * 128 + 128] = mixed.astype(jnp.bfloat16).reshape(
            out_ref.shape[0], out_ref.shape[1], 128
        )


SMEM = pl.BlockSpec(memory_space=pltpu.SMEM)
VMEM = pl.BlockSpec(memory_space=pltpu.VMEM)
ANYWHERE = pl.BlockSpec(memory_space=pl.ANY)


def attend(core, length, temp, frames, own_w, other_w):
    rows, width = frames.shape
    return pl.pallas_call(
        attend_kernel,
        out_shape=jax.ShapeDtypeStruct((6, rows // 6, 256), jnp.bfloat16),
        in_specs=[SMEM] * 3 + [ANYWHERE] * 3,
        out_specs=VMEM,
        scratch_shapes=[
            pltpu.VMEM((rows, width), jnp.bfloat16),
            pltpu.VMEM((width, 768), jnp.bfloat16),
            pltpu.VMEM((rows, 768), jnp.bfloat16),
            pltpu.SemaphoreType.DMA((14,)),
        ],
        compiler_params=pltpu.CompilerParams(vmem_limit_bytes=58 * 2**20),
        cost_estimate=pl.CostEstimate(
            flops=3 * 10**9, bytes_accessed=5 * 10**6, transcendentals=2 * 10**6
        ),
    )(core, length, temp, frames, own_w, other_w)


def project_kernel(core_ref, heads_any, own_any, other_any, out_ref, *scratch):
    heads_ref, own_ref, other_ref, sums, sems = scratch
    core = core_ref[0]
    copies = [(heads_any, heads_ref)]
    for source, goal in ((own_any, own_ref), (other_any, other_ref)):
        for number in range(4):
            rows = pl.ds(number * 384, 384)
            copies.append((source.at[rows], goal.at[rows]))
    copies = [
        pltpu.make_async_copy(source, goal, sems.at[number])
        for number, (source, goal) in enumerate(copies)
    ]
    for copy in copies:
        copy.start()
    copies[0].wait()
    first = jnp.concatenate([heads_ref[at, :, :128] for at in range(6)], axis=1)
    second = jnp.concatenate([heads_ref[at, :, 128:] for at in range(6)], axis=1)
    mine = jnp.where(core == 0, first, second).T
    given = jnp.where(core == 0, second, first).T
    for number in range(4):
        rows = pl.ds(number * 384, 384)
        copies[1 + number].wait()
        sums[rows] = jnp.dot(own_ref[rows], mine, preferred_element_type=jnp.float32)
    for number in range(4):
        rows = pl.ds(number * 384, 384)
        copies[5 + number].wait()
        sums[rows] += jnp.dot(other_ref[rows], given, preferred_element_type=jnp.float32)
    for x in range(4):
        pieces = []
        for zh in range(2):
            for y in range(8):
                at = ((y * 4 + x) * 2 + zh) * 24
                pieces.append(sums[at : at + 24, :])
        block = jnp.concatenate(pieces).T
        out_ref[:, x * 384 : x * 384 + 384] = block.astype(jnp.bfloat16)


def project(core, heads, own, other):
    rows = heads.shape[1]
    return pl.pallas_call(
        project_kernel,
        out_shape=jax.ShapeDtypeStruct((rows, 1536), jnp.bfloat16),
        in_specs=[SMEM] + [ANYWHERE] * 3,
        out_specs=VMEM,
        scratch_shapes=[
            pltpu.VMEM(heads.shape, jnp.bfloat16),
            pltpu.VMEM(own.shape, jnp.bfloat16),
            pltpu.VMEM(own.shape, jnp.bfloat16),
            pltpu.VMEM((1536, rows), jnp.float32),
            pltpu.SemaphoreType.DMA((9,)),
        ],
        compiler_params=pltpu.CompilerParams(vmem_limit_bytes=58 * 2**20),
        cost_estimate=pl.CostEstimate(
            flops=6 * 10**8, bytes_accessed=5 * 10**6, transcendentals=0
        ),
    )(core, heads, own, other)


def on_device(latents, norm_gain, w_qkv, w_out, head_temp, lengths):
    frames = latents[0]
    values = frames.astype(jnp.float32)
    rms = jnp.sqrt(jnp.mean(values * values, axis=-1, keepdims=True) + 1e-06)
    normed = (values / rms * norm_gain).astype(jnp.bfloat16)
    whole = lax.all_gather(normed, "zl", axis=0, tiled=True)

    rows = w_qkv.reshape(3, 12, 2, 128).transpose(2, 1, 0, 3).reshape(2, 12, 384)
    columns = w_out.T.reshape(12, 2, 128).transpose(1, 0, 2)
    both = jnp.concatenate([rows, columns], axis=2).reshape(1, 2, 48, 128)
    both = jnp.broadcast_to(both, (12, 2, 48, 128)).reshape(24, 48, 128)
    both = lax.all_to_all(after(both, normed), ("zh", "zl", "c"), 0, 0, tiled=True)
    both = both.reshape(2, 6, 2, 12, 512)
    rows = lax.dynamic_index_in_dim(both[..., :384], lax.axis_index("zl"), 1, keepdims=False)
    rows = rows.reshape(48, 384)
    by_y = gather(rows, "y", 8).reshape(8, 2, 24, 384).transpose(1, 0, 2, 3).reshape(384, 384)
    columns = both[..., 384:].transpose(0, 2, 3, 1, 4).reshape(48, 768)
    own_w = gather(by_y, "x", 4)
    out_by_x, own_w = lax.optimization_barrier((gather_x(columns), own_w))
    other_w = other_core(own_w)
    out_own = lax.all_gather(out_by_x, "y", axis=0, tiled=True)

    core = lax.axis_index("c").reshape(1).astype(jnp.int32)
    blocks = attend(core, lengths, head_temp, whole, own_w, other_w)
    own = lax.all_to_all(blocks, "zl", 0, 0, tiled=True)
    own, out_own = lax.optimization_barrier((own, out_own))
    out_other = other_core(out_own)
    return project(core, own, out_own, out_other)[None]


def solution(mesh):
    split = Mesh(mesh.devices.reshape(SIZES), AXES)
    clip = ("x", "zh", "y", "c")
    in_specs = (
        P(clip, "zl", None),
        P(),
        P(None, clip, "zl"),
        P("zl", clip),
        P("zl"),
        P(clip),
    )
    out_specs = P(clip, "zl", None)
    return jax.shard_map(
        on_device, mesh=split, in_specs=in_specs, out_specs=out_specs, check_vma=False
    )
```

time: 158 us -> 154 us (0.975)
  Pallas kernels: 20.7 us -> 14.3 us
  starting transfers between devices: 47.5 us -> 49.6 us
    pallas_call x1, Pallas kernels: 15 us -> 9.09 us  [attend(): pl.pallas_call(attend_kernel, out_shape=jax.ShapeDtypeStruct((6, rows //...]
    ppermute x5, starting transfers between devices: 19.5 us -> 21.7 us  [permute(): return lax.ppermute(value, AXES, pairs)]
  transfers between devices with their start and end apart: 10 -> 10, of which waited for: 6 -> 7; matrix products, arithmetic and copies ran while one was open for 3% -> 3% of each run, Pallas kernels for 10% -> 6%
where the time goes in v8:
time: 154 us
  starting transfers between devices  49.6 us (32%)
  waiting for transfers between devices  39.7 us (26%)
  blocking collectives  24.7 us (16%)
  Pallas kernels  14.3 us (9%)
  between operations  14.3 us (9%)
  local copies, waits for them, and re-layouts  7.87 us (5%)
  other arithmetic  3.1 us (2%)
    all_to_all x1, blocking collectives, on_device(): own = lax.all_to_all(blocks, 'zl', 0, 0, tiled=True)  24.7 us
    ppermute x5, starting transfers between devices, permute(): return lax.ppermute(value, AXES, pairs)  21.7 us
    all_to_all x1, starting transfers between devices, on_device(): lax.all_to_all(after(both, normed), ('zh', 'zl', 'c'), 0, 0, tiled=True)  16.7 us
    all_to_all x1, waiting for transfers between devices, on_device(): lax.all_to_all(after(both, normed), ('zh', 'zl', 'c'), 0, 0, tiled=True)  16.3 us
    ppermute x5, waiting for transfers between devices, permute(): return lax.ppermute(value, AXES, pairs)  12.5 us
    all_to_all x2, starting transfers between devices, gather(): lax.all_to_all(copies, axes, 0, 0, tiled=True).reshape(-1, value.shape[1])  11.2 us
    all_to_all x2, waiting for transfers between devices, gather(): lax.all_to_all(copies, axes, 0, 0, tiled=True).reshape(-1, value.shape[1])  10.2 us
    pallas_call x1, Pallas kernels, attend(): pl.pallas_call(attend_kernel, out_shape=jax.ShapeDtypeStruct((6, rows //...  9.09 us
  transfers between devices with their start and end apart: 10, of which 7 were waited for; matrix products, arithmetic and copies ran while one was open for 3% of the time, Pallas kernels for 6%

profile of v8, /device:TPU:1, one launch (start us, length us, event | category | flops | bytes accessed | tf_op | source)
XLA Modules:
  0.0 153.6 jit_solution(17196455242525277180)
XLA Ops:
  6.5 1.2 fusion
  7.7 1.9 %fusion.2 = bf16[128,1536]{1,0:T(8,128)(2,1)} fusion(bf16[1,128,1536]{2,1,0:T(8,128)(2,1)} %param.6, f32[1536]{0:T(1024)} %param.7, f32[128]{0:T(128)S(1)} %add_sqrt_fusion), kind=kLoop, calls=%fused_computation.4 | loop fusion | flops 786432 | bytes 793088 | tf_op jit(solution)/shard_map/convert_element_type | solution.py:200
  9.6 0.8 reshape.44
  11.2 0.7 broadcast_in_dim.40
  12.0 16.7 %all-to-all-start = ((bf16[24,48,128]{2,1,0:T(8,128)(2,1)}), bf16[24,48,128]{2,1,0:T(8,128)(2,1)S(1)}, u32[]{:S(2)}, u32[]{:S(2)}) async-start(bf16[24,48,128]{2,1,0:T(8,128)(2,1)} %bitcast.6), calls=%async_computation | async-start | bytes 589824 | tf_op jit(solution)/shard_map/all_to_all | solution.py:207
  28.7 16.3 %all-to-all-done = bf16[24,48,128]{2,1,0:T(8,128)(2,1)S(1)} async-done(((bf16[24,48,128]{2,1,0:T(8,128)(2,1)}), bf16[24,48,128]{2,1,0:T(8,128)(2,1)S(1)}, u32[]{:S(2)}, u32[]{:S(2)}) %all-to-all-start) | async-done | bytes 294944 | tf_op jit(solution)/shard_map/all_to_all | solution.py:207
  46.0 7.2 %all-to-all-start.1 = ((bf16[8,48,384]{2,1,0:T(8,128)(2,1)}), bf16[8,48,384]{2,1,0:T(8,128)(2,1)S(1)}, u32[]{:S(2)}, u32[]{:S(2)}) async-start(bf16[8,48,384]{2,1,0:T(8,128)(2,1)} %broadcast_in_dim.45), calls=%async_computation.1 | async-start | bytes 589824 | tf_op jit(solution)/shard_map/all_to_all | solution.py:38
  53.2 10.2 %all-to-all-done.1 = bf16[8,48,384]{2,1,0:T(8,128)(2,1)S(1)} async-done(((bf16[8,48,384]{2,1,0:T(8,128)(2,1)}), bf16[8,48,384]{2,1,0:T(8,128)(2,1)S(1)}, u32[]{:S(2)}, u32[]{:S(2)}) %all-to-all-start.1) | async-done | bytes 294944 | tf_op jit(solution)/shard_map/all_to_all | solution.py:38
  63.5 1.2 broadcast_in_dim.47
  64.7 4.0 %all-to-all-start.2 = ((bf16[4,384,384]{2,1,0:T(8,128)(2,1)}), bf16[4,384,384]{2,1,0:T(8,128)(2,1)S(1)}, u32[]{:S(2)}, u32[]{:S(2)}) async-start(bf16[4,384,384]{2,1,0:T(8,128)(2,1)} %broadcast_in_dim.47), calls=%async_computation.2 | async-start | bytes 2359296 | tf_op jit(solution)/shard_map/all_to_all | solution.py:38
  68.9 3.4 %collective-permute-start = (bf16[48,768]{1,0:T(8,128)(2,1)S(1)}, bf16[48,768]{1,0:T(8,128)(2,1)S(1)}, u32[]{:S(2)}, u32[]{:S(2)}) collective-permute-start(bf16[48,768]{1,0:T(8,128)(2,1)S(1)} %bitcast.40), channel_id=1, source_target_pairs={{0,192},{1,193},{2,194},{3,195},{4,196},{5,197},{6,198},{7,199},{8... | collective-permute-start | bytes 221192 | tf_op jit(solution)/shard_map/ppermute | solution.py:24
  72.2 3.7 %collective-permute-start.1 = (bf16[48,768]{1,0:T(8,128)(2,1)S(1)}, bf16[48,768]{1,0:T(8,128)(2,1)S(1)}, u32[]{:S(2)}, u32[]{:S(2)}) collective-permute-start(bf16[48,768]{1,0:T(8,128)(2,1)S(1)} %bitcast.41), channel_id=1, source_target_pairs={{0,576},{1,577},{2,578},{3,579},{4,580},{5,581},{6,582},{7,583},{8... | collective-permute-start | bytes 221192 | tf_op jit(solution)/shard_map/ppermute | solution.py:24
  75.9 2.5 %collective-permute-start.2 = (bf16[48,768]{1,0:T(8,128)(2,1)S(1)}, bf16[48,768]{1,0:T(8,128)(2,1)S(1)}, u32[]{:S(2)}, u32[]{:S(2)}) collective-permute-start(bf16[48,768]{1,0:T(8,128)(2,1)S(1)} %bitcast.42), channel_id=1, source_target_pairs={{0,384},{1,385},{2,386},{3,387},{4,388},{5,389},{6,390},{7,391},{8... | collective-permute-start | bytes 221192 | tf_op jit(solution)/shard_map/ppermute | solution.py:24
  78.5 3.3 %collective-permute-done = bf16[48,768]{1,0:T(8,128)(2,1)S(1)} collective-permute-done((bf16[48,768]{1,0:T(8,128)(2,1)S(1)}, bf16[48,768]{1,0:T(8,128)(2,1)S(1)}, u32[]{:S(2)}, u32[]{:S(2)}) %collective-permute-start) | collective-permute-done | bytes 73760 | tf_op jit(solution)/shard_map/ppermute | solution.py:24
  81.9 3.0 %collective-permute-done.2 = bf16[48,768]{1,0:T(8,128)(2,1)S(1)} collective-permute-done((bf16[48,768]{1,0:T(8,128)(2,1)S(1)}, bf16[48,768]{1,0:T(8,128)(2,1)S(1)}, u32[]{:S(2)}, u32[]{:S(2)}) %collective-permute-start.2) | collective-permute-done | bytes 73760 | tf_op jit(solution)/shard_map/ppermute | solution.py:24
  85.6 6.3 %collective-permute-start.3 = (bf16[1536,384]{1,0:T(8,128)(2,1)S(1)}, bf16[1536,384]{1,0:T(8,128)(2,1)S(1)}, u32[]{:S(2)}, u32[]{:S(2)}) collective-permute-start(bf16[1536,384]{1,0:T(8,128)(2,1)S(1)} %bitcast.33), channel_id=1, source_target_pairs={{0,6},{1,7},{2,8},{3,9},{4,10},{5,11},{6,0},{7,1},{8,2},{9,3},{10,... | collective-permute-start | bytes 3538952 | tf_op jit(solution)/shard_map/ppermute | solution.py:24
  92.6 1.8 %collective-permute-done.3.other_w = bf16[1536,384]{1,0:T(8,128)(2,1)S(1)} collective-permute-done((bf16[1536,384]{1,0:T(8,128)(2,1)S(1)}, bf16[1536,384]{1,0:T(8,128)(2,1)S(1)}, u32[]{:S(2)}, u32[]{:S(2)}) %collective-permute-start.3) | collective-permute-done | bytes 1179680 | tf_op jit(solution)/shard_map/ppermute | solution.py:24
  94.5 1.0 copy-done.3
  95.5 9.1 %shard_map.64 = bf16[6,128,256]{2,1,0:T(8,128)(2,1)} custom-call(s32[1]{0:T(128)} %bitcast.core_ref, s32[1]{0:T(128)S(6)} %copy.26.length_ref, f32[4]{0:T(128)} %temp_ref.1, bf16[768,1536]{1,0:T(8,128)(2,1)} %all-gather.3.cloned.1.call-done.frames, bf16[1536,384]{1,0:T(8,128)(2,1)} %bitcast.34, bf16[1536,384]{1,0:T(8,128)(2,1)} %copy-done.3), custom_call_target="tpu_custom_call" | custom-call | flops 3000000000 | bytes 5000000 | tf_op jit(solution)/shard_map/pallas_call | solution.py:120
  104.6 24.7 %all_to_all.20.heads_any = bf16[6,128,256]{2,1,0:T(8,128)(2,1)} all-to-all(bf16[6,128,256]{2,1,0:T(8,128)(2,1)} %shard_map.64), channel_id=1, replica_groups=mesh['x'=4,'zh'=2,'y'=8,'c'=2,'zl'=6] {'zl'}, dimensions={0} | all-to-all | bytes 786432 | tf_op jit(solution)/shard_map/all_to_all | solution.py:220
  129.9 5.7 %collective-permute-start.4 = (bf16[1536,768]{1,0:T(8,128)(2,1)}, bf16[1536,768]{1,0:T(8,128)(2,1)S(1)}, u32[]{:S(2)}, u32[]{:S(2)}) collective-permute-start(bf16[1536,768]{1,0:T(8,128)(2,1)} %all-gather.5.cloned.1.call-done.own_any), channel_id=1, source_target_pairs={{0,6},{1,7},{2,8},{3,9},{4,10},{5,11},{6,0},{7,1},{8,2},{9,3},{10,... | collective-permute-start | bytes 7077896 | tf_op jit(solution)/shard_map/ppermute | solution.py:24
  135.7 4.3 %collective-permute-done.4.other_any = bf16[1536,768]{1,0:T(8,128)(2,1)S(1)} collective-permute-done((bf16[1536,768]{1,0:T(8,128)(2,1)}, bf16[1536,768]{1,0:T(8,128)(2,1)S(1)}, u32[]{:S(2)}, u32[]{:S(2)}) %collective-permute-start.4) | collective-permute-done | bytes 2359328 | tf_op jit(solution)/shard_map/ppermute | solution.py:24
  140.0 1.4 copy-done
  141.4 5.3 %shard_map.65 = bf16[128,1536]{1,0:T(8,128)(2,1)} custom-call(s32[1]{0:T(128)} %bitcast.core_ref, bf16[6,128,256]{2,1,0:T(8,128)(2,1)} %all_to_all.20.heads_any, bf16[1536,768]{1,0:T(8,128)(2,1)} %all-gather.5.cloned.1.call-done.own_any, bf16[1536,768]{1,0:T(8,128)(2,1)} %copy-done), custom_call_target="tpu_custom_call" | custom-call | flops 600000000 | bytes 5000000 | tf_op jit(solution)/shard_map/pallas_call | solution.py:177
  (36 shorter events, 3.5 us)
Async XLA Ops:
  6.5 87.9 %all-gather.3.cloned.1.call-start = ((), (), s32[]{:S(2)}) async-start(), calls=%async_computation.4 | async-start | bytes 2752512 | tf_op jit(solution)/shard_map/all_gather | solution.py:201
  12.0 33.0 %all-to-all-start = ((bf16[24,48,128]{2,1,0:T(8,128)(2,1)}), bf16[24,48,128]{2,1,0:T(8,128)(2,1)S(1)}, u32[]{:S(2)}, u32[]{:S(2)}) async-start(bf16[24,48,128]{2,1,0:T(8,128)(2,1)} %bitcast.6), calls=%async_computation | async-start | bytes 589824 | tf_op jit(solution)/shard_map/all_to_all | solution.py:207
  46.0 17.5 %all-to-all-start.1 = ((bf16[8,48,384]{2,1,0:T(8,128)(2,1)}), bf16[8,48,384]{2,1,0:T(8,128)(2,1)S(1)}, u32[]{:S(2)}, u32[]{:S(2)}) async-start(bf16[8,48,384]{2,1,0:T(8,128)(2,1)} %broadcast_in_dim.45), calls=%async_computation.1 | async-start | bytes 589824 | tf_op jit(solution)/shard_map/all_to_all | solution.py:38
  64.7 20.2 %all-to-all-start.2 = ((bf16[4,384,384]{2,1,0:T(8,128)(2,1)}), bf16[4,384,384]{2,1,0:T(8,128)(2,1)S(1)}, u32[]{:S(2)}, u32[]{:S(2)}) async-start(bf16[4,384,384]{2,1,0:T(8,128)(2,1)} %broadcast_in_dim.47), calls=%async_computation.2 | async-start | bytes 2359296 | tf_op jit(solution)/shard_map/all_to_all | solution.py:38
  68.7 61.3 %all-gather.5.cloned.1.call-start = ((), (), s32[]{:S(2)}) async-start(), calls=%async_computation.5 | async-start | bytes 2654208 | tf_op jit(solution)/shard_map/all_gather | solution.py:216
  68.9 12.9 %collective-permute-start = (bf16[48,768]{1,0:T(8,128)(2,1)S(1)}, bf16[48,768]{1,0:T(8,128)(2,1)S(1)}, u32[]{:S(2)}, u32[]{:S(2)}) collective-permute-start(bf16[48,768]{1,0:T(8,128)(2,1)S(1)} %bitcast.40), channel_id=1, source_target_pairs={{0,192},{1,193},{2,194},{3,195},{4,196},{5,197},{6,198},{7,199},{8... | collective-permute-start | bytes 221192 | tf_op jit(solution)/shard_map/ppermute | solution.py:24
  72.2 9.6 %collective-permute-start.1 = (bf16[48,768]{1,0:T(8,128)(2,1)S(1)}, bf16[48,768]{1,0:T(8,128)(2,1)S(1)}, u32[]{:S(2)}, u32[]{:S(2)}) collective-permute-start(bf16[48,768]{1,0:T(8,128)(2,1)S(1)} %bitcast.41), channel_id=1, source_target_pairs={{0,576},{1,577},{2,578},{3,579},{4,580},{5,581},{6,582},{7,583},{8... | collective-permute-start | bytes 221192 | tf_op jit(solution)/shard_map/ppermute | solution.py:24
  75.9 8.9 %collective-permute-start.2 = (bf16[48,768]{1,0:T(8,128)(2,1)S(1)}, bf16[48,768]{1,0:T(8,128)(2,1)S(1)}, u32[]{:S(2)}, u32[]{:S(2)}) collective-permute-start(bf16[48,768]{1,0:T(8,128)(2,1)S(1)} %bitcast.42), channel_id=1, source_target_pairs={{0,384},{1,385},{2,386},{3,387},{4,388},{5,389},{6,390},{7,391},{8... | collective-permute-start | bytes 221192 | tf_op jit(solution)/shard_map/ppermute | solution.py:24
  84.9 0.7 copy-start.2
  84.9 9.5 %copy-start.1 = (bf16[4,384,384]{2,1,0:T(8,128)(2,1)}, bf16[4,384,384]{2,1,0:T(8,128)(2,1)S(1)}, u32[]{:S(2)}) copy-start(bf16[4,384,384]{2,1,0:T(8,128)(2,1)S(1)} %all-to-all-done.2) | copy-start | bytes 3538948
  85.6 8.8 %collective-permute-start.3 = (bf16[1536,384]{1,0:T(8,128)(2,1)S(1)}, bf16[1536,384]{1,0:T(8,128)(2,1)S(1)}, u32[]{:S(2)}, u32[]{:S(2)}) collective-permute-start(bf16[1536,384]{1,0:T(8,128)(2,1)S(1)} %bitcast.33), channel_id=1, source_target_pairs={{0,6},{1,7},{2,8},{3,9},{4,10},{5,11},{6,0},{7,1},{8,2},{9,3},{10,... | collective-permute-start | bytes 3538952 | tf_op jit(solution)/shard_map/ppermute | solution.py:24
  94.4 1.0 copy-start.3
  129.9 10.1 %collective-permute-start.4 = (bf16[1536,768]{1,0:T(8,128)(2,1)}, bf16[1536,768]{1,0:T(8,128)(2,1)S(1)}, u32[]{:S(2)}, u32[]{:S(2)}) collective-permute-start(bf16[1536,768]{1,0:T(8,128)(2,1)} %all-gather.5.cloned.1.call-done.own_any), channel_id=1, source_target_pairs={{0,6},{1,7},{2,8},{3,9},{4,10},{5,11},{6,0},{7,1},{8,2},{9,3},{10,... | collective-permute-start | bytes 7077896 | tf_op jit(solution)/shard_map/ppermute | solution.py:24
  140.0 1.4 copy-start
Sparse Core Ops, SparseCore 0:
  9.8 77.4 all-gather.2
  89.6 40.2 all-gather.4

commit v9 on v8

v9 whole, which is shorter than its diff:
```python
import functools

import jax
import jax.numpy as jnp
import numpy as np
from jax import lax
from jax.experimental import pallas as pl
from jax.experimental.pallas import tpu as pltpu
from jax.sharding import Mesh, PartitionSpec as P

HD = 64
AXES = ("x", "zh", "y", "c", "zl")
SIZES = (4, 2, 8, 2, 6)


def permute(value, move):
    pairs = []
    for place in np.ndindex(*SIZES):
        goal = move(*place)
        if goal is not None:
            pairs.append(
                (int(np.ravel_multi_index(place, SIZES)), int(np.ravel_multi_index(goal, SIZES)))
            )
    return lax.ppermute(value, AXES, pairs)


def other_core(value):
    return permute(value, lambda x, zh, y, c, zl: (x, zh, y, 1 - c, zl))


def other_triple(value):
    return permute(value, lambda x, zh, y, c, zl: (x, zh, y, c, (zl + 3) % 6))


def triple_shift(value, step):
    return permute(
        value, lambda x, zh, y, c, zl: (x, zh, y, c, zl // 3 * 3 + (zl + step) % 3)
    )


def x_swap(value, which):
    goal = {"even": (1, 0, 3, 2), "odd": (3, 2, 1, 0), "across": (2, 3, 0, 1)}[which]
    return permute(value, lambda x, zh, y, c, zl: (goal[x], zh, y, c, zl))


def gather(value, axes, count):
    copies = jnp.broadcast_to(value[None], (count,) + value.shape)
    return lax.all_to_all(copies, axes, 0, 0, tiled=True).reshape(-1, value.shape[1])


def after(value, *others):
    return lax.optimization_barrier((value,) + others)[0]


def neighbours_x(block):
    return [x_swap(block, which) for which in ("even", "odd", "across")]


def in_order_x(block, even, odd, across):
    x = lax.axis_index("x")
    whole = jnp.zeros((4,) + block.shape, block.dtype)
    for value, at in ((block, x), (even, x ^ 1), (odd, 3 - x), (across, (x + 2) % 4)):
        whole = lax.dynamic_update_slice_in_dim(whole, value[None], at, 0)
    return whole.reshape(-1, block.shape[1])


def attend_kernel(place_ref, length_ref, temp_ref, frames, own_w, other_w, *refs):
    tails, (out_ref, x_buf, w_buf, qkv, sems) = refs[:6], refs[6:]
    core, place = place_ref[0], place_ref[1]
    base, within = place // 3 * 3, lax.rem(place, 3)
    below, above = lax.rem(within + 2, 3), lax.rem(within + 1, 3)
    slots = (
        place,
        base + below,
        base + above,
        3 - base + within,
        3 - base + below,
        3 - base + above,
    )
    tail = tails[0].shape[0]
    head = frames.shape[0] // 6
    copies = []
    for number in range(4):
        rows = pl.ds(number * 384, 384)
        for source, half in ((own_w, core), (other_w, 1 - core)):
            columns = pl.ds(pl.multiple_of(half * 384, 128), 384)
            copies.append((source.at[rows], w_buf.at[rows, columns]))
    for number, slot in enumerate(slots):
        rows = pl.ds(number * (head + tail), head)
        copies.append((frames.at[pl.ds(number * head, head)], x_buf.at[rows]))
        rows = pl.ds(pl.multiple_of(slot * (head + tail) + head, tail), tail)
        copies.append((tails[number], x_buf.at[rows]))
    copies = [
        pltpu.make_async_copy(source, goal, sems.at[number])
        for number, (source, goal) in enumerate(copies)
    ]
    for copy in copies:
        copy.start()
    for copy in copies:
        copy.wait()
    qkv[...] = jnp.dot(
        x_buf[...], w_buf[...], preferred_element_type=jnp.float32
    ).astype(jnp.bfloat16)

    total = x_buf.shape[0]
    live = lax.broadcasted_iota(jnp.int32, (total, 1), 0) < length_ref[0]
    lane = lax.broadcasted_iota(jnp.int32, (total, 128), 1)
    place = lax.broadcasted_iota(jnp.int32, (1, 2 * total), 1)
    for two in range(2):
        query, key_part, value = (
            qkv[:, two * 384 + k * 128 : two * 384 + k * 128 + 128] for k in range(3)
        )
        none = jnp.zeros_like(query)
        query = jnp.concatenate(
            [jnp.where(lane < HD, query, none), jnp.where(lane < HD, none, query)]
        )
        scores = lax.dot_general(
            key_part, query, (((1,), (1,)), ((), ())), preferred_element_type=jnp.float32
        )
        scale = jnp.where(place < total, temp_ref[2 * two] / 8.0, temp_ref[2 * two + 1] / 8.0)
        scores = jnp.where(live, scores * scale, -1e30)
        scores = jnp.exp(scores - jnp.max(scores, axis=0, keepdims=True))
        mixed = lax.dot_general(
            value,
            scores.astype(jnp.bfloat16),
            (((0,), (0,)), ((), ())),
            preferred_element_type=jnp.float32,
        )
        mixed = mixed / jnp.sum(scores, axis=0, keepdims=True)
        mixed = jnp.concatenate([mixed[:HD, :total], mixed[HD:, total:]]).T
        out_ref[:, :, two * 128 : two * 128 + 128] = mixed.astype(jnp.bfloat16).reshape(
            out_ref.shape[0], out_ref.shape[1], 128
        )


SMEM = pl.BlockSpec(memory_space=pltpu.SMEM)
VMEM = pl.BlockSpec(memory_space=pltpu.VMEM)
ANYWHERE = pl.BlockSpec(memory_space=pl.ANY)


def attend(place, length, temp, frames, own_w, other_w, tails):
    rows, width = frames.shape
    rows += 6 * tails[0].shape[0]
    return pl.pallas_call(
        attend_kernel,
        out_shape=jax.ShapeDtypeStruct((6, rows // 6, 256), jnp.bfloat16),
        in_specs=[SMEM] * 3 + [ANYWHERE] * 9,
        out_specs=VMEM,
        scratch_shapes=[
            pltpu.VMEM((rows, width), jnp.bfloat16),
            pltpu.VMEM((width, 768), jnp.bfloat16),
            pltpu.VMEM((rows, 768), jnp.bfloat16),
            pltpu.SemaphoreType.DMA((20,)),
        ],
        compiler_params=pltpu.CompilerParams(vmem_limit_bytes=58 * 2**20),
        cost_estimate=pl.CostEstimate(
            flops=3 * 10**9, bytes_accessed=5 * 10**6, transcendentals=2 * 10**6
        ),
    )(place, length, temp, frames, own_w, other_w, *tails)


def turned_half(heads_ref, which):
    first = jnp.concatenate([heads_ref[at, :, :128] for at in range(6)], axis=1)
    second = jnp.concatenate([heads_ref[at, :, 128:] for at in range(6)], axis=1)
    return jnp.where(which == 0, first, second).T


def project_half_kernel(place_ref, heads_ref, own_any, out_ref, own_ref, sems):
    parts = [pl.ds(number * 384, 384) for number in range(4)]
    copies = [
        pltpu.make_async_copy(own_any.at[rows], own_ref.at[rows], sems.at[number])
        for number, rows in enumerate(parts)
    ]
    for copy in copies:
        copy.start()
    mine = turned_half(heads_ref, place_ref[0])
    for copy, rows in zip(copies, parts):
        copy.wait()
        out_ref[rows] = jnp.dot(own_ref[rows], mine, preferred_element_type=jnp.float32)


def project_kernel(place_ref, heads_ref, *refs):
    others, (sums_ref, out_ref, total) = refs[:4], refs[4:]
    given = turned_half(heads_ref, 1 - place_ref[0])
    for number, other in enumerate(others):
        rows = pl.ds(number * 384, 384)
        total[rows] = sums_ref[rows] + jnp.dot(
            other[...], given, preferred_element_type=jnp.float32
        )
    for x in range(4):
        pieces = []
        for zh in range(2):
            for y in range(8):
                at = ((y * 4 + x) * 2 + zh) * 24
                pieces.append(total[at : at + 24, :])
        block = jnp.concatenate(pieces).T
        out_ref[:, x * 384 : x * 384 + 384] = block.astype(jnp.bfloat16)


def project_half(place, heads, own):
    return pl.pallas_call(
        project_half_kernel,
        out_shape=jax.ShapeDtypeStruct((own.shape[0], heads.shape[1]), jnp.float32),
        in_specs=[SMEM, VMEM, ANYWHERE],
        out_specs=VMEM,
        scratch_shapes=[pltpu.VMEM(own.shape, jnp.bfloat16), pltpu.SemaphoreType.DMA((4,))],
        compiler_params=pltpu.CompilerParams(vmem_limit_bytes=16 * 2**20),
        cost_estimate=pl.CostEstimate(
            flops=3 * 10**8, bytes_accessed=3 * 10**6, transcendentals=0
        ),
    )(place, heads, own)


def project(place, heads, others, sums):
    return pl.pallas_call(
        project_kernel,
        out_shape=jax.ShapeDtypeStruct((heads.shape[1], 1536), jnp.bfloat16),
        in_specs=[SMEM] + [VMEM] * 6,
        out_specs=VMEM,
        scratch_shapes=[pltpu.VMEM(sums.shape, jnp.float32)],
        compiler_params=pltpu.CompilerParams(vmem_limit_bytes=16 * 2**20),
        cost_estimate=pl.CostEstimate(
            flops=3 * 10**8, bytes_accessed=4 * 10**6, transcendentals=0
        ),
    )(place, heads, *others, sums)


def on_device(latents, norm_gain, w_qkv, w_out, head_temp, lengths):
    frames = latents[0]
    values = frames.astype(jnp.float32)
    rms = jnp.sqrt(jnp.mean(values * values, axis=-1, keepdims=True) + 1e-06)
    normed = (values / rms * norm_gain).astype(jnp.bfloat16)
    head = 3 * normed.shape[0] // 4
    whole = lax.all_gather(normed[:head], "zl", axis=0, tiled=True)
    tail = normed[head:]
    far = other_triple(tail)
    near = [triple_shift(tail, 1), triple_shift(tail, 2)]

    rows = w_qkv.reshape(3, 12, 2, 128).transpose(2, 1, 0, 3).reshape(2, 12, 384)
    columns = w_out.T.reshape(12, 2, 128).transpose(1, 0, 2)
    both = jnp.concatenate([rows, columns], axis=2).reshape(1, 2, 48, 128)
    both = jnp.broadcast_to(both, (12, 2, 48, 128)).reshape(24, 48, 128)
    both = lax.all_to_all(both, ("zh", "zl", "c"), 0, 0, tiled=True)
    both, far, near = lax.optimization_barrier((both, far, near))
    both = both.reshape(2, 6, 2, 12, 512)
    rows = lax.dynamic_index_in_dim(both[..., :384], lax.axis_index("zl"), 1, keepdims=False)
    rows = rows.reshape(48, 384)
    by_y = gather(rows, "y", 8)
    columns = both[..., 384:].transpose(0, 2, 3, 1, 4).reshape(48, 768)
    by_y, others = lax.optimization_barrier((by_y, neighbours_x(columns)))
    by_y = by_y.reshape(8, 2, 24, 384).transpose(1, 0, 2, 3).reshape(384, 384)
    out_by_x = in_order_x(columns, *others)
    own_w = gather(by_y, "x", 4)
    beyond = [triple_shift(far, 1), triple_shift(far, 2)]
    own_w, beyond = lax.optimization_barrier((own_w, beyond))
    other_w = other_core(own_w)
    out_own = lax.all_gather(out_by_x, "y", axis=0, tiled=True)

    place = jnp.stack([lax.axis_index("c"), lax.axis_index("zl")]).astype(jnp.int32)
    tails = [tail] + near + [far] + beyond
    blocks = attend(place, lengths, head_temp, whole, own_w, other_w, tails)
    own = lax.all_to_all(blocks, "zl", 0, 0, tiled=True)
    out_own, one_head = lax.optimization_barrier((out_own, blocks[0, :1, 0].astype(jnp.float32)))
    place += (one_head * 0.0).astype(jnp.int32)
    out_others = [other_core(out_own[at : at + 384]) for at in range(0, 1536, 384)]
    sums = project_half(place, own, out_own)
    return project(place, own, out_others, sums)[None]


def solution(mesh):
    split = Mesh(mesh.devices.reshape(SIZES), AXES)
    clip = ("x", "zh", "y", "c")
    in_specs = (
        P(clip, "zl", None),
        P(),
        P(None, clip, "zl"),
        P("zl", clip),
        P("zl"),
        P(clip),
    )
    out_specs = P(clip, "zl", None)
    return jax.shard_map(
        on_device, mesh=split, in_specs=in_specs, out_specs=out_specs, check_vma=False
    )
```

time: 154 us -> 155 us (level)
  starting transfers between devices: 49.6 us -> 90.5 us
  blocking collectives: 24.7 us -> 0 us
  waiting for transfers between devices: 39.7 us -> 19.8 us
  local copies, waits for them, and re-layouts: 7.87 us -> 10.3 us
    ppermute x5 -> x13, starting transfers between devices: 21.7 us -> 51.1 us  [permute(): return lax.ppermute(value, AXES, pairs)]
    all_to_all x1 -> x0, blocking collectives: 24.7 us -> none  [on_device(): own = lax.all_to_all(blocks, 'zl', 0, 0, tiled=True)]
    all_to_all x1 -> x2, waiting for transfers between devices: 16.3 us -> 0.01 us  [the longest x1 0.01 us: on_device(): own = lax.all_to_all(blocks, 'zl', 0, 0, tiled=True)]
    all_to_all x1 -> x2, starting transfers between devices: 16.7 us -> 29 us  [the longest x1 16.7 us: on_device(): both = lax.all_to_all(both, ('zh', 'zl', 'c'), 0, 0, tiled=True)]
    all_to_all x2, waiting for transfers between devices: 10.2 us -> 0.01 us  [gather(): lax.all_to_all(copies, axes, 0, 0, tiled=True).reshape(-1, value.shape[1])]
    ppermute x5 -> x13, waiting for transfers between devices: 12.5 us -> 19.4 us  [permute(): return lax.ppermute(value, AXES, pairs)]
    slice x0 -> x4, local copies, waits for them, and re-layouts: none -> 5.2 us  [the longest x1 3.2 us: on_device(): out_own[at:at + 384]]
    unnamed x9 -> x25, local copies, waits for them, and re-layouts: 3.17 us -> 1.8 us
  transfers between devices with their start and end apart: 10 -> 19, of which waited for: 7 -> 9; matrix products, arithmetic and copies ran while one was open for 3% -> 5% of each run, Pallas kernels for 6% -> 8%
where the time goes in v9:
time: 155 us; the launch traced here: 154 us
  starting transfers between devices  90.5 us (58%)
  waiting for transfers between devices  19.8 us (13%)
  between operations  15.2 us (10%)
  Pallas kernels  15.1 us (10%)
  local copies, waits for them, and re-layouts  10.3 us (7%)
  other arithmetic  3.07 us (2%)
    ppermute x13, starting transfers between devices, permute(): return lax.ppermute(value, AXES, pairs)  51.1 us
    ppermute x13, waiting for transfers between devices, permute(): return lax.ppermute(value, AXES, pairs)  19.4 us
    all_to_all x1, starting transfers between devices, on_device(): both = lax.all_to_all(both, ('zh', 'zl', 'c'), 0, 0, tiled=True)  16.7 us
    all_to_all x1, starting transfers between devices, on_device(): own = lax.all_to_all(blocks, 'zl', 0, 0, tiled=True)  12.3 us
    all_to_all x2, starting transfers between devices, gather(): lax.all_to_all(copies, axes, 0, 0, tiled=True).reshape(-1, value.shape[1])  10.4 us
    pallas_call x1, Pallas kernels, attend(): pl.pallas_call(attend_kernel, out_shape=jax.ShapeDtypeStruct((6, rows //...  9.15 us
    slice x1, local copies, waits for them, and re-layouts, on_device(): out_own[at:at + 384]  3.2 us
  transfers between devices with their start and end apart: 19, of which 9 were waited for; matrix products, arithmetic and copies ran while one was open for 5% of the time, Pallas kernels for 8%

profile of v9, /device:TPU:1, one launch (start us, length us, event | category | flops | bytes accessed | tf_op | source)
XLA Modules:
  0.0 153.9 jit_solution(14942663548222405362)
XLA Ops:
  10.6 16.7 %all-to-all-start = ((bf16[24,48,128]{2,1,0:T(8,128)(2,1)}), bf16[24,48,128]{2,1,0:T(8,128)(2,1)S(1)}, u32[]{:S(2)}, u32[]{:S(2)}) async-start(bf16[24,48,128]{2,1,0:T(8,128)(2,1)} %bitcast.5), calls=%async_computation | async-start | bytes 589824 | tf_op jit(solution)/shard_map/all_to_all | solution.py:243
  27.3 5.1 %collective-permute-start = (bf16[32,1536]{1,0:T(8,128)(2,1)S(1)}, bf16[32,1536]{1,0:T(8,128)(2,1)S(1)}, u32[]{:S(2)}, u32[]{:S(2)}) collective-permute-start(bf16[32,1536]{1,0:T(8,128)(2,1)S(1)} %slice.36.refs_0_), channel_id=1, source_target_pairs={{0,3},{1,4},{2,5},{3,0},{4,1},{5,2},{6,9},{7,10},{8,11},{9,6},{10,... | collective-permute-start | bytes 294920 | tf_op jit(solution)/shard_map/ppermute | solution.py:24
  32.4 4.3 %collective-permute-start.1 = (bf16[32,1536]{1,0:T(8,128)(2,1)S(1)}, bf16[32,1536]{1,0:T(8,128)(2,1)S(1)}, u32[]{:S(2)}, u32[]{:S(2)}) collective-permute-start(bf16[32,1536]{1,0:T(8,128)(2,1)S(1)} %slice.36.refs_0_), channel_id=1, source_target_pairs={{0,1},{1,2},{2,0},{3,4},{4,5},{5,3},{6,7},{7,8},{8,6},{9,10},{10,1... | collective-permute-start | bytes 294920 | tf_op jit(solution)/shard_map/ppermute | solution.py:24
  36.7 2.8 %collective-permute-start.2 = (bf16[32,1536]{1,0:T(8,128)(2,1)S(1)}, bf16[32,1536]{1,0:T(8,128)(2,1)S(1)}, u32[]{:S(2)}, u32[]{:S(2)}) collective-permute-start(bf16[32,1536]{1,0:T(8,128)(2,1)S(1)} %slice.36.refs_0_), channel_id=1, source_target_pairs={{0,2},{1,0},{2,1},{3,5},{4,3},{5,4},{6,8},{7,6},{8,7},{9,11},{10,9... | collective-permute-start | bytes 294920 | tf_op jit(solution)/shard_map/ppermute | solution.py:24
  39.6 6.1 %collective-permute-done.refs_3_ = bf16[32,1536]{1,0:T(8,128)(2,1)S(1)} collective-permute-done((bf16[32,1536]{1,0:T(8,128)(2,1)S(1)}, bf16[32,1536]{1,0:T(8,128)(2,1)S(1)}, u32[]{:S(2)}, u32[]{:S(2)}) %collective-permute-start) | collective-permute-done | bytes 98336 | tf_op jit(solution)/shard_map/ppermute | solution.py:24
  45.6 3.3 %collective-permute-done.1.refs_1_ = bf16[32,1536]{1,0:T(8,128)(2,1)S(1)} collective-permute-done((bf16[32,1536]{1,0:T(8,128)(2,1)S(1)}, bf16[32,1536]{1,0:T(8,128)(2,1)S(1)}, u32[]{:S(2)}, u32[]{:S(2)}) %collective-permute-start.1) | collective-permute-done | bytes 98336 | tf_op jit(solution)/shard_map/ppermute | solution.py:24
  51.2 6.8 %all-to-all-start.1 = ((bf16[8,48,384]{2,1,0:T(8,128)(2,1)}), bf16[8,48,384]{2,1,0:T(8,128)(2,1)S(1)}, u32[]{:S(2)}, u32[]{:S(2)}) async-start(bf16[8,48,384]{2,1,0:T(8,128)(2,1)} %broadcast_in_dim.42), calls=%async_computation.1 | async-start | bytes 589824 | tf_op jit(solution)/shard_map/all_to_all | solution.py:48
  58.2 3.1 %collective-permute-start.3 = (bf16[48,768]{1,0:T(8,128)(2,1)S(1)}, bf16[48,768]{1,0:T(8,128)(2,1)S(1)}, u32[]{:S(2)}, u32[]{:S(2)}) collective-permute-start(bf16[48,768]{1,0:T(8,128)(2,1)S(1)} %bitcast.45), channel_id=1, source_target_pairs={{0,192},{1,193},{2,194},{3,195},{4,196},{5,197},{6,198},{7,199},{8... | collective-permute-start | bytes 221192 | tf_op jit(solution)/shard_map/ppermute | solution.py:24
  61.3 3.7 %collective-permute-start.4 = (bf16[48,768]{1,0:T(8,128)(2,1)S(1)}, bf16[48,768]{1,0:T(8,128)(2,1)S(1)}, u32[]{:S(2)}, u32[]{:S(2)}) collective-permute-start(bf16[48,768]{1,0:T(8,128)(2,1)S(1)} %bitcast.46), channel_id=1, source_target_pairs={{0,576},{1,577},{2,578},{3,579},{4,580},{5,581},{6,582},{7,583},{8... | collective-permute-start | bytes 221192 | tf_op jit(solution)/shard_map/ppermute | solution.py:24
  65.1 2.6 %collective-permute-start.5 = (bf16[48,768]{1,0:T(8,128)(2,1)S(1)}, bf16[48,768]{1,0:T(8,128)(2,1)S(1)}, u32[]{:S(2)}, u32[]{:S(2)}) collective-permute-start(bf16[48,768]{1,0:T(8,128)(2,1)S(1)} %bitcast.47), channel_id=1, source_target_pairs={{0,384},{1,385},{2,386},{3,387},{4,388},{5,389},{6,390},{7,391},{8... | collective-permute-start | bytes 221192 | tf_op jit(solution)/shard_map/ppermute | solution.py:24
  68.0 4.0 %collective-permute-done.5 = bf16[48,768]{1,0:T(8,128)(2,1)S(1)} collective-permute-done((bf16[48,768]{1,0:T(8,128)(2,1)S(1)}, bf16[48,768]{1,0:T(8,128)(2,1)S(1)}, u32[]{:S(2)}, u32[]{:S(2)}) %collective-permute-start.5) | collective-permute-done | bytes 73760 | tf_op jit(solution)/shard_map/ppermute | solution.py:24
  74.1 3.5 %all-to-all-start.2 = ((bf16[4,384,384]{2,1,0:T(8,128)(2,1)}), bf16[4,384,384]{2,1,0:T(8,128)(2,1)S(1)}, u32[]{:S(2)}, u32[]{:S(2)}) async-start(bf16[4,384,384]{2,1,0:T(8,128)(2,1)} %broadcast_in_dim.47), calls=%async_computation.2 | async-start | bytes 2359296 | tf_op jit(solution)/shard_map/all_to_all | solution.py:48
  77.6 8.0 %collective-permute-start.6 = (bf16[32,1536]{1,0:T(8,128)(2,1)S(1)}, bf16[32,1536]{1,0:T(8,128)(2,1)S(1)}, u32[]{:S(2)}, u32[]{:S(2)}) collective-permute-start(bf16[32,1536]{1,0:T(8,128)(2,1)S(1)} %collective-permute-done.refs_3_), channel_id=1, source_target_pairs={{0,1},{1,2},{2,0},{3,4},{4,5},{5,3},{6,7},{7,8},{8,6},{9,10},{10,1... | collective-permute-start | bytes 294920 | tf_op jit(solution)/shard_map/ppermute | solution.py:24
  85.7 4.4 %collective-permute-start.7 = (bf16[32,1536]{1,0:T(8,128)(2,1)S(1)}, bf16[32,1536]{1,0:T(8,128)(2,1)S(1)}, u32[]{:S(2)}, u32[]{:S(2)}) collective-permute-start(bf16[32,1536]{1,0:T(8,128)(2,1)S(1)} %collective-permute-done.refs_3_), channel_id=1, source_target_pairs={{0,2},{1,0},{2,1},{3,5},{4,3},{5,4},{6,8},{7,6},{8,7},{9,11},{10,9... | collective-permute-start | bytes 294920 | tf_op jit(solution)/shard_map/ppermute | solution.py:24
  90.5 3.0 %collective-permute-done.7.refs_5_ = bf16[32,1536]{1,0:T(8,128)(2,1)S(1)} collective-permute-done((bf16[32,1536]{1,0:T(8,128)(2,1)S(1)}, bf16[32,1536]{1,0:T(8,128)(2,1)S(1)}, u32[]{:S(2)}, u32[]{:S(2)}) %collective-permute-start.7) | collective-permute-done | bytes 98336 | tf_op jit(solution)/shard_map/ppermute | solution.py:24
  93.4 4.7 %collective-permute-start.8 = (bf16[1536,384]{1,0:T(8,128)(2,1)S(1)}, bf16[1536,384]{1,0:T(8,128)(2,1)S(1)}, u32[]{:S(2)}, u32[]{:S(2)}) collective-permute-start(bf16[1536,384]{1,0:T(8,128)(2,1)S(1)} %bitcast.38), channel_id=1, source_target_pairs={{0,6},{1,7},{2,8},{3,9},{4,10},{5,11},{6,0},{7,1},{8,2},{9,3},{10,... | collective-permute-start | bytes 3538952 | tf_op jit(solution)/shard_map/ppermute | solution.py:24
  101.7 9.2 %shard_map.64 = bf16[6,128,256]{2,1,0:T(8,128)(2,1)} custom-call(s32[2]{0:T(128)} %pad_add_fusion.place_ref, s32[1]{0:T(128)S(6)} %copy.26.length_ref, f32[4]{0:T(128)} %temp_ref.1, bf16[576,1536]{1,0:T(8,128)(2,1)} %all-gather.5.cloned.1.call-done.frames, bf16[1536,384]{1,0:T(8,128)(2,1)} %bitcast.39, bf16[1536,384]{1,0:T(8,128)(2,1)} %copy-done.6, ...), custom_call_target="tpu_custom_call" | custom-call | flops 3000000000 | bytes 5000000 | tf_op jit(solution)/shard_map/pallas_call | solution.py:144
  110.8 12.3 %all-to-all-start.3 = ((bf16[6,128,256]{2,1,0:T(8,128)(2,1)}), bf16[6,128,256]{2,1,0:T(8,128)(2,1)S(1)}, u32[]{:S(2)}, u32[]{:S(2)}) async-start(bf16[6,128,256]{2,1,0:T(8,128)(2,1)} %shard_map.64), calls=%async_computation.3 | async-start | bytes 786432 | tf_op jit(solution)/shard_map/all_to_all | solution.py:262
  125.4 3.2 %fusion.3 = (bf16[384,768]{1,0:T(8,128)(2,1)}, bf16[384,768]{1,0:T(8,128)(2,1)}, bf16[384,768]{1,0:T(8,128)(2,1)}, bf16[384,768]{1,0:T(8,128)(2,1)}) fusion(bf16[1536,768]{1,0:T(8,128)(2,1)} %all-gather.3.cloned.1.call-done.own_any), kind=kLoop, calls=%fused_computation.17 | loop fusion | bytes 4718592 | tf_op jit(solution)/shard_map/slice | solution.py:265
  128.6 6.0 %collective-permute-start.10 = (bf16[384,768]{1,0:T(8,128)(2,1)}, bf16[384,768]{1,0:T(8,128)(2,1)S(1)}, u32[]{:S(2)}, u32[]{:S(2)}) collective-permute-start(bf16[384,768]{1,0:T(8,128)(2,1)} %get-tuple-element.33), channel_id=1, source_target_pairs={{0,6},{1,7},{2,8},{3,9},{4,10},{5,11},{6,0},{7,1},{8,2},{9,3},{10,... | collective-permute-start | bytes 1769480 | tf_op jit(solution)/shard_map/ppermute | solution.py:24
  134.7 1.9 %collective-permute-start.11 = (bf16[384,768]{1,0:T(8,128)(2,1)}, bf16[384,768]{1,0:T(8,128)(2,1)}, u32[]{:S(2)}, u32[]{:S(2)}) collective-permute-start(bf16[384,768]{1,0:T(8,128)(2,1)} %get-tuple-element.32), channel_id=1, source_target_pairs={{0,6},{1,7},{2,8},{3,9},{4,10},{5,11},{6,0},{7,1},{8,2},{9,3},{10,... | collective-permute-start | bytes 1769480 | tf_op jit(solution)/shard_map/ppermute | solution.py:24
  136.6 2.4 %collective-permute-start.12 = (bf16[384,768]{1,0:T(8,128)(2,1)}, bf16[384,768]{1,0:T(8,128)(2,1)}, u32[]{:S(2)}, u32[]{:S(2)}) collective-permute-start(bf16[384,768]{1,0:T(8,128)(2,1)} %get-tuple-element.31), channel_id=1, source_target_pairs={{0,6},{1,7},{2,8},{3,9},{4,10},{5,11},{6,0},{7,1},{8,2},{9,3},{10,... | collective-permute-start | bytes 1769480 | tf_op jit(solution)/shard_map/ppermute | solution.py:24
  141.1 2.9 %shard_map.65.refs_4_ = f32[1536,128]{1,0:T(8,128)S(1)} custom-call(s32[2]{0:T(128)S(1)} %broadcast_add_fusion.place_ref, bf16[6,128,256]{2,1,0:T(8,128)(2,1)S(1)} %all-to-all-done.3.heads_ref, bf16[1536,768]{1,0:T(8,128)(2,1)S(1)} %copy-done), custom_call_target="tpu_custom_call" | custom-call | flops 300000000 | bytes 3000000 | tf_op jit(solution)/shard_map/pallas_call | solution.py:201
  144.0 3.1 %shard_map.66 = bf16[128,1536]{1,0:T(8,128)(2,1)} custom-call(s32[2]{0:T(128)S(1)} %broadcast_add_fusion.place_ref, bf16[6,128,256]{2,1,0:T(8,128)(2,1)S(1)} %all-to-all-done.3.heads_ref, bf16[384,768]{1,0:T(8,128)(2,1)} %collective-permute-done.9.refs_0_, bf16[384,768]{1,0:T(8,128)(2,1)S(1)} %collective-permute-done.10.refs_1_, ...), custom_call_target="tpu_custom_call" | custom-call | flops 300000000 | bytes 4000000 | tf_op jit(solution)/shard_map/pallas_call | solution.py:215
  (76 shorter events, 15.6 us)
Async XLA Ops:
  6.5 92.9 %all-gather.5.cloned.1.call-start = ((), (), s32[]{:S(2)}) async-start(), calls=%async_computation.5 | async-start | bytes 2064384 | tf_op jit(solution)/shard_map/all_gather | solution.py:234
  10.6 39.6 %all-to-all-start = ((bf16[24,48,128]{2,1,0:T(8,128)(2,1)}), bf16[24,48,128]{2,1,0:T(8,128)(2,1)S(1)}, u32[]{:S(2)}, u32[]{:S(2)}) async-start(bf16[24,48,128]{2,1,0:T(8,128)(2,1)} %bitcast.5), calls=%async_computation | async-start | bytes 589824 | tf_op jit(solution)/shard_map/all_to_all | solution.py:243
  27.3 40.5 %copy-start.3 = (bf16[32,1536]{1,0:T(8,128)(2,1)}, bf16[32,1536]{1,0:T(8,128)(2,1)S(1)}, u32[]{:S(2)}) copy-start(bf16[32,1536]{1,0:T(8,128)(2,1)S(1)} %slice.36.refs_0_) | copy-start | bytes 294916
  27.3 18.3 %collective-permute-start = (bf16[32,1536]{1,0:T(8,128)(2,1)S(1)}, bf16[32,1536]{1,0:T(8,128)(2,1)S(1)}, u32[]{:S(2)}, u32[]{:S(2)}) collective-permute-start(bf16[32,1536]{1,0:T(8,128)(2,1)S(1)} %slice.36.refs_0_), channel_id=1, source_target_pairs={{0,3},{1,4},{2,5},{3,0},{4,1},{5,2},{6,9},{7,10},{8,11},{9,6},{10,... | collective-permute-start | bytes 294920 | tf_op jit(solution)/shard_map/ppermute | solution.py:24
  32.4 16.5 %collective-permute-start.1 = (bf16[32,1536]{1,0:T(8,128)(2,1)S(1)}, bf16[32,1536]{1,0:T(8,128)(2,1)S(1)}, u32[]{:S(2)}, u32[]{:S(2)}) collective-permute-start(bf16[32,1536]{1,0:T(8,128)(2,1)S(1)} %slice.36.refs_0_), channel_id=1, source_target_pairs={{0,1},{1,2},{2,0},{3,4},{4,5},{5,3},{6,7},{7,8},{8,6},{9,10},{10,1... | collective-permute-start | bytes 294920 | tf_op jit(solution)/shard_map/ppermute | solution.py:24
  36.7 13.5 %collective-permute-start.2 = (bf16[32,1536]{1,0:T(8,128)(2,1)S(1)}, bf16[32,1536]{1,0:T(8,128)(2,1)S(1)}, u32[]{:S(2)}, u32[]{:S(2)}) collective-permute-start(bf16[32,1536]{1,0:T(8,128)(2,1)S(1)} %slice.36.refs_0_), channel_id=1, source_target_pairs={{0,2},{1,0},{2,1},{3,5},{4,3},{5,4},{6,8},{7,6},{8,7},{9,11},{10,9... | collective-permute-start | bytes 294920 | tf_op jit(solution)/shard_map/ppermute | solution.py:24
  45.6 40.0 %copy-start.7 = (bf16[32,1536]{1,0:T(8,128)(2,1)}, bf16[32,1536]{1,0:T(8,128)(2,1)S(1)}, u32[]{:S(2)}) copy-start(bf16[32,1536]{1,0:T(8,128)(2,1)S(1)} %collective-permute-done.refs_3_) | copy-start | bytes 294916
  48.9 18.9 %copy-start.8 = (bf16[32,1536]{1,0:T(8,128)(2,1)}, bf16[32,1536]{1,0:T(8,128)(2,1)S(1)}, u32[]{:S(2)}) copy-start(bf16[32,1536]{1,0:T(8,128)(2,1)S(1)} %collective-permute-done.1.refs_1_) | copy-start | bytes 294916
  50.2 17.6 %copy-start.9 = (bf16[32,1536]{1,0:T(8,128)(2,1)}, bf16[32,1536]{1,0:T(8,128)(2,1)S(1)}, u32[]{:S(2)}) copy-start(bf16[32,1536]{1,0:T(8,128)(2,1)S(1)} %collective-permute-done.2.refs_2_) | copy-start | bytes 294916
  51.2 20.9 %all-to-all-start.1 = ((bf16[8,48,384]{2,1,0:T(8,128)(2,1)}), bf16[8,48,384]{2,1,0:T(8,128)(2,1)S(1)}, u32[]{:S(2)}, u32[]{:S(2)}) async-start(bf16[8,48,384]{2,1,0:T(8,128)(2,1)} %broadcast_in_dim.42), calls=%async_computation.1 | async-start | bytes 589824 | tf_op jit(solution)/shard_map/all_to_all | solution.py:48
  58.1 67.4 %all-gather.3.cloned.1.call-start = ((), (), s32[]{:S(2)}) async-start(), calls=%async_computation.4 | async-start | bytes 2654208 | tf_op jit(solution)/shard_map/all_gather | solution.py:257
  58.2 9.6 %collective-permute-start.3 = (bf16[48,768]{1,0:T(8,128)(2,1)S(1)}, bf16[48,768]{1,0:T(8,128)(2,1)S(1)}, u32[]{:S(2)}, u32[]{:S(2)}) collective-permute-start(bf16[48,768]{1,0:T(8,128)(2,1)S(1)} %bitcast.45), channel_id=1, source_target_pairs={{0,192},{1,193},{2,194},{3,195},{4,196},{5,197},{6,198},{7,199},{8... | collective-permute-start | bytes 221192 | tf_op jit(solution)/shard_map/ppermute | solution.py:24
  61.3 6.7 %collective-permute-start.4 = (bf16[48,768]{1,0:T(8,128)(2,1)S(1)}, bf16[48,768]{1,0:T(8,128)(2,1)S(1)}, u32[]{:S(2)}, u32[]{:S(2)}) collective-permute-start(bf16[48,768]{1,0:T(8,128)(2,1)S(1)} %bitcast.46), channel_id=1, source_target_pairs={{0,576},{1,577},{2,578},{3,579},{4,580},{5,581},{6,582},{7,583},{8... | collective-permute-start | bytes 221192 | tf_op jit(solution)/shard_map/ppermute | solution.py:24
  65.1 7.0 %collective-permute-start.5 = (bf16[48,768]{1,0:T(8,128)(2,1)S(1)}, bf16[48,768]{1,0:T(8,128)(2,1)S(1)}, u32[]{:S(2)}, u32[]{:S(2)}) collective-permute-start(bf16[48,768]{1,0:T(8,128)(2,1)S(1)} %bitcast.47), channel_id=1, source_target_pairs={{0,384},{1,385},{2,386},{3,387},{4,388},{5,389},{6,390},{7,391},{8... | collective-permute-start | bytes 221192 | tf_op jit(solution)/shard_map/ppermute | solution.py:24
  74.1 19.3 %all-to-all-start.2 = ((bf16[4,384,384]{2,1,0:T(8,128)(2,1)}), bf16[4,384,384]{2,1,0:T(8,128)(2,1)S(1)}, u32[]{:S(2)}, u32[]{:S(2)}) async-start(bf16[4,384,384]{2,1,0:T(8,128)(2,1)} %broadcast_in_dim.47), calls=%async_computation.2 | async-start | bytes 2359296 | tf_op jit(solution)/shard_map/all_to_all | solution.py:48
  77.6 12.8 %collective-permute-start.6 = (bf16[32,1536]{1,0:T(8,128)(2,1)S(1)}, bf16[32,1536]{1,0:T(8,128)(2,1)S(1)}, u32[]{:S(2)}, u32[]{:S(2)}) collective-permute-start(bf16[32,1536]{1,0:T(8,128)(2,1)S(1)} %collective-permute-done.refs_3_), channel_id=1, source_target_pairs={{0,1},{1,2},{2,0},{3,4},{4,5},{5,3},{6,7},{7,8},{8,6},{9,10},{10,1... | collective-permute-start | bytes 294920 | tf_op jit(solution)/shard_map/ppermute | solution.py:24
  85.7 7.8 %collective-permute-start.7 = (bf16[32,1536]{1,0:T(8,128)(2,1)S(1)}, bf16[32,1536]{1,0:T(8,128)(2,1)S(1)}, u32[]{:S(2)}, u32[]{:S(2)}) collective-permute-start(bf16[32,1536]{1,0:T(8,128)(2,1)S(1)} %collective-permute-done.refs_3_), channel_id=1, source_target_pairs={{0,2},{1,0},{2,1},{3,5},{4,3},{5,4},{6,8},{7,6},{8,7},{9,11},{10,9... | collective-permute-start | bytes 294920 | tf_op jit(solution)/shard_map/ppermute | solution.py:24
  93.4 7.2 %collective-permute-start.8 = (bf16[1536,384]{1,0:T(8,128)(2,1)S(1)}, bf16[1536,384]{1,0:T(8,128)(2,1)S(1)}, u32[]{:S(2)}, u32[]{:S(2)}) collective-permute-start(bf16[1536,384]{1,0:T(8,128)(2,1)S(1)} %bitcast.38), channel_id=1, source_target_pairs={{0,6},{1,7},{2,8},{3,9},{4,10},{5,11},{6,0},{7,1},{8,2},{9,3},{10,... | collective-permute-start | bytes 3538952 | tf_op jit(solution)/shard_map/ppermute | solution.py:24
  110.8 30.2 %all-to-all-start.3 = ((bf16[6,128,256]{2,1,0:T(8,128)(2,1)}), bf16[6,128,256]{2,1,0:T(8,128)(2,1)S(1)}, u32[]{:S(2)}, u32[]{:S(2)}) async-start(bf16[6,128,256]{2,1,0:T(8,128)(2,1)} %shard_map.64), calls=%async_computation.3 | async-start | bytes 786432 | tf_op jit(solution)/shard_map/all_to_all | solution.py:262
  125.4 15.6 %copy-start = (bf16[1536,768]{1,0:T(8,128)(2,1)S(1)}, bf16[1536,768]{1,0:T(8,128)(2,1)}, u32[]{:S(2)}) copy-start(bf16[1536,768]{1,0:T(8,128)(2,1)} %all-gather.3.cloned.1.call-done.own_any) | copy-start | bytes 7077892
  128.6 15.3 %collective-permute-start.10 = (bf16[384,768]{1,0:T(8,128)(2,1)}, bf16[384,768]{1,0:T(8,128)(2,1)S(1)}, u32[]{:S(2)}, u32[]{:S(2)}) collective-permute-start(bf16[384,768]{1,0:T(8,128)(2,1)} %get-tuple-element.33), channel_id=1, source_target_pairs={{0,6},{1,7},{2,8},{3,9},{4,10},{5,11},{6,0},{7,1},{8,2},{9,3},{10,... | collective-permute-start | bytes 1769480 | tf_op jit(solution)/shard_map/ppermute | solution.py:24
  134.7 9.3 %collective-permute-start.11 = (bf16[384,768]{1,0:T(8,128)(2,1)}, bf16[384,768]{1,0:T(8,128)(2,1)}, u32[]{:S(2)}, u32[]{:S(2)}) collective-permute-start(bf16[384,768]{1,0:T(8,128)(2,1)} %get-tuple-element.32), channel_id=1, source_target_pairs={{0,6},{1,7},{2,8},{3,9},{4,10},{5,11},{6,0},{7,1},{8,2},{9,3},{10,... | collective-permute-start | bytes 1769480 | tf_op jit(solution)/shard_map/ppermute | solution.py:24
  136.6 7.3 %collective-permute-start.12 = (bf16[384,768]{1,0:T(8,128)(2,1)}, bf16[384,768]{1,0:T(8,128)(2,1)}, u32[]{:S(2)}, u32[]{:S(2)}) collective-permute-start(bf16[384,768]{1,0:T(8,128)(2,1)} %get-tuple-element.31), channel_id=1, source_target_pairs={{0,6},{1,7},{2,8},{3,9},{4,10},{5,11},{6,0},{7,1},{8,2},{9,3},{10,... | collective-permute-start | bytes 1769480 | tf_op jit(solution)/shard_map/ppermute | solution.py:24
  139.0 4.9 %collective-permute-start.9 = (bf16[384,768]{1,0:T(8,128)(2,1)}, bf16[384,768]{1,0:T(8,128)(2,1)}, u32[]{:S(2)}, u32[]{:S(2)}) collective-permute-start(bf16[384,768]{1,0:T(8,128)(2,1)} %get-tuple-element.34), channel_id=1, source_target_pairs={{0,6},{1,7},{2,8},{3,9},{4,10},{5,11},{6,0},{7,1},{8,2},{9,3},{10,... | collective-permute-start | bytes 1769480 | tf_op jit(solution)/shard_map/ppermute | solution.py:24
  (7 other events, 32.7 us)
Sparse Core Ops, SparseCore 0:
  9.8 72.0 all-gather.4
  84.3 41.0 all-gather.2

commit v10 on v8

--- a/solution.py
+++ b/solution.py
@@ -128,69 +128,74 @@
             pltpu.VMEM((rows, 768), jnp.bfloat16),
             pltpu.SemaphoreType.DMA((14,)),
         ],
-        compiler_params=pltpu.CompilerParams(vmem_limit_bytes=58 * 2**20),
+        compiler_params=pltpu.CompilerParams(vmem_limit_bytes=50 * 2**20),
         cost_estimate=pl.CostEstimate(
             flops=3 * 10**9, bytes_accessed=5 * 10**6, transcendentals=2 * 10**6
         ),
     )(core, length, temp, frames, own_w, other_w)
 
 
-def project_kernel(core_ref, heads_any, own_any, other_any, out_ref, *scratch):
-    heads_ref, own_ref, other_ref, sums, sems = scratch
-    core = core_ref[0]
-    copies = [(heads_any, heads_ref)]
-    for source, goal in ((own_any, own_ref), (other_any, other_ref)):
-        for number in range(4):
-            rows = pl.ds(number * 384, 384)
-            copies.append((source.at[rows], goal.at[rows]))
+def turned_half(heads_ref, which):
+    first = jnp.concatenate([heads_ref[at, :, :128] for at in range(6)], axis=1)
+    second = jnp.concatenate([heads_ref[at, :, 128:] for at in range(6)], axis=1)
+    return jnp.where(which == 0, first, second).T
+
+
+def project_half_kernel(place_ref, heads_ref, own_any, out_ref, own_ref, sems):
+    parts = [pl.ds(number * 384, 384) for number in range(4)]
     copies = [
-        pltpu.make_async_copy(source, goal, sems.at[number])
-        for number, (source, goal) in enumerate(copies)
+        pltpu.make_async_copy(own_any.at[rows], own_ref.at[rows], sems.at[number])
+        for number, rows in enumerate(parts)
     ]
     for copy in copies:
         copy.start()
-    copies[0].wait()
-    first = jnp.concatenate([heads_ref[at, :, :128] for at in range(6)], axis=1)
-    second = jnp.concatenate([heads_ref[at, :, 128:] for at in range(6)], axis=1)
-    mine = jnp.where(core == 0, first, second).T
-    given = jnp.where(core == 0, second, first).T
-    for number in range(4):
-        rows = pl.ds(number * 384, 384)
-        copies[1 + number].wait()
-        sums[rows] = jnp.dot(own_ref[rows], mine, preferred_element_type=jnp.float32)
-    for number in range(4):
-        rows = pl.ds(number * 384, 384)
-        copies[5 + number].wait()
-        sums[rows] += jnp.dot(other_ref[rows], given, preferred_element_type=jnp.float32)
+    mine = turned_half(heads_ref, place_ref[0])
+    for copy, rows in zip(copies, parts):
+        copy.wait()
+        out_ref[rows] = jnp.dot(own_ref[rows], mine, preferred_element_type=jnp.float32)
+
+
+def project_kernel(place_ref, heads_ref, other_ref, sums_ref, out_ref, total):
+    given = turned_half(heads_ref, 1 - place_ref[0])
+    total[...] = sums_ref[...] + jnp.dot(
+        other_ref[...], given, preferred_element_type=jnp.float32
+    )
     for x in range(4):
         pieces = []
         for zh in range(2):
             for y in range(8):
                 at = ((y * 4 + x) * 2 + zh) * 24
-                pieces.append(sums[at : at + 24, :])
+                pieces.append(total[at : at + 24, :])
         block = jnp.concatenate(pieces).T
         out_ref[:, x * 384 : x * 384 + 384] = block.astype(jnp.bfloat16)
 
 
-def project(core, heads, own, other):
-    rows = heads.shape[1]
+def project_half(place, heads, own):
+    return pl.pallas_call(
+        project_half_kernel,
+        out_shape=jax.ShapeDtypeStruct((own.shape[0], heads.shape[1]), jnp.float32),
+        in_specs=[SMEM, VMEM, ANYWHERE],
+        out_specs=VMEM,
+        scratch_shapes=[pltpu.VMEM(own.shape, jnp.bfloat16), pltpu.SemaphoreType.DMA((4,))],
+        compiler_params=pltpu.CompilerParams(vmem_limit_bytes=16 * 2**20),
+        cost_estimate=pl.CostEstimate(
+            flops=3 * 10**8, bytes_accessed=3 * 10**6, transcendentals=0
+        ),
+    )(place, heads, own)
+
+
+def project(place, heads, other, sums):
     return pl.pallas_call(
         project_kernel,
-        out_shape=jax.ShapeDtypeStruct((rows, 1536), jnp.bfloat16),
-        in_specs=[SMEM] + [ANYWHERE] * 3,
+        out_shape=jax.ShapeDtypeStruct((heads.shape[1], 1536), jnp.bfloat16),
+        in_specs=[SMEM] + [VMEM] * 3,
         out_specs=VMEM,
-        scratch_shapes=[
-            pltpu.VMEM(heads.shape, jnp.bfloat16),
-            pltpu.VMEM(own.shape, jnp.bfloat16),
-            pltpu.VMEM(own.shape, jnp.bfloat16),
-            pltpu.VMEM((1536, rows), jnp.float32),
-            pltpu.SemaphoreType.DMA((9,)),
-        ],
-        compiler_params=pltpu.CompilerParams(vmem_limit_bytes=58 * 2**20),
+        scratch_shapes=[pltpu.VMEM(sums.shape, jnp.float32)],
+        compiler_params=pltpu.CompilerParams(vmem_limit_bytes=16 * 2**20),
         cost_estimate=pl.CostEstimate(
-            flops=6 * 10**8, bytes_accessed=5 * 10**6, transcendentals=0
+            flops=3 * 10**8, bytes_accessed=4 * 10**6, transcendentals=0
         ),
-    )(core, heads, own, other)
+    )(place, heads, other, sums)
 
 
 def on_device(latents, norm_gain, w_qkv, w_out, head_temp, lengths):
@@ -220,7 +225,8 @@
     own = lax.all_to_all(blocks, "zl", 0, 0, tiled=True)
     own, out_own = lax.optimization_barrier((own, out_own))
     out_other = other_core(out_own)
-    return project(core, own, out_own, out_other)[None]
+    sums = project_half(core, own, out_own)
+    return project(core, own, out_other, sums)[None]
 
 
 def solution(mesh):

time: 154 us -> 149 us (0.968)
  Pallas kernels: 14.3 us -> 11.7 us
    ppermute x5, waiting for transfers between devices: 12.5 us -> 8.39 us  [permute(): return lax.ppermute(value, AXES, pairs)]
    all_gather x1, waiting for transfers between devices: 0.65 us -> 3.23 us  [on_device(): out_own = lax.all_gather(out_by_x, 'y', axis=0, tiled=True)]
    pallas_call x1 -> x2, Pallas kernels: 5.26 us -> 3.97 us  [the longest x1 2.33 us: project_half(): pl.pallas_call(project_half_kernel, out_shape=jax.ShapeDtypeStruct((own.s...]
    unnamed x9 -> x7, local copies, waits for them, and re-layouts: 3.17 us -> 2.38 us
  transfers between devices with their start and end apart: 10 -> 10, of which waited for: 7 -> 7; matrix products, arithmetic and copies ran while one was open for 3% -> 3% of each run, Pallas kernels for 6% -> 7%
where the time goes in v10:
time: 149 us
  starting transfers between devices  49.8 us (33%)
  waiting for transfers between devices  38.2 us (26%)
  blocking collectives  24.4 us (16%)
  between operations  14.3 us (10%)
  Pallas kernels  11.7 us (8%)
  local copies, waits for them, and re-layouts  7.05 us (5%)
  other arithmetic  3.11 us (2%)
    all_to_all x1, blocking collectives, on_device(): own = lax.all_to_all(blocks, 'zl', 0, 0, tiled=True)  24.4 us
    ppermute x5, starting transfers between devices, permute(): return lax.ppermute(value, AXES, pairs)  21.8 us
    all_to_all x1, starting transfers between devices, on_device(): lax.all_to_all(after(both, normed), ('zh', 'zl', 'c'), 0, 0, tiled=True)  16.7 us
    all_to_all x1, waiting for transfers between devices, on_device(): lax.all_to_all(after(both, normed), ('zh', 'zl', 'c'), 0, 0, tiled=True)  16.3 us
    all_to_all x2, starting transfers between devices, gather(): lax.all_to_all(copies, axes, 0, 0, tiled=True).reshape(-1, value.shape[1])  11.4 us
    all_to_all x2, waiting for transfers between devices, gather(): lax.all_to_all(copies, axes, 0, 0, tiled=True).reshape(-1, value.shape[1])  10.2 us
    ppermute x5, waiting for transfers between devices, permute(): return lax.ppermute(value, AXES, pairs)  8.39 us
    pallas_call x1, Pallas kernels, attend(): pl.pallas_call(attend_kernel, out_shape=jax.ShapeDtypeStruct((6, rows //...  7.75 us
  transfers between devices with their start and end apart: 10, of which 7 were waited for; matrix products, arithmetic and copies ran while one was open for 3% of the time, Pallas kernels for 7%

profile of v10, /device:TPU:1, one launch (start us, length us, event | category | flops | bytes accessed | tf_op | source)
XLA Modules:
  0.0 148.5 jit_solution(7087020603087579125)
XLA Ops:
  6.5 1.2 fusion
  7.7 1.9 %fusion.2 = bf16[128,1536]{1,0:T(8,128)(2,1)} fusion(bf16[1,128,1536]{2,1,0:T(8,128)(2,1)} %param.6, f32[1536]{0:T(1024)} %param.7, f32[128]{0:T(128)S(1)} %add_sqrt_fusion), kind=kLoop, calls=%fused_computation.4 | loop fusion | flops 786432 | bytes 793088 | tf_op jit(solution)/shard_map/convert_element_type | solution.py:205
  10.4 0.8 reshape.44
  11.2 0.7 broadcast_in_dim.40
  12.0 16.7 %all-to-all-start = ((bf16[24,48,128]{2,1,0:T(8,128)(2,1)}), bf16[24,48,128]{2,1,0:T(8,128)(2,1)S(1)}, u32[]{:S(2)}, u32[]{:S(2)}) async-start(bf16[24,48,128]{2,1,0:T(8,128)(2,1)} %bitcast.6), calls=%async_computation | async-start | bytes 589824 | tf_op jit(solution)/shard_map/all_to_all | solution.py:212
  28.7 16.3 %all-to-all-done = bf16[24,48,128]{2,1,0:T(8,128)(2,1)S(1)} async-done(((bf16[24,48,128]{2,1,0:T(8,128)(2,1)}), bf16[24,48,128]{2,1,0:T(8,128)(2,1)S(1)}, u32[]{:S(2)}, u32[]{:S(2)}) %all-to-all-start) | async-done | bytes 294944 | tf_op jit(solution)/shard_map/all_to_all | solution.py:212
  46.0 7.2 %all-to-all-start.1 = ((bf16[8,48,384]{2,1,0:T(8,128)(2,1)}), bf16[8,48,384]{2,1,0:T(8,128)(2,1)S(1)}, u32[]{:S(2)}, u32[]{:S(2)}) async-start(bf16[8,48,384]{2,1,0:T(8,128)(2,1)} %broadcast_in_dim.45), calls=%async_computation.1 | async-start | bytes 589824 | tf_op jit(solution)/shard_map/all_to_all | solution.py:38
  53.2 10.2 %all-to-all-done.1 = bf16[8,48,384]{2,1,0:T(8,128)(2,1)S(1)} async-done(((bf16[8,48,384]{2,1,0:T(8,128)(2,1)}), bf16[8,48,384]{2,1,0:T(8,128)(2,1)S(1)}, u32[]{:S(2)}, u32[]{:S(2)}) %all-to-all-start.1) | async-done | bytes 294944 | tf_op jit(solution)/shard_map/all_to_all | solution.py:38
  63.5 1.1 broadcast_in_dim.47
  64.7 4.1 %all-to-all-start.2 = ((bf16[4,384,384]{2,1,0:T(8,128)(2,1)}), bf16[4,384,384]{2,1,0:T(8,128)(2,1)S(1)}, u32[]{:S(2)}, u32[]{:S(2)}) async-start(bf16[4,384,384]{2,1,0:T(8,128)(2,1)} %broadcast_in_dim.47), calls=%async_computation.2 | async-start | bytes 2359296 | tf_op jit(solution)/shard_map/all_to_all | solution.py:38
  69.0 3.4 %collective-permute-start = (bf16[48,768]{1,0:T(8,128)(2,1)S(1)}, bf16[48,768]{1,0:T(8,128)(2,1)S(1)}, u32[]{:S(2)}, u32[]{:S(2)}) collective-permute-start(bf16[48,768]{1,0:T(8,128)(2,1)S(1)} %bitcast.40), channel_id=1, source_target_pairs={{0,192},{1,193},{2,194},{3,195},{4,196},{5,197},{6,198},{7,199},{8... | collective-permute-start | bytes 221192 | tf_op jit(solution)/shard_map/ppermute | solution.py:24
  72.4 3.7 %collective-permute-start.1 = (bf16[48,768]{1,0:T(8,128)(2,1)S(1)}, bf16[48,768]{1,0:T(8,128)(2,1)S(1)}, u32[]{:S(2)}, u32[]{:S(2)}) collective-permute-start(bf16[48,768]{1,0:T(8,128)(2,1)S(1)} %bitcast.41), channel_id=1, source_target_pairs={{0,576},{1,577},{2,578},{3,579},{4,580},{5,581},{6,582},{7,583},{8... | collective-permute-start | bytes 221192 | tf_op jit(solution)/shard_map/ppermute | solution.py:24
  76.1 2.5 %collective-permute-start.2 = (bf16[48,768]{1,0:T(8,128)(2,1)S(1)}, bf16[48,768]{1,0:T(8,128)(2,1)S(1)}, u32[]{:S(2)}, u32[]{:S(2)}) collective-permute-start(bf16[48,768]{1,0:T(8,128)(2,1)S(1)} %bitcast.42), channel_id=1, source_target_pairs={{0,384},{1,385},{2,386},{3,387},{4,388},{5,389},{6,390},{7,391},{8... | collective-permute-start | bytes 221192 | tf_op jit(solution)/shard_map/ppermute | solution.py:24
  78.7 3.3 %collective-permute-done = bf16[48,768]{1,0:T(8,128)(2,1)S(1)} collective-permute-done((bf16[48,768]{1,0:T(8,128)(2,1)S(1)}, bf16[48,768]{1,0:T(8,128)(2,1)S(1)}, u32[]{:S(2)}, u32[]{:S(2)}) %collective-permute-start) | collective-permute-done | bytes 73760 | tf_op jit(solution)/shard_map/ppermute | solution.py:24
  82.0 3.0 %collective-permute-done.2 = bf16[48,768]{1,0:T(8,128)(2,1)S(1)} collective-permute-done((bf16[48,768]{1,0:T(8,128)(2,1)S(1)}, bf16[48,768]{1,0:T(8,128)(2,1)S(1)}, u32[]{:S(2)}, u32[]{:S(2)}) %collective-permute-start.2) | collective-permute-done | bytes 73760 | tf_op jit(solution)/shard_map/ppermute | solution.py:24
  85.7 6.4 %collective-permute-start.3 = (bf16[1536,384]{1,0:T(8,128)(2,1)S(1)}, bf16[1536,384]{1,0:T(8,128)(2,1)S(1)}, u32[]{:S(2)}, u32[]{:S(2)}) collective-permute-start(bf16[1536,384]{1,0:T(8,128)(2,1)S(1)} %bitcast.33), channel_id=1, source_target_pairs={{0,6},{1,7},{2,8},{3,9},{4,10},{5,11},{6,0},{7,1},{8,2},{9,3},{10,... | collective-permute-start | bytes 3538952 | tf_op jit(solution)/shard_map/ppermute | solution.py:24
  92.8 1.8 %collective-permute-done.3.other_w = bf16[1536,384]{1,0:T(8,128)(2,1)S(1)} collective-permute-done((bf16[1536,384]{1,0:T(8,128)(2,1)S(1)}, bf16[1536,384]{1,0:T(8,128)(2,1)S(1)}, u32[]{:S(2)}, u32[]{:S(2)}) %collective-permute-start.3) | collective-permute-done | bytes 1179680 | tf_op jit(solution)/shard_map/ppermute | solution.py:24
  94.6 7.8 %shard_map.64 = bf16[6,128,256]{2,1,0:T(8,128)(2,1)S(1)} custom-call(s32[1]{0:T(128)} %bitcast.core_ref.place_ref, s32[1]{0:T(128)S(6)} %copy.26.length_ref, f32[4]{0:T(128)S(1)} %copy-done.1, bf16[768,1536]{1,0:T(8,128)(2,1)} %all-gather.3.cloned.1.call-done.frames, bf16[1536,384]{1,0:T(8,128)(2,1)S(1)} %bitcast.34, ...), custom_call_target="tpu_custom_call" | custom-call | flops 3000000000 | bytes 5000000 | tf_op jit(solution)/shard_map/pallas_call | solution.py:120
  102.3 24.4 %all_to_all.20.heads_ref = bf16[6,128,256]{2,1,0:T(8,128)(2,1)S(1)} all-to-all(bf16[6,128,256]{2,1,0:T(8,128)(2,1)S(1)} %shard_map.64), channel_id=1, replica_groups=mesh['x'=4,'zh'=2,'y'=8,'c'=2,'zl'=6] {'zl'}, dimensions={0} | all-to-all | bytes 786432 | tf_op jit(solution)/shard_map/all_to_all | solution.py:225
  126.7 3.2 %all-gather.5.cloned.1.call-done.own_any = bf16[1536,768]{1,0:T(8,128)(2,1)} async-done(((bf16[192,768]{1,0:T(8,128)(2,1)}), bf16[1536,768]{1,0:T(8,128)(2,1)}) %all-gather.5.cloned.1.call-update) | async-done | bytes 2359312 | tf_op jit(solution)/shard_map/all_gather | solution.py:221
  129.9 5.8 %collective-permute-start.4 = (bf16[1536,768]{1,0:T(8,128)(2,1)}, bf16[1536,768]{1,0:T(8,128)(2,1)S(1)}, u32[]{:S(2)}, u32[]{:S(2)}) collective-permute-start(bf16[1536,768]{1,0:T(8,128)(2,1)} %all-gather.5.cloned.1.call-done.own_any), channel_id=1, source_target_pairs={{0,6},{1,7},{2,8},{3,9},{4,10},{5,11},{6,0},{7,1},{8,2},{9,3},{10,... | collective-permute-start | bytes 7077896 | tf_op jit(solution)/shard_map/ppermute | solution.py:24
  135.7 1.7 %copy-done = bf16[1536,768]{1,0:T(8,128)(2,1)S(1)} copy-done((bf16[1536,768]{1,0:T(8,128)(2,1)S(1)}, bf16[1536,768]{1,0:T(8,128)(2,1)}, u32[]{:S(2)}) %copy-start) | copy-done | bytes 2359320
  137.4 2.3 %shard_map.65.sums_ref = f32[1536,128]{1,0:T(8,128)S(1)} custom-call(s32[1]{0:T(128)} %bitcast.core_ref.place_ref, bf16[6,128,256]{2,1,0:T(8,128)(2,1)S(1)} %all_to_all.20.heads_ref, bf16[1536,768]{1,0:T(8,128)(2,1)S(1)} %copy-done), custom_call_target="tpu_custom_call" | custom-call | flops 300000000 | bytes 3000000 | tf_op jit(solution)/shard_map/pallas_call | solution.py:174
  140.0 1.6 %shard_map.66 = bf16[128,1536]{1,0:T(8,128)(2,1)} custom-call(s32[1]{0:T(128)} %bitcast.core_ref.place_ref, bf16[6,128,256]{2,1,0:T(8,128)(2,1)S(1)} %all_to_all.20.heads_ref, bf16[1536,768]{1,0:T(8,128)(2,1)S(1)} %collective-permute-done.4.other_ref, f32[1536,128]{1,0:T(8,128)S(1)} %shard_map.65.sums_ref), custom_call_target="tpu_custom_call" | custom-call | flops 300000000 | bytes 4000000 | tf_op jit(solution)/shard_map/pallas_call | solution.py:188
  (35 shorter events, 3.2 us)
Async XLA Ops:
  6.5 88.0 %all-gather.3.cloned.1.call-start = ((), (), s32[]{:S(2)}) async-start(), calls=%async_computation.4 | async-start | bytes 2752512 | tf_op jit(solution)/shard_map/all_gather | solution.py:206
  12.0 33.0 %all-to-all-start = ((bf16[24,48,128]{2,1,0:T(8,128)(2,1)}), bf16[24,48,128]{2,1,0:T(8,128)(2,1)S(1)}, u32[]{:S(2)}, u32[]{:S(2)}) async-start(bf16[24,48,128]{2,1,0:T(8,128)(2,1)} %bitcast.6), calls=%async_computation | async-start | bytes 589824 | tf_op jit(solution)/shard_map/all_to_all | solution.py:212
  46.0 17.5 %all-to-all-start.1 = ((bf16[8,48,384]{2,1,0:T(8,128)(2,1)}), bf16[8,48,384]{2,1,0:T(8,128)(2,1)S(1)}, u32[]{:S(2)}, u32[]{:S(2)}) async-start(bf16[8,48,384]{2,1,0:T(8,128)(2,1)} %broadcast_in_dim.45), calls=%async_computation.1 | async-start | bytes 589824 | tf_op jit(solution)/shard_map/all_to_all | solution.py:38
  64.7 29.9 %copy-start.1 = (f32[4]{0:T(128)S(1)}, f32[4]{0:T(128)}, u32[]{:S(2)}) copy-start(f32[4]{0:T(128)} %temp_ref.1) | copy-start | bytes 52
  64.7 20.3 %all-to-all-start.2 = ((bf16[4,384,384]{2,1,0:T(8,128)(2,1)}), bf16[4,384,384]{2,1,0:T(8,128)(2,1)S(1)}, u32[]{:S(2)}, u32[]{:S(2)}) async-start(bf16[4,384,384]{2,1,0:T(8,128)(2,1)} %broadcast_in_dim.47), calls=%async_computation.2 | async-start | bytes 2359296 | tf_op jit(solution)/shard_map/all_to_all | solution.py:38
  68.8 61.1 %all-gather.5.cloned.1.call-start = ((), (), s32[]{:S(2)}) async-start(), calls=%async_computation.5 | async-start | bytes 2654208 | tf_op jit(solution)/shard_map/all_gather | solution.py:221
  69.0 12.9 %collective-permute-start = (bf16[48,768]{1,0:T(8,128)(2,1)S(1)}, bf16[48,768]{1,0:T(8,128)(2,1)S(1)}, u32[]{:S(2)}, u32[]{:S(2)}) collective-permute-start(bf16[48,768]{1,0:T(8,128)(2,1)S(1)} %bitcast.40), channel_id=1, source_target_pairs={{0,192},{1,193},{2,194},{3,195},{4,196},{5,197},{6,198},{7,199},{8... | collective-permute-start | bytes 221192 | tf_op jit(solution)/shard_map/ppermute | solution.py:24
  72.4 9.6 %collective-permute-start.1 = (bf16[48,768]{1,0:T(8,128)(2,1)S(1)}, bf16[48,768]{1,0:T(8,128)(2,1)S(1)}, u32[]{:S(2)}, u32[]{:S(2)}) collective-permute-start(bf16[48,768]{1,0:T(8,128)(2,1)S(1)} %bitcast.41), channel_id=1, source_target_pairs={{0,576},{1,577},{2,578},{3,579},{4,580},{5,581},{6,582},{7,583},{8... | collective-permute-start | bytes 221192 | tf_op jit(solution)/shard_map/ppermute | solution.py:24
  76.1 8.9 %collective-permute-start.2 = (bf16[48,768]{1,0:T(8,128)(2,1)S(1)}, bf16[48,768]{1,0:T(8,128)(2,1)S(1)}, u32[]{:S(2)}, u32[]{:S(2)}) collective-permute-start(bf16[48,768]{1,0:T(8,128)(2,1)S(1)} %bitcast.42), channel_id=1, source_target_pairs={{0,384},{1,385},{2,386},{3,387},{4,388},{5,389},{6,390},{7,391},{8... | collective-permute-start | bytes 221192 | tf_op jit(solution)/shard_map/ppermute | solution.py:24
  85.0 0.7 copy-start.2
  85.7 8.9 %collective-permute-start.3 = (bf16[1536,384]{1,0:T(8,128)(2,1)S(1)}, bf16[1536,384]{1,0:T(8,128)(2,1)S(1)}, u32[]{:S(2)}, u32[]{:S(2)}) collective-permute-start(bf16[1536,384]{1,0:T(8,128)(2,1)S(1)} %bitcast.33), channel_id=1, source_target_pairs={{0,6},{1,7},{2,8},{3,9},{4,10},{5,11},{6,0},{7,1},{8,2},{9,3},{10,... | collective-permute-start | bytes 3538952 | tf_op jit(solution)/shard_map/ppermute | solution.py:24
  129.9 10.1 %collective-permute-start.4 = (bf16[1536,768]{1,0:T(8,128)(2,1)}, bf16[1536,768]{1,0:T(8,128)(2,1)S(1)}, u32[]{:S(2)}, u32[]{:S(2)}) collective-permute-start(bf16[1536,768]{1,0:T(8,128)(2,1)} %all-gather.5.cloned.1.call-done.own_any), channel_id=1, source_target_pairs={{0,6},{1,7},{2,8},{3,9},{4,10},{5,11},{6,0},{7,1},{8,2},{9,3},{10,... | collective-permute-start | bytes 7077896 | tf_op jit(solution)/shard_map/ppermute | solution.py:24
  135.7 1.7 %copy-start = (bf16[1536,768]{1,0:T(8,128)(2,1)S(1)}, bf16[1536,768]{1,0:T(8,128)(2,1)}, u32[]{:S(2)}) copy-start(bf16[1536,768]{1,0:T(8,128)(2,1)} %all-gather.5.cloned.1.call-done.own_any) | copy-start | bytes 7077892
Sparse Core Ops, SparseCore 0:
  9.8 77.4 all-gather.2
  89.6 40.2 all-gather.4

commit v11 on v10

--- a/solution.py
+++ b/solution.py
@@ -156,16 +156,17 @@
 
 
 def project_kernel(place_ref, heads_ref, other_ref, sums_ref, out_ref, total):
-    given = turned_half(heads_ref, 1 - place_ref[0])
-    total[...] = sums_ref[...] + jnp.dot(
-        other_ref[...], given, preferred_element_type=jnp.float32
-    )
+    core = place_ref[0]
+    given = turned_half(heads_ref, 1 - core)
+    total[...] = jnp.dot(other_ref[...], given, preferred_element_type=jnp.float32)
     for x in range(4):
         pieces = []
         for zh in range(2):
             for y in range(8):
-                at = ((y * 4 + x) * 2 + zh) * 24
-                pieces.append(total[at : at + 24, :])
+                own_y = jnp.where(core == 0, y, 7 - y)
+                own_at = pl.multiple_of(((own_y * 4 + x) * 2 + zh) * 24, 8)
+                other_at = pl.multiple_of((((7 - own_y) * 4 + x) * 2 + zh) * 24, 8)
+                pieces.append(sums_ref[pl.ds(own_at, 24), :] + total[pl.ds(other_at, 24), :])
         block = jnp.concatenate(pieces).T
         out_ref[:, x * 384 : x * 384 + 384] = block.astype(jnp.bfloat16)
 
@@ -218,7 +219,13 @@
     own_w = gather(by_y, "x", 4)
     out_by_x, own_w = lax.optimization_barrier((gather_x(columns), own_w))
     other_w = other_core(own_w)
-    out_own = lax.all_gather(out_by_x, "y", axis=0, tiled=True)
+    out_own = lax.all_gather(
+        out_by_x,
+        ("y", "c"),
+        axis=0,
+        tiled=True,
+        axis_index_groups=[list(range(0, 16, 2)), list(range(15, 0, -2))],
+    )
 
     core = lax.axis_index("c").reshape(1).astype(jnp.int32)
     blocks = attend(core, lengths, head_temp, whole, own_w, other_w)

time: 149 us -> 149 us (level)
  no operation moved by 1% of the time
where the time goes in v11:
time: 149 us
  starting transfers between devices  49.1 us (33%)
  waiting for transfers between devices  38.9 us (26%)
  blocking collectives  24.4 us (16%)
  between operations  14.3 us (10%)
  Pallas kernels  11.8 us (8%)
  local copies, waits for them, and re-layouts  7.05 us (5%)
  other arithmetic  3.11 us (2%)
    all_to_all x1, blocking collectives, on_device(): own = lax.all_to_all(blocks, 'zl', 0, 0, tiled=True)  24.4 us
    ppermute x5, starting transfers between devices, permute(): return lax.ppermute(value, AXES, pairs)  21 us
    all_to_all x1, starting transfers between devices, on_device(): lax.all_to_all(after(both, normed), ('zh', 'zl', 'c'), 0, 0, tiled=True)  16.7 us
    all_to_all x1, waiting for transfers between devices, on_device(): lax.all_to_all(after(both, normed), ('zh', 'zl', 'c'), 0, 0, tiled=True)  16.3 us
    all_to_all x2, starting transfers between devices, gather(): lax.all_to_all(copies, axes, 0, 0, tiled=True).reshape(-1, value.shape[1])  11.4 us
    all_to_all x2, waiting for transfers between devices, gather(): lax.all_to_all(copies, axes, 0, 0, tiled=True).reshape(-1, value.shape[1])  10.2 us
    ppermute x5, waiting for transfers between devices, permute(): return lax.ppermute(value, AXES, pairs)  8.39 us
    pallas_call x1, Pallas kernels, attend(): pl.pallas_call(attend_kernel, out_shape=jax.ShapeDtypeStruct((6, rows //...  7.75 us
  transfers between devices with their start and end apart: 10, of which 7 were waited for; matrix products, arithmetic and copies ran while one was open for 3% of the time, Pallas kernels for 7%

profile of v11, /device:TPU:1, one launch (start us, length us, event | category | flops | bytes accessed | tf_op | source)
XLA Modules:
  0.0 148.6 jit_solution(3887660524842345896)
XLA Ops:
  6.5 1.2 fusion
  7.7 1.9 %fusion.2 = bf16[128,1536]{1,0:T(8,128)(2,1)} fusion(bf16[1,128,1536]{2,1,0:T(8,128)(2,1)} %param.6, f32[1536]{0:T(1024)} %param.7, f32[128]{0:T(128)S(1)} %add_sqrt_fusion), kind=kLoop, calls=%fused_computation.4 | loop fusion | flops 786432 | bytes 793088 | tf_op jit(solution)/shard_map/convert_element_type | solution.py:206
  10.4 0.8 reshape.44
  11.2 0.7 broadcast_in_dim.40
  12.0 16.7 %all-to-all-start = ((bf16[24,48,128]{2,1,0:T(8,128)(2,1)}), bf16[24,48,128]{2,1,0:T(8,128)(2,1)S(1)}, u32[]{:S(2)}, u32[]{:S(2)}) async-start(bf16[24,48,128]{2,1,0:T(8,128)(2,1)} %bitcast.6), calls=%async_computation | async-start | bytes 589824 | tf_op jit(solution)/shard_map/all_to_all | solution.py:213
  28.7 16.3 %all-to-all-done = bf16[24,48,128]{2,1,0:T(8,128)(2,1)S(1)} async-done(((bf16[24,48,128]{2,1,0:T(8,128)(2,1)}), bf16[24,48,128]{2,1,0:T(8,128)(2,1)S(1)}, u32[]{:S(2)}, u32[]{:S(2)}) %all-to-all-start) | async-done | bytes 294944 | tf_op jit(solution)/shard_map/all_to_all | solution.py:213
  46.0 7.2 %all-to-all-start.1 = ((bf16[8,48,384]{2,1,0:T(8,128)(2,1)}), bf16[8,48,384]{2,1,0:T(8,128)(2,1)S(1)}, u32[]{:S(2)}, u32[]{:S(2)}) async-start(bf16[8,48,384]{2,1,0:T(8,128)(2,1)} %broadcast_in_dim.45), calls=%async_computation.1 | async-start | bytes 589824 | tf_op jit(solution)/shard_map/all_to_all | solution.py:38
  53.2 10.2 %all-to-all-done.1 = bf16[8,48,384]{2,1,0:T(8,128)(2,1)S(1)} async-done(((bf16[8,48,384]{2,1,0:T(8,128)(2,1)}), bf16[8,48,384]{2,1,0:T(8,128)(2,1)S(1)}, u32[]{:S(2)}, u32[]{:S(2)}) %all-to-all-start.1) | async-done | bytes 294944 | tf_op jit(solution)/shard_map/all_to_all | solution.py:38
  63.5 1.1 broadcast_in_dim.47
  64.7 4.1 %all-to-all-start.2 = ((bf16[4,384,384]{2,1,0:T(8,128)(2,1)}), bf16[4,384,384]{2,1,0:T(8,128)(2,1)S(1)}, u32[]{:S(2)}, u32[]{:S(2)}) async-start(bf16[4,384,384]{2,1,0:T(8,128)(2,1)} %broadcast_in_dim.47), calls=%async_computation.2 | async-start | bytes 2359296 | tf_op jit(solution)/shard_map/all_to_all | solution.py:38
  69.0 3.4 %collective-permute-start = (bf16[48,768]{1,0:T(8,128)(2,1)S(1)}, bf16[48,768]{1,0:T(8,128)(2,1)S(1)}, u32[]{:S(2)}, u32[]{:S(2)}) collective-permute-start(bf16[48,768]{1,0:T(8,128)(2,1)S(1)} %bitcast.40), channel_id=1, source_target_pairs={{0,192},{1,193},{2,194},{3,195},{4,196},{5,197},{6,198},{7,199},{8... | collective-permute-start | bytes 221192 | tf_op jit(solution)/shard_map/ppermute | solution.py:24
  72.4 3.7 %collective-permute-start.1 = (bf16[48,768]{1,0:T(8,128)(2,1)S(1)}, bf16[48,768]{1,0:T(8,128)(2,1)S(1)}, u32[]{:S(2)}, u32[]{:S(2)}) collective-permute-start(bf16[48,768]{1,0:T(8,128)(2,1)S(1)} %bitcast.41), channel_id=1, source_target_pairs={{0,576},{1,577},{2,578},{3,579},{4,580},{5,581},{6,582},{7,583},{8... | collective-permute-start | bytes 221192 | tf_op jit(solution)/shard_map/ppermute | solution.py:24
  76.1 2.5 %collective-permute-start.2 = (bf16[48,768]{1,0:T(8,128)(2,1)S(1)}, bf16[48,768]{1,0:T(8,128)(2,1)S(1)}, u32[]{:S(2)}, u32[]{:S(2)}) collective-permute-start(bf16[48,768]{1,0:T(8,128)(2,1)S(1)} %bitcast.42), channel_id=1, source_target_pairs={{0,384},{1,385},{2,386},{3,387},{4,388},{5,389},{6,390},{7,391},{8... | collective-permute-start | bytes 221192 | tf_op jit(solution)/shard_map/ppermute | solution.py:24
  78.7 3.3 %collective-permute-done = bf16[48,768]{1,0:T(8,128)(2,1)S(1)} collective-permute-done((bf16[48,768]{1,0:T(8,128)(2,1)S(1)}, bf16[48,768]{1,0:T(8,128)(2,1)S(1)}, u32[]{:S(2)}, u32[]{:S(2)}) %collective-permute-start) | collective-permute-done | bytes 73760 | tf_op jit(solution)/shard_map/ppermute | solution.py:24
  82.0 3.0 %collective-permute-done.2 = bf16[48,768]{1,0:T(8,128)(2,1)S(1)} collective-permute-done((bf16[48,768]{1,0:T(8,128)(2,1)S(1)}, bf16[48,768]{1,0:T(8,128)(2,1)S(1)}, u32[]{:S(2)}, u32[]{:S(2)}) %collective-permute-start.2) | collective-permute-done | bytes 73760 | tf_op jit(solution)/shard_map/ppermute | solution.py:24
  85.7 6.4 %collective-permute-start.3 = (bf16[1536,384]{1,0:T(8,128)(2,1)S(1)}, bf16[1536,384]{1,0:T(8,128)(2,1)S(1)}, u32[]{:S(2)}, u32[]{:S(2)}) collective-permute-start(bf16[1536,384]{1,0:T(8,128)(2,1)S(1)} %bitcast.33), channel_id=1, source_target_pairs={{0,6},{1,7},{2,8},{3,9},{4,10},{5,11},{6,0},{7,1},{8,2},{9,3},{10,... | collective-permute-start | bytes 3538952 | tf_op jit(solution)/shard_map/ppermute | solution.py:24
  92.8 1.8 %collective-permute-done.3.other_w = bf16[1536,384]{1,0:T(8,128)(2,1)S(1)} collective-permute-done((bf16[1536,384]{1,0:T(8,128)(2,1)S(1)}, bf16[1536,384]{1,0:T(8,128)(2,1)S(1)}, u32[]{:S(2)}, u32[]{:S(2)}) %collective-permute-start.3) | collective-permute-done | bytes 1179680 | tf_op jit(solution)/shard_map/ppermute | solution.py:24
  94.6 7.8 %shard_map.64 = bf16[6,128,256]{2,1,0:T(8,128)(2,1)S(1)} custom-call(s32[1]{0:T(128)} %bitcast.core_ref.place_ref, s32[1]{0:T(128)S(6)} %copy.26.length_ref, f32[4]{0:T(128)S(1)} %copy-done.1, bf16[768,1536]{1,0:T(8,128)(2,1)} %all-gather.3.cloned.1.call-done.frames, bf16[1536,384]{1,0:T(8,128)(2,1)S(1)} %bitcast.34, ...), custom_call_target="tpu_custom_call" | custom-call | flops 3000000000 | bytes 5000000 | tf_op jit(solution)/shard_map/pallas_call | solution.py:120
  102.3 24.4 %all_to_all.20.heads_ref = bf16[6,128,256]{2,1,0:T(8,128)(2,1)S(1)} all-to-all(bf16[6,128,256]{2,1,0:T(8,128)(2,1)S(1)} %shard_map.64), channel_id=1, replica_groups=mesh['x'=4,'zh'=2,'y'=8,'c'=2,'zl'=6] {'zl'}, dimensions={0} | all-to-all | bytes 786432 | tf_op jit(solution)/shard_map/all_to_all | solution.py:232
  126.7 3.9 %all-gather.5.cloned.1.call-done.own_any = bf16[1536,768]{1,0:T(8,128)(2,1)} async-done(((bf16[192,768]{1,0:T(8,128)(2,1)}), bf16[1536,768]{1,0:T(8,128)(2,1)}) %all-gather.5.cloned.1.call-update) | async-done | bytes 2359312 | tf_op jit(solution)/shard_map/all_gather | solution.py:222
  130.6 5.0 %collective-permute-start.4 = (bf16[1536,768]{1,0:T(8,128)(2,1)}, bf16[1536,768]{1,0:T(8,128)(2,1)S(1)}, u32[]{:S(2)}, u32[]{:S(2)}) collective-permute-start(bf16[1536,768]{1,0:T(8,128)(2,1)} %all-gather.5.cloned.1.call-done.own_any), channel_id=1, source_target_pairs={{0,6},{1,7},{2,8},{3,9},{4,10},{5,11},{6,0},{7,1},{8,2},{9,3},{10,... | collective-permute-start | bytes 7077896 | tf_op jit(solution)/shard_map/ppermute | solution.py:24
  135.7 1.7 %copy-done = bf16[1536,768]{1,0:T(8,128)(2,1)S(1)} copy-done((bf16[1536,768]{1,0:T(8,128)(2,1)S(1)}, bf16[1536,768]{1,0:T(8,128)(2,1)}, u32[]{:S(2)}) %copy-start) | copy-done | bytes 2359320
  137.3 2.3 %shard_map.65.sums_ref = f32[1536,128]{1,0:T(8,128)S(1)} custom-call(s32[1]{0:T(128)} %bitcast.core_ref.place_ref, bf16[6,128,256]{2,1,0:T(8,128)(2,1)S(1)} %all_to_all.20.heads_ref, bf16[1536,768]{1,0:T(8,128)(2,1)S(1)} %copy-done), custom_call_target="tpu_custom_call" | custom-call | flops 300000000 | bytes 3000000 | tf_op jit(solution)/shard_map/pallas_call | solution.py:175
  140.0 1.7 %shard_map.66 = bf16[128,1536]{1,0:T(8,128)(2,1)} custom-call(s32[1]{0:T(128)} %bitcast.core_ref.place_ref, bf16[6,128,256]{2,1,0:T(8,128)(2,1)S(1)} %all_to_all.20.heads_ref, bf16[1536,768]{1,0:T(8,128)(2,1)S(1)} %collective-permute-done.4.other_ref, f32[1536,128]{1,0:T(8,128)S(1)} %shard_map.65.sums_ref), custom_call_target="tpu_custom_call" | custom-call | flops 300000000 | bytes 4000000 | tf_op jit(solution)/shard_map/pallas_call | solution.py:189
  (35 shorter events, 3.2 us)
Async XLA Ops:
  6.5 88.0 %all-gather.3.cloned.1.call-start = ((), (), s32[]{:S(2)}) async-start(), calls=%async_computation.4 | async-start | bytes 2752512 | tf_op jit(solution)/shard_map/all_gather | solution.py:207
  12.0 33.0 %all-to-all-start = ((bf16[24,48,128]{2,1,0:T(8,128)(2,1)}), bf16[24,48,128]{2,1,0:T(8,128)(2,1)S(1)}, u32[]{:S(2)}, u32[]{:S(2)}) async-start(bf16[24,48,128]{2,1,0:T(8,128)(2,1)} %bitcast.6), calls=%async_computation | async-start | bytes 589824 | tf_op jit(solution)/shard_map/all_to_all | solution.py:213
  46.0 17.5 %all-to-all-start.1 = ((bf16[8,48,384]{2,1,0:T(8,128)(2,1)}), bf16[8,48,384]{2,1,0:T(8,128)(2,1)S(1)}, u32[]{:S(2)}, u32[]{:S(2)}) async-start(bf16[8,48,384]{2,1,0:T(8,128)(2,1)} %broadcast_in_dim.45), calls=%async_computation.1 | async-start | bytes 589824 | tf_op jit(solution)/shard_map/all_to_all | solution.py:38
  64.7 29.9 %copy-start.1 = (f32[4]{0:T(128)S(1)}, f32[4]{0:T(128)}, u32[]{:S(2)}) copy-start(f32[4]{0:T(128)} %temp_ref.1) | copy-start | bytes 52
  64.7 20.3 %all-to-all-start.2 = ((bf16[4,384,384]{2,1,0:T(8,128)(2,1)}), bf16[4,384,384]{2,1,0:T(8,128)(2,1)S(1)}, u32[]{:S(2)}, u32[]{:S(2)}) async-start(bf16[4,384,384]{2,1,0:T(8,128)(2,1)} %broadcast_in_dim.47), calls=%async_computation.2 | async-start | bytes 2359296 | tf_op jit(solution)/shard_map/all_to_all | solution.py:38
  68.8 61.8 %all-gather.5.cloned.1.call-start = ((), (), s32[]{:S(2)}) async-start(), calls=%async_computation.5 | async-start | bytes 2654208 | tf_op jit(solution)/shard_map/all_gather | solution.py:222
  69.0 12.9 %collective-permute-start = (bf16[48,768]{1,0:T(8,128)(2,1)S(1)}, bf16[48,768]{1,0:T(8,128)(2,1)S(1)}, u32[]{:S(2)}, u32[]{:S(2)}) collective-permute-start(bf16[48,768]{1,0:T(8,128)(2,1)S(1)} %bitcast.40), channel_id=1, source_target_pairs={{0,192},{1,193},{2,194},{3,195},{4,196},{5,197},{6,198},{7,199},{8... | collective-permute-start | bytes 221192 | tf_op jit(solution)/shard_map/ppermute | solution.py:24
  72.4 9.6 %collective-permute-start.1 = (bf16[48,768]{1,0:T(8,128)(2,1)S(1)}, bf16[48,768]{1,0:T(8,128)(2,1)S(1)}, u32[]{:S(2)}, u32[]{:S(2)}) collective-permute-start(bf16[48,768]{1,0:T(8,128)(2,1)S(1)} %bitcast.41), channel_id=1, source_target_pairs={{0,576},{1,577},{2,578},{3,579},{4,580},{5,581},{6,582},{7,583},{8... | collective-permute-start | bytes 221192 | tf_op jit(solution)/shard_map/ppermute | solution.py:24
  76.1 8.9 %collective-permute-start.2 = (bf16[48,768]{1,0:T(8,128)(2,1)S(1)}, bf16[48,768]{1,0:T(8,128)(2,1)S(1)}, u32[]{:S(2)}, u32[]{:S(2)}) collective-permute-start(bf16[48,768]{1,0:T(8,128)(2,1)S(1)} %bitcast.42), channel_id=1, source_target_pairs={{0,384},{1,385},{2,386},{3,387},{4,388},{5,389},{6,390},{7,391},{8... | collective-permute-start | bytes 221192 | tf_op jit(solution)/shard_map/ppermute | solution.py:24
  85.0 0.7 copy-start.2
  85.7 8.9 %collective-permute-start.3 = (bf16[1536,384]{1,0:T(8,128)(2,1)S(1)}, bf16[1536,384]{1,0:T(8,128)(2,1)S(1)}, u32[]{:S(2)}, u32[]{:S(2)}) collective-permute-start(bf16[1536,384]{1,0:T(8,128)(2,1)S(1)} %bitcast.33), channel_id=1, source_target_pairs={{0,6},{1,7},{2,8},{3,9},{4,10},{5,11},{6,0},{7,1},{8,2},{9,3},{10,... | collective-permute-start | bytes 3538952 | tf_op jit(solution)/shard_map/ppermute | solution.py:24
  130.6 9.4 %collective-permute-start.4 = (bf16[1536,768]{1,0:T(8,128)(2,1)}, bf16[1536,768]{1,0:T(8,128)(2,1)S(1)}, u32[]{:S(2)}, u32[]{:S(2)}) collective-permute-start(bf16[1536,768]{1,0:T(8,128)(2,1)} %all-gather.5.cloned.1.call-done.own_any), channel_id=1, source_target_pairs={{0,6},{1,7},{2,8},{3,9},{4,10},{5,11},{6,0},{7,1},{8,2},{9,3},{10,... | collective-permute-start | bytes 7077896 | tf_op jit(solution)/shard_map/ppermute | solution.py:24
  135.7 1.7 %copy-start = (bf16[1536,768]{1,0:T(8,128)(2,1)S(1)}, bf16[1536,768]{1,0:T(8,128)(2,1)}, u32[]{:S(2)}) copy-start(bf16[1536,768]{1,0:T(8,128)(2,1)} %all-gather.5.cloned.1.call-done.own_any) | copy-start | bytes 7077892
Sparse Core Ops, SparseCore 0:
  9.8 77.4 all-gather.2
  89.6 40.9 all-gather.4

commit v12 on v10

--- a/solution.py
+++ b/solution.py
@@ -198,11 +198,27 @@
     )(place, heads, other, sums)
 
 
+def normalise_kernel(frames_ref, gain_ref, out_ref):
+    values = frames_ref[...].astype(jnp.float32)
+    rms = jnp.sqrt(jnp.mean(values * values, axis=-1, keepdims=True) + 1e-06)
+    out_ref[...] = (values / rms * gain_ref[...]).astype(jnp.bfloat16)
+
+
+def normalise(frames, gain):
+    return pl.pallas_call(
+        normalise_kernel,
+        out_shape=jax.ShapeDtypeStruct(frames.shape, jnp.bfloat16),
+        in_specs=[VMEM] * 2,
+        out_specs=VMEM,
+        compiler_params=pltpu.CompilerParams(vmem_limit_bytes=8 * 2**20),
+        cost_estimate=pl.CostEstimate(
+            flops=10**6, bytes_accessed=8 * 10**5, transcendentals=0
+        ),
+    )(frames, gain[None])
+
+
 def on_device(latents, norm_gain, w_qkv, w_out, head_temp, lengths):
-    frames = latents[0]
-    values = frames.astype(jnp.float32)
-    rms = jnp.sqrt(jnp.mean(values * values, axis=-1, keepdims=True) + 1e-06)
-    normed = (values / rms * norm_gain).astype(jnp.bfloat16)
+    normed = normalise(latents[0], norm_gain)
     whole = lax.all_gather(normed, "zl", axis=0, tiled=True)
 
     rows = w_qkv.reshape(3, 12, 2, 128).transpose(2, 1, 0, 3).reshape(2, 12, 384)

time: 149 us -> 149 us (level)
  other arithmetic: 3.11 us -> 0.03 us
  local copies, waits for them, and re-layouts: 7.05 us -> 8.76 us
    convert_element_type x1 -> x0, other arithmetic: 1.91 us -> none  [on_device(): normed = (values / rms * norm_gain).astype(jnp.bfloat16)]
    unnamed x7 -> x9, local copies, waits for them, and re-layouts: 2.38 us -> 3.38 us
where the time goes in v12:
time: 149 us; the launch traced here: 148 us
  starting transfers between devices  50 us (34%)
  waiting for transfers between devices  37.8 us (25%)
  blocking collectives  24.6 us (17%)
  between operations  14.3 us (10%)
  Pallas kernels  12.7 us (9%)
  local copies, waits for them, and re-layouts  8.76 us (6%)
    all_to_all x1, blocking collectives, on_device(): own = lax.all_to_all(blocks, 'zl', 0, 0, tiled=True)  24.6 us
    ppermute x5, starting transfers between devices, permute(): return lax.ppermute(value, AXES, pairs)  21.9 us
    all_to_all x1, starting transfers between devices, on_device(): lax.all_to_all(after(both, normed), ('zh', 'zl', 'c'), 0, 0, tiled=True)  16.7 us
    all_to_all x1, waiting for transfers between devices, on_device(): lax.all_to_all(after(both, normed), ('zh', 'zl', 'c'), 0, 0, tiled=True)  15.9 us
    all_to_all x2, starting transfers between devices, gather(): lax.all_to_all(copies, axes, 0, 0, tiled=True).reshape(-1, value.shape[1])  11.4 us
    all_to_all x2, waiting for transfers between devices, gather(): lax.all_to_all(copies, axes, 0, 0, tiled=True).reshape(-1, value.shape[1])  10.1 us
    ppermute x5, waiting for transfers between devices, permute(): return lax.ppermute(value, AXES, pairs)  8.22 us
    pallas_call x1, Pallas kernels, attend(): pl.pallas_call(attend_kernel, out_shape=jax.ShapeDtypeStruct((6, rows //...  7.75 us
  transfers between devices with their start and end apart: 10, of which 7 were waited for; matrix products, arithmetic and copies ran while one was open for 3% of the time, Pallas kernels for 7%

profile of v12, /device:TPU:1, one launch (start us, length us, event | category | flops | bytes accessed | tf_op | source)
XLA Modules:
  0.0 148.1 jit_solution(10183627154711992440)
XLA Ops:
  7.2 1.0 copy-done.1
  8.2 1.0 shard_map.64
  9.9 0.8 reshape.33
  10.8 0.8 broadcast_in_dim.42
  11.6 16.7 %all-to-all-start = ((bf16[24,48,128]{2,1,0:T(8,128)(2,1)}), bf16[24,48,128]{2,1,0:T(8,128)(2,1)S(1)}, u32[]{:S(2)}, u32[]{:S(2)}) async-start(bf16[24,48,128]{2,1,0:T(8,128)(2,1)} %bitcast.5), calls=%async_computation | async-start | bytes 589824 | tf_op jit(solution)/shard_map/all_to_all | solution.py:228
  28.3 15.9 %all-to-all-done = bf16[24,48,128]{2,1,0:T(8,128)(2,1)S(1)} async-done(((bf16[24,48,128]{2,1,0:T(8,128)(2,1)}), bf16[24,48,128]{2,1,0:T(8,128)(2,1)S(1)}, u32[]{:S(2)}, u32[]{:S(2)}) %all-to-all-start) | async-done | bytes 294944 | tf_op jit(solution)/shard_map/all_to_all | solution.py:228
  45.1 7.2 %all-to-all-start.1 = ((bf16[8,48,384]{2,1,0:T(8,128)(2,1)}), bf16[8,48,384]{2,1,0:T(8,128)(2,1)S(1)}, u32[]{:S(2)}, u32[]{:S(2)}) async-start(bf16[8,48,384]{2,1,0:T(8,128)(2,1)} %broadcast_in_dim.47), calls=%async_computation.1 | async-start | bytes 589824 | tf_op jit(solution)/shard_map/all_to_all | solution.py:38
  52.3 10.1 %all-to-all-done.1 = bf16[8,48,384]{2,1,0:T(8,128)(2,1)S(1)} async-done(((bf16[8,48,384]{2,1,0:T(8,128)(2,1)}), bf16[8,48,384]{2,1,0:T(8,128)(2,1)S(1)}, u32[]{:S(2)}, u32[]{:S(2)}) %all-to-all-start.1) | async-done | bytes 294944 | tf_op jit(solution)/shard_map/all_to_all | solution.py:38
  62.5 1.1 broadcast_in_dim.49
  63.6 4.2 %all-to-all-start.2 = ((bf16[4,384,384]{2,1,0:T(8,128)(2,1)}), bf16[4,384,384]{2,1,0:T(8,128)(2,1)S(1)}, u32[]{:S(2)}, u32[]{:S(2)}) async-start(bf16[4,384,384]{2,1,0:T(8,128)(2,1)} %broadcast_in_dim.49), calls=%async_computation.2 | async-start | bytes 2359296 | tf_op jit(solution)/shard_map/all_to_all | solution.py:38
  68.0 3.4 %collective-permute-start = (bf16[48,768]{1,0:T(8,128)(2,1)S(1)}, bf16[48,768]{1,0:T(8,128)(2,1)S(1)}, u32[]{:S(2)}, u32[]{:S(2)}) collective-permute-start(bf16[48,768]{1,0:T(8,128)(2,1)S(1)} %bitcast.38), channel_id=1, source_target_pairs={{0,192},{1,193},{2,194},{3,195},{4,196},{5,197},{6,198},{7,199},{8... | collective-permute-start | bytes 221192 | tf_op jit(solution)/shard_map/ppermute | solution.py:24
  71.4 3.7 %collective-permute-start.1 = (bf16[48,768]{1,0:T(8,128)(2,1)S(1)}, bf16[48,768]{1,0:T(8,128)(2,1)S(1)}, u32[]{:S(2)}, u32[]{:S(2)}) collective-permute-start(bf16[48,768]{1,0:T(8,128)(2,1)S(1)} %bitcast.39), channel_id=1, source_target_pairs={{0,576},{1,577},{2,578},{3,579},{4,580},{5,581},{6,582},{7,583},{8... | collective-permute-start | bytes 221192 | tf_op jit(solution)/shard_map/ppermute | solution.py:24
  75.1 2.5 %collective-permute-start.2 = (bf16[48,768]{1,0:T(8,128)(2,1)S(1)}, bf16[48,768]{1,0:T(8,128)(2,1)S(1)}, u32[]{:S(2)}, u32[]{:S(2)}) collective-permute-start(bf16[48,768]{1,0:T(8,128)(2,1)S(1)} %bitcast.40), channel_id=1, source_target_pairs={{0,384},{1,385},{2,386},{3,387},{4,388},{5,389},{6,390},{7,391},{8... | collective-permute-start | bytes 221192 | tf_op jit(solution)/shard_map/ppermute | solution.py:24
  77.7 3.1 %collective-permute-done = bf16[48,768]{1,0:T(8,128)(2,1)S(1)} collective-permute-done((bf16[48,768]{1,0:T(8,128)(2,1)S(1)}, bf16[48,768]{1,0:T(8,128)(2,1)S(1)}, u32[]{:S(2)}, u32[]{:S(2)}) %collective-permute-start) | collective-permute-done | bytes 73760 | tf_op jit(solution)/shard_map/ppermute | solution.py:24
  80.9 3.0 %collective-permute-done.2 = bf16[48,768]{1,0:T(8,128)(2,1)S(1)} collective-permute-done((bf16[48,768]{1,0:T(8,128)(2,1)S(1)}, bf16[48,768]{1,0:T(8,128)(2,1)S(1)}, u32[]{:S(2)}, u32[]{:S(2)}) %collective-permute-start.2) | collective-permute-done | bytes 73760 | tf_op jit(solution)/shard_map/ppermute | solution.py:24
  84.6 6.6 %collective-permute-start.3 = (bf16[1536,384]{1,0:T(8,128)(2,1)S(1)}, bf16[1536,384]{1,0:T(8,128)(2,1)S(1)}, u32[]{:S(2)}, u32[]{:S(2)}) collective-permute-start(bf16[1536,384]{1,0:T(8,128)(2,1)S(1)} %bitcast.30), channel_id=1, source_target_pairs={{0,6},{1,7},{2,8},{3,9},{4,10},{5,11},{6,0},{7,1},{8,2},{9,3},{10,... | collective-permute-start | bytes 3538952 | tf_op jit(solution)/shard_map/ppermute | solution.py:24
  91.8 1.8 %collective-permute-done.3.other_w = bf16[1536,384]{1,0:T(8,128)(2,1)S(1)} collective-permute-done((bf16[1536,384]{1,0:T(8,128)(2,1)S(1)}, bf16[1536,384]{1,0:T(8,128)(2,1)S(1)}, u32[]{:S(2)}, u32[]{:S(2)}) %collective-permute-start.3) | collective-permute-done | bytes 1179680 | tf_op jit(solution)/shard_map/ppermute | solution.py:24
  93.6 7.8 %shard_map.65 = bf16[6,128,256]{2,1,0:T(8,128)(2,1)S(1)} custom-call(s32[1]{0:T(128)} %bitcast.core_ref.place_ref, s32[1]{0:T(128)S(6)} %copy.26.length_ref, f32[4]{0:T(128)S(1)} %copy-done.2, bf16[768,1536]{1,0:T(8,128)(2,1)} %all-gather.3.cloned.1.call-done.frames, bf16[1536,384]{1,0:T(8,128)(2,1)S(1)} %bitcast.31, ...), custom_call_target="tpu_custom_call" | custom-call | flops 3000000000 | bytes 5000000 | tf_op jit(solution)/shard_map/pallas_call | solution.py:120
  101.4 24.6 %all_to_all.20.heads_ref = bf16[6,128,256]{2,1,0:T(8,128)(2,1)S(1)} all-to-all(bf16[6,128,256]{2,1,0:T(8,128)(2,1)S(1)} %shard_map.65), channel_id=1, replica_groups=mesh['x'=4,'zh'=2,'y'=8,'c'=2,'zl'=6] {'zl'}, dimensions={0} | all-to-all | bytes 786432 | tf_op jit(solution)/shard_map/all_to_all | solution.py:241
  125.9 3.6 %all-gather.5.cloned.1.call-done.own_any = bf16[1536,768]{1,0:T(8,128)(2,1)} async-done(((bf16[192,768]{1,0:T(8,128)(2,1)}), bf16[1536,768]{1,0:T(8,128)(2,1)}) %all-gather.5.cloned.1.call-update) | async-done | bytes 2359312 | tf_op jit(solution)/shard_map/all_gather | solution.py:237
  129.5 5.8 %collective-permute-start.4 = (bf16[1536,768]{1,0:T(8,128)(2,1)}, bf16[1536,768]{1,0:T(8,128)(2,1)S(1)}, u32[]{:S(2)}, u32[]{:S(2)}) collective-permute-start(bf16[1536,768]{1,0:T(8,128)(2,1)} %all-gather.5.cloned.1.call-done.own_any), channel_id=1, source_target_pairs={{0,6},{1,7},{2,8},{3,9},{4,10},{5,11},{6,0},{7,1},{8,2},{9,3},{10,... | collective-permute-start | bytes 7077896 | tf_op jit(solution)/shard_map/ppermute | solution.py:24
  135.3 1.7 %copy-done = bf16[1536,768]{1,0:T(8,128)(2,1)S(1)} copy-done((bf16[1536,768]{1,0:T(8,128)(2,1)S(1)}, bf16[1536,768]{1,0:T(8,128)(2,1)}, u32[]{:S(2)}) %copy-start) | copy-done | bytes 2359320
  136.9 2.3 %shard_map.66.sums_ref = f32[1536,128]{1,0:T(8,128)S(1)} custom-call(s32[1]{0:T(128)} %bitcast.core_ref.place_ref, bf16[6,128,256]{2,1,0:T(8,128)(2,1)S(1)} %all_to_all.20.heads_ref, bf16[1536,768]{1,0:T(8,128)(2,1)S(1)} %copy-done), custom_call_target="tpu_custom_call" | custom-call | flops 300000000 | bytes 3000000 | tf_op jit(solution)/shard_map/pallas_call | solution.py:174
  139.6 1.6 %shard_map.67 = bf16[128,1536]{1,0:T(8,128)(2,1)} custom-call(s32[1]{0:T(128)} %bitcast.core_ref.place_ref, bf16[6,128,256]{2,1,0:T(8,128)(2,1)S(1)} %all_to_all.20.heads_ref, bf16[1536,768]{1,0:T(8,128)(2,1)S(1)} %collective-permute-done.4.other_ref, f32[1536,128]{1,0:T(8,128)S(1)} %shard_map.66.sums_ref), custom_call_target="tpu_custom_call" | custom-call | flops 300000000 | bytes 4000000 | tf_op jit(solution)/shard_map/pallas_call | solution.py:188
  (36 shorter events, 3.9 us)
Async XLA Ops:
  6.5 87.1 %all-gather.3.cloned.1.call-start = ((), (), s32[]{:S(2)}) async-start(), calls=%async_computation.4 | async-start | bytes 2752512 | tf_op jit(solution)/shard_map/all_gather | solution.py:222
  7.2 1.0 copy-start.1
  11.6 32.6 %all-to-all-start = ((bf16[24,48,128]{2,1,0:T(8,128)(2,1)}), bf16[24,48,128]{2,1,0:T(8,128)(2,1)S(1)}, u32[]{:S(2)}, u32[]{:S(2)}) async-start(bf16[24,48,128]{2,1,0:T(8,128)(2,1)} %bitcast.5), calls=%async_computation | async-start | bytes 589824 | tf_op jit(solution)/shard_map/all_to_all | solution.py:228
  45.1 17.3 %all-to-all-start.1 = ((bf16[8,48,384]{2,1,0:T(8,128)(2,1)}), bf16[8,48,384]{2,1,0:T(8,128)(2,1)S(1)}, u32[]{:S(2)}, u32[]{:S(2)}) async-start(bf16[8,48,384]{2,1,0:T(8,128)(2,1)} %broadcast_in_dim.47), calls=%async_computation.1 | async-start | bytes 589824 | tf_op jit(solution)/shard_map/all_to_all | solution.py:38
  63.6 30.0 %copy-start.2 = (f32[4]{0:T(128)S(1)}, f32[4]{0:T(128)}, u32[]{:S(2)}) copy-start(f32[4]{0:T(128)} %temp_ref.1) | copy-start | bytes 52
  63.6 20.2 %all-to-all-start.2 = ((bf16[4,384,384]{2,1,0:T(8,128)(2,1)}), bf16[4,384,384]{2,1,0:T(8,128)(2,1)S(1)}, u32[]{:S(2)}, u32[]{:S(2)}) async-start(bf16[4,384,384]{2,1,0:T(8,128)(2,1)} %broadcast_in_dim.49), calls=%async_computation.2 | async-start | bytes 2359296 | tf_op jit(solution)/shard_map/all_to_all | solution.py:38
  67.8 61.7 %all-gather.5.cloned.1.call-start = ((), (), s32[]{:S(2)}) async-start(), calls=%async_computation.5 | async-start | bytes 2654208 | tf_op jit(solution)/shard_map/all_gather | solution.py:237
  68.0 12.8 %collective-permute-start = (bf16[48,768]{1,0:T(8,128)(2,1)S(1)}, bf16[48,768]{1,0:T(8,128)(2,1)S(1)}, u32[]{:S(2)}, u32[]{:S(2)}) collective-permute-start(bf16[48,768]{1,0:T(8,128)(2,1)S(1)} %bitcast.38), channel_id=1, source_target_pairs={{0,192},{1,193},{2,194},{3,195},{4,196},{5,197},{6,198},{7,199},{8... | collective-permute-start | bytes 221192 | tf_op jit(solution)/shard_map/ppermute | solution.py:24
  71.4 9.4 %collective-permute-start.1 = (bf16[48,768]{1,0:T(8,128)(2,1)S(1)}, bf16[48,768]{1,0:T(8,128)(2,1)S(1)}, u32[]{:S(2)}, u32[]{:S(2)}) collective-permute-start(bf16[48,768]{1,0:T(8,128)(2,1)S(1)} %bitcast.39), channel_id=1, source_target_pairs={{0,576},{1,577},{2,578},{3,579},{4,580},{5,581},{6,582},{7,583},{8... | collective-permute-start | bytes 221192 | tf_op jit(solution)/shard_map/ppermute | solution.py:24
  75.1 8.7 %collective-permute-start.2 = (bf16[48,768]{1,0:T(8,128)(2,1)S(1)}, bf16[48,768]{1,0:T(8,128)(2,1)S(1)}, u32[]{:S(2)}, u32[]{:S(2)}) collective-permute-start(bf16[48,768]{1,0:T(8,128)(2,1)S(1)} %bitcast.40), channel_id=1, source_target_pairs={{0,384},{1,385},{2,386},{3,387},{4,388},{5,389},{6,390},{7,391},{8... | collective-permute-start | bytes 221192 | tf_op jit(solution)/shard_map/ppermute | solution.py:24
  83.8 0.7 copy-start.3
  84.6 9.0 %collective-permute-start.3 = (bf16[1536,384]{1,0:T(8,128)(2,1)S(1)}, bf16[1536,384]{1,0:T(8,128)(2,1)S(1)}, u32[]{:S(2)}, u32[]{:S(2)}) collective-permute-start(bf16[1536,384]{1,0:T(8,128)(2,1)S(1)} %bitcast.30), channel_id=1, source_target_pairs={{0,6},{1,7},{2,8},{3,9},{4,10},{5,11},{6,0},{7,1},{8,2},{9,3},{10,... | collective-permute-start | bytes 3538952 | tf_op jit(solution)/shard_map/ppermute | solution.py:24
  129.5 10.1 %collective-permute-start.4 = (bf16[1536,768]{1,0:T(8,128)(2,1)}, bf16[1536,768]{1,0:T(8,128)(2,1)S(1)}, u32[]{:S(2)}, u32[]{:S(2)}) collective-permute-start(bf16[1536,768]{1,0:T(8,128)(2,1)} %all-gather.5.cloned.1.call-done.own_any), channel_id=1, source_target_pairs={{0,6},{1,7},{2,8},{3,9},{4,10},{5,11},{6,0},{7,1},{8,2},{9,3},{10,... | collective-permute-start | bytes 7077896 | tf_op jit(solution)/shard_map/ppermute | solution.py:24
  135.3 1.7 %copy-start = (bf16[1536,768]{1,0:T(8,128)(2,1)S(1)}, bf16[1536,768]{1,0:T(8,128)(2,1)}, u32[]{:S(2)}) copy-start(bf16[1536,768]{1,0:T(8,128)(2,1)} %all-gather.5.cloned.1.call-done.own_any) | copy-start | bytes 7077892
Sparse Core Ops, SparseCore 0:
  9.7 77.0 all-gather.2
  89.2 40.2 all-gather.4

commit v13 on v12

--- a/solution.py
+++ b/solution.py
@@ -210,7 +210,7 @@
         out_shape=jax.ShapeDtypeStruct(frames.shape, jnp.bfloat16),
         in_specs=[VMEM] * 2,
         out_specs=VMEM,
-        compiler_params=pltpu.CompilerParams(vmem_limit_bytes=8 * 2**20),
+        compiler_params=pltpu.CompilerParams(vmem_limit_bytes=58 * 2**20),
         cost_estimate=pl.CostEstimate(
             flops=10**6, bytes_accessed=8 * 10**5, transcendentals=0
         ),

time: 149 us -> 149 us (level)
    unnamed x9 -> x7, local copies, waits for them, and re-layouts: 3.38 us -> 2.39 us
where the time goes in v13:
time: 149 us
  starting transfers between devices  49.8 us (33%)
  waiting for transfers between devices  38.1 us (26%)
  blocking collectives  24.4 us (16%)
  between operations  14.3 us (10%)
  Pallas kernels  13.7 us (9%)
  local copies, waits for them, and re-layouts  8.37 us (6%)
    all_to_all x1, blocking collectives, on_device(): own = lax.all_to_all(blocks, 'zl', 0, 0, tiled=True)  24.4 us
    ppermute x5, starting transfers between devices, permute(): return lax.ppermute(value, AXES, pairs)  21.8 us
    all_to_all x1, starting transfers between devices, on_device(): lax.all_to_all(after(both, normed), ('zh', 'zl', 'c'), 0, 0, tiled=True)  16.7 us
    all_to_all x1, waiting for transfers between devices, on_device(): lax.all_to_all(after(both, normed), ('zh', 'zl', 'c'), 0, 0, tiled=True)  16.3 us
    all_to_all x2, starting transfers between devices, gather(): lax.all_to_all(copies, axes, 0, 0, tiled=True).reshape(-1, value.shape[1])  11.4 us
    all_to_all x2, waiting for transfers between devices, gather(): lax.all_to_all(copies, axes, 0, 0, tiled=True).reshape(-1, value.shape[1])  10.2 us
    ppermute x5, waiting for transfers between devices, permute(): return lax.ppermute(value, AXES, pairs)  8.38 us
    pallas_call x1, Pallas kernels, attend(): pl.pallas_call(attend_kernel, out_shape=jax.ShapeDtypeStruct((6, rows //...  7.75 us
  transfers between devices with their start and end apart: 10, of which 7 were waited for; matrix products, arithmetic and copies ran while one was open for 3% of the time, Pallas kernels for 7%

profile of v13, /device:TPU:1, one launch (start us, length us, event | category | flops | bytes accessed | tf_op | source)
XLA Modules:
  0.0 148.7 jit_solution(2122568927382545269)
XLA Ops:
  6.5 1.3 broadcast_in_dim.39.gain_ref
  7.8 2.0 %shard_map.64 = bf16[128,1536]{1,0:T(8,128)(2,1)} custom-call(bf16[128,1536]{1,0:T(8,128)(2,1)} %bitcast.36, f32[1,1536]{1,0:T(1,128)} %broadcast_in_dim.39.gain_ref), custom_call_target="tpu_custom_call" | custom-call | flops 1000000 | bytes 800000 | tf_op jit(solution)/shard_map/pallas_call | solution.py:208
  10.5 0.8 reshape.33
  11.4 0.8 broadcast_in_dim.42
  12.2 16.7 %all-to-all-start = ((bf16[24,48,128]{2,1,0:T(8,128)(2,1)}), bf16[24,48,128]{2,1,0:T(8,128)(2,1)S(1)}, u32[]{:S(2)}, u32[]{:S(2)}) async-start(bf16[24,48,128]{2,1,0:T(8,128)(2,1)} %bitcast.5), calls=%async_computation | async-start | bytes 589824 | tf_op jit(solution)/shard_map/all_to_all | solution.py:228
  28.9 16.3 %all-to-all-done = bf16[24,48,128]{2,1,0:T(8,128)(2,1)S(1)} async-done(((bf16[24,48,128]{2,1,0:T(8,128)(2,1)}), bf16[24,48,128]{2,1,0:T(8,128)(2,1)S(1)}, u32[]{:S(2)}, u32[]{:S(2)}) %all-to-all-start) | async-done | bytes 294944 | tf_op jit(solution)/shard_map/all_to_all | solution.py:228
  46.2 7.2 %all-to-all-start.1 = ((bf16[8,48,384]{2,1,0:T(8,128)(2,1)}), bf16[8,48,384]{2,1,0:T(8,128)(2,1)S(1)}, u32[]{:S(2)}, u32[]{:S(2)}) async-start(bf16[8,48,384]{2,1,0:T(8,128)(2,1)} %broadcast_in_dim.47), calls=%async_computation.1 | async-start | bytes 589824 | tf_op jit(solution)/shard_map/all_to_all | solution.py:38
  53.4 10.2 %all-to-all-done.1 = bf16[8,48,384]{2,1,0:T(8,128)(2,1)S(1)} async-done(((bf16[8,48,384]{2,1,0:T(8,128)(2,1)}), bf16[8,48,384]{2,1,0:T(8,128)(2,1)S(1)}, u32[]{:S(2)}, u32[]{:S(2)}) %all-to-all-start.1) | async-done | bytes 294944 | tf_op jit(solution)/shard_map/all_to_all | solution.py:38
  63.7 1.1 broadcast_in_dim.49
  64.8 4.1 %all-to-all-start.2 = ((bf16[4,384,384]{2,1,0:T(8,128)(2,1)}), bf16[4,384,384]{2,1,0:T(8,128)(2,1)S(1)}, u32[]{:S(2)}, u32[]{:S(2)}) async-start(bf16[4,384,384]{2,1,0:T(8,128)(2,1)} %broadcast_in_dim.49), calls=%async_computation.2 | async-start | bytes 2359296 | tf_op jit(solution)/shard_map/all_to_all | solution.py:38
  69.2 3.4 %collective-permute-start = (bf16[48,768]{1,0:T(8,128)(2,1)S(1)}, bf16[48,768]{1,0:T(8,128)(2,1)S(1)}, u32[]{:S(2)}, u32[]{:S(2)}) collective-permute-start(bf16[48,768]{1,0:T(8,128)(2,1)S(1)} %bitcast.38), channel_id=1, source_target_pairs={{0,192},{1,193},{2,194},{3,195},{4,196},{5,197},{6,198},{7,199},{8... | collective-permute-start | bytes 221192 | tf_op jit(solution)/shard_map/ppermute | solution.py:24
  72.5 3.7 %collective-permute-start.1 = (bf16[48,768]{1,0:T(8,128)(2,1)S(1)}, bf16[48,768]{1,0:T(8,128)(2,1)S(1)}, u32[]{:S(2)}, u32[]{:S(2)}) collective-permute-start(bf16[48,768]{1,0:T(8,128)(2,1)S(1)} %bitcast.39), channel_id=1, source_target_pairs={{0,576},{1,577},{2,578},{3,579},{4,580},{5,581},{6,582},{7,583},{8... | collective-permute-start | bytes 221192 | tf_op jit(solution)/shard_map/ppermute | solution.py:24
  76.2 2.5 %collective-permute-start.2 = (bf16[48,768]{1,0:T(8,128)(2,1)S(1)}, bf16[48,768]{1,0:T(8,128)(2,1)S(1)}, u32[]{:S(2)}, u32[]{:S(2)}) collective-permute-start(bf16[48,768]{1,0:T(8,128)(2,1)S(1)} %bitcast.40), channel_id=1, source_target_pairs={{0,384},{1,385},{2,386},{3,387},{4,388},{5,389},{6,390},{7,391},{8... | collective-permute-start | bytes 221192 | tf_op jit(solution)/shard_map/ppermute | solution.py:24
  78.8 3.3 %collective-permute-done = bf16[48,768]{1,0:T(8,128)(2,1)S(1)} collective-permute-done((bf16[48,768]{1,0:T(8,128)(2,1)S(1)}, bf16[48,768]{1,0:T(8,128)(2,1)S(1)}, u32[]{:S(2)}, u32[]{:S(2)}) %collective-permute-start) | collective-permute-done | bytes 73760 | tf_op jit(solution)/shard_map/ppermute | solution.py:24
  82.2 3.0 %collective-permute-done.2 = bf16[48,768]{1,0:T(8,128)(2,1)S(1)} collective-permute-done((bf16[48,768]{1,0:T(8,128)(2,1)S(1)}, bf16[48,768]{1,0:T(8,128)(2,1)S(1)}, u32[]{:S(2)}, u32[]{:S(2)}) %collective-permute-start.2) | collective-permute-done | bytes 73760 | tf_op jit(solution)/shard_map/ppermute | solution.py:24
  85.9 6.4 %collective-permute-start.3 = (bf16[1536,384]{1,0:T(8,128)(2,1)S(1)}, bf16[1536,384]{1,0:T(8,128)(2,1)S(1)}, u32[]{:S(2)}, u32[]{:S(2)}) collective-permute-start(bf16[1536,384]{1,0:T(8,128)(2,1)S(1)} %bitcast.30), channel_id=1, source_target_pairs={{0,6},{1,7},{2,8},{3,9},{4,10},{5,11},{6,0},{7,1},{8,2},{9,3},{10,... | collective-permute-start | bytes 3538952 | tf_op jit(solution)/shard_map/ppermute | solution.py:24
  93.0 1.8 %collective-permute-done.3.other_w = bf16[1536,384]{1,0:T(8,128)(2,1)S(1)} collective-permute-done((bf16[1536,384]{1,0:T(8,128)(2,1)S(1)}, bf16[1536,384]{1,0:T(8,128)(2,1)S(1)}, u32[]{:S(2)}, u32[]{:S(2)}) %collective-permute-start.3) | collective-permute-done | bytes 1179680 | tf_op jit(solution)/shard_map/ppermute | solution.py:24
  94.8 7.7 %shard_map.65 = bf16[6,128,256]{2,1,0:T(8,128)(2,1)S(1)} custom-call(s32[1]{0:T(128)} %bitcast.core_ref.place_ref, s32[1]{0:T(128)S(6)} %copy.26.length_ref, f32[4]{0:T(128)S(1)} %copy-done.1, bf16[768,1536]{1,0:T(8,128)(2,1)} %all-gather.3.cloned.1.call-done.frames, bf16[1536,384]{1,0:T(8,128)(2,1)S(1)} %bitcast.31, ...), custom_call_target="tpu_custom_call" | custom-call | flops 3000000000 | bytes 5000000 | tf_op jit(solution)/shard_map/pallas_call | solution.py:120
  102.5 24.4 %all_to_all.20.heads_ref = bf16[6,128,256]{2,1,0:T(8,128)(2,1)S(1)} all-to-all(bf16[6,128,256]{2,1,0:T(8,128)(2,1)S(1)} %shard_map.65), channel_id=1, replica_groups=mesh['x'=4,'zh'=2,'y'=8,'c'=2,'zl'=6] {'zl'}, dimensions={0} | all-to-all | bytes 786432 | tf_op jit(solution)/shard_map/all_to_all | solution.py:241
  126.9 3.2 %all-gather.5.cloned.1.call-done.own_any = bf16[1536,768]{1,0:T(8,128)(2,1)} async-done(((bf16[192,768]{1,0:T(8,128)(2,1)}), bf16[1536,768]{1,0:T(8,128)(2,1)}) %all-gather.5.cloned.1.call-update) | async-done | bytes 2359312 | tf_op jit(solution)/shard_map/all_gather | solution.py:237
  130.1 5.8 %collective-permute-start.4 = (bf16[1536,768]{1,0:T(8,128)(2,1)}, bf16[1536,768]{1,0:T(8,128)(2,1)S(1)}, u32[]{:S(2)}, u32[]{:S(2)}) collective-permute-start(bf16[1536,768]{1,0:T(8,128)(2,1)} %all-gather.5.cloned.1.call-done.own_any), channel_id=1, source_target_pairs={{0,6},{1,7},{2,8},{3,9},{4,10},{5,11},{6,0},{7,1},{8,2},{9,3},{10,... | collective-permute-start | bytes 7077896 | tf_op jit(solution)/shard_map/ppermute | solution.py:24
  135.9 1.7 %copy-done = bf16[1536,768]{1,0:T(8,128)(2,1)S(1)} copy-done((bf16[1536,768]{1,0:T(8,128)(2,1)S(1)}, bf16[1536,768]{1,0:T(8,128)(2,1)}, u32[]{:S(2)}) %copy-start) | copy-done | bytes 2359320
  137.5 2.3 %shard_map.66.sums_ref = f32[1536,128]{1,0:T(8,128)S(1)} custom-call(s32[1]{0:T(128)} %bitcast.core_ref.place_ref, bf16[6,128,256]{2,1,0:T(8,128)(2,1)S(1)} %all_to_all.20.heads_ref, bf16[1536,768]{1,0:T(8,128)(2,1)S(1)} %copy-done), custom_call_target="tpu_custom_call" | custom-call | flops 300000000 | bytes 3000000 | tf_op jit(solution)/shard_map/pallas_call | solution.py:174
  140.2 1.6 %shard_map.67 = bf16[128,1536]{1,0:T(8,128)(2,1)} custom-call(s32[1]{0:T(128)} %bitcast.core_ref.place_ref, bf16[6,128,256]{2,1,0:T(8,128)(2,1)S(1)} %all_to_all.20.heads_ref, bf16[1536,768]{1,0:T(8,128)(2,1)S(1)} %collective-permute-done.4.other_ref, f32[1536,128]{1,0:T(8,128)S(1)} %shard_map.66.sums_ref), custom_call_target="tpu_custom_call" | custom-call | flops 300000000 | bytes 4000000 | tf_op jit(solution)/shard_map/pallas_call | solution.py:188
  (34 shorter events, 3.2 us)
Async XLA Ops:
  6.5 88.2 %all-gather.3.cloned.1.call-start = ((), (), s32[]{:S(2)}) async-start(), calls=%async_computation.4 | async-start | bytes 2752512 | tf_op jit(solution)/shard_map/all_gather | solution.py:222
  12.2 33.0 %all-to-all-start = ((bf16[24,48,128]{2,1,0:T(8,128)(2,1)}), bf16[24,48,128]{2,1,0:T(8,128)(2,1)S(1)}, u32[]{:S(2)}, u32[]{:S(2)}) async-start(bf16[24,48,128]{2,1,0:T(8,128)(2,1)} %bitcast.5), calls=%async_computation | async-start | bytes 589824 | tf_op jit(solution)/shard_map/all_to_all | solution.py:228
  46.2 17.5 %all-to-all-start.1 = ((bf16[8,48,384]{2,1,0:T(8,128)(2,1)}), bf16[8,48,384]{2,1,0:T(8,128)(2,1)S(1)}, u32[]{:S(2)}, u32[]{:S(2)}) async-start(bf16[8,48,384]{2,1,0:T(8,128)(2,1)} %broadcast_in_dim.47), calls=%async_computation.1 | async-start | bytes 589824 | tf_op jit(solution)/shard_map/all_to_all | solution.py:38
  64.8 29.9 %copy-start.1 = (f32[4]{0:T(128)S(1)}, f32[4]{0:T(128)}, u32[]{:S(2)}) copy-start(f32[4]{0:T(128)} %temp_ref.1) | copy-start | bytes 52
  64.8 20.3 %all-to-all-start.2 = ((bf16[4,384,384]{2,1,0:T(8,128)(2,1)}), bf16[4,384,384]{2,1,0:T(8,128)(2,1)S(1)}, u32[]{:S(2)}, u32[]{:S(2)}) async-start(bf16[4,384,384]{2,1,0:T(8,128)(2,1)} %broadcast_in_dim.49), calls=%async_computation.2 | async-start | bytes 2359296 | tf_op jit(solution)/shard_map/all_to_all | solution.py:38
  69.0 61.1 %all-gather.5.cloned.1.call-start = ((), (), s32[]{:S(2)}) async-start(), calls=%async_computation.5 | async-start | bytes 2654208 | tf_op jit(solution)/shard_map/all_gather | solution.py:237
  69.2 12.9 %collective-permute-start = (bf16[48,768]{1,0:T(8,128)(2,1)S(1)}, bf16[48,768]{1,0:T(8,128)(2,1)S(1)}, u32[]{:S(2)}, u32[]{:S(2)}) collective-permute-start(bf16[48,768]{1,0:T(8,128)(2,1)S(1)} %bitcast.38), channel_id=1, source_target_pairs={{0,192},{1,193},{2,194},{3,195},{4,196},{5,197},{6,198},{7,199},{8... | collective-permute-start | bytes 221192 | tf_op jit(solution)/shard_map/ppermute | solution.py:24
  72.5 9.6 %collective-permute-start.1 = (bf16[48,768]{1,0:T(8,128)(2,1)S(1)}, bf16[48,768]{1,0:T(8,128)(2,1)S(1)}, u32[]{:S(2)}, u32[]{:S(2)}) collective-permute-start(bf16[48,768]{1,0:T(8,128)(2,1)S(1)} %bitcast.39), channel_id=1, source_target_pairs={{0,576},{1,577},{2,578},{3,579},{4,580},{5,581},{6,582},{7,583},{8... | collective-permute-start | bytes 221192 | tf_op jit(solution)/shard_map/ppermute | solution.py:24
  76.2 8.9 %collective-permute-start.2 = (bf16[48,768]{1,0:T(8,128)(2,1)S(1)}, bf16[48,768]{1,0:T(8,128)(2,1)S(1)}, u32[]{:S(2)}, u32[]{:S(2)}) collective-permute-start(bf16[48,768]{1,0:T(8,128)(2,1)S(1)} %bitcast.40), channel_id=1, source_target_pairs={{0,384},{1,385},{2,386},{3,387},{4,388},{5,389},{6,390},{7,391},{8... | collective-permute-start | bytes 221192 | tf_op jit(solution)/shard_map/ppermute | solution.py:24
  85.1 0.7 copy-start.2
  85.9 8.9 %collective-permute-start.3 = (bf16[1536,384]{1,0:T(8,128)(2,1)S(1)}, bf16[1536,384]{1,0:T(8,128)(2,1)S(1)}, u32[]{:S(2)}, u32[]{:S(2)}) collective-permute-start(bf16[1536,384]{1,0:T(8,128)(2,1)S(1)} %bitcast.30), channel_id=1, source_target_pairs={{0,6},{1,7},{2,8},{3,9},{4,10},{5,11},{6,0},{7,1},{8,2},{9,3},{10,... | collective-permute-start | bytes 3538952 | tf_op jit(solution)/shard_map/ppermute | solution.py:24
  130.1 10.1 %collective-permute-start.4 = (bf16[1536,768]{1,0:T(8,128)(2,1)}, bf16[1536,768]{1,0:T(8,128)(2,1)S(1)}, u32[]{:S(2)}, u32[]{:S(2)}) collective-permute-start(bf16[1536,768]{1,0:T(8,128)(2,1)} %all-gather.5.cloned.1.call-done.own_any), channel_id=1, source_target_pairs={{0,6},{1,7},{2,8},{3,9},{4,10},{5,11},{6,0},{7,1},{8,2},{9,3},{10,... | collective-permute-start | bytes 7077896 | tf_op jit(solution)/shard_map/ppermute | solution.py:24
  135.9 1.7 %copy-start = (bf16[1536,768]{1,0:T(8,128)(2,1)S(1)}, bf16[1536,768]{1,0:T(8,128)(2,1)}, u32[]{:S(2)}) copy-start(bf16[1536,768]{1,0:T(8,128)(2,1)} %all-gather.5.cloned.1.call-done.own_any) | copy-start | bytes 7077892
Sparse Core Ops, SparseCore 0:
  9.9 77.4 all-gather.2
  89.8 40.2 all-gather.4
